TPU v7x, 32 devices: a whole 2x2x4 slice. The times are simulated.
32 devices in a mesh: member: 2 (over y), tile: 8 (over z, x), comp: 2 (over core).
Axes of the slice: x: 2, y: 2, z: 4, core: 2. Of those that a mesh axis runs over, the one named last changes fastest.
Arguments:
- sky_warmth_deviation: float32 [72, 1024, 128], P(None, ('member', 'tile', 'comp')), parts along dimension 1, may hold values from -6 to 6
- random_forcing_pattern: float32 [4, 1024, 128], P(None, ('member', 'tile', 'comp')), parts along dimension 1, may hold values from -6 to 6
- vertical_shape_curve: float32 [72], replicated, may hold values from 0.2 to 1
- sky_felt_skin_warmth: float32 [1024, 128], P(('member', 'tile', 'comp')), parts along dimension 0, may hold values from -6 to 6
- exchange_rate_factor: float32 [512, 128], P(('tile', 'comp')), may hold values from 0.05 to 0.5
- sky_diffusive_solve: float32 [72, 72], replicated, may hold values from -1 to 1
- crossing_share_matrix: bfloat16 [4, 128, 128], replicated, may hold values from -0.5 to 0.5
- owning_patch_number: int32 [512, 4], P(('tile', 'comp')), may hold values from 0 to 7, all different within a row; in each aligned block of 32 rows (0 to 31, 32 to 63, ...) at most 32 rows name the same one
- local_latitude_number: int32 [512, 4], P(('tile', 'comp')), may hold values from 0 to 15
- marine_warmth_deviation: float32 [62, 512, 128], P(None, ('member', 'tile', 'comp')), parts along dimension 1, may hold values from -6 to 6
- marine_brine_deviation: float32 [62, 512, 128], P(None, ('member', 'tile', 'comp')), parts along dimension 1, may hold values from -6 to 6
- wet_cell_indicator: int32 [256, 128], P(('tile', 'comp')), may hold values 0 or 1
- marine_diffusive_solve: float32 [62, 62], replicated, may hold values from -1 to 1
Outputs:
- atm_out: float32 [72, 1024, 128], P(None, ('member', 'tile', 'comp')), parts along dimension 1
- final_marine_warmth: float32 [62, 512, 128], P(None, ('member', 'tile', 'comp')), parts along dimension 1
- final_brine_level: float32 [62, 512, 128], P(None, ('member', 'tile', 'comp')), parts along dimension 1
There are 2 independent parts, one for each index of `member`. A program takes and returns all parts, laid end to end along the dimension named above; an argument that names none is the same for every part. Nothing has to cross between parts.
Inputs may be any that keep to these rules, and one draw needn't show every extreme that they name: `owning_patch_number`: each row names 4 different tiles; in the 32 rows of one device no tile is named by more than 32 rows, a bound that some block reaches.
All inputs are finite; a program needn't handle non-finite values. No bound on the sum of `wet_cell_indicator` on one device may be relied on, other than what follows from the above.
Results may differ from a plain program's by a relative error of at most 0.0003.
Values sent between devices are 32-bit elements; how exact they have to be, the bound alone decides.
No kernel may reach another device: no remote copies, remote signals or barrier semaphores. Data moves between devices by JAX's collectives and lax.ppermute only.
A program may use at most 64 MiB of HBM per device.

v0:
```python
import jax
import jax.numpy as jnp
from jax import lax
from jax.sharding import PartitionSpec as P

atm_diffusion = 0.2
ocean_diffusion = 0.2


def extended(cells, sides, width):
    for axis, dim in sides:
        count = lax.axis_size(axis)
        ends = count - 1
        head = lax.slice_in_dim(cells, 0, width, axis=dim)
        tail = lax.slice_in_dim(cells, cells.shape[dim] - width, cells.shape[dim], axis=dim)
        cells = jnp.concatenate(
            [
                lax.ppermute(tail, axis, [(i, (i + 1) % count) for i in range(ends)]),
                cells,
                lax.ppermute(head, axis, [((i + 1) % count, i) for i in range(ends)]),
            ],
            axis=dim,
        )
    return cells


def advance_air_column(bordered_arrays, forcing, surface, coefficient, vmix, vertical_shape_curve):
    center = bordered_arrays[:, 1:-1, :]
    laplace = (
        bordered_arrays[:, 2:, :]
        + bordered_arrays[:, :-2, :]
        + jnp.roll(center, 1, 2)
        + jnp.roll(center, -1, 2)
        - 4.0 * center
    )
    interface_heat_flux = coefficient * (center[-1] - surface)
    updated = center + atm_diffusion * laplace + vertical_shape_curve[:, None, None] * forcing[None]
    updated = jnp.concatenate([updated[:-1], (updated[-1] - interface_heat_flux)[None]], 0)
    mixed = jnp.einsum("kl,lrx->krx", vmix, updated, precision=lax.Precision.HIGHEST)
    return (mixed, interface_heat_flux)


def marine_refresh(bordered_arrays, temp, salt, wet_indicator_real, thermal_energy, vmix):
    levels = temp.shape[0]
    center = bordered_arrays[:, 1:-1, :]
    summed = (
        bordered_arrays[:, 2:, :]
        + bordered_arrays[:, :-2, :]
        + jnp.roll(center, 1, 2)
        + jnp.roll(center, -1, 2)
    )
    count = summed[2 * levels]
    laplace_t = wet_indicator_real * (summed[:levels] - temp * count)
    laplace_s = wet_indicator_real * (summed[levels : 2 * levels] - salt * count)
    temp_pre = temp + ocean_diffusion * laplace_t
    temp_pre = jnp.concatenate(
        [(temp_pre[0] + wet_indicator_real * thermal_energy)[None], temp_pre[1:]], 0
    )
    salt_pre = salt + ocean_diffusion * laplace_s
    mixed_t = jnp.einsum("kl,lrx->krx", vmix, temp_pre, precision=lax.Precision.HIGHEST)
    mixed_s = jnp.einsum("kl,lrx->krx", vmix, salt_pre, precision=lax.Precision.HIGHEST)
    temp_new = wet_indicator_real * mixed_t + (1.0 - wet_indicator_real) * temp
    salt_new = wet_indicator_real * mixed_s + (1.0 - wet_indicator_real) * salt
    return (temp_new, salt_new)


def body(
    sky_warmth_deviation,
    random_forcing_pattern,
    vertical_shape_curve,
    sky_felt_skin_warmth,
    exchange_rate_factor,
    sky_diffusive_solve,
    crossing_share_matrix,
    owning_patch_number,
    local_latitude_number,
    marine_warmth_deviation,
    marine_brine_deviation,
    wet_cell_indicator,
    marine_diffusive_solve,
):
    latitude_lines = sky_warmth_deviation.shape[1]
    breadth_extent = sky_warmth_deviation.shape[2]
    steps = random_forcing_pattern.shape[0]
    grand_total = jnp.zeros((latitude_lines, breadth_extent), jnp.float32)
    joint_condition = sky_warmth_deviation
    for advance_window in range(steps):
        bordered_arrays = extended(joint_condition, ((("tile", "comp"), 1),), 1)
        joint_condition, interface_heat_flux = advance_air_column(
            bordered_arrays,
            random_forcing_pattern[advance_window],
            sky_felt_skin_warmth,
            exchange_rate_factor,
            sky_diffusive_solve,
            vertical_shape_curve,
        )
        grand_total = grand_total + interface_heat_flux
    flux_mean = (grand_total / steps).astype(jnp.bfloat16)
    projected = jnp.einsum(
        "rc,kcd->rkd", flux_mean, crossing_share_matrix, preferred_element_type=jnp.float32
    )
    marine_latitudes = marine_warmth_deviation.shape[1]
    marine_breadth = marine_warmth_deviation.shape[2]
    row_ids = jnp.arange(marine_latitudes, dtype=jnp.int32)
    tiles = lax.axis_size("tile")
    topk = owning_patch_number.shape[1]
    capacity = max(2, latitude_lines * topk * 2 // tiles)
    flat_owner = owning_patch_number.reshape(-1)
    owner_hot = (flat_owner[:, None] == jnp.arange(tiles, dtype=jnp.int32)[None, :]).astype(
        jnp.int32
    )
    before = jnp.cumsum(owner_hot, 0) - owner_hot
    rank = jnp.sum(before * owner_hot, 1)
    slot_id = flat_owner * capacity + rank
    place = jnp.arange(tiles * capacity, dtype=jnp.int32)[:, None] == slot_id[None, :]
    send_values = jnp.dot(
        place.astype(jnp.float32),
        projected.reshape(-1, marine_breadth),
        precision=lax.Precision.HIGHEST,
    ).reshape(tiles, capacity, marine_breadth)
    send_targets = (
        jnp.sum(place.astype(jnp.int32) * (local_latitude_number.reshape(-1) + 1)[None, :], 1) - 1
    ).reshape(tiles, capacity)
    got_values, got_targets = (
        lax.all_to_all(send_values, "tile", split_axis=0, concat_axis=0, tiled=True),
        lax.all_to_all(send_targets, "tile", split_axis=0, concat_axis=0, tiled=True),
    )
    pick = (got_targets.reshape(-1)[None, :] == row_ids[:, None]).astype(jnp.float32)
    thermal_energy = jnp.dot(
        pick, got_values.reshape(-1, marine_breadth), precision=lax.Precision.HIGHEST
    )
    wet_indicator_real = wet_cell_indicator.astype(jnp.float32)
    piled_arrays = jnp.concatenate(
        [
            wet_indicator_real[None] * marine_warmth_deviation,
            wet_indicator_real[None] * marine_brine_deviation,
            wet_indicator_real[None],
        ],
        0,
    )
    bordered_arrays = extended(piled_arrays, ((("tile", "comp"), 1),), 1)
    final_marine_warmth, final_brine_level = marine_refresh(
        bordered_arrays,
        marine_warmth_deviation,
        marine_brine_deviation,
        wet_indicator_real,
        thermal_energy,
        marine_diffusive_solve,
    )
    return (joint_condition, final_marine_warmth, final_brine_level)


def solution(mesh):
    return jax.shard_map(
        body,
        mesh=mesh,
        in_specs=(
            P(None, ("member", "tile", "comp"), None),
            P(None, ("member", "tile", "comp"), None),
            P(),
            P(("member", "tile", "comp"), None),
            P(("tile", "comp"), None),
            P(),
            P(),
            P(("tile", "comp"), None),
            P(("tile", "comp"), None),
            P(None, ("member", "tile", "comp"), None),
            P(None, ("member", "tile", "comp"), None),
            P(("tile", "comp"), None),
            P(),
        ),
        out_specs=(
            P(None, ("member", "tile", "comp"), None),
            P(None, ("member", "tile", "comp"), None),
            P(None, ("member", "tile", "comp"), None),
        ),
        check_vma=False,
    )
```

profile of v0, /device:TPU:0, one launch (start us, length us, event | category | flops | bytes accessed | tf_op | source)
XLA Modules:
  0.0 97.3 jit_solution(10133740911347970990)
XLA Ops:
  0.6 1.8 %fusion.101 = (f32[72,1,128]{2,1,0:T(1,128)}, f32[72,1,128]{2,1,0:T(1,128)}) fusion(f32[72,32,128]{2,1,0:T(8,128)} %param.13), kind=kLoop, calls=%fused_computation.156 | loop fusion | bytes 147456 | tf_op jit(solution)/shard_map/slice | solution.py:14
  2.4 1.3 %collective-permute-start = (f32[72,1,128]{2,1,0:T(1,128)}, f32[72,1,128]{2,1,0:T(1,128)}, u32[]{:S(2)}, u32[]{:S(2)}) collective-permute-start(f32[72,1,128]{2,1,0:T(1,128)} %get-tuple-element.34), channel_id=1, source_target_pairs={{1,0},{2,1},{3,2},{4,3},{5,4},{6,5},{7,6},{8,7},{9,8},{10,9},{11,1... | collective-permute-start | bytes 110600 | tf_op jit(solution)/shard_map/ppermute | solution.py:20
  3.7 3.6 %collective-permute-start.1 = (f32[72,1,128]{2,1,0:T(1,128)}, f32[72,1,128]{2,1,0:T(1,128)}, u32[]{:S(2)}, u32[]{:S(2)}) collective-permute-start(f32[72,1,128]{2,1,0:T(1,128)} %get-tuple-element.35), channel_id=1, source_target_pairs={{0,1},{1,2},{2,3},{3,4},{4,5},{5,6},{6,7},{7,8},{8,9},{9,10},{10,1... | collective-permute-start | bytes 110600 | tf_op jit(solution)/shard_map/ppermute | solution.py:18
  8.1 1.3 %broadcast_multiply_fusion.1 = (f32[62,16,128]{2,1,0:T(8,128)S(1)}, f32[62,16,128]{2,1,0:T(8,128)S(1)}) fusion(f32[62,16,128]{2,1,0:T(8,128)} %param.22, f32[16,128]{1,0:T(8,128)S(1)} %get-tuple-element.50, f32[62,16,128]{2,1,0:T(8,128)} %param.23), kind=kLoop, calls=%fused_computation.85 | loop fusion | flops 253952 | bytes 2039808 | tf_op jit(solution)/shard_map/mul | solution.py:135
  10.1 1.3 %collective-permute-start.8 = (f32[125,1,128]{2,1,0:T(1,128)}, f32[125,1,128]{2,1,0:T(1,128)}, u32[]{:S(2)}, u32[]{:S(2)}) collective-permute-start(f32[125,1,128]{2,1,0:T(1,128)} %get-tuple-element.40), channel_id=1, source_target_pairs={{1,0},{2,1},{3,2},{4,3},{5,4},{6,5},{7,6},{8,7},{9,8},{10,9},{11,1... | collective-permute-start | bytes 192008 | tf_op jit(solution)/shard_map/ppermute | solution.py:20
  11.4 5.1 %collective-permute-start.9 = (f32[125,1,128]{2,1,0:T(1,128)}, f32[125,1,128]{2,1,0:T(1,128)}, u32[]{:S(2)}, u32[]{:S(2)}) collective-permute-start(f32[125,1,128]{2,1,0:T(1,128)} %get-tuple-element.41), channel_id=1, source_target_pairs={{0,1},{1,2},{2,3},{3,4},{4,5},{5,6},{6,7},{7,8},{8,9},{9,10},{10,1... | collective-permute-start | bytes 192008 | tf_op jit(solution)/shard_map/ppermute | solution.py:18
  18.2 6.1 %all-to-all-start = ((s32[8,1,32]{2,1,0:T(1,128)}), s32[8,1,32]{2,1,0:T(1,128)S(1)}, u32[]{:S(2)}, u32[]{:S(2)}) async-start(s32[8,1,32]{2,1,0:T(1,128)} %sub.70), calls=%async_computation | async-start | bytes 8192 | tf_op jit(solution)/shard_map/all_to_all | solution.py:126
  24.3 1.4 %fusion.99 = (f32[72,32,127]{2,1,0:T(8,128)S(1)}, f32[72,32,127]{2,1,0:T(8,128)}) fusion(f32[72,32,128]{2,1,0:T(8,128)S(1)} %copy-done.1), kind=kLoop, calls=%fused_computation.154 | loop fusion | bytes 4681728 | tf_op jit(solution)/shard_map/jit(_roll_static)/slice | solution.py:33
  25.7 1.8 %fusion.100 = (f32[72,32,1]{2,1,0:T(8,128)}, f32[72,32,1]{2,1,0:T(8,128)}) fusion(f32[72,32,128]{2,1,0:T(8,128)S(1)} %copy-done.1), kind=kLoop, calls=%fused_computation.155 | loop fusion | bytes 36864 | tf_op jit(solution)/shard_map/jit(_roll_static)/slice | solution.py:33
  27.7 1.7 %fusion.102 = (f32[125,16,127]{2,1,0:T(8,128)}, f32[125,16,127]{2,1,0:T(8,128)}) fusion(f32[125,16,128]{2,1,0:T(8,128)S(1)} %pad_maximum_fusion.17), kind=kLoop, calls=%fused_computation.157 | loop fusion | bytes 4064000 | tf_op jit(solution)/shard_map/jit(_roll_static)/slice | solution.py:50
  29.3 1.7 %fusion.103 = (f32[125,16,1]{2,1,0:T(8,128)}, f32[125,16,1]{2,1,0:T(8,128)}) fusion(f32[125,16,128]{2,1,0:T(8,128)S(1)} %pad_maximum_fusion.17), kind=kLoop, calls=%fused_computation.158 | loop fusion | bytes 32000 | tf_op jit(solution)/shard_map/jit(_roll_static)/slice | solution.py:50
  34.1 3.0 %fusion.31 = f32[72,32,128]{2,1,0:T(8,128)S(1)} fusion(f32[72,32,128]{2,1,0:T(8,128)S(1)} %copy-done.1, f32[72,1,128]{2,1,0:T(1,128)} %collective-permute-done.1, f32[72,1,128]{2,1,0:T(1,128)} %collective-permute-done, f32[72,32,127]{2,1,0:T(8,128)} %get-tuple-element.31, f32[72,32,1]{2,1,0:T(8,128)} %get-tuple-element.33, ...), kind=kLoop, calls=%fused_computation.41 | loop fusion | flops 3833856 | bytes 4808992 | tf_op jit(solution)/shard_map/add | solution.py:37
  38.1 1.2 %fusion.32 = f32[32,128,72]{1,2,0:T(8,128)S(1)} fusion(f32[1,32,128]{2,0,1:T(1,128)S(1)} %bitcast.152, f32[71,32,128]{2,0,1:T(8,128)S(1)} %copy.49, f32[72,72]{1,0:T(8,128)S(1)} %copy-done.9), kind=kOutput, calls=%fused_computation.43 | convolution fusion | flops 255098880 | bytes 2380032 | tf_op jit(solution)/shard_map/kl,lrx->krx/dot_general | solution.py:39
  40.5 1.4 %collective-permute-start.2 = (f32[72,1,128]{2,1,0:T(1,128)S(1)}, f32[72,1,128]{2,1,0:T(1,128)S(1)}, u32[]{:S(2)}, u32[]{:S(2)}) collective-permute-start(f32[72,1,128]{2,1,0:T(1,128)S(1)} %get-tuple-element.28), channel_id=1, source_target_pairs={{1,0},{2,1},{3,2},{4,3},{5,4},{6,5},{7,6},{8,7},{9,8},{10,9},{11,1... | collective-permute-start | bytes 110600 | tf_op jit(solution)/shard_map/ppermute | solution.py:20
  41.9 4.0 %collective-permute-start.3 = (f32[72,1,128]{2,1,0:T(1,128)S(1)}, f32[72,1,128]{2,1,0:T(1,128)S(1)}, u32[]{:S(2)}, u32[]{:S(2)}) collective-permute-start(f32[72,1,128]{2,1,0:T(1,128)S(1)} %get-tuple-element.29), channel_id=1, source_target_pairs={{0,1},{1,2},{2,3},{3,4},{4,5},{5,6},{6,7},{7,8},{8,9},{9,10},{10,1... | collective-permute-start | bytes 110600 | tf_op jit(solution)/shard_map/ppermute | solution.py:18
  46.0 1.7 %fusion.45 = f32[125,16,128]{2,1,0:T(8,128)S(1)} fusion(f32[125,1,128]{2,1,0:T(1,128)} %collective-permute-done.9, f32[1,16,128]{2,1,0:T(8,128)S(1)} %get-tuple-element.51, f32[62,16,128]{2,1,0:T(8,128)S(1)} %get-tuple-element.49, f32[62,16,128]{2,1,0:T(8,128)S(1)} %get-tuple-element.48, f32[125,1,128]{2,1,0:T(1,128)} %collective-permute-done.8, ...), kind=kLoop, calls=%fused_computation.64 | loop fusion | flops 2816000 | bytes 4224000 | tf_op jit(solution)/shard_map/add | solution.py:47
  48.9 1.4 %fusion.50 = (f32[62,16,128]{2,1,0:T(8,128)S(1)}, f32[62,16,128]{2,1,0:T(8,128)S(1)}) fusion(f32[62,16,128]{2,1,0:T(8,128)S(1)} %copy-done.6, f32[125,16,1]{2,1,0:T(8,128)S(1)} %copy-done.4, f32[125,16,127]{2,1,0:T(8,128)S(1)} %copy-done.2, f32[125,16,127]{2,1,0:T(8,128)S(1)} %copy-done.3, f32[125,16,1]{2,1,0:T(8,128)S(1)} %copy-done.5, ...), kind=kLoop, calls=%fused_computation.78 | loop fusion | flops 2666496 | bytes 5755904 | tf_op jit(solution)/shard_map/add | solution.py:59
  53.1 1.1 %fusion.24 = f32[72,32,128]{2,1,0:T(8,128)S(1)} fusion(f32[72,32,128]{2,1,0:T(8,128)S(1)} %bitcast.135, f32[72,1,128]{2,1,0:T(1,128)S(1)} %collective-permute-done.3, f32[72,1,128]{2,1,0:T(1,128)S(1)} %collective-permute-done.2, f32[72,32,127]{2,1,0:T(8,128)S(1)} %get-tuple-element.25, f32[72,32,1]{2,1,0:T(8,128)S(1)} %get-tuple-element.27, ...), kind=kLoop, calls=%fused_computation.32 | loop fusion | flops 3833856 | bytes 4808992 | tf_op jit(solution)/shard_map/add | solution.py:37
  54.4 1.9 %fusion.39 = f32[32,128,72]{1,2,0:T(8,128)S(1)} fusion(f32[72,32,128]{2,1,0:T(8,128)S(1)} %pad_maximum_fusion.8, f32[72,72]{1,0:T(8,128)S(1)} %copy-done.9), kind=kOutput, calls=%fused_computation.55 | convolution fusion | flops 254803968 | bytes 2380032 | tf_op jit(solution)/shard_map/kl,lrx->krx/dot_general | solution.py:39
  57.0 1.3 %collective-permute-start.4 = (f32[72,1,128]{2,1,0:T(1,128)S(1)}, f32[72,1,128]{2,1,0:T(1,128)S(1)}, u32[]{:S(2)}, u32[]{:S(2)}) collective-permute-start(f32[72,1,128]{2,1,0:T(1,128)S(1)} %get-tuple-element.22), channel_id=1, source_target_pairs={{1,0},{2,1},{3,2},{4,3},{5,4},{6,5},{7,6},{8,7},{9,8},{10,9},{11,1... | collective-permute-start | bytes 110600 | tf_op jit(solution)/shard_map/ppermute | solution.py:20
  58.4 4.3 %collective-permute-start.5 = (f32[72,1,128]{2,1,0:T(1,128)S(1)}, f32[72,1,128]{2,1,0:T(1,128)S(1)}, u32[]{:S(2)}, u32[]{:S(2)}) collective-permute-start(f32[72,1,128]{2,1,0:T(1,128)S(1)} %get-tuple-element.23), channel_id=1, source_target_pairs={{0,1},{1,2},{2,3},{3,4},{4,5},{5,6},{6,7},{7,8},{8,9},{9,10},{10,1... | collective-permute-start | bytes 110600 | tf_op jit(solution)/shard_map/ppermute | solution.py:18
  63.5 1.1 %fusion.17 = f32[72,32,128]{2,1,0:T(8,128)S(1)} fusion(f32[72,32,128]{2,1,0:T(8,128)S(1)} %bitcast.141, f32[72,1,128]{2,1,0:T(1,128)S(1)} %collective-permute-done.5, f32[72,1,128]{2,1,0:T(1,128)S(1)} %collective-permute-done.4, f32[72,32,127]{2,1,0:T(8,128)S(1)} %get-tuple-element.19, f32[72,32,1]{2,1,0:T(8,128)S(1)} %get-tuple-element.21, ...), kind=kLoop, calls=%fused_computation.23 | loop fusion | flops 3833856 | bytes 4808992 | tf_op jit(solution)/shard_map/add | solution.py:37
  64.8 1.9 %fusion.37 = f32[32,128,72]{1,2,0:T(8,128)S(1)} fusion(f32[72,32,128]{2,1,0:T(8,128)S(1)} %pad_maximum_fusion.9, f32[72,72]{1,0:T(8,128)S(1)} %copy-done.9), kind=kOutput, calls=%fused_computation.52 | convolution fusion | flops 254803968 | bytes 2380032 | tf_op jit(solution)/shard_map/kl,lrx->krx/dot_general | solution.py:39
  66.9 1.8 %fusion.90 = (f32[72,32,127]{2,1,0:T(8,128)}, f32[72,32,127]{2,1,0:T(8,128)}) fusion(f32[72,32,128]{2,1,0:T(8,128)S(1)} %bitcast.144), kind=kLoop, calls=%fused_computation.145 | loop fusion | bytes 4681728 | tf_op jit(solution)/shard_map/jit(_roll_static)/slice | solution.py:33
  68.8 1.8 %fusion.91 = (f32[72,32,1]{2,1,0:T(8,128)}, f32[72,32,1]{2,1,0:T(8,128)}) fusion(f32[72,32,128]{2,1,0:T(8,128)S(1)} %bitcast.145), kind=kLoop, calls=%fused_computation.146 | loop fusion | bytes 36864 | tf_op jit(solution)/shard_map/jit(_roll_static)/slice | solution.py:33
  71.5 1.3 %collective-permute-start.6 = (f32[72,1,128]{2,1,0:T(1,128)}, f32[72,1,128]{2,1,0:T(1,128)S(1)}, u32[]{:S(2)}, u32[]{:S(2)}) collective-permute-start(f32[72,1,128]{2,1,0:T(1,128)} %get-tuple-element.16), channel_id=1, source_target_pairs={{1,0},{2,1},{3,2},{4,3},{5,4},{6,5},{7,6},{8,7},{9,8},{10,9},{11,1... | collective-permute-start | bytes 110600 | tf_op jit(solution)/shard_map/ppermute | solution.py:20
  72.8 4.5 %collective-permute-start.7 = (f32[72,1,128]{2,1,0:T(1,128)}, f32[72,1,128]{2,1,0:T(1,128)S(1)}, u32[]{:S(2)}, u32[]{:S(2)}) collective-permute-start(f32[72,1,128]{2,1,0:T(1,128)} %get-tuple-element.17), channel_id=1, source_target_pairs={{0,1},{1,2},{2,3},{3,4},{4,5},{5,6},{6,7},{7,8},{8,9},{9,10},{10,1... | collective-permute-start | bytes 110600 | tf_op jit(solution)/shard_map/ppermute | solution.py:18
  78.2 8.8 %all-to-all-start.1 = ((f32[8,32,128]{2,1,0:T(8,128)}), f32[8,32,128]{2,1,0:T(8,128)S(1)}, u32[]{:S(2)}, u32[]{:S(2)}) async-start(f32[8,32,128]{2,1,0:T(8,128)} %fusion.54), calls=%async_computation.1 | async-start | bytes 262144 | tf_op jit(solution)/shard_map/all_to_all | solution.py:125
  86.9 3.4 %fusion.10 = f32[72,32,128]{2,1,0:T(8,128)S(1)} fusion(f32[72,32,128]{2,1,0:T(8,128)S(1)} %bitcast.148, f32[72,1,128]{2,1,0:T(1,128)S(1)} %collective-permute-done.7, f32[72,1,128]{2,1,0:T(1,128)S(1)} %collective-permute-done.6, f32[72,32,127]{2,1,0:T(8,128)} %get-tuple-element.13, f32[72,32,1]{2,1,0:T(8,128)} %get-tuple-element.15, ...), kind=kLoop, calls=%fused_computation.14 | loop fusion | flops 3833856 | bytes 4808992 | tf_op jit(solution)/shard_map/add | solution.py:37
  91.2 1.9 %convolution_bitcast_fusion = f32[72,32,128]{2,0,1:T(8,128)S(1)} fusion(f32[72,32,128]{2,1,0:T(8,128)S(1)} %pad_maximum_fusion.10, f32[72,72]{1,0:T(8,128)S(1)} %copy-done.9), kind=kOutput, calls=%fused_computation | convolution fusion | flops 254803968 | bytes 2380032 | tf_op jit(solution)/shard_map/kl,lrx->krx/dot_general | solution.py:39
  93.1 1.2 %copy.63 = f32[72,32,128]{2,1,0:T(8,128)} copy(f32[72,32,128]{2,0,1:T(8,128)S(1)} %convolution_bitcast_fusion) | data formatting | bytes 2359296
  96.3 1.1 %copy.64 = f32[62,16,128]{2,1,0:T(8,128)} copy(f32[62,16,128]{2,0,1:T(8,128)S(1)} %fusion.3) | data formatting | bytes 1015808
  (131 shorter events, 18.9 us)
Async XLA Ops:
  0.6 70.6 %copy-start = (bf16[4,128,128]{2,1,0:T(8,128)(2,1)S(1)}, bf16[4,128,128]{2,1,0:T(8,128)(2,1)}, u32[]{:S(2)}) copy-start(bf16[4,128,128]{2,1,0:T(8,128)(2,1)} %param.19) | copy-start | bytes 393220
  2.4 31.7 %collective-permute-start = (f32[72,1,128]{2,1,0:T(1,128)}, f32[72,1,128]{2,1,0:T(1,128)}, u32[]{:S(2)}, u32[]{:S(2)}) collective-permute-start(f32[72,1,128]{2,1,0:T(1,128)} %get-tuple-element.34), channel_id=1, source_target_pairs={{1,0},{2,1},{3,2},{4,3},{5,4},{6,5},{7,6},{8,7},{9,8},{10,9},{11,1... | collective-permute-start | bytes 110600 | tf_op jit(solution)/shard_map/ppermute | solution.py:20
  3.7 30.4 %collective-permute-start.1 = (f32[72,1,128]{2,1,0:T(1,128)}, f32[72,1,128]{2,1,0:T(1,128)}, u32[]{:S(2)}, u32[]{:S(2)}) collective-permute-start(f32[72,1,128]{2,1,0:T(1,128)} %get-tuple-element.35), channel_id=1, source_target_pairs={{0,1},{1,2},{2,3},{3,4},{4,5},{5,6},{6,7},{7,8},{8,9},{9,10},{10,1... | collective-permute-start | bytes 110600 | tf_op jit(solution)/shard_map/ppermute | solution.py:18
  8.1 2.0 %copy-start.14 = (f32[16,128]{1,0:T(8,128)}, f32[16,128]{1,0:T(8,128)S(1)}, u32[]{:S(2)}) copy-start(f32[16,128]{1,0:T(8,128)S(1)} %get-tuple-element.50) | copy-start | bytes 24580
  8.1 8.5 %copy-start.31 = (s32[32,4]{0,1:T(4,128)S(1)}, s32[32,4]{0,1:T(4,128)}, u32[]{:S(2)}) copy-start(s32[32,4]{0,1:T(4,128)} %param.20) | copy-start | bytes 1540
  9.3 7.8 %copy-start.32 = (s32[32,4]{0,1:T(4,128)S(1)}, s32[32,4]{0,1:T(4,128)}, u32[]{:S(2)}) copy-start(s32[32,4]{0,1:T(4,128)} %param.21) | copy-start | bytes 1540
  9.3 15.0 %copy-start.1 = (f32[72,32,128]{2,1,0:T(8,128)S(1)}, f32[72,32,128]{2,1,0:T(8,128)}, u32[]{:S(2)}) copy-start(f32[72,32,128]{2,1,0:T(8,128)} %param.13) | copy-start | bytes 3538948
  10.1 35.8 %collective-permute-start.8 = (f32[125,1,128]{2,1,0:T(1,128)}, f32[125,1,128]{2,1,0:T(1,128)}, u32[]{:S(2)}, u32[]{:S(2)}) collective-permute-start(f32[125,1,128]{2,1,0:T(1,128)} %get-tuple-element.40), channel_id=1, source_target_pairs={{1,0},{2,1},{3,2},{4,3},{5,4},{6,5},{7,6},{8,7},{9,8},{10,9},{11,1... | collective-permute-start | bytes 192008 | tf_op jit(solution)/shard_map/ppermute | solution.py:20
  11.4 34.6 %collective-permute-start.9 = (f32[125,1,128]{2,1,0:T(1,128)}, f32[125,1,128]{2,1,0:T(1,128)}, u32[]{:S(2)}, u32[]{:S(2)}) collective-permute-start(f32[125,1,128]{2,1,0:T(1,128)} %get-tuple-element.41), channel_id=1, source_target_pairs={{0,1},{1,2},{2,3},{3,4},{4,5},{5,6},{6,7},{7,8},{8,9},{9,10},{10,1... | collective-permute-start | bytes 192008 | tf_op jit(solution)/shard_map/ppermute | solution.py:18
  18.2 14.0 %all-to-all-start = ((s32[8,1,32]{2,1,0:T(1,128)}), s32[8,1,32]{2,1,0:T(1,128)S(1)}, u32[]{:S(2)}, u32[]{:S(2)}) async-start(s32[8,1,32]{2,1,0:T(1,128)} %sub.70), calls=%async_computation | async-start | bytes 8192 | tf_op jit(solution)/shard_map/all_to_all | solution.py:126
  29.3 2.3 %copy-start.25 = (f32[4,32,128]{2,1,0:T(8,128)S(1)}, f32[4,32,128]{2,1,0:T(8,128)}, u32[]{:S(2)}) copy-start(f32[4,32,128]{2,1,0:T(8,128)} %param.14) | copy-start | bytes 196612
  29.3 4.8 %copy-start.26 = (f32[72]{0:T(128)S(1)}, f32[72]{0:T(128)}, u32[]{:S(2)}) copy-start(f32[72]{0:T(128)} %param.15) | copy-start | bytes 868
  40.0 6.0 %copy-start.2 = (f32[125,16,127]{2,1,0:T(8,128)S(1)}, f32[125,16,127]{2,1,0:T(8,128)}, u32[]{:S(2)}) copy-start(f32[125,16,127]{2,1,0:T(8,128)} %get-tuple-element.36) | copy-start | bytes 3048004
  40.0 6.0 %copy-start.3 = (f32[125,16,127]{2,1,0:T(8,128)S(1)}, f32[125,16,127]{2,1,0:T(8,128)}, u32[]{:S(2)}) copy-start(f32[125,16,127]{2,1,0:T(8,128)} %get-tuple-element.37) | copy-start | bytes 3048004
  40.0 6.0 %copy-start.4 = (f32[125,16,1]{2,1,0:T(8,128)S(1)}, f32[125,16,1]{2,1,0:T(8,128)}, u32[]{:S(2)}) copy-start(f32[125,16,1]{2,1,0:T(8,128)} %get-tuple-element.38) | copy-start | bytes 24004
  40.0 6.0 %copy-start.5 = (f32[125,16,1]{2,1,0:T(8,128)S(1)}, f32[125,16,1]{2,1,0:T(8,128)}, u32[]{:S(2)}) copy-start(f32[125,16,1]{2,1,0:T(8,128)} %get-tuple-element.39) | copy-start | bytes 24004
  40.5 12.6 %collective-permute-start.2 = (f32[72,1,128]{2,1,0:T(1,128)S(1)}, f32[72,1,128]{2,1,0:T(1,128)S(1)}, u32[]{:S(2)}, u32[]{:S(2)}) collective-permute-start(f32[72,1,128]{2,1,0:T(1,128)S(1)} %get-tuple-element.28), channel_id=1, source_target_pairs={{1,0},{2,1},{3,2},{4,3},{5,4},{6,5},{7,6},{8,7},{9,8},{10,9},{11,1... | collective-permute-start | bytes 110600 | tf_op jit(solution)/shard_map/ppermute | solution.py:20
  41.9 11.2 %collective-permute-start.3 = (f32[72,1,128]{2,1,0:T(1,128)S(1)}, f32[72,1,128]{2,1,0:T(1,128)S(1)}, u32[]{:S(2)}, u32[]{:S(2)}) collective-permute-start(f32[72,1,128]{2,1,0:T(1,128)S(1)} %get-tuple-element.29), channel_id=1, source_target_pairs={{0,1},{1,2},{2,3},{3,4},{4,5},{5,6},{6,7},{7,8},{8,9},{9,10},{10,1... | collective-permute-start | bytes 110600 | tf_op jit(solution)/shard_map/ppermute | solution.py:18
  51.2 1.9 %copy-start.24 = (f32[32,128]{1,0:T(8,128)S(1)}, f32[32,128]{1,0:T(8,128)}, u32[]{:S(2)}) copy-start(f32[32,128]{1,0:T(8,128)} %get-tuple-element.43) | copy-start | bytes 49156
  57.0 6.0 %collective-permute-start.4 = (f32[72,1,128]{2,1,0:T(1,128)S(1)}, f32[72,1,128]{2,1,0:T(1,128)S(1)}, u32[]{:S(2)}, u32[]{:S(2)}) collective-permute-start(f32[72,1,128]{2,1,0:T(1,128)S(1)} %get-tuple-element.22), channel_id=1, source_target_pairs={{1,0},{2,1},{3,2},{4,3},{5,4},{6,5},{7,6},{8,7},{9,8},{10,9},{11,1... | collective-permute-start | bytes 110600 | tf_op jit(solution)/shard_map/ppermute | solution.py:20
  58.3 5.1 %copy-start.23 = (f32[32,128]{1,0:T(8,128)S(1)}, f32[32,128]{1,0:T(8,128)}, u32[]{:S(2)}) copy-start(f32[32,128]{1,0:T(8,128)} %get-tuple-element.45) | copy-start | bytes 49156
  58.4 5.1 %collective-permute-start.5 = (f32[72,1,128]{2,1,0:T(1,128)S(1)}, f32[72,1,128]{2,1,0:T(1,128)S(1)}, u32[]{:S(2)}, u32[]{:S(2)}) collective-permute-start(f32[72,1,128]{2,1,0:T(1,128)S(1)} %get-tuple-element.23), channel_id=1, source_target_pairs={{0,1},{1,2},{2,3},{3,4},{4,5},{5,6},{6,7},{7,8},{8,9},{9,10},{10,1... | collective-permute-start | bytes 110600 | tf_op jit(solution)/shard_map/ppermute | solution.py:18
  68.8 8.5 %copy-start.30 = (s32[128]{0:T(128)S(1)}, s32[128]{0:T(128)}, u32[]{:S(2)}) copy-start(s32[128]{0:T(128)} %copy-done.29) | copy-start | bytes 1540
  71.5 15.5 %collective-permute-start.6 = (f32[72,1,128]{2,1,0:T(1,128)}, f32[72,1,128]{2,1,0:T(1,128)S(1)}, u32[]{:S(2)}, u32[]{:S(2)}) collective-permute-start(f32[72,1,128]{2,1,0:T(1,128)} %get-tuple-element.16), channel_id=1, source_target_pairs={{1,0},{2,1},{3,2},{4,3},{5,4},{6,5},{7,6},{8,7},{9,8},{10,9},{11,1... | collective-permute-start | bytes 110600 | tf_op jit(solution)/shard_map/ppermute | solution.py:20
  72.8 14.2 %collective-permute-start.7 = (f32[72,1,128]{2,1,0:T(1,128)}, f32[72,1,128]{2,1,0:T(1,128)S(1)}, u32[]{:S(2)}, u32[]{:S(2)}) collective-permute-start(f32[72,1,128]{2,1,0:T(1,128)} %get-tuple-element.17), channel_id=1, source_target_pairs={{0,1},{1,2},{2,3},{3,4},{4,5},{5,6},{6,7},{7,8},{8,9},{9,10},{10,1... | collective-permute-start | bytes 110600 | tf_op jit(solution)/shard_map/ppermute | solution.py:18
  78.2 17.0 %all-to-all-start.1 = ((f32[8,32,128]{2,1,0:T(8,128)}), f32[8,32,128]{2,1,0:T(8,128)S(1)}, u32[]{:S(2)}, u32[]{:S(2)}) async-start(f32[8,32,128]{2,1,0:T(8,128)} %fusion.54), calls=%async_computation.1 | async-start | bytes 262144 | tf_op jit(solution)/shard_map/all_to_all | solution.py:125
  93.0 2.1 %copy-start.22 = (s32[16,128]{1,0:T(8,128)S(1)}, s32[16,128]{1,0:T(8,128)}, u32[]{:S(2)}) copy-start(s32[16,128]{1,0:T(8,128)} %param.24) | copy-start | bytes 24580
  93.0 2.1 %copy-start.28 = (s32[256]{0:T(256)S(1)}, s32[256]{0:T(256)}, u32[]{:S(2)}) copy-start(s32[256]{0:T(256)} %eq.64) | copy-start | bytes 3076
  93.1 2.2 %copy-start.8 = (f32[61,16,128]{2,1,0:T(8,128)S(1)}, f32[61,16,128]{2,1,0:T(8,128)}, u32[]{:S(2)}) copy-start(f32[61,16,128]{2,1,0:T(8,128)} %slice.297) | copy-start | bytes 1499140
  93.1 2.3 %copy-start.16 = (f32[16,128]{1,0:T(8,128)S(1)}, f32[16,128]{1,0:T(8,128)}, u32[]{:S(2)}) copy-start(f32[16,128]{1,0:T(8,128)} %copy-done.14) | copy-start | bytes 24580
  93.1 2.3 %copy-start.18 = (f32[62,62]{1,0:T(8,128)S(1)}, f32[62,62]{1,0:T(8,128)}, u32[]{:S(2)}) copy-start(f32[62,62]{1,0:T(8,128)} %param.25) | copy-start | bytes 46132
  93.1 2.3 %copy-start.20 = (f32[16,128]{1,0:T(8,128)S(1)}, f32[16,128]{1,0:T(8,128)}, u32[]{:S(2)}) copy-start(f32[16,128]{1,0:T(8,128)} %broadcast_subtract_fusion) | copy-start | bytes 24580
  (13 other events, 14.5 us)
where the time goes:
time: 98.3 us; the launch traced here: 97.3 us
  starting transfers between devices  42.9 us (44%)
  local copies, waits for them, and re-layouts  24.4 us (25%)
  other arithmetic  17.6 us (18%)
  matrix products  9.81 us (10%)
  between operations  1.36 us (1%)
  waiting for transfers between devices  1.24 us (1%)
    ppermute x5, starting transfers between devices, extended(): lax.ppermute(tail, axis, [(i, (i + 1) % count) for i in range(ends)])  21.5 us
    all_to_all x1, starting transfers between devices, body(): lax.all_to_all(send_values, 'tile', split_axis=0, concat_axis=0, tiled=True)  8.76 us
    add x4, other arithmetic, advance_air_column(): center + atm_diffusion * laplace  8.69 us
    slice x8, local copies, waits for them, and re-layouts, advance_air_column(): jnp.roll(center, -1, 2)  8.56 us
    dot_general x4, matrix products, advance_air_column(): jnp.einsum('kl,lrx->krx', vmix, updated, precision=lax.Precision.HIGHEST)  6.86 us
    ppermute x5, starting transfers between devices, extended(): lax.ppermute(head, axis, [((i + 1) % count, i) for i in range(ends)])  6.57 us
    all_to_all x1, starting transfers between devices, body(): lax.all_to_all(send_targets, 'tile', split_axis=0, concat_axis=0, tiled=T...  6.11 us
    unnamed x70, local copies, waits for them, and re-layouts  4.63 us
  transfers between devices with their start and end apart: 12, of which 2 were waited for; matrix products, arithmetic and copies ran while one was open for 36% of the time, Pallas kernels for 0%

commit v1 on v0

v1 whole, which is shorter than its diff:
```python
import functools

import jax
import jax.numpy as jnp
from jax import lax
from jax.experimental import pallas as pl
from jax.experimental.pallas import tpu as pltpu
from jax.sharding import PartitionSpec as P

atm_diffusion = 0.2
ocean_diffusion = 0.2
HALO = 4
EXACT = lax.Precision.HIGHEST
VMEM = pl.BlockSpec(memory_space=pltpu.VMEM)
f32, bf16 = jnp.float32, jnp.bfloat16


def up_to(n, m):
    return -(-n // m) * m


def call(kernel, out_shape, *args, scratch=(), in_specs=None, flops=0, moved=0):
    return pl.pallas_call(
        kernel,
        out_shape=out_shape,
        in_specs=in_specs or [VMEM] * len(args),
        out_specs=jax.tree.map(lambda _: VMEM, out_shape),
        scratch_shapes=list(scratch),
        compiler_params=pltpu.CompilerParams(vmem_limit_bytes=24 * 2**20),
        cost_estimate=pl.CostEstimate(flops=flops, bytes_accessed=moved, transcendentals=0),
    )(*args)


def pack_kernel(sizes, sky, forcing, surface, rate, warmth, brine, wet, up, down):
    levels, rows, steps, sea_levels, sea_rows, stride, sea_stride = sizes
    width = sky.shape[1]
    m = wet[...].astype(f32)
    for out, first, sea_row in ((up, 0, 0), (down, rows - HALO, sea_rows - 1)):
        for j in range(HALO):
            row = first + j
            out[j * stride : j * stride + levels, :] = sky[pl.ds(row, levels, stride=rows), :]
            base = j * stride + levels
            tail = [forcing[s * rows + row : s * rows + row + 1, :] for s in range(steps)]
            tail += [surface[row : row + 1, :], rate[row : row + 1, :], jnp.ones((1, width), f32)]
            tail += [jnp.zeros((stride - levels - len(tail), width), f32)]
            out[base : (j + 1) * stride, :] = jnp.concatenate(tail, 0)
        base = HALO * stride
        edge = m[sea_row : sea_row + 1]
        out[base : base + sea_levels, :] = warmth[pl.ds(sea_row, sea_levels, stride=sea_rows), :] * edge
        base += sea_stride
        out[base : base + sea_levels, :] = brine[pl.ds(sea_row, sea_levels, stride=sea_rows), :] * edge
        base += sea_stride
        out[base : base + 8, :] = jnp.concatenate([edge, jnp.zeros((7, width), f32)], 0)


def split(x):
    high = x.astype(bf16)
    return high, (x - high.astype(f32)).astype(bf16)


def three_terms(w, depth):
    high = w.astype(bf16).astype(f32)
    low = w - high
    return (high + pltpu.roll(high, depth, 1) + pltpu.roll(low, 2 * depth, 1)).astype(bf16)


def local_kernel(sizes, vmix, curve, sea_mix, sky, rows_of_mix, source_rows, weights, sea_weights, sea_first, own):
    levels, rows, steps, sea_levels, sea_rows, stride, sea_stride = sizes
    width = sky.shape[1]
    depth = up_to(levels + 2 * steps, 16)
    v = vmix[...]
    dot = functools.partial(jnp.dot, precision=EXACT, preferred_element_type=f32)
    powers = [v]
    for _ in range(steps - 1):
        powers.append(dot(v, powers[-1]))
    last = (lax.broadcasted_iota(jnp.int32, (levels, width), 0) == levels - 1).astype(f32)
    for s in range(1, steps):
        rows_of_mix[(s - 1) * levels : s * levels, :] = lax.dot_general(
            powers[s - 1], last, (((0,), (0,)), ((), ())), precision=EXACT, preferred_element_type=f32
        )
    by_curve = jnp.broadcast_to(curve[...], (width, levels))
    of_curve = [
        lax.dot_general(p, by_curve, (((1,), (1,)), ((), ())), precision=EXACT, preferred_element_type=f32)
        for p in powers
    ]
    of_last = [jnp.broadcast_to(p[:, levels - 1 : levels], (levels, width)) for p in powers]
    found = [of_curve[i][levels - 1 :] for i in range(steps - 1)]
    found += [of_last[i][levels - 1 :] for i in range(steps - 1)]
    found += [jnp.zeros((8 - len(found), width), f32)]
    source_rows[...] = jnp.concatenate(found, 0)
    lane = lax.broadcasted_iota(jnp.int32, (levels, width), 1)
    wide = jnp.concatenate(
        [powers[-1] * atm_diffusion**steps, jnp.zeros((levels, width - levels), f32)], 1
    )
    for j in range(steps):
        factor = atm_diffusion ** (steps - 1 - j)
        wide = jnp.where(lane == levels + j, of_curve[steps - 1 - j] * factor, wide)
        wide = jnp.where(lane == levels + steps + j, of_last[steps - 1 - j] * -factor, wide)
    wide = jnp.concatenate([wide, jnp.zeros((levels, width), f32)], 1)
    wide = jnp.concatenate([wide, jnp.zeros((weights.shape[0] - levels, 2 * width), f32)], 0)
    weights[...] = three_terms(wide, depth)
    sea = sea_mix[...]
    sea = jnp.concatenate([sea, jnp.zeros((sea_levels, 2 * width - sea_levels), f32)], 1)
    sea = jnp.concatenate([sea, jnp.zeros((sea_stride - sea_levels, 2 * width), f32)], 0)
    sea_weights[...] = three_terms(sea, sea_stride)
    sea_first[...] = jnp.broadcast_to(sea[:, 0:1], sea_first.shape)
    sums = [jnp.zeros((rows, width), f32) for _ in range(steps - 1)]
    for l in range(levels):
        x = sky[l * rows : (l + 1) * rows, :]
        for s in range(steps - 1):
            sums[s] = sums[s] + rows_of_mix[s * levels + l : s * levels + l + 1, :] * x
    for s in range(steps - 1):
        own[s * rows : (s + 1) * rows, :] = sums[s]


def cross(x):
    n, w = x.shape
    return (
        x + pltpu.roll(x, 1, 0) + pltpu.roll(x, n - 1, 0) + pltpu.roll(x, 1, 1) + pltpu.roll(x, w - 1, 1)
    )


def masked(x, rows, inside):
    return jnp.concatenate([x[:rows], x[rows:] * inside], 0)


def flux_kernel(
    sizes, sky, forcing, surface, rate, rows_of_mix, source_rows, own, owners, locals_, below, above,
    sent, fluxes, halo
):
    levels, rows, steps, sea_levels, sea_rows, stride, sea_stride = sizes
    width = sky.shape[1]
    halo[: HALO * stride, :] = below[: HALO * stride, :]
    halo[HALO * stride :, :] = above[: HALO * stride, :]

    def edge(l):
        return halo[pl.ds(l, 2 * HALO, stride=stride), :]

    inside = edge(levels + steps + 2)
    sums = [jnp.zeros((2 * HALO, width), f32) for _ in range(steps - 1)]
    for l in range(levels):
        x = edge(l)
        for s in range(steps - 1):
            sums[s] = sums[s] + rows_of_mix[s * levels + l : s * levels + l + 1, :] * x
    tops = [jnp.concatenate([sky[...], edge(levels - 1)], 0)]
    tops += [jnp.concatenate([own[s * rows : (s + 1) * rows, :], sums[s]], 0) for s in range(steps - 1)]
    surf = jnp.concatenate([surface[...], edge(levels + steps)], 0)
    coef = jnp.concatenate([rate[...], edge(levels + steps + 1)], 0)
    force = [
        jnp.concatenate([forcing[s * rows : (s + 1) * rows, :], edge(levels + s)], 0) for s in range(steps)
    ]

    flux = []
    for s in range(steps):
        state = tops[s]
        for i in range(s):
            m = s - 1 - i
            state = masked(cross(state) * atm_diffusion, rows, inside)
            state = state + source_rows[m : m + 1, :] * force[i]
            state = state - source_rows[steps - 1 + m : steps + m, :] * flux[i]
        flux.append(coef * (state - surf))
        fluxes[s * (rows + 2 * HALO) : (s + 1) * (rows + 2 * HALO), :] = flux[s]
    total = flux[0][:rows]
    for s in range(1, steps):
        total = total + flux[s][:rows]
    mean = (total / steps).astype(bf16).astype(f32)
    times = width // rows
    owner = owners[...].astype(f32)
    row = locals_[...].astype(f32)
    table = jnp.concatenate(
        [jnp.concatenate([owner] * times, 1), jnp.concatenate([row] * times, 1)], 0
    )
    per = mean.shape[0] + table.shape[0]
    for t in range(sent.shape[0] // per):
        sent[t * per : t * per + rows, :] = mean
        sent[t * per + rows : (t + 1) * per, :] = table


def sky_kernel(sizes, sky, forcing, fluxes, weights, below, above, out, halo, spread):
    levels, rows, steps, sea_levels, sea_rows, stride, sea_stride = sizes
    width = sky.shape[1]
    depth = up_to(levels + 2 * steps, 16)
    halo[: HALO * stride, :] = below[: HALO * stride, :]
    halo[HALO * stride :, :] = above[: HALO * stride, :]

    def edge(l):
        return halo[pl.ds(l, 2 * HALO, stride=stride), :]

    inside = edge(levels + steps + 2)

    def times(x, n):
        for i in range(n):
            x = cross(x)
            if i < n - 1:
                x = masked(x, rows, inside)
        return x[:rows]

    @pl.loop(0, levels // 4)
    def _(q):
        for i in range(4):
            l = q * 4 + i
            at = pl.multiple_of(l * rows, 8)
            x = jnp.concatenate([sky[pl.ds(at, rows), :], edge(l)], 0)
            spread[pl.ds(at, rows), :] = times(x, steps)

    for j in range(steps):
        x = jnp.concatenate([forcing[j * rows : (j + 1) * rows, :], edge(levels + j)], 0)
        spread[(levels + j) * rows : (levels + j + 1) * rows, :] = times(x, steps - 1 - j)
        x = fluxes[j * (rows + 2 * HALO) : (j + 1) * (rows + 2 * HALO), :]
        spread[(levels + steps + j) * rows : (levels + steps + j + 1) * rows, :] = times(
            x, steps - 1 - j
        )

    w = weights[:, : 3 * depth]
    for r in range(0, rows, 2):
        x = jnp.concatenate([spread[pl.ds(r + i, depth, stride=rows), :] for i in range(2)], 1)
        high, low = split(x)
        y = jnp.dot(w, jnp.concatenate([high, low, high], 0), preferred_element_type=f32)
        for i in range(2):
            out[pl.ds(r + i, levels, stride=rows), :] = y[:levels, i * width : (i + 1) * width]


def sea_kernel(sizes, warmth, brine, wet, weights, below, above, warm_out, brine_out, edges, spread):
    levels, rows, steps, sea_levels, sea_rows, stride, sea_stride = sizes
    width = warmth.shape[1]
    base = HALO * stride
    m = wet[...].astype(f32)
    at = lax.broadcasted_iota(jnp.int32, (sea_rows, width), 0)

    def around(x, top, bottom):
        north = jnp.where(at == 0, top, pltpu.roll(x, 1, 0))
        south = jnp.where(at == sea_rows - 1, bottom, pltpu.roll(x, sea_rows - 1, 0))
        return north + south + pltpu.roll(x, 1, 1) + pltpu.roll(x, width - 1, 1)

    mark = base + 2 * sea_stride
    count = around(m, above[mark : mark + 1, :], below[mark : mark + 1, :])
    for f, field in enumerate((warmth, brine)):
        first = base + f * sea_stride
        for l in range(sea_levels):
            x = field[l * sea_rows : (l + 1) * sea_rows, :]
            near = around(m * x, above[first + l : first + l + 1, :], below[first + l : first + l + 1, :])
            spread[f, l * sea_rows : (l + 1) * sea_rows, :] = x + ocean_diffusion * (m * (near - x * count))
        if sea_stride > sea_levels:
            spread[f, sea_levels * sea_rows :, :] = jnp.zeros(((sea_stride - sea_levels) * sea_rows, width), f32)

    w = weights[:, : 3 * sea_stride]
    for r in range(sea_rows):
        x = jnp.concatenate([spread[f, pl.ds(r, sea_stride, stride=sea_rows), :] for f in range(2)], 1)
        high, low = split(x)
        y = jnp.dot(w, jnp.concatenate([high, low, high], 0), preferred_element_type=f32)
        wet_row = m[r : r + 1]
        for f, (field, out) in enumerate(((warmth, warm_out), (brine, brine_out))):
            old = field[pl.ds(r, sea_levels, stride=sea_rows), :]
            new = y[:sea_levels, f * width : (f + 1) * width]
            out[pl.ds(r, sea_levels, stride=sea_rows), :] = wet_row * new + (1.0 - wet_row) * old


def heat_kernel(sizes, topk, got, mine, shares, wet, sea_first, before, after):
    levels, rows, steps, sea_levels, sea_rows, stride, sea_stride = sizes
    width = before.shape[1]
    per = rows + 2 * topk
    group = width // rows
    me = mine[0].astype(f32)
    part = lax.broadcasted_iota(jnp.int32, (1, width), 1) // rows
    to = lax.broadcasted_iota(jnp.int32, (sea_rows, width), 0).astype(f32)
    picked = jnp.zeros((topk * sea_rows, width), f32)
    for g in range(got.shape[0] // (per * group)):
        at = [(g * group + i) * per for i in range(group)]
        mean = jnp.concatenate([got[a : a + rows, :] for a in at], 0).astype(bf16)
        table = got[at[0] + rows : at[0] + per, :]
        for i in range(1, group):
            table = jnp.where(part == i, got[at[i] + rows : at[i] + per, :], table)
        hot = []
        for k in range(topk):
            row = jnp.where(table[k : k + 1] == me, table[topk + k : topk + k + 1], -1.0)
            hot.append(jnp.where(to == row, 1.0, 0.0))
        hot = jnp.concatenate(hot, 0).astype(bf16)
        picked = picked + jnp.dot(hot, mean, preferred_element_type=f32)
    side = jnp.concatenate([picked[k * sea_rows : (k + 1) * sea_rows] for k in range(topk)], 1)
    first = side.astype(bf16).astype(f32)
    second = (side - first).astype(bf16).astype(f32)
    third = side - first - second
    parts = jnp.concatenate([first, second, third], 0).astype(bf16)
    y = jnp.dot(parts, shares[...], preferred_element_type=f32)
    heat = y[:sea_rows] + y[sea_rows : 2 * sea_rows] + y[2 * sea_rows :]
    heat = wet[...].astype(f32) * heat
    for l in range(sea_levels):
        after[l * sea_rows : (l + 1) * sea_rows, :] = (
            before[l * sea_rows : (l + 1) * sea_rows, :] + sea_first[l : l + 1, :] * heat
        )


def body(sky, forcing, curve, surface, rate, vmix, shares, owners, locals_, warmth, brine, wet, sea_mix):
    levels, rows, width = sky.shape
    steps = forcing.shape[0]
    sea_levels, sea_rows, _ = warmth.shape
    topk = owners.shape[1]
    stride = up_to(levels + steps + 3, 8)
    sea_stride = up_to(sea_levels, 16)
    sizes = (levels, rows, steps, sea_levels, sea_rows, stride, sea_stride)
    tiles = lax.axis_size("tile")
    sky2, forcing2 = sky.reshape(-1, width), forcing.reshape(-1, width)
    warmth2, brine2 = warmth.reshape(-1, width), brine.reshape(-1, width)
    flat = lambda n, kind=f32: jax.ShapeDtypeStruct((n, width), kind)

    length = HALO * stride + 2 * sea_stride + 8
    up, down = call(
        functools.partial(pack_kernel, sizes), [flat(length)] * 2,
        sky2, forcing2, surface, rate, warmth2, brine2, wet, moved=4 << 20,
    )
    count = lax.axis_size(("tile", "comp"))
    above = lax.ppermute(down, ("tile", "comp"), [(i, i + 1) for i in range(count - 1)])
    below = lax.ppermute(up, ("tile", "comp"), [(i + 1, i) for i in range(count - 1)])

    mix_rows = up_to(levels, 16)
    rows_of_mix, source_rows, weights, sea_weights, sea_first, own = call(
        functools.partial(local_kernel, sizes),
        [
            flat((steps - 1) * levels), flat(8), jax.ShapeDtypeStruct((mix_rows, 2 * width), bf16),
            jax.ShapeDtypeStruct((sea_stride, 2 * width), bf16), flat(sea_stride), flat((steps - 1) * rows),
        ],
        vmix, curve[None], sea_mix, sky2, flops=1 << 30, moved=4 << 20,
    )

    per = rows + 2 * topk
    sent, fluxes = call(
        functools.partial(flux_kernel, sizes), [flat(tiles * per), flat(steps * (rows + 2 * HALO))],
        sky[-1], forcing2, surface, rate, rows_of_mix, source_rows, own, owners.T, locals_.T, below, above,
        scratch=[pltpu.VMEM((2 * HALO * stride, width), f32)], moved=2 << 20,
    )
    got = lax.all_to_all(sent.reshape(tiles, per, width), "tile", split_axis=0, concat_axis=0, tiled=True)
    got = got.reshape(-1, width)

    sky_out = call(
        functools.partial(sky_kernel, sizes), flat(levels * rows),
        sky2, forcing2, fluxes, weights, below, above,
        scratch=[
            pltpu.VMEM((2 * HALO * stride, width), f32),
            pltpu.VMEM((up_to(levels + 2 * steps, 16) * rows, width), f32),
        ],
        flops=4 << 30, moved=8 << 20,
    )
    warm, salt = call(
        functools.partial(sea_kernel, sizes), [flat(sea_levels * sea_rows)] * 2,
        warmth2, brine2, wet, sea_weights, below, above,
        scratch=[pltpu.VMEM((8, width), f32), pltpu.VMEM((2, sea_stride * sea_rows, width), f32)],
        flops=2 << 30, moved=4 << 20,
    )
    mine = lax.axis_index("tile").astype(jnp.int32)[None]
    warm = call(
        functools.partial(heat_kernel, sizes, topk), flat(sea_levels * sea_rows),
        got, mine, shares.reshape(-1, width), wet, sea_first, warm,
        in_specs=[VMEM, pl.BlockSpec(memory_space=pltpu.SMEM)] + [VMEM] * 4, moved=2 << 20,
    )
    return sky_out.reshape(sky.shape), warm.reshape(warmth.shape), salt.reshape(brine.shape)


def solution(mesh):
    both = P(None, ("member", "tile", "comp"), None)
    one = P(("tile", "comp"), None)
    return jax.shard_map(
        body,
        mesh=mesh,
        in_specs=(
            both, both, P(), P(("member", "tile", "comp"), None), one, P(), P(), one, one, both, both, one, P(),
        ),
        out_specs=(both, both, both),
        check_vma=False,
    )
```

time: 98.3 us -> 39.1 us (0.40)
  starting transfers between devices: 42.9 us -> 15.9 us
  local copies, waits for them, and re-layouts: 24.4 us -> 6.38 us
  other arithmetic: 17.6 us -> 0 us
  Pallas kernels: 0 us -> 15.4 us
  matrix products: 9.81 us -> 0 us
  waiting for transfers between devices: 1.24 us -> 0.01 us
    ppermute x10 -> x2, starting transfers between devices: 28.1 us -> 4.47 us  [the longest x1 3.04 us: body(): lax.ppermute(down, ('tile', 'comp'), [(i, i + 1) for i in range(count - 1)])]
    slice x20 -> x0, local copies, waits for them, and re-layouts: 16.2 us -> none  [the longest x8 8.56 us: advance_air_column(): jnp.roll(center, -1, 2)]
    pallas_call x0 -> x6, Pallas kernels: none -> 15.4 us  [call(): pl.pallas_call(kernel, out_shape=out_shape, in_specs=in_specs or [VMEM] *...]
    add x8 -> x0, other arithmetic: 11.8 us -> none  [the longest x4 8.69 us: advance_air_column(): center + atm_diffusion * laplace]
    dot_general x9 -> x0, matrix products: 9.81 us -> none  [the longest x4 6.86 us: advance_air_column(): jnp.einsum('kl,lrx->krx', vmix, updated, precision=lax.Precision.HIGHEST)]
    all_to_all x2 -> x1, starting transfers between devices: 14.9 us -> 11.4 us  [body(): lax.all_to_all(sent.reshape(tiles, per, width), 'tile', split_axis=0, con...]
    mul x2 -> x0, other arithmetic: 2.12 us -> none  [the longest x1 1.27 us: body(): wet_indicator_real[None] * marine_warmth_deviation]
    unnamed x70 -> x40, local copies, waits for them, and re-layouts: 4.63 us -> 6.38 us
  transfers between devices with their start and end apart: 12 -> 3, of which waited for: 2 -> 0; matrix products, arithmetic and copies ran while one was open for 36% -> 0% of each run, Pallas kernels for 0% -> 34%
where the time goes in v1:
time: 39.1 us; the launch traced here: 38.5 us
  starting transfers between devices  15.9 us (41%)
  Pallas kernels  15.4 us (39%)
  local copies, waits for them, and re-layouts  6.38 us (16%)
  between operations  0.85 us (2%)
    pallas_call x6, Pallas kernels, call(): pl.pallas_call(kernel, out_shape=out_shape, in_specs=in_specs or [VMEM] *...  15.4 us
    all_to_all x1, starting transfers between devices, body(): lax.all_to_all(sent.reshape(tiles, per, width), 'tile', split_axis=0, con...  11.4 us
    unnamed x40, local copies, waits for them, and re-layouts  6.38 us
    ppermute x1, starting transfers between devices, body(): lax.ppermute(down, ('tile', 'comp'), [(i, i + 1) for i in range(count - 1)])  3.04 us
    ppermute x1, starting transfers between devices, body(): lax.ppermute(up, ('tile', 'comp'), [(i + 1, i) for i in range(count - 1)])  1.42 us
  transfers between devices with their start and end apart: 3, of which 0 were waited for; matrix products, arithmetic and copies ran while one was open for 0% of the time, Pallas kernels for 34%

profile of v1, /device:TPU:0, one launch (start us, length us, event | category | flops | bytes accessed | tf_op | source)
XLA Modules:
  0.0 38.5 jit_solution(12188689627631705720)
XLA Ops:
  0.6 0.0 copy-start.19
  0.6 0.0 copy-start
  0.7 1.3 %copy-done = f32[72,32,128]{2,1,0:T(8,128)S(1)} copy-done((f32[72,32,128]{2,1,0:T(8,128)S(1)}, f32[72,32,128]{2,1,0:T(8,128)}, u32[]{:S(2)}) %copy-start) | copy-done | bytes 1179672
  1.9 1.0 %copy-done.2 = f32[62,16,128]{2,1,0:T(8,128)S(1)} copy-done((f32[62,16,128]{2,1,0:T(8,128)S(1)}, f32[62,16,128]{2,1,0:T(8,128)}, u32[]{:S(2)}) %copy-start.2) | copy-done | bytes 507928
  3.0 1.0 %copy-done.4 = f32[62,16,128]{2,1,0:T(8,128)S(1)} copy-done((f32[62,16,128]{2,1,0:T(8,128)S(1)}, f32[62,16,128]{2,1,0:T(8,128)}, u32[]{:S(2)}) %copy-start.4) | copy-done | bytes 507928
  4.0 0.8 %copy-done.6 = f32[4,32,128]{2,1,0:T(8,128)S(1)} copy-done((f32[4,32,128]{2,1,0:T(8,128)S(1)}, f32[4,32,128]{2,1,0:T(8,128)}, u32[]{:S(2)}) %copy-start.6) | copy-done | bytes 65560
  4.8 0.7 %copy-done.9 = f32[32,128]{1,0:T(8,128)S(1)} copy-done((f32[32,128]{1,0:T(8,128)S(1)}, f32[32,128]{1,0:T(8,128)}, u32[]{:S(2)}) %copy-start.9) | copy-done | bytes 16408
  5.6 0.7 %copy-done.11 = f32[32,128]{1,0:T(8,128)S(1)} copy-done((f32[32,128]{1,0:T(8,128)S(1)}, f32[32,128]{1,0:T(8,128)}, u32[]{:S(2)}) %copy-start.11) | copy-done | bytes 16408
  6.3 0.7 %copy-done.13 = s32[16,128]{1,0:T(8,128)S(1)} copy-done((s32[16,128]{1,0:T(8,128)S(1)}, s32[16,128]{1,0:T(8,128)}, u32[]{:S(2)}) %copy-start.13) | copy-done | bytes 8216
  7.0 0.3 shard_map.149
  7.3 1.4 %collective-permute-start = (f32[456,128]{1,0:T(8,128)S(1)}, f32[456,128]{1,0:T(8,128)S(1)}, u32[]{:S(2)}, u32[]{:S(2)}) collective-permute-start(f32[456,128]{1,0:T(8,128)S(1)} %get-tuple-element.18), channel_id=1, source_target_pairs={{1,0},{2,1},{3,2},{4,3},{5,4},{6,5},{7,6},{8,7},{9,8},{10,9},{11,1... | collective-permute-start | bytes 700424 | tf_op jit(solution)/shard_map/ppermute | solution.py:313
  8.7 3.0 %collective-permute-start.1 = (f32[456,128]{1,0:T(8,128)S(1)}, f32[456,128]{1,0:T(8,128)S(1)}, u32[]{:S(2)}, u32[]{:S(2)}) collective-permute-start(f32[456,128]{1,0:T(8,128)S(1)} %get-tuple-element.19), channel_id=1, source_target_pairs={{0,1},{1,2},{2,3},{3,4},{4,5},{5,6},{6,7},{7,8},{8,9},{9,10},{10,1... | collective-permute-start | bytes 700424 | tf_op jit(solution)/shard_map/ppermute | solution.py:312
  11.7 0.0 copy-done.19
  11.8 0.0 copy-done.1
  11.8 0.0 copy-done.17
  11.8 0.0 copy-start.7
  11.8 0.0 copy-start.10
  11.8 0.0 copy-start.12
  11.8 0.0 copy-start.15
  11.8 0.0 copy-start.16
  11.8 1.4 %shard_map.148 = (f32[216,128]{1,0:T(8,128)S(1)}, f32[8,128]{1,0:T(8,128)S(1)}, bf16[80,256]{1,0:T(8,128)(2,1)S(1)}, bf16[64,256]{1,0:T(8,128)(2,1)S(1)}, f32[64,128]{1,0:T(8,128)S(1)}, /*index=5*/f32[96,128]{1,0:T(8,128)S(1)}) custom-call(f32[72,72]{1,0:T(8,128)S(1)} %copy-done.17, f32[1,72]{1,0:T(1,128)S(1)} %bitcast.30, f32[62,62]{1,0:T(8,128)S(1)} %copy-done.18, ...), custom_call_target="tpu_custom_call" | custom-call | flops 1073741824 | bytes 4194304 | tf_op jit(solution)/shard_map/pallas_call | solution.py:23
  13.2 0.0 collective-permute-done.below
  13.3 0.0 collective-permute-done.1.above
  13.3 1.1 %shard_map.150 = (f32[320,128]{1,0:T(8,128)}, f32[160,128]{1,0:T(8,128)S(1)}) custom-call(f32[32,128]{1,0:T(8,128)S(1)} %slice_bitcast_fusion.sky, f32[128,128]{1,0:T(8,128)S(1)} %bitcast.25, f32[32,128]{1,0:T(8,128)S(1)} %copy-done.10, f32[32,128]{1,0:T(8,128)S(1)} %copy-done.12, f32[216,128]{1,0:T(8,128)S(1)} %get-tuple-element.15.rows_of_mix, ...), custom_call_target="tpu_custom_call" | custom-call | bytes 2097152 | tf_op jit(solution)/shard_map/pallas_call | solution.py:23
  14.4 11.4 %all-to-all-start = ((f32[8,40,128]{2,1,0:T(8,128)}), f32[8,40,128]{2,1,0:T(8,128)S(1)}, u32[]{:S(2)}, u32[]{:S(2)}) async-start(f32[8,40,128]{2,1,0:T(8,128)} %bitcast.9), calls=%async_computation | async-start | bytes 327680 | tf_op jit(solution)/shard_map/all_to_all | solution.py:331
  25.8 0.0 copy-start.5
  25.9 0.0 copy-start.14
  25.9 9.2 %shard_map.151 = f32[2304,128]{1,0:T(8,128)} custom-call(f32[2304,128]{1,0:T(8,128)S(1)} %bitcast.18, f32[128,128]{1,0:T(8,128)S(1)} %bitcast.26, f32[160,128]{1,0:T(8,128)S(1)} %get-tuple-element.20.fluxes, bf16[80,256]{1,0:T(8,128)(2,1)S(1)} %get-tuple-element.21.weights, f32[456,128]{1,0:T(8,128)S(1)} %collective-permute-done.below, ...), custom_call_target="tpu_custom_call" | custom-call | flops 4294967296 | bytes 8388608 | tf_op jit(solution)/shard_map/pallas_call | solution.py:23
  35.0 0.0 copy-done.3
  35.0 2.4 %shard_map.152 = (f32[992,128]{1,0:T(8,128)S(1)}, f32[992,128]{1,0:T(8,128)}) custom-call(f32[992,128]{1,0:T(8,128)S(1)} %bitcast.21, f32[992,128]{1,0:T(8,128)S(1)} %bitcast.23, s32[16,128]{1,0:T(8,128)S(1)} %copy-done.14, bf16[64,256]{1,0:T(8,128)(2,1)S(1)} %get-tuple-element.24.weights, f32[456,128]{1,0:T(8,128)S(1)} %collective-permute-done.below, ...), custom_call_target="tpu_custom_call" | custom-call | flops 2147483648 | bytes 4194304 | tf_op jit(solution)/shard_map/pallas_call | solution.py:23
  37.4 0.0 all-to-all-done
  37.4 1.1 %shard_map.153 = f32[992,128]{1,0:T(8,128)} custom-call(f32[320,128]{1,0:T(8,128)S(1)} %bitcast.19, s32[1]{0:T(128)} %bitcast.11.mine, bf16[512,128]{1,0:T(8,128)(2,1)S(1)} %bitcast.27, s32[16,128]{1,0:T(8,128)S(1)} %copy-done.14, f32[64,128]{1,0:T(8,128)S(1)} %get-tuple-element.23.sea_first, f32[992,128]{1,0:T(8,128)S(1)} %get-tuple-element.25.before), custom_call_target="tpu_custom_call" | custom-call | bytes 2097152 | tf_op jit(solution)/shard_map/pallas_call | solution.py:23
  (21 shorter events, 0.0 us)
Async XLA Ops:
  0.6 11.1 %copy-start.19 = (f32[72]{0:T(128)S(1)}, f32[72]{0:T(128)}, u32[]{:S(2)}) copy-start(f32[72]{0:T(128)} %param.15) | copy-start | bytes 868
  0.6 1.3 %copy-start = (f32[72,32,128]{2,1,0:T(8,128)S(1)}, f32[72,32,128]{2,1,0:T(8,128)}, u32[]{:S(2)}) copy-start(f32[72,32,128]{2,1,0:T(8,128)} %param.13) | copy-start | bytes 3538948
  1.9 1.0 %copy-start.2 = (f32[62,16,128]{2,1,0:T(8,128)S(1)}, f32[62,16,128]{2,1,0:T(8,128)}, u32[]{:S(2)}) copy-start(f32[62,16,128]{2,1,0:T(8,128)} %param.22) | copy-start | bytes 1523716
  3.0 1.0 %copy-start.4 = (f32[62,16,128]{2,1,0:T(8,128)S(1)}, f32[62,16,128]{2,1,0:T(8,128)}, u32[]{:S(2)}) copy-start(f32[62,16,128]{2,1,0:T(8,128)} %param.23) | copy-start | bytes 1523716
  4.0 0.8 %copy-start.6 = (f32[4,32,128]{2,1,0:T(8,128)S(1)}, f32[4,32,128]{2,1,0:T(8,128)}, u32[]{:S(2)}) copy-start(f32[4,32,128]{2,1,0:T(8,128)} %param.14) | copy-start | bytes 196612
  4.8 0.7 %copy-start.9 = (f32[32,128]{1,0:T(8,128)S(1)}, f32[32,128]{1,0:T(8,128)}, u32[]{:S(2)}) copy-start(f32[32,128]{1,0:T(8,128)} %surface.3) | copy-start | bytes 49156
  5.5 0.7 %copy-start.11 = (f32[32,128]{1,0:T(8,128)S(1)}, f32[32,128]{1,0:T(8,128)}, u32[]{:S(2)}) copy-start(f32[32,128]{1,0:T(8,128)} %rate.3) | copy-start | bytes 49156
  6.3 0.7 %copy-start.13 = (s32[16,128]{1,0:T(8,128)S(1)}, s32[16,128]{1,0:T(8,128)}, u32[]{:S(2)}) copy-start(s32[16,128]{1,0:T(8,128)} %wet.5) | copy-start | bytes 24580
  7.0 4.8 %copy-start.1 = (f32[72,32,128]{2,1,0:T(8,128)S(1)}, f32[72,32,128]{2,1,0:T(8,128)}, u32[]{:S(2)}) copy-start(f32[72,32,128]{2,1,0:T(8,128)} %param.13) | copy-start | bytes 3538948
  7.0 4.8 %copy-start.17 = (f32[72,72]{1,0:T(8,128)S(1)}, f32[72,72]{1,0:T(8,128)}, u32[]{:S(2)}) copy-start(f32[72,72]{1,0:T(8,128)} %vmix.1) | copy-start | bytes 62212
  7.0 4.8 %copy-start.18 = (f32[62,62]{1,0:T(8,128)S(1)}, f32[62,62]{1,0:T(8,128)}, u32[]{:S(2)}) copy-start(f32[62,62]{1,0:T(8,128)} %sea_mix.1) | copy-start | bytes 46132
  7.3 6.0 %collective-permute-start = (f32[456,128]{1,0:T(8,128)S(1)}, f32[456,128]{1,0:T(8,128)S(1)}, u32[]{:S(2)}, u32[]{:S(2)}) collective-permute-start(f32[456,128]{1,0:T(8,128)S(1)} %get-tuple-element.18), channel_id=1, source_target_pairs={{1,0},{2,1},{3,2},{4,3},{5,4},{6,5},{7,6},{8,7},{9,8},{10,9},{11,1... | collective-permute-start | bytes 700424 | tf_op jit(solution)/shard_map/ppermute | solution.py:313
  8.7 4.6 %collective-permute-start.1 = (f32[456,128]{1,0:T(8,128)S(1)}, f32[456,128]{1,0:T(8,128)S(1)}, u32[]{:S(2)}, u32[]{:S(2)}) collective-permute-start(f32[456,128]{1,0:T(8,128)S(1)} %get-tuple-element.19), channel_id=1, source_target_pairs={{0,1},{1,2},{2,3},{3,4},{4,5},{5,6},{6,7},{7,8},{8,9},{9,10},{10,1... | collective-permute-start | bytes 700424 | tf_op jit(solution)/shard_map/ppermute | solution.py:312
  11.8 1.5 %copy-start.7 = (f32[4,32,128]{2,1,0:T(8,128)S(1)}, f32[4,32,128]{2,1,0:T(8,128)}, u32[]{:S(2)}) copy-start(f32[4,32,128]{2,1,0:T(8,128)} %param.14) | copy-start | bytes 196612
  11.8 1.5 %copy-start.10 = (f32[32,128]{1,0:T(8,128)S(1)}, f32[32,128]{1,0:T(8,128)}, u32[]{:S(2)}) copy-start(f32[32,128]{1,0:T(8,128)} %surface.3) | copy-start | bytes 49156
  11.8 1.5 %copy-start.12 = (f32[32,128]{1,0:T(8,128)S(1)}, f32[32,128]{1,0:T(8,128)}, u32[]{:S(2)}) copy-start(f32[32,128]{1,0:T(8,128)} %rate.3) | copy-start | bytes 49156
  11.8 1.5 %copy-start.15 = (s32[32,4]{0,1:T(4,128)S(1)}, s32[32,4]{0,1:T(4,128)}, u32[]{:S(2)}) copy-start(s32[32,4]{0,1:T(4,128)} %param.20) | copy-start | bytes 1540
  11.8 1.5 %copy-start.16 = (s32[32,4]{0,1:T(4,128)S(1)}, s32[32,4]{0,1:T(4,128)}, u32[]{:S(2)}) copy-start(s32[32,4]{0,1:T(4,128)} %param.21) | copy-start | bytes 1540
  14.4 23.0 %all-to-all-start = ((f32[8,40,128]{2,1,0:T(8,128)}), f32[8,40,128]{2,1,0:T(8,128)S(1)}, u32[]{:S(2)}, u32[]{:S(2)}) async-start(f32[8,40,128]{2,1,0:T(8,128)} %bitcast.9), calls=%async_computation | async-start | bytes 327680 | tf_op jit(solution)/shard_map/all_to_all | solution.py:331
  25.8 9.2 %copy-start.3 = (f32[62,16,128]{2,1,0:T(8,128)S(1)}, f32[62,16,128]{2,1,0:T(8,128)}, u32[]{:S(2)}) copy-start(f32[62,16,128]{2,1,0:T(8,128)} %param.22) | copy-start | bytes 1523716
  25.8 9.2 %copy-start.5 = (f32[62,16,128]{2,1,0:T(8,128)S(1)}, f32[62,16,128]{2,1,0:T(8,128)}, u32[]{:S(2)}) copy-start(f32[62,16,128]{2,1,0:T(8,128)} %param.23) | copy-start | bytes 1523716
  25.9 9.2 %copy-start.14 = (s32[16,128]{1,0:T(8,128)S(1)}, s32[16,128]{1,0:T(8,128)}, u32[]{:S(2)}) copy-start(s32[16,128]{1,0:T(8,128)} %wet.5) | copy-start | bytes 24580
  35.0 2.4 %copy-start.8 = (bf16[4,128,128]{2,1,0:T(8,128)(2,1)S(1)}, bf16[4,128,128]{2,1,0:T(8,128)(2,1)}, u32[]{:S(2)}) copy-start(bf16[4,128,128]{2,1,0:T(8,128)(2,1)} %param.19) | copy-start | bytes 393220

commit v2 on v1

--- a/solution.py
+++ b/solution.py
@@ -19,14 +19,14 @@
     return -(-n // m) * m
 
 
-def call(kernel, out_shape, *args, scratch=(), in_specs=None, flops=0, moved=0):
+def call(kernel, out_shape, *args, scratch=(), in_specs=None, flops=0, moved=0, grant=24):
     return pl.pallas_call(
         kernel,
         out_shape=out_shape,
         in_specs=in_specs or [VMEM] * len(args),
         out_specs=jax.tree.map(lambda _: VMEM, out_shape),
         scratch_shapes=list(scratch),
-        compiler_params=pltpu.CompilerParams(vmem_limit_bytes=24 * 2**20),
+        compiler_params=pltpu.CompilerParams(vmem_limit_bytes=grant * 2**20),
         cost_estimate=pl.CostEstimate(flops=flops, bytes_accessed=moved, transcendentals=0),
     )(*args)
 
@@ -170,10 +170,8 @@
     table = jnp.concatenate(
         [jnp.concatenate([owner] * times, 1), jnp.concatenate([row] * times, 1)], 0
     )
-    per = mean.shape[0] + table.shape[0]
-    for t in range(sent.shape[0] // per):
-        sent[t * per : t * per + rows, :] = mean
-        sent[t * per + rows : (t + 1) * per, :] = table
+    sent[:rows, :] = mean
+    sent[rows:, :] = table
 
 
 def sky_kernel(sizes, sky, forcing, fluxes, weights, below, above, out, halo, spread):
@@ -298,7 +296,6 @@
     stride = up_to(levels + steps + 3, 8)
     sea_stride = up_to(sea_levels, 16)
     sizes = (levels, rows, steps, sea_levels, sea_rows, stride, sea_stride)
-    tiles = lax.axis_size("tile")
     sky2, forcing2 = sky.reshape(-1, width), forcing.reshape(-1, width)
     warmth2, brine2 = warmth.reshape(-1, width), brine.reshape(-1, width)
     flat = lambda n, kind=f32: jax.ShapeDtypeStruct((n, width), kind)
@@ -306,7 +303,7 @@
     length = HALO * stride + 2 * sea_stride + 8
     up, down = call(
         functools.partial(pack_kernel, sizes), [flat(length)] * 2,
-        sky2, forcing2, surface, rate, warmth2, brine2, wet, moved=4 << 20,
+        sky2, forcing2, surface, rate, warmth2, brine2, wet, moved=4 << 20, grant=60,
     )
     count = lax.axis_size(("tile", "comp"))
     above = lax.ppermute(down, ("tile", "comp"), [(i, i + 1) for i in range(count - 1)])
@@ -324,12 +321,11 @@
 
     per = rows + 2 * topk
     sent, fluxes = call(
-        functools.partial(flux_kernel, sizes), [flat(tiles * per), flat(steps * (rows + 2 * HALO))],
+        functools.partial(flux_kernel, sizes), [flat(per), flat(steps * (rows + 2 * HALO))],
         sky[-1], forcing2, surface, rate, rows_of_mix, source_rows, own, owners.T, locals_.T, below, above,
         scratch=[pltpu.VMEM((2 * HALO * stride, width), f32)], moved=2 << 20,
     )
-    got = lax.all_to_all(sent.reshape(tiles, per, width), "tile", split_axis=0, concat_axis=0, tiled=True)
-    got = got.reshape(-1, width)
+    got = lax.all_gather(sent, "tile", axis=0, tiled=True)
 
     sky_out = call(
         functools.partial(sky_kernel, sizes), flat(levels * rows),

time: 39.1 us -> 60.2 us (1.54)
  blocking collectives: 0 us -> 37.6 us
  starting transfers between devices: 15.9 us -> 4.32 us
  local copies, waits for them, and re-layouts: 6.38 us -> 0.08 us
  Pallas kernels: 15.4 us -> 17.2 us
    all_gather x0 -> x1, blocking collectives: none -> 37.6 us  [body(): got = lax.all_gather(sent, 'tile', axis=0, tiled=True)]
    all_to_all x1 -> x0, starting transfers between devices: 11.4 us -> none  [body(): lax.all_to_all(sent.reshape(tiles, per, width), 'tile', split_axis=0, con...]
    unnamed x40 -> x26, local copies, waits for them, and re-layouts: 6.38 us -> 0.07 us
    pallas_call x6, Pallas kernels: 15.4 us -> 17.2 us  [call(): pl.pallas_call(kernel, out_shape=out_shape, in_specs=in_specs or [VMEM] *...]
  transfers between devices with their start and end apart: 3 -> 2, of which waited for: 0 -> 0; matrix products, arithmetic and copies ran while one was open for 0% -> 0% of each run, Pallas kernels for 34% -> 2%
where the time goes in v2:
time: 60.2 us; the launch traced here: 60 us
  blocking collectives  37.6 us (62%)
  Pallas kernels  17.2 us (29%)
  starting transfers between devices  4.32 us (7%)
  between operations  0.87 us (1%)
    all_gather x1, blocking collectives, body(): got = lax.all_gather(sent, 'tile', axis=0, tiled=True)  37.6 us
    pallas_call x6, Pallas kernels, call(): pl.pallas_call(kernel, out_shape=out_shape, in_specs=in_specs or [VMEM] *...  17.2 us
    ppermute x1, starting transfers between devices, body(): lax.ppermute(down, ('tile', 'comp'), [(i, i + 1) for i in range(count - 1)])  3.04 us
    ppermute x1, starting transfers between devices, body(): lax.ppermute(up, ('tile', 'comp'), [(i + 1, i) for i in range(count - 1)])  1.28 us
  transfers between devices with their start and end apart: 2, of which 0 were waited for; matrix products, arithmetic and copies ran while one was open for 0% of the time, Pallas kernels for 2%

profile of v2, /device:TPU:0, one launch (start us, length us, event | category | flops | bytes accessed | tf_op | source)
XLA Modules:
  0.0 60.0 jit_solution(4582541698989501761)
XLA Ops:
  0.6 0.0 copy-start
  0.6 0.0 copy-start.11
  0.7 0.0 copy-start.10
  0.7 0.0 copy-start.12
  0.7 2.7 %shard_map.149 = (f32[456,128]{1,0:T(8,128)}, f32[456,128]{1,0:T(8,128)}) custom-call(f32[2304,128]{1,0:T(8,128)} %bitcast.14, f32[128,128]{1,0:T(8,128)} %bitcast.21, f32[32,128]{1,0:T(8,128)} %surface.3, f32[32,128]{1,0:T(8,128)} %rate.3, f32[992,128]{1,0:T(8,128)} %bitcast.17, f32[992,128]{1,0:T(8,128)} %bitcast.19, s32[16,128]{1,0:T(8,128)} %wet.5), custom_call_target="tpu_custom_call" | custom-call | bytes 4194304 | tf_op jit(solution)/shard_map/pallas_call | solution.py:23
  3.3 1.3 %collective-permute-start = (f32[456,128]{1,0:T(8,128)}, f32[456,128]{1,0:T(8,128)S(1)}, u32[]{:S(2)}, u32[]{:S(2)}) collective-permute-start(f32[456,128]{1,0:T(8,128)} %get-tuple-element.18), channel_id=1, source_target_pairs={{1,0},{2,1},{3,2},{4,3},{5,4},{6,5},{7,6},{8,7},{9,8},{10,9},{11,1... | collective-permute-start | bytes 700424 | tf_op jit(solution)/shard_map/ppermute | solution.py:310
  4.6 3.0 %collective-permute-start.1 = (f32[456,128]{1,0:T(8,128)}, f32[456,128]{1,0:T(8,128)S(1)}, u32[]{:S(2)}, u32[]{:S(2)}) collective-permute-start(f32[456,128]{1,0:T(8,128)} %get-tuple-element.19), channel_id=1, source_target_pairs={{0,1},{1,2},{2,3},{3,4},{4,5},{5,6},{6,7},{7,8},{8,9},{9,10},{10,1... | collective-permute-start | bytes 700424 | tf_op jit(solution)/shard_map/ppermute | solution.py:309
  7.7 0.0 copy-done
  7.7 0.0 copy-done.11
  7.7 0.0 copy-done.10
  7.7 0.0 copy-done.12
  7.7 0.0 copy-start.3
  7.7 0.0 copy-start.5
  7.7 0.0 copy-start.6
  7.8 0.0 copy-start.8
  7.8 0.0 copy-start.9
  7.8 0.0 copy-start.1
  7.8 0.0 copy-start.2
  7.8 0.0 copy-start.7
  7.8 1.4 %shard_map.148 = (f32[216,128]{1,0:T(8,128)S(1)}, f32[8,128]{1,0:T(8,128)S(1)}, bf16[80,256]{1,0:T(8,128)(2,1)S(1)}, bf16[64,256]{1,0:T(8,128)(2,1)S(1)}, f32[64,128]{1,0:T(8,128)S(1)}, /*index=5*/f32[96,128]{1,0:T(8,128)S(1)}) custom-call(f32[72,72]{1,0:T(8,128)S(1)} %copy-done.10, f32[1,72]{1,0:T(1,128)S(1)} %bitcast.27, f32[62,62]{1,0:T(8,128)S(1)} %copy-done.11, ...), custom_call_target="tpu_custom_call" | custom-call | flops 1073741824 | bytes 4194304 | tf_op jit(solution)/shard_map/pallas_call | solution.py:23
  9.3 0.0 collective-permute-done.below
  9.3 0.0 collective-permute-done.1.above
  9.3 0.0 copy-done.3
  9.3 0.0 copy-done.5
  9.3 0.0 copy-done.6
  9.3 0.0 copy-done.8
  9.3 0.4 shard_map.150
  9.7 37.6 %all_gather.3.got = f32[320,128]{1,0:T(8,128)S(1)} all-gather(f32[40,128]{1,0:T(8,128)S(1)} %get-tuple-element.22), channel_id=1, replica_groups=mesh['member'=2,'tile'=8,'comp'=2] {'tile'}, dimensions={0}, use_global_device_ids=true | all-gather | bytes 184320 | tf_op jit(solution)/shard_map/all_gather | solution.py:328
  47.4 0.0 copy-start.4
  47.4 2.4 %shard_map.152 = (f32[992,128]{1,0:T(8,128)S(1)}, f32[992,128]{1,0:T(8,128)}) custom-call(f32[992,128]{1,0:T(8,128)S(1)} %bitcast.18, f32[992,128]{1,0:T(8,128)S(1)} %bitcast.20, s32[16,128]{1,0:T(8,128)S(1)} %copy-done.7, bf16[64,256]{1,0:T(8,128)(2,1)S(1)} %get-tuple-element.24.weights, f32[456,128]{1,0:T(8,128)S(1)} %collective-permute-done.below, ...), custom_call_target="tpu_custom_call" | custom-call | flops 2147483648 | bytes 4194304 | tf_op jit(solution)/shard_map/pallas_call | solution.py:23
  49.8 1.1 %shard_map.153 = f32[992,128]{1,0:T(8,128)} custom-call(f32[320,128]{1,0:T(8,128)S(1)} %all_gather.3.got, s32[1]{0:T(128)} %bitcast.9.mine, bf16[512,128]{1,0:T(8,128)(2,1)S(1)} %bitcast.24, s32[16,128]{1,0:T(8,128)S(1)} %copy-done.7, f32[64,128]{1,0:T(8,128)S(1)} %get-tuple-element.23.sea_first, f32[992,128]{1,0:T(8,128)S(1)} %get-tuple-element.25.before), custom_call_target="tpu_custom_call" | custom-call | bytes 2097152 | tf_op jit(solution)/shard_map/pallas_call | solution.py:23
  50.9 9.1 %shard_map.151 = f32[2304,128]{1,0:T(8,128)} custom-call(f32[2304,128]{1,0:T(8,128)S(1)} %bitcast.16, f32[128,128]{1,0:T(8,128)S(1)} %bitcast.23, f32[160,128]{1,0:T(8,128)S(1)} %get-tuple-element.20.fluxes, bf16[80,256]{1,0:T(8,128)(2,1)S(1)} %get-tuple-element.21.weights, f32[456,128]{1,0:T(8,128)S(1)} %collective-permute-done.below, ...), custom_call_target="tpu_custom_call" | custom-call | flops 4294967296 | bytes 8388608 | tf_op jit(solution)/shard_map/pallas_call | solution.py:23
  (6 shorter events, 0.0 us)
Async XLA Ops:
  0.6 7.1 %copy-start = (f32[72,32,128]{2,1,0:T(8,128)S(1)}, f32[72,32,128]{2,1,0:T(8,128)}, u32[]{:S(2)}) copy-start(f32[72,32,128]{2,1,0:T(8,128)} %param.13) | copy-start | bytes 3538948
  0.6 7.1 %copy-start.11 = (f32[62,62]{1,0:T(8,128)S(1)}, f32[62,62]{1,0:T(8,128)}, u32[]{:S(2)}) copy-start(f32[62,62]{1,0:T(8,128)} %sea_mix.1) | copy-start | bytes 46132
  0.7 7.1 %copy-start.10 = (f32[72,72]{1,0:T(8,128)S(1)}, f32[72,72]{1,0:T(8,128)}, u32[]{:S(2)}) copy-start(f32[72,72]{1,0:T(8,128)} %vmix.1) | copy-start | bytes 62212
  0.7 7.1 %copy-start.12 = (f32[72]{0:T(128)S(1)}, f32[72]{0:T(128)}, u32[]{:S(2)}) copy-start(f32[72]{0:T(128)} %param.15) | copy-start | bytes 868
  3.3 5.9 %collective-permute-start = (f32[456,128]{1,0:T(8,128)}, f32[456,128]{1,0:T(8,128)S(1)}, u32[]{:S(2)}, u32[]{:S(2)}) collective-permute-start(f32[456,128]{1,0:T(8,128)} %get-tuple-element.18), channel_id=1, source_target_pairs={{1,0},{2,1},{3,2},{4,3},{5,4},{6,5},{7,6},{8,7},{9,8},{10,9},{11,1... | collective-permute-start | bytes 700424 | tf_op jit(solution)/shard_map/ppermute | solution.py:310
  4.6 4.6 %collective-permute-start.1 = (f32[456,128]{1,0:T(8,128)}, f32[456,128]{1,0:T(8,128)S(1)}, u32[]{:S(2)}, u32[]{:S(2)}) collective-permute-start(f32[456,128]{1,0:T(8,128)} %get-tuple-element.19), channel_id=1, source_target_pairs={{0,1},{1,2},{2,3},{3,4},{4,5},{5,6},{6,7},{7,8},{8,9},{9,10},{10,1... | collective-permute-start | bytes 700424 | tf_op jit(solution)/shard_map/ppermute | solution.py:309
  7.7 1.6 %copy-start.3 = (f32[4,32,128]{2,1,0:T(8,128)S(1)}, f32[4,32,128]{2,1,0:T(8,128)}, u32[]{:S(2)}) copy-start(f32[4,32,128]{2,1,0:T(8,128)} %param.14) | copy-start | bytes 196612
  7.7 1.6 %copy-start.5 = (f32[32,128]{1,0:T(8,128)S(1)}, f32[32,128]{1,0:T(8,128)}, u32[]{:S(2)}) copy-start(f32[32,128]{1,0:T(8,128)} %surface.3) | copy-start | bytes 49156
  7.7 1.6 %copy-start.6 = (f32[32,128]{1,0:T(8,128)S(1)}, f32[32,128]{1,0:T(8,128)}, u32[]{:S(2)}) copy-start(f32[32,128]{1,0:T(8,128)} %rate.3) | copy-start | bytes 49156
  7.8 1.6 %copy-start.8 = (s32[32,4]{0,1:T(4,128)S(1)}, s32[32,4]{0,1:T(4,128)}, u32[]{:S(2)}) copy-start(s32[32,4]{0,1:T(4,128)} %param.20) | copy-start | bytes 1540
  7.8 1.6 %copy-start.9 = (s32[32,4]{0,1:T(4,128)S(1)}, s32[32,4]{0,1:T(4,128)}, u32[]{:S(2)}) copy-start(s32[32,4]{0,1:T(4,128)} %param.21) | copy-start | bytes 1540
  7.8 39.6 %copy-start.1 = (f32[62,16,128]{2,1,0:T(8,128)S(1)}, f32[62,16,128]{2,1,0:T(8,128)}, u32[]{:S(2)}) copy-start(f32[62,16,128]{2,1,0:T(8,128)} %param.22) | copy-start | bytes 1523716
  7.8 39.6 %copy-start.2 = (f32[62,16,128]{2,1,0:T(8,128)S(1)}, f32[62,16,128]{2,1,0:T(8,128)}, u32[]{:S(2)}) copy-start(f32[62,16,128]{2,1,0:T(8,128)} %param.23) | copy-start | bytes 1523716
  7.8 39.6 %copy-start.7 = (s32[16,128]{1,0:T(8,128)S(1)}, s32[16,128]{1,0:T(8,128)}, u32[]{:S(2)}) copy-start(s32[16,128]{1,0:T(8,128)} %wet.5) | copy-start | bytes 24580
  47.4 2.4 %copy-start.4 = (bf16[4,128,128]{2,1,0:T(8,128)(2,1)S(1)}, bf16[4,128,128]{2,1,0:T(8,128)(2,1)}, u32[]{:S(2)}) copy-start(bf16[4,128,128]{2,1,0:T(8,128)(2,1)} %param.19) | copy-start | bytes 393220

commit v3 on v1

--- a/solution.py
+++ b/solution.py
@@ -19,14 +19,14 @@
     return -(-n // m) * m
 
 
-def call(kernel, out_shape, *args, scratch=(), in_specs=None, flops=0, moved=0):
+def call(kernel, out_shape, *args, scratch=(), in_specs=None, flops=0, moved=0, grant=24):
     return pl.pallas_call(
         kernel,
         out_shape=out_shape,
         in_specs=in_specs or [VMEM] * len(args),
         out_specs=jax.tree.map(lambda _: VMEM, out_shape),
         scratch_shapes=list(scratch),
-        compiler_params=pltpu.CompilerParams(vmem_limit_bytes=24 * 2**20),
+        compiler_params=pltpu.CompilerParams(vmem_limit_bytes=grant * 2**20),
         cost_estimate=pl.CostEstimate(flops=flops, bytes_accessed=moved, transcendentals=0),
     )(*args)
 
@@ -64,7 +64,31 @@
     return (high + pltpu.roll(high, depth, 1) + pltpu.roll(low, 2 * depth, 1)).astype(bf16)
 
 
-def local_kernel(sizes, vmix, curve, sea_mix, sky, rows_of_mix, source_rows, weights, sea_weights, sea_first, own):
+def row_of(ref, first, count, step, size):
+    x = ref[pl.ds(first, count, stride=step), :]
+    if count < size:
+        x = jnp.concatenate([x, jnp.zeros((size - count, x.shape[1]), f32)], 0)
+    return x
+
+
+def beside(x):
+    return pltpu.roll(x, 1, 1) + pltpu.roll(x, x.shape[1] - 1, 1)
+
+
+def stencil(x):
+    return [x[i - 1] + x[i] + x[i + 1] + beside(x[i]) for i in range(1, len(x) - 1)]
+
+
+def product(weights, x):
+    high, low = split(x)
+    return jnp.dot(weights, jnp.concatenate([high, low, high], 0), preferred_element_type=f32)
+
+
+def local_kernel(
+    sizes, vmix, curve, sea_mix, sky, warmth, brine, wet,
+    rows_of_mix, source_rows, weights, source_weights, sea_weights, sea_first, own, middle, warm_out, brine_out,
+    spread, sea_spread,
+):
     levels, rows, steps, sea_levels, sea_rows, stride, sea_stride = sizes
     width = sky.shape[1]
     depth = up_to(levels + 2 * steps, 16)
@@ -92,13 +116,17 @@
     wide = jnp.concatenate(
         [powers[-1] * atm_diffusion**steps, jnp.zeros((levels, width - levels), f32)], 1
     )
+    sources = jnp.zeros((levels, width), f32)
     for j in range(steps):
         factor = atm_diffusion ** (steps - 1 - j)
-        wide = jnp.where(lane == levels + j, of_curve[steps - 1 - j] * factor, wide)
-        wide = jnp.where(lane == levels + steps + j, of_last[steps - 1 - j] * -factor, wide)
-    wide = jnp.concatenate([wide, jnp.zeros((levels, width), f32)], 1)
-    wide = jnp.concatenate([wide, jnp.zeros((weights.shape[0] - levels, 2 * width), f32)], 0)
+        for at, value in ((j, of_curve[steps - 1 - j] * factor), (steps + j, of_last[steps - 1 - j] * -factor)):
+            wide = jnp.where(lane == levels + at, value, wide)
+            sources = jnp.where(lane == at, value, sources)
+    more = jnp.zeros((weights.shape[0] - levels, width), f32)
+    wide = jnp.concatenate([wide, more], 0)
+    wide = jnp.concatenate([wide, jnp.zeros_like(wide)], 1)
     weights[...] = three_terms(wide, depth)
+    source_weights[...] = three_terms(jnp.concatenate([sources, more], 0), 16)
     sea = sea_mix[...]
     sea = jnp.concatenate([sea, jnp.zeros((sea_levels, 2 * width - sea_levels), f32)], 1)
     sea = jnp.concatenate([sea, jnp.zeros((sea_stride - sea_levels, 2 * width), f32)], 0)
@@ -111,6 +139,55 @@
             sums[s] = sums[s] + rows_of_mix[s * levels + l : s * levels + l + 1, :] * x
     for s in range(steps - 1):
         own[s * rows : (s + 1) * rows, :] = sums[s]
+
+    inner = rows - 2 * HALO
+
+    @pl.loop(0, levels // 8)
+    def _(c):
+        x = [sky[pl.ds(c * 8 * rows + r, 8, stride=rows), :] for r in range(rows)]
+        for _ in range(steps):
+            x = stencil(x)
+        for r in range(inner):
+            spread[pl.ds(pl.multiple_of(r * depth + c * 8, 8), 8), :] = x[r]
+
+    if depth > levels:
+        for r in range(inner):
+            spread[r * depth + levels : (r + 1) * depth, :] = jnp.zeros((depth - levels, width), f32)
+    w = weights[:, : 3 * depth]
+    for r in range(0, inner, 2):
+        x = jnp.concatenate([spread[(r + i) * depth : (r + i + 1) * depth, :] for i in range(2)], 1)
+        y = product(w, x)
+        for i in range(2):
+            middle[(r + i) * levels : (r + i + 1) * levels, :] = y[:levels, i * width : (i + 1) * width]
+
+    m = wet[...].astype(f32)
+    mark = [m[r : r + 1] for r in range(sea_rows)]
+    edge = jnp.zeros((1, width), f32)
+
+    def near(x):
+        x = [jnp.zeros_like(x[0])] + x + [jnp.zeros_like(x[0])]
+        return [x[i - 1] + x[i + 1] + beside(x[i]) for i in range(1, len(x) - 1)]
+
+    around = (
+        jnp.concatenate([edge, m[:-1]], 0) + jnp.concatenate([m[1:], edge], 0) + beside(m)
+    ) * ocean_diffusion
+    share = [around[r : r + 1] for r in range(sea_rows)]
+    for f, field in enumerate((warmth, brine)):
+        for c in range(sea_stride // 8):
+            count = min(8, sea_levels - c * 8)
+            x = [row_of(field, c * 8 * sea_rows + r, count, sea_rows, 8) for r in range(sea_rows)]
+            y = near([mark[r] * x[r] for r in range(sea_rows)])
+            for r in range(sea_rows):
+                at = r * sea_stride + c * 8
+                sea_spread[f, at : at + 8, :] = x[r] + mark[r] * (ocean_diffusion * y[r] - x[r] * share[r])
+    w = sea_weights[:, : 3 * sea_stride]
+    for r in range(sea_rows):
+        x = jnp.concatenate([sea_spread[f, r * sea_stride : (r + 1) * sea_stride, :] for f in range(2)], 1)
+        y = product(w, x)
+        for f, (field, out) in enumerate(((warmth, warm_out), (brine, brine_out))):
+            old = field[pl.ds(r, sea_levels, stride=sea_rows), :]
+            new = y[:sea_levels, f * width : (f + 1) * width]
+            out[pl.ds(r, sea_levels, stride=sea_rows), :] = mark[r] * new + (1.0 - mark[r]) * old
 
 
 def cross(x):
@@ -159,7 +236,9 @@
             state = state + source_rows[m : m + 1, :] * force[i]
             state = state - source_rows[steps - 1 + m : steps + m, :] * flux[i]
         flux.append(coef * (state - surf))
-        fluxes[s * (rows + 2 * HALO) : (s + 1) * (rows + 2 * HALO), :] = flux[s]
+        reach = rows + 2 * HALO
+        fluxes[pl.ds(s, reach, stride=2 * steps), :] = force[s]
+        fluxes[pl.ds(steps + s, reach, stride=2 * steps), :] = flux[s]
     total = flux[0][:rows]
     for s in range(1, steps):
         total = total + flux[s][:rows]
@@ -176,83 +255,87 @@
         sent[t * per + rows : (t + 1) * per, :] = table
 
 
-def sky_kernel(sizes, sky, forcing, fluxes, weights, below, above, out, halo, spread):
+def rest_kernel(
+    sizes, sky, fluxes, weights, source_weights, middle, warmth, brine, wet, sea_weights, warm, salt, below, above,
+    out, warm_out, brine_out, spread, sources
+):
     levels, rows, steps, sea_levels, sea_rows, stride, sea_stride = sizes
     width = sky.shape[1]
     depth = up_to(levels + 2 * steps, 16)
-    halo[: HALO * stride, :] = below[: HALO * stride, :]
-    halo[HALO * stride :, :] = above[: HALO * stride, :]
-
-    def edge(l):
-        return halo[pl.ds(l, 2 * HALO, stride=stride), :]
-
-    inside = edge(levels + steps + 2)
-
-    def times(x, n):
-        for i in range(n):
-            x = cross(x)
-            if i < n - 1:
-                x = masked(x, rows, inside)
-        return x[:rows]
-
-    @pl.loop(0, levels // 4)
-    def _(q):
-        for i in range(4):
-            l = q * 4 + i
-            at = pl.multiple_of(l * rows, 8)
-            x = jnp.concatenate([sky[pl.ds(at, rows), :], edge(l)], 0)
-            spread[pl.ds(at, rows), :] = times(x, steps)
-
-    for j in range(steps):
-        x = jnp.concatenate([forcing[j * rows : (j + 1) * rows, :], edge(levels + j)], 0)
-        spread[(levels + j) * rows : (levels + j + 1) * rows, :] = times(x, steps - 1 - j)
-        x = fluxes[j * (rows + 2 * HALO) : (j + 1) * (rows + 2 * HALO), :]
-        spread[(levels + steps + j) * rows : (levels + steps + j + 1) * rows, :] = times(
-            x, steps - 1 - j
+    flag = levels + steps + 2
+    inside_above, inside_below = above[flag : flag + 1, :], below[flag : flag + 1, :]
+
+    reach = rows + 2 * HALO
+    x = [fluxes[(r % reach) * 2 * steps : (r % reach + 1) * 2 * steps, :] for r in range(1 - steps, rows + steps - 1)]
+    field = lax.broadcasted_iota(jnp.int32, (2 * steps, width), 0) % steps
+    for n in range(1, steps):
+        y = stencil(x)
+        x = [jnp.where(field < steps - n, y[i], x[i + 1]) for i in range(len(y))]
+        for i in range(steps - 1 - n):
+            x[i] = x[i] * inside_above
+            x[-1 - i] = x[-1 - i] * inside_below
+    for r in range(rows):
+        sources[r * 16 : (r + 1) * 16, :] = jnp.concatenate([x[r], jnp.zeros((16 - 2 * steps, width), f32)], 0)
+
+    @pl.loop(0, levels // 8)
+    def _(c):
+        def own(r):
+            return sky[pl.ds(c * 8 * rows + r, 8, stride=rows), :]
+
+        def other(ref, j):
+            return ref[pl.ds(pl.multiple_of(j * stride + c * 8, 8), 8), :]
+
+        top = [other(above, j) for j in range(HALO)] + [own(r) for r in range(2 * HALO)]
+        low = [own(rows - 2 * HALO + r) for r in range(2 * HALO)] + [other(below, j) for j in range(HALO)]
+        for n in range(steps):
+            top, low = stencil(top), stencil(low)
+            for i in range(steps - 1 - n):
+                top[i] = top[i] * inside_above
+                low[-1 - i] = low[-1 - i] * inside_below
+        for i, value in enumerate(top + low):
+            spread[pl.ds(pl.multiple_of(i * depth + c * 8, 8), 8), :] = value
+
+    w = weights[:, : 3 * depth]
+    for i in range(0, 2 * HALO, 2):
+        at = [q if q < HALO else rows - 2 * HALO + q for q in (i, i + 1)]
+        x = jnp.concatenate(
+            [
+                jnp.concatenate([spread[(i + q) * depth : i * depth + q * depth + levels, :],
+                                 sources[at[q] * 16 : at[q] * 16 + depth - levels, :]], 0)
+                for q in range(2)
+            ],
+            1,
         )
-
-    w = weights[:, : 3 * depth]
-    for r in range(0, rows, 2):
-        x = jnp.concatenate([spread[pl.ds(r + i, depth, stride=rows), :] for i in range(2)], 1)
-        high, low = split(x)
-        y = jnp.dot(w, jnp.concatenate([high, low, high], 0), preferred_element_type=f32)
-        for i in range(2):
-            out[pl.ds(r + i, levels, stride=rows), :] = y[:levels, i * width : (i + 1) * width]
-
-
-def sea_kernel(sizes, warmth, brine, wet, weights, below, above, warm_out, brine_out, edges, spread):
-    levels, rows, steps, sea_levels, sea_rows, stride, sea_stride = sizes
-    width = warmth.shape[1]
+        y = product(w, x)
+        for q in range(2):
+            out[pl.ds(at[q], levels, stride=rows), :] = y[:levels, q * width : (q + 1) * width]
+    w = source_weights[:, :48]
+    for r in range(HALO, rows - HALO, 2):
+        y = product(w, jnp.concatenate([sources[(r + q) * 16 : (r + q + 1) * 16, :] for q in range(2)], 1))
+        for q in range(2):
+            at = (r + q - HALO) * levels
+            out[pl.ds(r + q, levels, stride=rows), :] = (
+                middle[at : at + levels, :] + y[:levels, q * width : (q + 1) * width]
+            )
+
+    warm_out[...] = warm[...]
+    brine_out[...] = salt[...]
+    m = wet[...].astype(f32)
     base = HALO * stride
-    m = wet[...].astype(f32)
-    at = lax.broadcasted_iota(jnp.int32, (sea_rows, width), 0)
-
-    def around(x, top, bottom):
-        north = jnp.where(at == 0, top, pltpu.roll(x, 1, 0))
-        south = jnp.where(at == sea_rows - 1, bottom, pltpu.roll(x, sea_rows - 1, 0))
-        return north + south + pltpu.roll(x, 1, 1) + pltpu.roll(x, width - 1, 1)
-
-    mark = base + 2 * sea_stride
-    count = around(m, above[mark : mark + 1, :], below[mark : mark + 1, :])
-    for f, field in enumerate((warmth, brine)):
-        first = base + f * sea_stride
-        for l in range(sea_levels):
-            x = field[l * sea_rows : (l + 1) * sea_rows, :]
-            near = around(m * x, above[first + l : first + l + 1, :], below[first + l : first + l + 1, :])
-            spread[f, l * sea_rows : (l + 1) * sea_rows, :] = x + ocean_diffusion * (m * (near - x * count))
-        if sea_stride > sea_levels:
-            spread[f, sea_levels * sea_rows :, :] = jnp.zeros(((sea_stride - sea_levels) * sea_rows, width), f32)
-
-    w = weights[:, : 3 * sea_stride]
-    for r in range(sea_rows):
-        x = jnp.concatenate([spread[f, pl.ds(r, sea_stride, stride=sea_rows), :] for f in range(2)], 1)
-        high, low = split(x)
-        y = jnp.dot(w, jnp.concatenate([high, low, high], 0), preferred_element_type=f32)
-        wet_row = m[r : r + 1]
-        for f, (field, out) in enumerate(((warmth, warm_out), (brine, brine_out))):
-            old = field[pl.ds(r, sea_levels, stride=sea_rows), :]
-            new = y[:sea_levels, f * width : (f + 1) * width]
-            out[pl.ds(r, sea_levels, stride=sea_rows), :] = wet_row * new + (1.0 - wet_row) * old
+    w = sea_weights[:, : 3 * sea_stride]
+    for r, other in ((0, above), (sea_rows - 1, below)):
+        mark = m[r : r + 1]
+        far = other[base + 2 * sea_stride : base + 2 * sea_stride + 1, :]
+        x = []
+        for f, field in enumerate((warmth, brine)):
+            at = base + f * sea_stride
+            step = other[at : at + sea_levels, :] - field[pl.ds(r, sea_levels, stride=sea_rows), :] * far
+            step = ocean_diffusion * (mark * step)
+            x.append(jnp.concatenate([step, jnp.zeros((sea_stride - sea_levels, width), f32)], 0))
+        y = product(w, jnp.concatenate(x, 1))
+        for f, to in enumerate((warm_out, brine_out)):
+            rows_at = pl.ds(r, sea_levels, stride=sea_rows)
+            to[rows_at, :] = to[rows_at, :] + mark * y[:sea_levels, f * width : (f + 1) * width]
 
 
 def heat_kernel(sizes, topk, got, mine, shares, wet, sea_first, before, after):
@@ -298,7 +381,6 @@
     stride = up_to(levels + steps + 3, 8)
     sea_stride = up_to(sea_levels, 16)
     sizes = (levels, rows, steps, sea_levels, sea_rows, stride, sea_stride)
-    tiles = lax.axis_size("tile")
     sky2, forcing2 = sky.reshape(-1, width), forcing.reshape(-1, width)
     warmth2, brine2 = warmth.reshape(-1, width), brine.reshape(-1, width)
     flat = lambda n, kind=f32: jax.ShapeDtypeStruct((n, width), kind)
@@ -306,45 +388,43 @@
     length = HALO * stride + 2 * sea_stride + 8
     up, down = call(
         functools.partial(pack_kernel, sizes), [flat(length)] * 2,
-        sky2, forcing2, surface, rate, warmth2, brine2, wet, moved=4 << 20,
+        sky2, forcing2, surface, rate, warmth2, brine2, wet, moved=4 << 20, grant=60,
     )
     count = lax.axis_size(("tile", "comp"))
     above = lax.ppermute(down, ("tile", "comp"), [(i, i + 1) for i in range(count - 1)])
     below = lax.ppermute(up, ("tile", "comp"), [(i + 1, i) for i in range(count - 1)])
 
+    depth = up_to(levels + 2 * steps, 16)
+    inner = rows - 2 * HALO
     mix_rows = up_to(levels, 16)
-    rows_of_mix, source_rows, weights, sea_weights, sea_first, own = call(
+    sea_flat = flat(sea_levels * sea_rows)
+    (rows_of_mix, source_rows, weights, source_weights, sea_weights, sea_first, own, middle, warm, salt) = call(
         functools.partial(local_kernel, sizes),
         [
             flat((steps - 1) * levels), flat(8), jax.ShapeDtypeStruct((mix_rows, 2 * width), bf16),
-            jax.ShapeDtypeStruct((sea_stride, 2 * width), bf16), flat(sea_stride), flat((steps - 1) * rows),
+            flat(mix_rows, bf16), jax.ShapeDtypeStruct((sea_stride, 2 * width), bf16), flat(sea_stride),
+            flat((steps - 1) * rows), flat(inner * levels), sea_flat, sea_flat,
         ],
-        vmix, curve[None], sea_mix, sky2, flops=1 << 30, moved=4 << 20,
+        vmix, curve[None], sea_mix, sky2, warmth2, brine2, wet,
+        scratch=[pltpu.VMEM((inner * depth, width), f32), pltpu.VMEM((2, sea_rows * sea_stride, width), f32)],
+        flops=4 << 30, moved=8 << 20,
     )
 
     per = rows + 2 * topk
+    tiles = lax.axis_size("tile")
     sent, fluxes = call(
-        functools.partial(flux_kernel, sizes), [flat(tiles * per), flat(steps * (rows + 2 * HALO))],
+        functools.partial(flux_kernel, sizes), [flat(tiles * per), flat(2 * steps * (rows + 2 * HALO))],
         sky[-1], forcing2, surface, rate, rows_of_mix, source_rows, own, owners.T, locals_.T, below, above,
         scratch=[pltpu.VMEM((2 * HALO * stride, width), f32)], moved=2 << 20,
     )
     got = lax.all_to_all(sent.reshape(tiles, per, width), "tile", split_axis=0, concat_axis=0, tiled=True)
     got = got.reshape(-1, width)
 
-    sky_out = call(
-        functools.partial(sky_kernel, sizes), flat(levels * rows),
-        sky2, forcing2, fluxes, weights, below, above,
-        scratch=[
-            pltpu.VMEM((2 * HALO * stride, width), f32),
-            pltpu.VMEM((up_to(levels + 2 * steps, 16) * rows, width), f32),
-        ],
-        flops=4 << 30, moved=8 << 20,
-    )
-    warm, salt = call(
-        functools.partial(sea_kernel, sizes), [flat(sea_levels * sea_rows)] * 2,
-        warmth2, brine2, wet, sea_weights, below, above,
-        scratch=[pltpu.VMEM((8, width), f32), pltpu.VMEM((2, sea_stride * sea_rows, width), f32)],
-        flops=2 << 30, moved=4 << 20,
+    sky_out, warm, salt = call(
+        functools.partial(rest_kernel, sizes), [flat(levels * rows), sea_flat, sea_flat],
+        sky2, fluxes, weights, source_weights, middle, warmth2, brine2, wet, sea_weights, warm, salt, below, above,
+        scratch=[pltpu.VMEM((2 * HALO * depth, width), f32), pltpu.VMEM((rows * 16, width), f32)],
+        flops=2 << 30, moved=8 << 20,
     )
     mine = lax.axis_index("tile").astype(jnp.int32)[None]
     warm = call(

time: 39.1 us -> 37.4 us (0.957)
  the two profiles are of different devices: /device:TPU:0 before, /device:TPU:1 now
where the time goes in v3:
time: 37.4 us; the launch traced here: 36.8 us
  Pallas kernels  16.1 us (43%)
  starting transfers between devices  11.8 us (32%)
  local copies, waits for them, and re-layouts  8.06 us (22%)
  between operations  0.89 us (2%)
    pallas_call x5, Pallas kernels, call(): pl.pallas_call(kernel, out_shape=out_shape, in_specs=in_specs or [VMEM] *...  16.1 us
    unnamed x50, local copies, waits for them, and re-layouts  8.06 us
    all_to_all x1, starting transfers between devices, body(): lax.all_to_all(sent.reshape(tiles, per, width), 'tile', split_axis=0, con...  5.38 us
    ppermute x1, starting transfers between devices, body(): lax.ppermute(down, ('tile', 'comp'), [(i, i + 1) for i in range(count - 1)])  4.46 us
    ppermute x1, starting transfers between devices, body(): lax.ppermute(up, ('tile', 'comp'), [(i + 1, i) for i in range(count - 1)])  1.95 us
  transfers between devices with their start and end apart: 3, of which 0 were waited for; matrix products, arithmetic and copies ran while one was open for 0% of the time, Pallas kernels for 30%

profile of v3, /device:TPU:1, one launch (start us, length us, event | category | flops | bytes accessed | tf_op | source)
XLA Modules:
  0.0 36.8 jit_solution(8541582803775348517)
XLA Ops:
  0.6 0.0 copy-start
  0.6 0.0 copy-start.1
  0.7 0.0 copy-start.2
  0.7 0.0 copy-start.7
  0.7 0.0 copy-start.14
  0.7 2.7 %shard_map.149 = (f32[456,128]{1,0:T(8,128)}, f32[456,128]{1,0:T(8,128)}) custom-call(f32[2304,128]{1,0:T(8,128)} %bitcast.16, f32[128,128]{1,0:T(8,128)} %bitcast.26, f32[32,128]{1,0:T(8,128)} %surface.3, f32[32,128]{1,0:T(8,128)} %rate.3, f32[992,128]{1,0:T(8,128)} %bitcast.20, f32[992,128]{1,0:T(8,128)} %bitcast.23, s32[16,128]{1,0:T(8,128)} %wet.7), custom_call_target="tpu_custom_call" | custom-call | bytes 4194304 | tf_op jit(solution)/shard_map/pallas_call | solution.py:23
  3.4 2.0 %collective-permute-start = (f32[456,128]{1,0:T(8,128)}, f32[456,128]{1,0:T(8,128)S(1)}, u32[]{:S(2)}, u32[]{:S(2)}) collective-permute-start(f32[456,128]{1,0:T(8,128)} %get-tuple-element.23), channel_id=1, source_target_pairs={{1,0},{2,1},{3,2},{4,3},{5,4},{6,5},{7,6},{8,7},{9,8},{10,9},{11,1... | collective-permute-start | bytes 700424 | tf_op jit(solution)/shard_map/ppermute | solution.py:395
  5.4 4.5 %collective-permute-start.1 = (f32[456,128]{1,0:T(8,128)}, f32[456,128]{1,0:T(8,128)S(1)}, u32[]{:S(2)}, u32[]{:S(2)}) collective-permute-start(f32[456,128]{1,0:T(8,128)} %get-tuple-element.24), channel_id=1, source_target_pairs={{0,1},{1,2},{2,3},{3,4},{4,5},{5,6},{6,7},{7,8},{8,9},{9,10},{10,1... | collective-permute-start | bytes 700424 | tf_op jit(solution)/shard_map/ppermute | solution.py:394
  9.9 0.0 copy-start.3
  9.9 0.0 copy-start.5
  9.9 0.0 copy-start.6
  10.0 0.0 copy-start.8
  10.0 0.0 copy-start.9
  10.0 5.9 %shard_map.148 = (f32[216,128]{1,0:T(8,128)S(1)}, f32[8,128]{1,0:T(8,128)S(1)}, bf16[80,256]{1,0:T(8,128)(2,1)S(1)}, bf16[80,128]{1,0:T(8,128)(2,1)S(1)}, bf16[6...) custom-call(f32[72,72]{1,0:T(8,128)S(1)} %copy-done.12, ...), custom_call_target="tpu_custom_call" | custom-call | flops 4294967296 | bytes 8388608 | tf_op jit(solution)/shard_map/pallas_call | solution.py:23
  15.9 0.0 copy-start.15
  15.9 0.9 %copy-done.15 = f32[1728,128]{1,0:T(8,128)} copy-done((f32[1728,128]{1,0:T(8,128)}, f32[1728,128]{1,0:T(8,128)S(1)}, u32[]{:S(2)}) %copy-start.15) | copy-done | bytes 884760
  16.8 0.8 %copy-done.19 = f32[992,128]{1,0:T(8,128)} copy-done((f32[992,128]{1,0:T(8,128)}, f32[992,128]{1,0:T(8,128)S(1)}, u32[]{:S(2)}) %copy-start.19) | copy-done | bytes 507928
  17.6 0.0 collective-permute-done.below
  17.6 0.0 collective-permute-done.1.above
  17.7 1.1 %shard_map.150 = (f32[320,128]{1,0:T(8,128)}, f32[320,128]{1,0:T(8,128)S(1)}) custom-call(f32[32,128]{1,0:T(8,128)S(1)} %slice_bitcast_fusion.sky, f32[128,128]{1,0:T(8,128)S(1)} %bitcast.27, f32[32,128]{1,0:T(8,128)S(1)} %copy-done.5, f32[32,128]{1,0:T(8,128)S(1)} %copy-done.6, f32[216,128]{1,0:T(8,128)S(1)} %get-tuple-element.20.rows_of_mix, ...), custom_call_target="tpu_custom_call" | custom-call | bytes 2097152 | tf_op jit(solution)/shard_map/pallas_call | solution.py:23
  18.7 0.7 %copy-done.10 = f32[320,128]{1,0:T(8,128)} copy-done((f32[320,128]{1,0:T(8,128)}, f32[320,128]{1,0:T(8,128)S(1)}, u32[]{:S(2)}) %copy-start.10) | copy-done | bytes 163864
  19.4 0.0 copy-done.23
  19.4 5.4 %all-to-all-start = ((f32[8,40,128]{2,1,0:T(8,128)}), f32[8,40,128]{2,1,0:T(8,128)S(1)}, u32[]{:S(2)}, u32[]{:S(2)}) async-start(f32[8,40,128]{2,1,0:T(8,128)} %bitcast.9), calls=%async_computation | async-start | bytes 327680 | tf_op jit(solution)/shard_map/all_to_all | solution.py:420
  24.8 0.9 %copy-done.11 = f32[320,128]{1,0:T(8,128)S(1)} copy-done((f32[320,128]{1,0:T(8,128)S(1)}, f32[320,128]{1,0:T(8,128)}, u32[]{:S(2)}) %copy-start.11) | copy-done | bytes 163864
  25.7 1.2 %copy-done.16 = f32[1728,128]{1,0:T(8,128)S(1)} copy-done((f32[1728,128]{1,0:T(8,128)S(1)}, f32[1728,128]{1,0:T(8,128)}, u32[]{:S(2)}) %copy-start.16) | copy-done | bytes 884760
  26.9 1.0 %copy-done.18 = f32[992,128]{1,0:T(8,128)S(1)} copy-done((f32[992,128]{1,0:T(8,128)S(1)}, f32[992,128]{1,0:T(8,128)}, u32[]{:S(2)}) %copy-start.18) | copy-done | bytes 507928
  27.9 1.0 %copy-done.20 = f32[992,128]{1,0:T(8,128)S(1)} copy-done((f32[992,128]{1,0:T(8,128)S(1)}, f32[992,128]{1,0:T(8,128)}, u32[]{:S(2)}) %copy-start.20) | copy-done | bytes 507928
  28.9 0.8 %copy-done.22 = bf16[64,256]{1,0:T(8,128)(2,1)S(1)} copy-done((bf16[64,256]{1,0:T(8,128)(2,1)S(1)}, bf16[64,256]{1,0:T(8,128)(2,1)}, u32[]{:S(2)}) %copy-start.22) | copy-done | bytes 32792
  29.7 0.7 %copy-done.24 = bf16[80,128]{1,0:T(8,128)(2,1)S(1)} copy-done((bf16[80,128]{1,0:T(8,128)(2,1)S(1)}, bf16[80,128]{1,0:T(8,128)(2,1)}, u32[]{:S(2)}) %copy-start.24) | copy-done | bytes 20504
  30.4 5.3 %shard_map.151 = (f32[2304,128]{1,0:T(8,128)}, f32[992,128]{1,0:T(8,128)S(1)}, f32[992,128]{1,0:T(8,128)}) custom-call(f32[2304,128]{1,0:T(8,128)S(1)} %bitcast.18, f32[320,128]{1,0:T(8,128)S(1)} %copy-done.11, bf16[80,256]{1,0:T(8,128)(2,1)S(1)} %get-tuple-element.26.weights, bf16[80,128]{1,0:T(8,128)(2,1)S(1)} %copy-done.24, f32[1728,128]{1,0:T(8,128)S(1)} %copy-done.16, ...), custom_call_target="tpu_custom_call" | custom-call | flops 2147483648 | bytes 8388608 | tf_op jit(solution)/shard_map/pallas_call | solution.py:23
  35.7 0.0 all-to-all-done
  35.7 1.1 %shard_map.152 = f32[992,128]{1,0:T(8,128)} custom-call(f32[320,128]{1,0:T(8,128)S(1)} %bitcast.19, s32[1]{0:T(128)} %bitcast.11.mine, bf16[512,128]{1,0:T(8,128)(2,1)S(1)} %bitcast.28, s32[16,128]{1,0:T(8,128)S(1)} %copy-done.7, f32[64,128]{1,0:T(8,128)S(1)} %get-tuple-element.34.sea_first, f32[992,128]{1,0:T(8,128)S(1)} %get-tuple-element.35.before), custom_call_target="tpu_custom_call" | custom-call | bytes 2097152 | tf_op jit(solution)/shard_map/pallas_call | solution.py:23
  (30 shorter events, 0.1 us)
Async XLA Ops:
  0.6 9.2 %copy-start = (f32[72,32,128]{2,1,0:T(8,128)S(1)}, f32[72,32,128]{2,1,0:T(8,128)}, u32[]{:S(2)}) copy-start(f32[72,32,128]{2,1,0:T(8,128)} %param.13) | copy-start | bytes 3538948
  0.6 9.2 %copy-start.1 = (f32[62,16,128]{2,1,0:T(8,128)S(1)}, f32[62,16,128]{2,1,0:T(8,128)}, u32[]{:S(2)}) copy-start(f32[62,16,128]{2,1,0:T(8,128)} %param.22) | copy-start | bytes 1523716
  0.7 9.2 %copy-start.2 = (f32[62,16,128]{2,1,0:T(8,128)S(1)}, f32[62,16,128]{2,1,0:T(8,128)}, u32[]{:S(2)}) copy-start(f32[62,16,128]{2,1,0:T(8,128)} %param.23) | copy-start | bytes 1523716
  0.7 9.2 %copy-start.7 = (s32[16,128]{1,0:T(8,128)S(1)}, s32[16,128]{1,0:T(8,128)}, u32[]{:S(2)}) copy-start(s32[16,128]{1,0:T(8,128)} %wet.7) | copy-start | bytes 24580
  0.7 9.2 %copy-start.14 = (f32[72]{0:T(128)S(1)}, f32[72]{0:T(128)}, u32[]{:S(2)}) copy-start(f32[72]{0:T(128)} %param.15) | copy-start | bytes 868
  0.7 9.2 %copy-start.12 = (f32[72,72]{1,0:T(8,128)S(1)}, f32[72,72]{1,0:T(8,128)}, u32[]{:S(2)}) copy-start(f32[72,72]{1,0:T(8,128)} %vmix.1) | copy-start | bytes 62212
  0.7 9.2 %copy-start.13 = (f32[62,62]{1,0:T(8,128)S(1)}, f32[62,62]{1,0:T(8,128)}, u32[]{:S(2)}) copy-start(f32[62,62]{1,0:T(8,128)} %sea_mix.1) | copy-start | bytes 46132
  3.4 14.2 %collective-permute-start = (f32[456,128]{1,0:T(8,128)}, f32[456,128]{1,0:T(8,128)S(1)}, u32[]{:S(2)}, u32[]{:S(2)}) collective-permute-start(f32[456,128]{1,0:T(8,128)} %get-tuple-element.23), channel_id=1, source_target_pairs={{1,0},{2,1},{3,2},{4,3},{5,4},{6,5},{7,6},{8,7},{9,8},{10,9},{11,1... | collective-permute-start | bytes 700424 | tf_op jit(solution)/shard_map/ppermute | solution.py:395
  5.4 12.2 %collective-permute-start.1 = (f32[456,128]{1,0:T(8,128)}, f32[456,128]{1,0:T(8,128)S(1)}, u32[]{:S(2)}, u32[]{:S(2)}) collective-permute-start(f32[456,128]{1,0:T(8,128)} %get-tuple-element.24), channel_id=1, source_target_pairs={{0,1},{1,2},{2,3},{3,4},{4,5},{5,6},{6,7},{7,8},{8,9},{9,10},{10,1... | collective-permute-start | bytes 700424 | tf_op jit(solution)/shard_map/ppermute | solution.py:394
  9.9 7.7 %copy-start.3 = (f32[4,32,128]{2,1,0:T(8,128)S(1)}, f32[4,32,128]{2,1,0:T(8,128)}, u32[]{:S(2)}) copy-start(f32[4,32,128]{2,1,0:T(8,128)} %param.14) | copy-start | bytes 196612
  9.9 7.7 %copy-start.5 = (f32[32,128]{1,0:T(8,128)S(1)}, f32[32,128]{1,0:T(8,128)}, u32[]{:S(2)}) copy-start(f32[32,128]{1,0:T(8,128)} %surface.3) | copy-start | bytes 49156
  9.9 7.7 %copy-start.6 = (f32[32,128]{1,0:T(8,128)S(1)}, f32[32,128]{1,0:T(8,128)}, u32[]{:S(2)}) copy-start(f32[32,128]{1,0:T(8,128)} %rate.3) | copy-start | bytes 49156
  10.0 7.7 %copy-start.8 = (s32[32,4]{0,1:T(4,128)S(1)}, s32[32,4]{0,1:T(4,128)}, u32[]{:S(2)}) copy-start(s32[32,4]{0,1:T(4,128)} %param.20) | copy-start | bytes 1540
  10.0 7.7 %copy-start.9 = (s32[32,4]{0,1:T(4,128)S(1)}, s32[32,4]{0,1:T(4,128)}, u32[]{:S(2)}) copy-start(s32[32,4]{0,1:T(4,128)} %param.21) | copy-start | bytes 1540
  15.9 0.9 %copy-start.15 = (f32[1728,128]{1,0:T(8,128)}, f32[1728,128]{1,0:T(8,128)S(1)}, u32[]{:S(2)}) copy-start(f32[1728,128]{1,0:T(8,128)S(1)} %get-tuple-element.28.middle) | copy-start | bytes 2654212
  16.8 0.8 %copy-start.19 = (f32[992,128]{1,0:T(8,128)}, f32[992,128]{1,0:T(8,128)S(1)}, u32[]{:S(2)}) copy-start(f32[992,128]{1,0:T(8,128)S(1)} %get-tuple-element.31.salt) | copy-start | bytes 1523716
  17.6 1.2 %copy-start.17 = (f32[992,128]{1,0:T(8,128)}, f32[992,128]{1,0:T(8,128)S(1)}, u32[]{:S(2)}) copy-start(f32[992,128]{1,0:T(8,128)S(1)} %get-tuple-element.30.warm) | copy-start | bytes 1523716
  17.6 1.8 %copy-start.21 = (bf16[64,256]{1,0:T(8,128)(2,1)}, bf16[64,256]{1,0:T(8,128)(2,1)S(1)}, u32[]{:S(2)}) copy-start(bf16[64,256]{1,0:T(8,128)(2,1)S(1)} %get-tuple-element.29.sea_weights) | copy-start | bytes 98308
  17.6 1.8 %copy-start.23 = (bf16[80,128]{1,0:T(8,128)(2,1)}, bf16[80,128]{1,0:T(8,128)(2,1)S(1)}, u32[]{:S(2)}) copy-start(bf16[80,128]{1,0:T(8,128)(2,1)S(1)} %get-tuple-element.27.source_weights) | copy-start | bytes 61444
  18.7 0.7 %copy-start.10 = (f32[320,128]{1,0:T(8,128)}, f32[320,128]{1,0:T(8,128)S(1)}, u32[]{:S(2)}) copy-start(f32[320,128]{1,0:T(8,128)S(1)} %get-tuple-element.25.fluxes) | copy-start | bytes 491524
  19.4 16.3 %all-to-all-start = ((f32[8,40,128]{2,1,0:T(8,128)}), f32[8,40,128]{2,1,0:T(8,128)S(1)}, u32[]{:S(2)}, u32[]{:S(2)}) async-start(f32[8,40,128]{2,1,0:T(8,128)} %bitcast.9), calls=%async_computation | async-start | bytes 327680 | tf_op jit(solution)/shard_map/all_to_all | solution.py:420
  24.8 0.9 %copy-start.11 = (f32[320,128]{1,0:T(8,128)S(1)}, f32[320,128]{1,0:T(8,128)}, u32[]{:S(2)}) copy-start(f32[320,128]{1,0:T(8,128)} %copy-done.10) | copy-start | bytes 491524
  25.7 1.2 %copy-start.16 = (f32[1728,128]{1,0:T(8,128)S(1)}, f32[1728,128]{1,0:T(8,128)}, u32[]{:S(2)}) copy-start(f32[1728,128]{1,0:T(8,128)} %copy-done.15) | copy-start | bytes 2654212
  26.9 1.0 %copy-start.18 = (f32[992,128]{1,0:T(8,128)S(1)}, f32[992,128]{1,0:T(8,128)}, u32[]{:S(2)}) copy-start(f32[992,128]{1,0:T(8,128)} %copy-done.17) | copy-start | bytes 1523716
  27.9 1.0 %copy-start.20 = (f32[992,128]{1,0:T(8,128)S(1)}, f32[992,128]{1,0:T(8,128)}, u32[]{:S(2)}) copy-start(f32[992,128]{1,0:T(8,128)} %copy-done.19) | copy-start | bytes 1523716
  28.9 0.8 %copy-start.22 = (bf16[64,256]{1,0:T(8,128)(2,1)S(1)}, bf16[64,256]{1,0:T(8,128)(2,1)}, u32[]{:S(2)}) copy-start(bf16[64,256]{1,0:T(8,128)(2,1)} %copy-done.21) | copy-start | bytes 98308
  29.7 0.7 %copy-start.24 = (bf16[80,128]{1,0:T(8,128)(2,1)S(1)}, bf16[80,128]{1,0:T(8,128)(2,1)}, u32[]{:S(2)}) copy-start(bf16[80,128]{1,0:T(8,128)(2,1)} %copy-done.23) | copy-start | bytes 61444
  30.4 5.3 %copy-start.4 = (bf16[4,128,128]{2,1,0:T(8,128)(2,1)S(1)}, bf16[4,128,128]{2,1,0:T(8,128)(2,1)}, u32[]{:S(2)}) copy-start(bf16[4,128,128]{2,1,0:T(8,128)(2,1)} %param.19) | copy-start | bytes 393220

commit v4 on v3

--- a/solution.py
+++ b/solution.py
@@ -12,6 +12,7 @@
 HALO = 4
 EXACT = lax.Precision.HIGHEST
 VMEM = pl.BlockSpec(memory_space=pltpu.VMEM)
+HBM = pl.BlockSpec(memory_space=pltpu.HBM)
 f32, bf16 = jnp.float32, jnp.bfloat16
 
 
@@ -19,37 +20,56 @@
     return -(-n // m) * m
 
 
-def call(kernel, out_shape, *args, scratch=(), in_specs=None, flops=0, moved=0, grant=24):
+def call(kernel, out_shape, *args, scratch=(), in_specs=None, out_specs=None, flops=0, moved=0):
     return pl.pallas_call(
         kernel,
         out_shape=out_shape,
         in_specs=in_specs or [VMEM] * len(args),
-        out_specs=jax.tree.map(lambda _: VMEM, out_shape),
+        out_specs=out_specs or jax.tree.map(lambda _: VMEM, out_shape),
         scratch_shapes=list(scratch),
-        compiler_params=pltpu.CompilerParams(vmem_limit_bytes=grant * 2**20),
+        compiler_params=pltpu.CompilerParams(vmem_limit_bytes=24 * 2**20),
         cost_estimate=pl.CostEstimate(flops=flops, bytes_accessed=moved, transcendentals=0),
     )(*args)
 
 
-def pack_kernel(sizes, sky, forcing, surface, rate, warmth, brine, wet, up, down):
+def copies(pairs, done):
+    return [pltpu.make_async_copy(src, dst, done.at[i]) for i, (src, dst) in enumerate(pairs)]
+
+
+def pack_kernel(
+    sizes, sky, forcing, surface, rate, warmth, brine, wet, up, down,
+    ends, force, sea, flat, marks, done
+):
     levels, rows, steps, sea_levels, sea_rows, stride, sea_stride = sizes
-    width = sky.shape[1]
-    m = wet[...].astype(f32)
-    for out, first, sea_row in ((up, 0, 0), (down, rows - HALO, sea_rows - 1)):
+    width = sky.shape[2]
+    low = rows - 8
+    moves = copies(
+        [
+            (sky.at[:, 0:8, :], ends.at[0]), (sky.at[:, low:rows, :], ends.at[1]), (forcing, force),
+            (surface, flat.at[0]), (rate, flat.at[1]), (warmth, sea.at[0]), (brine, sea.at[1]), (wet, marks),
+        ],
+        done,
+    )
+    for move in moves:
+        move.start()
+    for move in moves:
+        move.wait()
+    m = marks[...].astype(f32)
+    for which, out, first, sea_row in ((0, up, 0, 0), (1, down, rows - HALO, sea_rows - 1)):
+        end = ends.at[which].reshape(levels * 8, width)
         for j in range(HALO):
             row = first + j
-            out[j * stride : j * stride + levels, :] = sky[pl.ds(row, levels, stride=rows), :]
+            out[j * stride : j * stride + levels, :] = end[pl.ds(row - which * low, levels, stride=8), :]
             base = j * stride + levels
-            tail = [forcing[s * rows + row : s * rows + row + 1, :] for s in range(steps)]
-            tail += [surface[row : row + 1, :], rate[row : row + 1, :], jnp.ones((1, width), f32)]
+            tail = [force[s, row : row + 1, :] for s in range(steps)]
+            tail += [flat[0, row : row + 1, :], flat[1, row : row + 1, :], jnp.ones((1, width), f32)]
             tail += [jnp.zeros((stride - levels - len(tail), width), f32)]
             out[base : (j + 1) * stride, :] = jnp.concatenate(tail, 0)
         base = HALO * stride
         edge = m[sea_row : sea_row + 1]
-        out[base : base + sea_levels, :] = warmth[pl.ds(sea_row, sea_levels, stride=sea_rows), :] * edge
-        base += sea_stride
-        out[base : base + sea_levels, :] = brine[pl.ds(sea_row, sea_levels, stride=sea_rows), :] * edge
-        base += sea_stride
+        for f in range(2):
+            out[base : base + sea_levels, :] = sea[f, pl.ds(sea_row, sea_levels, stride=sea_rows), :] * edge
+            base += sea_stride
         out[base : base + 8, :] = jnp.concatenate([edge, jnp.zeros((7, width), f32)], 0)
 
 
@@ -86,9 +106,11 @@
 
 def local_kernel(
     sizes, vmix, curve, sea_mix, sky, warmth, brine, wet,
-    rows_of_mix, source_rows, weights, source_weights, sea_weights, sea_first, own, middle, warm_out, brine_out,
-    spread, sea_spread,
+    rows_of_mix, source_rows, own, *others
 ):
+    kept, found, (spread, sea_spread, done) = others[:8], others[8:16], others[16:]
+    weights, source_weights, sea_weights, sea_first, middle, warm_out, brine_out, sea_ends = found
+    moves = copies(list(zip(found, kept)), done)
     levels, rows, steps, sea_levels, sea_rows, stride, sea_stride = sizes
     width = sky.shape[1]
     depth = up_to(levels + 2 * steps, 16)
@@ -132,6 +154,8 @@
     sea = jnp.concatenate([sea, jnp.zeros((sea_stride - sea_levels, 2 * width), f32)], 0)
     sea_weights[...] = three_terms(sea, sea_stride)
     sea_first[...] = jnp.broadcast_to(sea[:, 0:1], sea_first.shape)
+    for move in moves[:4]:
+        move.start()
     sums = [jnp.zeros((rows, width), f32) for _ in range(steps - 1)]
     for l in range(levels):
         x = sky[l * rows : (l + 1) * rows, :]
@@ -159,6 +183,7 @@
         y = product(w, x)
         for i in range(2):
             middle[(r + i) * levels : (r + i + 1) * levels, :] = y[:levels, i * width : (i + 1) * width]
+    moves[4].start()
 
     m = wet[...].astype(f32)
     mark = [m[r : r + 1] for r in range(sea_rows)]
@@ -188,6 +213,13 @@
             old = field[pl.ds(r, sea_levels, stride=sea_rows), :]
             new = y[:sea_levels, f * width : (f + 1) * width]
             out[pl.ds(r, sea_levels, stride=sea_rows), :] = mark[r] * new + (1.0 - mark[r]) * old
+            if r in (0, sea_rows - 1):
+                at = (2 * f + (r > 0)) * sea_stride
+                sea_ends[at : at + sea_levels, :] = old
+    for move in moves[5:]:
+        move.start()
+    for move in moves:
+        move.wait()
 
 
 def cross(x):
@@ -203,7 +235,7 @@
 
 def flux_kernel(
     sizes, sky, forcing, surface, rate, rows_of_mix, source_rows, own, owners, locals_, below, above,
-    sent, fluxes, halo
+    sent, kept, fluxes, halo, done
 ):
     levels, rows, steps, sea_levels, sea_rows, stride, sea_stride = sizes
     width = sky.shape[1]
@@ -239,6 +271,8 @@
         reach = rows + 2 * HALO
         fluxes[pl.ds(s, reach, stride=2 * steps), :] = force[s]
         fluxes[pl.ds(steps + s, reach, stride=2 * steps), :] = flux[s]
+    move = pltpu.make_async_copy(fluxes, kept, done)
+    move.start()
     total = flux[0][:rows]
     for s in range(1, steps):
         total = total + flux[s][:rows]
@@ -253,18 +287,32 @@
     for t in range(sent.shape[0] // per):
         sent[t * per : t * per + rows, :] = mean
         sent[t * per + rows : (t + 1) * per, :] = table
+    move.wait()
 
 
 def rest_kernel(
-    sizes, sky, fluxes, weights, source_weights, middle, warmth, brine, wet, sea_weights, warm, salt, below, above,
-    out, warm_out, brine_out, spread, sources
+    sizes, sky, fluxes_in, weights_in, source_weights_in, sea_weights_in, middle_in, warm_in, salt_in, sea_ends_in,
+    wet, below, above, out, brine_out, warm_out,
+    ends, fluxes, weights, source_weights, sea_weights, middle, salt, sea_ends, spread, sources, result, done
 ):
     levels, rows, steps, sea_levels, sea_rows, stride, sea_stride = sizes
-    width = sky.shape[1]
+    width = sky.shape[2]
     depth = up_to(levels + 2 * steps, 16)
+    moves = copies(
+        [
+            (fluxes_in, fluxes), (sky.at[:, 0:8, :], ends.at[0]), (sky.at[:, rows - 8 : rows, :], ends.at[1]),
+            (sea_weights_in, sea_weights), (sea_ends_in, sea_ends), (salt_in, salt), (warm_in, warm_out),
+            (weights_in, weights), (source_weights_in, source_weights), (middle_in, middle),
+        ],
+        done,
+    )
+    count = len(moves)
+    for move in moves:
+        move.start()
     flag = levels + steps + 2
     inside_above, inside_below = above[flag : flag + 1, :], below[flag : flag + 1, :]
 
+    moves[0].wait()
     reach = rows + 2 * HALO
     x = [fluxes[(r % reach) * 2 * steps : (r % reach + 1) * 2 * steps, :] for r in range(1 - steps, rows + steps - 1)]
     field = lax.broadcasted_iota(jnp.int32, (2 * steps, width), 0) % steps
@@ -277,16 +325,42 @@
     for r in range(rows):
         sources[r * 16 : (r + 1) * 16, :] = jnp.concatenate([x[r], jnp.zeros((16 - 2 * steps, width), f32)], 0)
 
+    for move in moves[3:7]:
+        move.wait()
+    m = wet[...].astype(f32)
+    base = HALO * stride
+    w = sea_weights[:, : 3 * sea_stride]
+    for e, (r, other) in enumerate(((0, above), (sea_rows - 1, below))):
+        mark = m[r : r + 1]
+        far = other[base + 2 * sea_stride : base + 2 * sea_stride + 1, :]
+        x = []
+        for f in range(2):
+            at = base + f * sea_stride
+            mine = (2 * f + e) * sea_stride
+            step = other[at : at + sea_levels, :] - sea_ends[mine : mine + sea_levels, :] * far
+            step = ocean_diffusion * (mark * step)
+            x.append(jnp.concatenate([step, jnp.zeros((sea_stride - sea_levels, width), f32)], 0))
+        y = product(w, jnp.concatenate(x, 1))
+        for f, to in enumerate((warm_out, salt)):
+            rows_at = pl.ds(r, sea_levels, stride=sea_rows)
+            to[rows_at, :] = to[rows_at, :] + mark * y[:sea_levels, f * width : (f + 1) * width]
+    leave = [pltpu.make_async_copy(salt, brine_out, done.at[count])]
+    leave[0].start()
+
+    moves[1].wait()
+    moves[2].wait()
+    first, final = (ends.at[i].reshape(levels * 8, width) for i in range(2))
+
     @pl.loop(0, levels // 8)
     def _(c):
-        def own(r):
-            return sky[pl.ds(c * 8 * rows + r, 8, stride=rows), :]
+        def own(ref, r):
+            return ref[pl.ds(c * 64 + r, 8, stride=8), :]
 
         def other(ref, j):
             return ref[pl.ds(pl.multiple_of(j * stride + c * 8, 8), 8), :]
 
-        top = [other(above, j) for j in range(HALO)] + [own(r) for r in range(2 * HALO)]
-        low = [own(rows - 2 * HALO + r) for r in range(2 * HALO)] + [other(below, j) for j in range(HALO)]
+        top = [other(above, j) for j in range(HALO)] + [own(first, r) for r in range(2 * HALO)]
+        low = [own(final, r) for r in range(2 * HALO)] + [other(below, j) for j in range(HALO)]
         for n in range(steps):
             top, low = stencil(top), stencil(low)
             for i in range(steps - 1 - n):
@@ -295,47 +369,36 @@
         for i, value in enumerate(top + low):
             spread[pl.ds(pl.multiple_of(i * depth + c * 8, 8), 8), :] = value
 
+    for move in moves[7:]:
+        move.wait()
     w = weights[:, : 3 * depth]
-    for i in range(0, 2 * HALO, 2):
-        at = [q if q < HALO else rows - 2 * HALO + q for q in (i, i + 1)]
-        x = jnp.concatenate(
-            [
-                jnp.concatenate([spread[(i + q) * depth : i * depth + q * depth + levels, :],
-                                 sources[at[q] * 16 : at[q] * 16 + depth - levels, :]], 0)
-                for q in range(2)
-            ],
-            1,
-        )
-        y = product(w, x)
-        for q in range(2):
-            out[pl.ds(at[q], levels, stride=rows), :] = y[:levels, q * width : (q + 1) * width]
-    w = source_weights[:, :48]
-    for r in range(HALO, rows - HALO, 2):
-        y = product(w, jnp.concatenate([sources[(r + q) * 16 : (r + q + 1) * 16, :] for q in range(2)], 1))
-        for q in range(2):
-            at = (r + q - HALO) * levels
-            out[pl.ds(r + q, levels, stride=rows), :] = (
-                middle[at : at + levels, :] + y[:levels, q * width : (q + 1) * width]
-            )
-
-    warm_out[...] = warm[...]
-    brine_out[...] = salt[...]
-    m = wet[...].astype(f32)
-    base = HALO * stride
-    w = sea_weights[:, : 3 * sea_stride]
-    for r, other in ((0, above), (sea_rows - 1, below)):
-        mark = m[r : r + 1]
-        far = other[base + 2 * sea_stride : base + 2 * sea_stride + 1, :]
-        x = []
-        for f, field in enumerate((warmth, brine)):
-            at = base + f * sea_stride
-            step = other[at : at + sea_levels, :] - field[pl.ds(r, sea_levels, stride=sea_rows), :] * far
-            step = ocean_diffusion * (mark * step)
-            x.append(jnp.concatenate([step, jnp.zeros((sea_stride - sea_levels, width), f32)], 0))
-        y = product(w, jnp.concatenate(x, 1))
-        for f, to in enumerate((warm_out, brine_out)):
-            rows_at = pl.ds(r, sea_levels, stride=sea_rows)
-            to[rows_at, :] = to[rows_at, :] + mark * y[:sea_levels, f * width : (f + 1) * width]
+    v = source_weights[:, :48]
+    for g in range(rows // 8):
+        to = result.at[g].reshape(levels * 8, width)
+        for r in range(g * 8, g * 8 + 8, 2):
+            x = [sources[(r + q) * 16 : (r + q + 1) * 16, :] for q in range(2)]
+            if HALO <= r < rows - HALO:
+                y = product(v, jnp.concatenate(x, 1))
+                for q in range(2):
+                    at = (r + q - HALO) * levels
+                    to[pl.ds((r + q) % 8, levels, stride=8), :] = (
+                        middle[at : at + levels, :] + y[:levels, q * width : (q + 1) * width]
+                    )
+            else:
+                i = r if r < HALO else r - rows + 2 * HALO
+                x = [
+                    jnp.concatenate(
+                        [spread[(i + q) * depth : (i + q) * depth + levels, :], x[q][: depth - levels]], 0
+                    )
+                    for q in range(2)
+                ]
+                y = product(w, jnp.concatenate(x, 1))
+                for q in range(2):
+                    to[pl.ds((r + q) % 8, levels, stride=8), :] = y[:levels, q * width : (q + 1) * width]
+        leave.append(pltpu.make_async_copy(result.at[g], out.at[:, g], done.at[count + 1 + g]))
+        leave[-1].start()
+    for move in leave:
+        move.wait()
 
 
 def heat_kernel(sizes, topk, got, mine, shares, wet, sea_first, before, after):
@@ -385,10 +448,15 @@
     warmth2, brine2 = warmth.reshape(-1, width), brine.reshape(-1, width)
     flat = lambda n, kind=f32: jax.ShapeDtypeStruct((n, width), kind)
 
+    space = lambda *shape: pltpu.VMEM(shape, f32)
     length = HALO * stride + 2 * sea_stride + 8
     up, down = call(
         functools.partial(pack_kernel, sizes), [flat(length)] * 2,
-        sky2, forcing2, surface, rate, warmth2, brine2, wet, moved=4 << 20, grant=60,
+        sky, forcing, surface, rate, warmth2, brine2, wet, moved=4 << 20, in_specs=[HBM] * 7,
+        scratch=[
+            space(2, levels, 8, width), space(steps, rows, width), space(2, sea_levels * sea_rows, width),
+            space(2, rows, width), pltpu.VMEM(wet.shape, wet.dtype), pltpu.SemaphoreType.DMA((8,)),
+        ],
     )
     count = lax.axis_size(("tile", "comp"))
     above = lax.ppermute(down, ("tile", "comp"), [(i, i + 1) for i in range(count - 1)])
@@ -398,32 +466,45 @@
     inner = rows - 2 * HALO
     mix_rows = up_to(levels, 16)
     sea_flat = flat(sea_levels * sea_rows)
-    (rows_of_mix, source_rows, weights, source_weights, sea_weights, sea_first, own, middle, warm, salt) = call(
+    kept = [
+        jax.ShapeDtypeStruct((mix_rows, 2 * width), bf16), flat(mix_rows, bf16),
+        jax.ShapeDtypeStruct((sea_stride, 2 * width), bf16), flat(sea_stride), flat(inner * levels),
+        sea_flat, sea_flat, flat(4 * sea_stride),
+    ]
+    found = [pltpu.VMEM(k.shape, k.dtype) for k in kept]
+    (rows_of_mix, source_rows, own, weights, source_weights, sea_weights, sea_first, middle, warm, salt, sea_ends) = call(
         functools.partial(local_kernel, sizes),
-        [
-            flat((steps - 1) * levels), flat(8), jax.ShapeDtypeStruct((mix_rows, 2 * width), bf16),
-            flat(mix_rows, bf16), jax.ShapeDtypeStruct((sea_stride, 2 * width), bf16), flat(sea_stride),
-            flat((steps - 1) * rows), flat(inner * levels), sea_flat, sea_flat,
+        [flat((steps - 1) * levels), flat(8), flat((steps - 1) * rows)] + kept,
+        vmix, curve[None], sea_mix, sky2, warmth2, brine2, wet,
+        out_specs=[VMEM] * 3 + [HBM] * 8,
+        scratch=found + [
+            space(inner * depth, width), space(2, sea_rows * sea_stride, width), pltpu.SemaphoreType.DMA((8,)),
         ],
-        vmix, curve[None], sea_mix, sky2, warmth2, brine2, wet,
-        scratch=[pltpu.VMEM((inner * depth, width), f32), pltpu.VMEM((2, sea_rows * sea_stride, width), f32)],
         flops=4 << 30, moved=8 << 20,
     )
 
     per = rows + 2 * topk
     tiles = lax.axis_size("tile")
+    reach = 2 * steps * (rows + 2 * HALO)
     sent, fluxes = call(
-        functools.partial(flux_kernel, sizes), [flat(tiles * per), flat(2 * steps * (rows + 2 * HALO))],
+        functools.partial(flux_kernel, sizes), [flat(tiles * per), flat(reach)],
         sky[-1], forcing2, surface, rate, rows_of_mix, source_rows, own, owners.T, locals_.T, below, above,
-        scratch=[pltpu.VMEM((2 * HALO * stride, width), f32)], moved=2 << 20,
+        scratch=[space(reach, width), space(2 * HALO * stride, width), pltpu.SemaphoreType.DMA],
+        out_specs=[VMEM, HBM], moved=2 << 20,
     )
     got = lax.all_to_all(sent.reshape(tiles, per, width), "tile", split_axis=0, concat_axis=0, tiled=True)
     got = got.reshape(-1, width)
 
-    sky_out, warm, salt = call(
-        functools.partial(rest_kernel, sizes), [flat(levels * rows), sea_flat, sea_flat],
-        sky2, fluxes, weights, source_weights, middle, warmth2, brine2, wet, sea_weights, warm, salt, below, above,
-        scratch=[pltpu.VMEM((2 * HALO * depth, width), f32), pltpu.VMEM((rows * 16, width), f32)],
+    sky_out, salt, warm = call(
+        functools.partial(rest_kernel, sizes),
+        [jax.ShapeDtypeStruct((levels, rows // 8, 8, width), f32), sea_flat, sea_flat],
+        sky, fluxes, weights, source_weights, sea_weights, middle, warm, salt, sea_ends, wet, below, above,
+        in_specs=[HBM] * 9 + [VMEM] * 3, out_specs=[HBM, HBM, VMEM],
+        scratch=[
+            space(2, levels, 8, width), space(reach, width), found[0], found[1], found[2], found[4], found[6], found[7],
+            space(2 * HALO * depth, width), space(rows * 16, width), space(rows // 8, levels, 8, width),
+            pltpu.SemaphoreType.DMA((11 + rows // 8,)),
+        ],
         flops=2 << 30, moved=8 << 20,
     )
     mine = lax.axis_index("tile").astype(jnp.int32)[None]

time: 37.4 us -> 44 us (1.18)
  local copies, waits for them, and re-layouts: 8.06 us -> 13 us
  Pallas kernels: 16.1 us -> 17.3 us
    unnamed x50 -> x58, local copies, waits for them, and re-layouts: 8.06 us -> 13 us
    pallas_call x5, Pallas kernels: 16.1 us -> 17.3 us  [call(): pl.pallas_call(kernel, out_shape=out_shape, in_specs=in_specs or [VMEM] *...]
  transfers between devices with their start and end apart: 3 -> 3, of which waited for: 0 -> 0; matrix products, arithmetic and copies ran while one was open for 0% -> 0% of each run, Pallas kernels for 30% -> 32%
where the time goes in v4:
time: 44 us; the launch traced here: 43.1 us
  Pallas kernels  17.3 us (39%)
  local copies, waits for them, and re-layouts  13 us (30%)
  starting transfers between devices  11.8 us (27%)
  between operations  0.91 us (2%)
    pallas_call x5, Pallas kernels, call(): pl.pallas_call(kernel, out_shape=out_shape, in_specs=in_specs or [VMEM] *...  17.3 us
    unnamed x58, local copies, waits for them, and re-layouts  13 us
    all_to_all x1, starting transfers between devices, body(): lax.all_to_all(sent.reshape(tiles, per, width), 'tile', split_axis=0, con...  5.39 us
    ppermute x1, starting transfers between devices, body(): lax.ppermute(down, ('tile', 'comp'), [(i, i + 1) for i in range(count - 1)])  4.46 us
    ppermute x1, starting transfers between devices, body(): lax.ppermute(up, ('tile', 'comp'), [(i + 1, i) for i in range(count - 1)])  1.97 us
  transfers between devices with their start and end apart: 3, of which 0 were waited for; matrix products, arithmetic and copies ran while one was open for 0% of the time, Pallas kernels for 32%

profile of v4, /device:TPU:1, one launch (start us, length us, event | category | flops | bytes accessed | tf_op | source)
XLA Modules:
  0.0 43.1 jit_solution(5711373169013231116)
XLA Ops:
  0.7 1.3 %copy-done = f32[72,32,128]{2,1,0:T(8,128)S(1)} copy-done((f32[72,32,128]{2,1,0:T(8,128)S(1)}, f32[72,32,128]{2,1,0:T(8,128)}, u32[]{:S(2)}) %copy-start) | copy-done | bytes 1179672
  1.9 1.0 %copy-done.2 = f32[62,16,128]{2,1,0:T(8,128)S(1)} copy-done((f32[62,16,128]{2,1,0:T(8,128)S(1)}, f32[62,16,128]{2,1,0:T(8,128)}, u32[]{:S(2)}) %copy-start.2) | copy-done | bytes 507928
  3.0 1.0 %copy-done.3 = f32[62,16,128]{2,1,0:T(8,128)S(1)} copy-done((f32[62,16,128]{2,1,0:T(8,128)S(1)}, f32[62,16,128]{2,1,0:T(8,128)}, u32[]{:S(2)}) %copy-start.3) | copy-done | bytes 507928
  4.0 0.8 %copy-done.4 = f32[4,32,128]{2,1,0:T(8,128)S(1)} copy-done((f32[4,32,128]{2,1,0:T(8,128)S(1)}, f32[4,32,128]{2,1,0:T(8,128)}, u32[]{:S(2)}) %copy-start.4) | copy-done | bytes 65560
  4.8 0.7 %copy-done.6 = f32[32,128]{1,0:T(8,128)S(1)} copy-done((f32[32,128]{1,0:T(8,128)S(1)}, f32[32,128]{1,0:T(8,128)}, u32[]{:S(2)}) %copy-start.6) | copy-done | bytes 16408
  5.6 0.7 %copy-done.8 = f32[32,128]{1,0:T(8,128)S(1)} copy-done((f32[32,128]{1,0:T(8,128)S(1)}, f32[32,128]{1,0:T(8,128)}, u32[]{:S(2)}) %copy-start.8) | copy-done | bytes 16408
  6.3 0.7 %copy-done.10 = s32[16,128]{1,0:T(8,128)S(1)} copy-done((s32[16,128]{1,0:T(8,128)S(1)}, s32[16,128]{1,0:T(8,128)}, u32[]{:S(2)}) %copy-start.10) | copy-done | bytes 8216
  7.0 1.1 %shard_map.149 = (f32[456,128]{1,0:T(8,128)S(1)}, f32[456,128]{1,0:T(8,128)S(1)}) custom-call(f32[72,32,128]{2,1,0:T(8,128)S(1)} %copy-done, f32[4,32,128]{2,1,0:T(8,128)S(1)} %copy-done.4, f32[32,128]{1,0:T(8,128)S(1)} %copy-done.6, f32[32,128]{1,0:T(8,128)S(1)} %copy-done.8, f32[992,128]{1,0:T(8,128)S(1)} %bitcast.18, f32[992,128]{1,0:T(8,128)S(1)} %bitcast.20, ...), custom_call_target="tpu_custom_call" | custom-call | bytes 4194304 | tf_op jit(solution)/shard_map/pallas_call | solution.py:24
  8.1 2.0 %collective-permute-start = (f32[456,128]{1,0:T(8,128)S(1)}, f32[456,128]{1,0:T(8,128)S(1)}, u32[]{:S(2)}, u32[]{:S(2)}) collective-permute-start(f32[456,128]{1,0:T(8,128)S(1)} %get-tuple-element.24), channel_id=1, source_target_pairs={{1,0},{2,1},{3,2},{4,3},{5,4},{6,5},{7,6},{8,7},{9,8},{10,9},{11,1... | collective-permute-start | bytes 700424 | tf_op jit(solution)/shard_map/ppermute | solution.py:463
  10.0 4.5 %collective-permute-start.1 = (f32[456,128]{1,0:T(8,128)S(1)}, f32[456,128]{1,0:T(8,128)S(1)}, u32[]{:S(2)}, u32[]{:S(2)}) collective-permute-start(f32[456,128]{1,0:T(8,128)S(1)} %get-tuple-element.25), channel_id=1, source_target_pairs={{0,1},{1,2},{2,3},{3,4},{4,5},{5,6},{6,7},{7,8},{8,9},{9,10},{10,1... | collective-permute-start | bytes 700424 | tf_op jit(solution)/shard_map/ppermute | solution.py:462
  14.6 0.0 copy-start.7
  14.6 0.0 copy-start.9
  14.6 0.0 copy-start.12
  14.6 0.0 copy-start.13
  14.6 0.0 copy-start.11
  14.6 7.8 %shard_map.148 = (f32[216,128]{1,0:T(8,128)S(1)}, f32[8,128]{1,0:T(8,128)S(1)}, f32[96,128]{1,0:T(8,128)S(1)}, bf16[80,256]{1,0:T(8,128)(2,1)S(1)}, bf16[80,128]...) custom-call(f32[72,72]{1,0:T(8,128)S(1)} %copy-done.14, ...), custom_call_target="tpu_custom_call" | custom-call | flops 4294967296 | bytes 8388608 | tf_op jit(solution)/shard_map/pallas_call | solution.py:24
  22.4 0.0 copy-start.19
  22.5 0.8 %copy-done.19 = f32[992,128]{1,0:T(8,128)} copy-done((f32[992,128]{1,0:T(8,128)}, f32[992,128]{1,0:T(8,128)S(1)}, u32[]{:S(2)}) %copy-start.19) | copy-done | bytes 507928
  23.2 0.7 %copy-done.21 = f32[256,128]{1,0:T(8,128)} copy-done((f32[256,128]{1,0:T(8,128)}, f32[256,128]{1,0:T(8,128)S(1)}, u32[]{:S(2)}) %copy-start.21) | copy-done | bytes 131096
  23.9 0.0 collective-permute-done.below
  24.0 1.4 %shard_map.150 = (f32[320,128]{1,0:T(8,128)}, f32[320,128]{1,0:T(8,128)S(1)}) custom-call(f32[32,128]{1,0:T(8,128)S(1)} %slice_bitcast_fusion.sky, f32[128,128]{1,0:T(8,128)S(1)} %bitcast.22, f32[32,128]{1,0:T(8,128)S(1)} %copy-done.7, f32[32,128]{1,0:T(8,128)S(1)} %copy-done.9, f32[216,128]{1,0:T(8,128)S(1)} %get-tuple-element.21.rows_of_mix, ...), custom_call_target="tpu_custom_call" | custom-call | bytes 2097152 | tf_op jit(solution)/shard_map/pallas_call | solution.py:24
  25.4 5.4 %all-to-all-start = ((f32[8,40,128]{2,1,0:T(8,128)}), f32[8,40,128]{2,1,0:T(8,128)S(1)}, u32[]{:S(2)}, u32[]{:S(2)}) async-start(f32[8,40,128]{2,1,0:T(8,128)} %bitcast.9), calls=%async_computation | async-start | bytes 327680 | tf_op jit(solution)/shard_map/all_to_all | solution.py:495
  30.8 0.0 copy-start.18
  30.8 1.0 %copy-done.18 = f32[992,128]{1,0:T(8,128)S(1)} copy-done((f32[992,128]{1,0:T(8,128)S(1)}, f32[992,128]{1,0:T(8,128)}, u32[]{:S(2)}) %copy-start.18) | copy-done | bytes 507928
  31.8 1.0 %copy-done.20 = f32[992,128]{1,0:T(8,128)S(1)} copy-done((f32[992,128]{1,0:T(8,128)S(1)}, f32[992,128]{1,0:T(8,128)}, u32[]{:S(2)}) %copy-start.20) | copy-done | bytes 507928
  32.9 0.9 %copy-done.22 = f32[256,128]{1,0:T(8,128)S(1)} copy-done((f32[256,128]{1,0:T(8,128)S(1)}, f32[256,128]{1,0:T(8,128)}, u32[]{:S(2)}) %copy-start.22) | copy-done | bytes 131096
  33.8 0.8 %copy-done.24 = bf16[80,256]{1,0:T(8,128)(2,1)S(1)} copy-done((bf16[80,256]{1,0:T(8,128)(2,1)S(1)}, bf16[80,256]{1,0:T(8,128)(2,1)}, u32[]{:S(2)}) %copy-start.24) | copy-done | bytes 40984
  34.5 0.8 %copy-done.26 = bf16[64,256]{1,0:T(8,128)(2,1)S(1)} copy-done((bf16[64,256]{1,0:T(8,128)(2,1)S(1)}, bf16[64,256]{1,0:T(8,128)(2,1)}, u32[]{:S(2)}) %copy-start.26) | copy-done | bytes 32792
  35.3 0.7 %copy-done.28 = bf16[80,128]{1,0:T(8,128)(2,1)S(1)} copy-done((bf16[80,128]{1,0:T(8,128)(2,1)S(1)}, bf16[80,128]{1,0:T(8,128)(2,1)}, u32[]{:S(2)}) %copy-start.28) | copy-done | bytes 20504
  36.0 5.9 %shard_map.151 = (f32[72,4,8,128]{3,2,1,0:T(8,128)}, f32[992,128]{1,0:T(8,128)}, f32[992,128]{1,0:T(8,128)S(1)}) custom-call(f32[72,32,128]{2,1,0:T(8,128)S(1)} %copy-done.1, f32[320,128]{1,0:T(8,128)S(1)} %get-tuple-element.26.fluxes_in, bf16[80,256]{1,0:T(8,128)(2,1)S(1)} %copy-done.24, bf16[80,128]{1,0:T(8,128)(2,1)S(1)} %copy-done.28, ...), custom_call_target="tpu_custom_call" | custom-call | flops 2147483648 | bytes 8388608 | tf_op jit(solution)/shard_map/pallas_call | solution.py:24
  42.0 0.0 all-to-all-done
  42.0 1.1 %shard_map.152 = f32[992,128]{1,0:T(8,128)} custom-call(f32[320,128]{1,0:T(8,128)S(1)} %bitcast.17, s32[1]{0:T(128)} %bitcast.11.mine, bf16[512,128]{1,0:T(8,128)(2,1)S(1)} %bitcast.23, s32[16,128]{1,0:T(8,128)S(1)} %copy-done.11, f32[64,128]{1,0:T(8,128)S(1)} %get-tuple-element.36.sea_first, f32[992,128]{1,0:T(8,128)S(1)} %get-tuple-element.37.before), custom_call_target="tpu_custom_call" | custom-call | bytes 2097152 | tf_op jit(solution)/shard_map/pallas_call | solution.py:24
  (38 shorter events, 0.1 us)
Async XLA Ops:
  0.6 13.9 %copy-start.16 = (f32[72]{0:T(128)S(1)}, f32[72]{0:T(128)}, u32[]{:S(2)}) copy-start(f32[72]{0:T(128)} %param.15) | copy-start | bytes 868
  0.6 1.3 %copy-start = (f32[72,32,128]{2,1,0:T(8,128)S(1)}, f32[72,32,128]{2,1,0:T(8,128)}, u32[]{:S(2)}) copy-start(f32[72,32,128]{2,1,0:T(8,128)} %sky.3) | copy-start | bytes 3538948
  1.9 1.0 %copy-start.2 = (f32[62,16,128]{2,1,0:T(8,128)S(1)}, f32[62,16,128]{2,1,0:T(8,128)}, u32[]{:S(2)}) copy-start(f32[62,16,128]{2,1,0:T(8,128)} %param.22) | copy-start | bytes 1523716
  3.0 1.0 %copy-start.3 = (f32[62,16,128]{2,1,0:T(8,128)S(1)}, f32[62,16,128]{2,1,0:T(8,128)}, u32[]{:S(2)}) copy-start(f32[62,16,128]{2,1,0:T(8,128)} %param.23) | copy-start | bytes 1523716
  4.0 0.8 %copy-start.4 = (f32[4,32,128]{2,1,0:T(8,128)S(1)}, f32[4,32,128]{2,1,0:T(8,128)}, u32[]{:S(2)}) copy-start(f32[4,32,128]{2,1,0:T(8,128)} %forcing.1) | copy-start | bytes 196612
  4.8 0.7 %copy-start.6 = (f32[32,128]{1,0:T(8,128)S(1)}, f32[32,128]{1,0:T(8,128)}, u32[]{:S(2)}) copy-start(f32[32,128]{1,0:T(8,128)} %surface.3) | copy-start | bytes 49156
  5.6 0.7 %copy-start.8 = (f32[32,128]{1,0:T(8,128)S(1)}, f32[32,128]{1,0:T(8,128)}, u32[]{:S(2)}) copy-start(f32[32,128]{1,0:T(8,128)} %rate.3) | copy-start | bytes 49156
  6.3 0.7 %copy-start.10 = (s32[16,128]{1,0:T(8,128)S(1)}, s32[16,128]{1,0:T(8,128)}, u32[]{:S(2)}) copy-start(s32[16,128]{1,0:T(8,128)} %wet.7) | copy-start | bytes 24580
  7.0 7.6 %copy-start.1 = (f32[72,32,128]{2,1,0:T(8,128)S(1)}, f32[72,32,128]{2,1,0:T(8,128)}, u32[]{:S(2)}) copy-start(f32[72,32,128]{2,1,0:T(8,128)} %sky.3) | copy-start | bytes 3538948
  7.0 7.6 %copy-start.14 = (f32[72,72]{1,0:T(8,128)S(1)}, f32[72,72]{1,0:T(8,128)}, u32[]{:S(2)}) copy-start(f32[72,72]{1,0:T(8,128)} %vmix.1) | copy-start | bytes 62212
  7.0 7.6 %copy-start.15 = (f32[62,62]{1,0:T(8,128)S(1)}, f32[62,62]{1,0:T(8,128)}, u32[]{:S(2)}) copy-start(f32[62,62]{1,0:T(8,128)} %sea_mix.1) | copy-start | bytes 46132
  8.1 15.8 %collective-permute-start = (f32[456,128]{1,0:T(8,128)S(1)}, f32[456,128]{1,0:T(8,128)S(1)}, u32[]{:S(2)}, u32[]{:S(2)}) collective-permute-start(f32[456,128]{1,0:T(8,128)S(1)} %get-tuple-element.24), channel_id=1, source_target_pairs={{1,0},{2,1},{3,2},{4,3},{5,4},{6,5},{7,6},{8,7},{9,8},{10,9},{11,1... | collective-permute-start | bytes 700424 | tf_op jit(solution)/shard_map/ppermute | solution.py:463
  10.0 13.9 %collective-permute-start.1 = (f32[456,128]{1,0:T(8,128)S(1)}, f32[456,128]{1,0:T(8,128)S(1)}, u32[]{:S(2)}, u32[]{:S(2)}) collective-permute-start(f32[456,128]{1,0:T(8,128)S(1)} %get-tuple-element.25), channel_id=1, source_target_pairs={{0,1},{1,2},{2,3},{3,4},{4,5},{5,6},{6,7},{7,8},{8,9},{9,10},{10,1... | collective-permute-start | bytes 700424 | tf_op jit(solution)/shard_map/ppermute | solution.py:462
  14.6 9.4 %copy-start.7 = (f32[32,128]{1,0:T(8,128)S(1)}, f32[32,128]{1,0:T(8,128)}, u32[]{:S(2)}) copy-start(f32[32,128]{1,0:T(8,128)} %surface.3) | copy-start | bytes 49156
  14.6 9.4 %copy-start.9 = (f32[32,128]{1,0:T(8,128)S(1)}, f32[32,128]{1,0:T(8,128)}, u32[]{:S(2)}) copy-start(f32[32,128]{1,0:T(8,128)} %rate.3) | copy-start | bytes 49156
  14.6 9.4 %copy-start.12 = (s32[32,4]{0,1:T(4,128)S(1)}, s32[32,4]{0,1:T(4,128)}, u32[]{:S(2)}) copy-start(s32[32,4]{0,1:T(4,128)} %param.20) | copy-start | bytes 1540
  14.6 9.4 %copy-start.13 = (s32[32,4]{0,1:T(4,128)S(1)}, s32[32,4]{0,1:T(4,128)}, u32[]{:S(2)}) copy-start(s32[32,4]{0,1:T(4,128)} %param.21) | copy-start | bytes 1540
  14.6 16.2 %copy-start.11 = (s32[16,128]{1,0:T(8,128)S(1)}, s32[16,128]{1,0:T(8,128)}, u32[]{:S(2)}) copy-start(s32[16,128]{1,0:T(8,128)} %wet.7) | copy-start | bytes 24580
  22.4 0.8 %copy-start.19 = (f32[992,128]{1,0:T(8,128)}, f32[992,128]{1,0:T(8,128)S(1)}, u32[]{:S(2)}) copy-start(f32[992,128]{1,0:T(8,128)S(1)} %get-tuple-element.32.salt_in) | copy-start | bytes 1523716
  23.2 0.7 %copy-start.21 = (f32[256,128]{1,0:T(8,128)}, f32[256,128]{1,0:T(8,128)S(1)}, u32[]{:S(2)}) copy-start(f32[256,128]{1,0:T(8,128)S(1)} %get-tuple-element.33.sea_ends_in) | copy-start | bytes 393220
  23.9 1.5 %copy-start.17 = (f32[992,128]{1,0:T(8,128)}, f32[992,128]{1,0:T(8,128)S(1)}, u32[]{:S(2)}) copy-start(f32[992,128]{1,0:T(8,128)S(1)} %get-tuple-element.31.warm_in) | copy-start | bytes 1523716
  23.9 1.5 %copy-start.23 = (bf16[80,256]{1,0:T(8,128)(2,1)}, bf16[80,256]{1,0:T(8,128)(2,1)S(1)}, u32[]{:S(2)}) copy-start(bf16[80,256]{1,0:T(8,128)(2,1)S(1)} %get-tuple-element.27.weights_in) | copy-start | bytes 122884
  23.9 1.5 %copy-start.25 = (bf16[64,256]{1,0:T(8,128)(2,1)}, bf16[64,256]{1,0:T(8,128)(2,1)S(1)}, u32[]{:S(2)}) copy-start(bf16[64,256]{1,0:T(8,128)(2,1)S(1)} %get-tuple-element.29.sea_weights_in) | copy-start | bytes 98308
  23.9 1.5 %copy-start.27 = (bf16[80,128]{1,0:T(8,128)(2,1)}, bf16[80,128]{1,0:T(8,128)(2,1)S(1)}, u32[]{:S(2)}) copy-start(bf16[80,128]{1,0:T(8,128)(2,1)S(1)} %get-tuple-element.28.source_weights_in) | copy-start | bytes 61444
  25.4 16.6 %all-to-all-start = ((f32[8,40,128]{2,1,0:T(8,128)}), f32[8,40,128]{2,1,0:T(8,128)S(1)}, u32[]{:S(2)}, u32[]{:S(2)}) async-start(f32[8,40,128]{2,1,0:T(8,128)} %bitcast.9), calls=%async_computation | async-start | bytes 327680 | tf_op jit(solution)/shard_map/all_to_all | solution.py:495
  30.8 1.0 %copy-start.18 = (f32[992,128]{1,0:T(8,128)S(1)}, f32[992,128]{1,0:T(8,128)}, u32[]{:S(2)}) copy-start(f32[992,128]{1,0:T(8,128)} %copy-done.17) | copy-start | bytes 1523716
  31.8 1.0 %copy-start.20 = (f32[992,128]{1,0:T(8,128)S(1)}, f32[992,128]{1,0:T(8,128)}, u32[]{:S(2)}) copy-start(f32[992,128]{1,0:T(8,128)} %copy-done.19) | copy-start | bytes 1523716
  32.8 0.9 %copy-start.22 = (f32[256,128]{1,0:T(8,128)S(1)}, f32[256,128]{1,0:T(8,128)}, u32[]{:S(2)}) copy-start(f32[256,128]{1,0:T(8,128)} %copy-done.21) | copy-start | bytes 393220
  33.8 0.8 %copy-start.24 = (bf16[80,256]{1,0:T(8,128)(2,1)S(1)}, bf16[80,256]{1,0:T(8,128)(2,1)}, u32[]{:S(2)}) copy-start(bf16[80,256]{1,0:T(8,128)(2,1)} %copy-done.23) | copy-start | bytes 122884
  34.5 0.8 %copy-start.26 = (bf16[64,256]{1,0:T(8,128)(2,1)S(1)}, bf16[64,256]{1,0:T(8,128)(2,1)}, u32[]{:S(2)}) copy-start(bf16[64,256]{1,0:T(8,128)(2,1)} %copy-done.25) | copy-start | bytes 98308
  35.3 0.7 %copy-start.28 = (bf16[80,128]{1,0:T(8,128)(2,1)S(1)}, bf16[80,128]{1,0:T(8,128)(2,1)}, u32[]{:S(2)}) copy-start(bf16[80,128]{1,0:T(8,128)(2,1)} %copy-done.27) | copy-start | bytes 61444
  36.0 6.0 %copy-start.5 = (bf16[4,128,128]{2,1,0:T(8,128)(2,1)S(1)}, bf16[4,128,128]{2,1,0:T(8,128)(2,1)}, u32[]{:S(2)}) copy-start(bf16[4,128,128]{2,1,0:T(8,128)(2,1)} %param.19) | copy-start | bytes 393220

commit v5 on v4

--- a/solution.py
+++ b/solution.py
@@ -10,6 +10,7 @@
 atm_diffusion = 0.2
 ocean_diffusion = 0.2
 HALO = 4
+FULL = 64
 EXACT = lax.Precision.HIGHEST
 VMEM = pl.BlockSpec(memory_space=pltpu.VMEM)
 HBM = pl.BlockSpec(memory_space=pltpu.HBM)
@@ -20,14 +21,14 @@
     return -(-n // m) * m
 
 
-def call(kernel, out_shape, *args, scratch=(), in_specs=None, out_specs=None, flops=0, moved=0):
+def call(kernel, out_shape, *args, scratch=(), in_specs=None, out_specs=None, flops=0, moved=0, grant=24):
     return pl.pallas_call(
         kernel,
         out_shape=out_shape,
         in_specs=in_specs or [VMEM] * len(args),
         out_specs=out_specs or jax.tree.map(lambda _: VMEM, out_shape),
         scratch_shapes=list(scratch),
-        compiler_params=pltpu.CompilerParams(vmem_limit_bytes=24 * 2**20),
+        compiler_params=pltpu.CompilerParams(vmem_limit_bytes=grant * 2**20),
         cost_estimate=pl.CostEstimate(flops=flops, bytes_accessed=moved, transcendentals=0),
     )(*args)
 
@@ -105,10 +106,18 @@
 
 
 def local_kernel(
-    sizes, vmix, curve, sea_mix, sky, warmth, brine, wet,
+    sizes, vmix_in, curve_in, sea_mix_in, sky_in, warmth_in, brine_in, wet_in,
     rows_of_mix, source_rows, own, *others
 ):
-    kept, found, (spread, sea_spread, done) = others[:8], others[8:16], others[16:]
+    kept, found, held, (spread, sea_spread, done, here) = others[:8], others[8:16], others[16:23], others[23:]
+    vmix, curve, sea_mix, sky, warmth, brine, wet = held
+    fetches = copies(
+        list(zip((vmix_in, curve_in, sea_mix_in, sky_in, warmth_in, brine_in, wet_in), held)), here
+    )
+    for fetch in fetches:
+        fetch.start()
+    for fetch in fetches[:3]:
+        fetch.wait()
     weights, source_weights, sea_weights, sea_first, middle, warm_out, brine_out, sea_ends = found
     moves = copies(list(zip(found, kept)), done)
     levels, rows, steps, sea_levels, sea_rows, stride, sea_stride = sizes
@@ -156,6 +165,7 @@
     sea_first[...] = jnp.broadcast_to(sea[:, 0:1], sea_first.shape)
     for move in moves[:4]:
         move.start()
+    fetches[3].wait()
     sums = [jnp.zeros((rows, width), f32) for _ in range(steps - 1)]
     for l in range(levels):
         x = sky[l * rows : (l + 1) * rows, :]
@@ -185,6 +195,8 @@
             middle[(r + i) * levels : (r + i + 1) * levels, :] = y[:levels, i * width : (i + 1) * width]
     moves[4].start()
 
+    for fetch in fetches[4:]:
+        fetch.wait()
     m = wet[...].astype(f32)
     mark = [m[r : r + 1] for r in range(sea_rows)]
     edge = jnp.zeros((1, width), f32)
@@ -452,7 +464,7 @@
     length = HALO * stride + 2 * sea_stride + 8
     up, down = call(
         functools.partial(pack_kernel, sizes), [flat(length)] * 2,
-        sky, forcing, surface, rate, warmth2, brine2, wet, moved=4 << 20, in_specs=[HBM] * 7,
+        sky, forcing, surface, rate, warmth2, brine2, wet, moved=4 << 20, in_specs=[HBM] * 7, grant=FULL,
         scratch=[
             space(2, levels, 8, width), space(steps, rows, width), space(2, sea_levels * sea_rows, width),
             space(2, rows, width), pltpu.VMEM(wet.shape, wet.dtype), pltpu.SemaphoreType.DMA((8,)),
@@ -472,15 +484,18 @@
         sea_flat, sea_flat, flat(4 * sea_stride),
     ]
     found = [pltpu.VMEM(k.shape, k.dtype) for k in kept]
+    local_args = (vmix, curve[None], sea_mix, sky2, warmth2, brine2, wet)
+    held = [pltpu.VMEM(x.shape, x.dtype) for x in local_args]
     (rows_of_mix, source_rows, own, weights, source_weights, sea_weights, sea_first, middle, warm, salt, sea_ends) = call(
         functools.partial(local_kernel, sizes),
         [flat((steps - 1) * levels), flat(8), flat((steps - 1) * rows)] + kept,
-        vmix, curve[None], sea_mix, sky2, warmth2, brine2, wet,
-        out_specs=[VMEM] * 3 + [HBM] * 8,
-        scratch=found + [
+        *local_args,
+        in_specs=[HBM] * 7, out_specs=[VMEM] * 3 + [HBM] * 8,
+        scratch=found + held + [
             space(inner * depth, width), space(2, sea_rows * sea_stride, width), pltpu.SemaphoreType.DMA((8,)),
+            pltpu.SemaphoreType.DMA((7,)),
         ],
-        flops=4 << 30, moved=8 << 20,
+        flops=4 << 30, moved=8 << 20, grant=FULL,
     )
 
     per = rows + 2 * topk
@@ -505,7 +520,7 @@
             space(2 * HALO * depth, width), space(rows * 16, width), space(rows // 8, levels, 8, width),
             pltpu.SemaphoreType.DMA((11 + rows // 8,)),
         ],
-        flops=2 << 30, moved=8 << 20,
+        flops=2 << 30, moved=8 << 20, grant=FULL,
     )
     mine = lax.axis_index("tile").astype(jnp.int32)[None]
     warm = call(

time: 44 us -> 48.6 us (1.10)
  the two profiles are of different devices: /device:TPU:1 before, /device:TPU:0 now
where the time goes in v5:
time: 48.6 us; the launch traced here: 47.7 us
  Pallas kernels  23.6 us (49%)
  starting transfers between devices  12.3 us (25%)
  local copies, waits for them, and re-layouts  10.8 us (22%)
  between operations  0.7 us (1%)
    pallas_call x5, Pallas kernels, call(): pl.pallas_call(kernel, out_shape=out_shape, in_specs=in_specs or [VMEM] *...  23.6 us
    unnamed x26, local copies, waits for them, and re-layouts  10.1 us
    all_to_all x1, starting transfers between devices, body(): lax.all_to_all(sent.reshape(tiles, per, width), 'tile', split_axis=0, con...  7.26 us
    ppermute x1, starting transfers between devices, body(): lax.ppermute(down, ('tile', 'comp'), [(i, i + 1) for i in range(count - 1)])  3.73 us
    ppermute x1, starting transfers between devices, body(): lax.ppermute(up, ('tile', 'comp'), [(i + 1, i) for i in range(count - 1)])  1.29 us
  transfers between devices with their start and end apart: 3, of which 1 were waited for; matrix products, arithmetic and copies ran while one was open for 2% of the time, Pallas kernels for 35%

profile of v5, /device:TPU:0, one launch (start us, length us, event | category | flops | bytes accessed | tf_op | source)
XLA Modules:
  0.0 47.7 jit_solution(3183943403211630104)
XLA Ops:
  0.6 2.4 %shard_map.149 = (f32[456,128]{1,0:T(8,128)}, f32[456,128]{1,0:T(8,128)}) custom-call(f32[72,32,128]{2,1,0:T(8,128)} %sky.3, f32[4,32,128]{2,1,0:T(8,128)} %forcing.1, f32[32,128]{1,0:T(8,128)} %surface.3, f32[32,128]{1,0:T(8,128)} %rate.3, f32[992,128]{1,0:T(8,128)} %bitcast.22, f32[992,128]{1,0:T(8,128)} %bitcast.24, s32[16,128]{1,0:T(8,128)} %wet.5), custom_call_target="tpu_custom_call" | custom-call | bytes 4194304 | tf_op jit(solution)/shard_map/pallas_call | solution.py:25
  3.0 1.3 %collective-permute-start = (f32[456,128]{1,0:T(8,128)}, f32[456,128]{1,0:T(8,128)}, u32[]{:S(2)}, u32[]{:S(2)}) collective-permute-start(f32[456,128]{1,0:T(8,128)} %get-tuple-element.24), channel_id=1, source_target_pairs={{1,0},{2,1},{3,2},{4,3},{5,4},{6,5},{7,6},{8,7},{9,8},{10,9},{11,1... | collective-permute-start | bytes 700424 | tf_op jit(solution)/shard_map/ppermute | solution.py:475
  4.3 3.7 %collective-permute-start.1 = (f32[456,128]{1,0:T(8,128)}, f32[456,128]{1,0:T(8,128)}, u32[]{:S(2)}, u32[]{:S(2)}) collective-permute-start(f32[456,128]{1,0:T(8,128)} %get-tuple-element.25), channel_id=1, source_target_pairs={{0,1},{1,2},{2,3},{3,4},{4,5},{5,6},{6,7},{7,8},{8,9},{9,10},{10,1... | collective-permute-start | bytes 700424 | tf_op jit(solution)/shard_map/ppermute | solution.py:474
  8.0 9.1 %shard_map.148 = (f32[216,128]{1,0:T(8,128)}, f32[8,128]{1,0:T(8,128)}, f32[96,128]{1,0:T(8,128)}, bf16[80,256]{1,0:T(8,128)(2,1)}, bf16[80,128]{1,0:T(8,128)(2,...) custom-call(f32[72,72]{1,0:T(8,128)} %vmix_in.1, ...), custom_call_target="tpu_custom_call" | custom-call | flops 4294967296 | bytes 8388608 | tf_op jit(solution)/shard_map/pallas_call | solution.py:25
  17.2 0.7 %slice_bitcast_fusion.sky = f32[32,128]{1,0:T(8,128)S(1)} fusion(f32[72,32,128]{2,1,0:T(8,128)} %sky.3), kind=kLoop, calls=%fused_computation | loop fusion | bytes 32768 | tf_op jit(solution)/shard_map/squeeze | solution.py:506
  17.9 0.0 collective-permute-done.below
  17.9 0.0 collective-permute-done.1.above
  17.9 0.0 copy-start.1
  17.9 0.8 %copy-done.1 = f32[4,32,128]{2,1,0:T(8,128)S(1)} copy-done((f32[4,32,128]{2,1,0:T(8,128)S(1)}, f32[4,32,128]{2,1,0:T(8,128)}, u32[]{:S(2)}) %copy-start.1) | copy-done | bytes 65560
  18.7 0.0 copy-start.3
  18.7 0.9 %copy-done.3 = f32[216,128]{1,0:T(8,128)S(1)} copy-done((f32[216,128]{1,0:T(8,128)S(1)}, f32[216,128]{1,0:T(8,128)}, u32[]{:S(2)}) %copy-start.3) | copy-done | bytes 110616
  19.6 0.0 copy-start.4
  19.6 0.7 %copy-done.4 = f32[32,128]{1,0:T(8,128)S(1)} copy-done((f32[32,128]{1,0:T(8,128)S(1)}, f32[32,128]{1,0:T(8,128)}, u32[]{:S(2)}) %copy-start.4) | copy-done | bytes 16408
  20.3 0.0 copy-start.5
  20.4 0.7 %copy-done.5 = f32[32,128]{1,0:T(8,128)S(1)} copy-done((f32[32,128]{1,0:T(8,128)S(1)}, f32[32,128]{1,0:T(8,128)}, u32[]{:S(2)}) %copy-start.5) | copy-done | bytes 16408
  21.1 0.0 copy-start.6
  21.1 0.8 %copy-done.6 = f32[96,128]{1,0:T(8,128)S(1)} copy-done((f32[96,128]{1,0:T(8,128)S(1)}, f32[96,128]{1,0:T(8,128)}, u32[]{:S(2)}) %copy-start.6) | copy-done | bytes 49176
  21.9 0.0 copy-start.9
  21.9 0.7 %copy-done.9 = f32[8,128]{1,0:T(8,128)S(1)} copy-done((f32[8,128]{1,0:T(8,128)S(1)}, f32[8,128]{1,0:T(8,128)}, u32[]{:S(2)}) %copy-start.9) | copy-done | bytes 4120
  22.5 0.7 %copy-done.10 = s32[32,4]{0,1:T(4,128)S(1)} copy-done((s32[32,4]{0,1:T(4,128)S(1)}, s32[32,4]{0,1:T(4,128)}, u32[]{:S(2)}) %copy-start.10) | copy-done | bytes 536
  23.2 0.7 %copy-done.11 = s32[32,4]{0,1:T(4,128)S(1)} copy-done((s32[32,4]{0,1:T(4,128)S(1)}, s32[32,4]{0,1:T(4,128)}, u32[]{:S(2)}) %copy-start.11) | copy-done | bytes 536
  23.9 2.4 %shard_map.150 = (f32[320,128]{1,0:T(8,128)}, f32[320,128]{1,0:T(8,128)S(1)}) custom-call(f32[32,128]{1,0:T(8,128)S(1)} %slice_bitcast_fusion.sky, f32[128,128]{1,0:T(8,128)S(1)} %bitcast.16, f32[32,128]{1,0:T(8,128)S(1)} %copy-done.4, f32[32,128]{1,0:T(8,128)S(1)} %copy-done.5, f32[216,128]{1,0:T(8,128)S(1)} %copy-done.3, f32[8,128]{1,0:T(8,128)S(1)} %copy-done.9, ...), custom_call_target="tpu_custom_call" | custom-call | bytes 2097152 | tf_op jit(solution)/shard_map/pallas_call | solution.py:25
  26.3 0.0 copy-start.12
  26.4 0.7 %copy-done.12 = f32[320,128]{1,0:T(8,128)} copy-done((f32[320,128]{1,0:T(8,128)}, f32[320,128]{1,0:T(8,128)S(1)}, u32[]{:S(2)}) %copy-start.12) | copy-done | bytes 163864
  27.0 7.3 %all-to-all-start = ((f32[8,40,128]{2,1,0:T(8,128)}), f32[8,40,128]{2,1,0:T(8,128)}, u32[]{:S(2)}, u32[]{:S(2)}) async-start(f32[8,40,128]{2,1,0:T(8,128)} %bitcast.9), calls=%async_computation | async-start | bytes 327680 | tf_op jit(solution)/shard_map/all_to_all | solution.py:510
  34.3 7.6 %shard_map.151 = (f32[72,4,8,128]{3,2,1,0:T(8,128)}, f32[992,128]{1,0:T(8,128)}, f32[992,128]{1,0:T(8,128)}) custom-call(f32[72,32,128]{2,1,0:T(8,128)} %sky.3, f32[320,128]{1,0:T(8,128)} %copy-done.12, bf16[80,256]{1,0:T(8,128)(2,1)} %get-tuple-element.27.weights_in, bf16[80,128]{1,0:T(8,128)(2,1)} %get-tuple-element.28.source_weights_in, ...), custom_call_target="tpu_custom_call" | custom-call | flops 2147483648 | bytes 8388608 | tf_op jit(solution)/shard_map/pallas_call | solution.py:25
  41.9 0.4 all-to-all-done
  42.3 1.0 %copy-done = f32[992,128]{1,0:T(8,128)S(1)} copy-done((f32[992,128]{1,0:T(8,128)S(1)}, f32[992,128]{1,0:T(8,128)}, u32[]{:S(2)}) %copy-start) | copy-done | bytes 507928
  43.3 0.9 %copy-done.2 = bf16[4,128,128]{2,1,0:T(8,128)(2,1)S(1)} copy-done((bf16[4,128,128]{2,1,0:T(8,128)(2,1)S(1)}, bf16[4,128,128]{2,1,0:T(8,128)(2,1)}, u32[]{:S(2)}) %copy-start.2) | copy-done | bytes 131096
  44.2 0.7 %copy-done.7 = s32[16,128]{1,0:T(8,128)S(1)} copy-done((s32[16,128]{1,0:T(8,128)S(1)}, s32[16,128]{1,0:T(8,128)}, u32[]{:S(2)}) %copy-start.7) | copy-done | bytes 8216
  44.9 0.8 %copy-done.8 = f32[64,128]{1,0:T(8,128)S(1)} copy-done((f32[64,128]{1,0:T(8,128)S(1)}, f32[64,128]{1,0:T(8,128)}, u32[]{:S(2)}) %copy-start.8) | copy-done | bytes 32792
  45.7 2.0 %shard_map.152 = f32[992,128]{1,0:T(8,128)} custom-call(f32[320,128]{1,0:T(8,128)} %bitcast.10.got, s32[1]{0:T(128)} %bitcast.11.mine, bf16[512,128]{1,0:T(8,128)(2,1)S(1)} %bitcast.17, s32[16,128]{1,0:T(8,128)S(1)} %copy-done.7, f32[64,128]{1,0:T(8,128)S(1)} %copy-done.8, f32[992,128]{1,0:T(8,128)S(1)} %copy-done), custom_call_target="tpu_custom_call" | custom-call | bytes 2097152 | tf_op jit(solution)/shard_map/pallas_call | solution.py:25
  (6 shorter events, 0.0 us)
Async XLA Ops:
  3.0 14.9 %collective-permute-start = (f32[456,128]{1,0:T(8,128)}, f32[456,128]{1,0:T(8,128)}, u32[]{:S(2)}, u32[]{:S(2)}) collective-permute-start(f32[456,128]{1,0:T(8,128)} %get-tuple-element.24), channel_id=1, source_target_pairs={{1,0},{2,1},{3,2},{4,3},{5,4},{6,5},{7,6},{8,7},{9,8},{10,9},{11,1... | collective-permute-start | bytes 700424 | tf_op jit(solution)/shard_map/ppermute | solution.py:475
  4.3 13.6 %collective-permute-start.1 = (f32[456,128]{1,0:T(8,128)}, f32[456,128]{1,0:T(8,128)}, u32[]{:S(2)}, u32[]{:S(2)}) collective-permute-start(f32[456,128]{1,0:T(8,128)} %get-tuple-element.25), channel_id=1, source_target_pairs={{0,1},{1,2},{2,3},{3,4},{4,5},{5,6},{6,7},{7,8},{8,9},{9,10},{10,1... | collective-permute-start | bytes 700424 | tf_op jit(solution)/shard_map/ppermute | solution.py:474
  17.9 0.8 %copy-start.1 = (f32[4,32,128]{2,1,0:T(8,128)S(1)}, f32[4,32,128]{2,1,0:T(8,128)}, u32[]{:S(2)}) copy-start(f32[4,32,128]{2,1,0:T(8,128)} %forcing.1) | copy-start | bytes 196612
  18.7 0.9 %copy-start.3 = (f32[216,128]{1,0:T(8,128)S(1)}, f32[216,128]{1,0:T(8,128)}, u32[]{:S(2)}) copy-start(f32[216,128]{1,0:T(8,128)} %get-tuple-element.21.rows_of_mix) | copy-start | bytes 331780
  19.6 0.7 %copy-start.4 = (f32[32,128]{1,0:T(8,128)S(1)}, f32[32,128]{1,0:T(8,128)}, u32[]{:S(2)}) copy-start(f32[32,128]{1,0:T(8,128)} %surface.3) | copy-start | bytes 49156
  20.3 0.7 %copy-start.5 = (f32[32,128]{1,0:T(8,128)S(1)}, f32[32,128]{1,0:T(8,128)}, u32[]{:S(2)}) copy-start(f32[32,128]{1,0:T(8,128)} %rate.3) | copy-start | bytes 49156
  21.1 0.8 %copy-start.6 = (f32[96,128]{1,0:T(8,128)S(1)}, f32[96,128]{1,0:T(8,128)}, u32[]{:S(2)}) copy-start(f32[96,128]{1,0:T(8,128)} %get-tuple-element.23.own) | copy-start | bytes 147460
  21.9 0.7 %copy-start.9 = (f32[8,128]{1,0:T(8,128)S(1)}, f32[8,128]{1,0:T(8,128)}, u32[]{:S(2)}) copy-start(f32[8,128]{1,0:T(8,128)} %get-tuple-element.22.source_rows) | copy-start | bytes 12292
  22.5 0.7 %copy-start.10 = (s32[32,4]{0,1:T(4,128)S(1)}, s32[32,4]{0,1:T(4,128)}, u32[]{:S(2)}) copy-start(s32[32,4]{0,1:T(4,128)} %param.20) | copy-start | bytes 1540
  23.2 0.7 %copy-start.11 = (s32[32,4]{0,1:T(4,128)S(1)}, s32[32,4]{0,1:T(4,128)}, u32[]{:S(2)}) copy-start(s32[32,4]{0,1:T(4,128)} %param.21) | copy-start | bytes 1540
  26.3 0.7 %copy-start.12 = (f32[320,128]{1,0:T(8,128)}, f32[320,128]{1,0:T(8,128)S(1)}, u32[]{:S(2)}) copy-start(f32[320,128]{1,0:T(8,128)S(1)} %get-tuple-element.26.fluxes_in) | copy-start | bytes 491524
  27.0 15.3 %all-to-all-start = ((f32[8,40,128]{2,1,0:T(8,128)}), f32[8,40,128]{2,1,0:T(8,128)}, u32[]{:S(2)}, u32[]{:S(2)}) async-start(f32[8,40,128]{2,1,0:T(8,128)} %bitcast.9), calls=%async_computation | async-start | bytes 327680 | tf_op jit(solution)/shard_map/all_to_all | solution.py:510
  42.3 1.0 %copy-start = (f32[992,128]{1,0:T(8,128)S(1)}, f32[992,128]{1,0:T(8,128)}, u32[]{:S(2)}) copy-start(f32[992,128]{1,0:T(8,128)} %get-tuple-element.37.before) | copy-start | bytes 1523716
  43.3 0.9 %copy-start.2 = (bf16[4,128,128]{2,1,0:T(8,128)(2,1)S(1)}, bf16[4,128,128]{2,1,0:T(8,128)(2,1)}, u32[]{:S(2)}) copy-start(bf16[4,128,128]{2,1,0:T(8,128)(2,1)} %param.19) | copy-start | bytes 393220
  44.2 0.7 %copy-start.7 = (s32[16,128]{1,0:T(8,128)S(1)}, s32[16,128]{1,0:T(8,128)}, u32[]{:S(2)}) copy-start(s32[16,128]{1,0:T(8,128)} %wet.5) | copy-start | bytes 24580
  44.9 0.8 %copy-start.8 = (f32[64,128]{1,0:T(8,128)S(1)}, f32[64,128]{1,0:T(8,128)}, u32[]{:S(2)}) copy-start(f32[64,128]{1,0:T(8,128)} %get-tuple-element.36.sea_first) | copy-start | bytes 98308

commit v6 on v4

--- a/solution.py
+++ b/solution.py
@@ -10,6 +10,7 @@
 atm_diffusion = 0.2
 ocean_diffusion = 0.2
 HALO = 4
+FULL = 60
 EXACT = lax.Precision.HIGHEST
 VMEM = pl.BlockSpec(memory_space=pltpu.VMEM)
 HBM = pl.BlockSpec(memory_space=pltpu.HBM)
@@ -20,14 +21,14 @@
     return -(-n // m) * m
 
 
-def call(kernel, out_shape, *args, scratch=(), in_specs=None, out_specs=None, flops=0, moved=0):
+def call(kernel, out_shape, *args, scratch=(), in_specs=None, out_specs=None, flops=0, moved=0, grant=24):
     return pl.pallas_call(
         kernel,
         out_shape=out_shape,
         in_specs=in_specs or [VMEM] * len(args),
         out_specs=out_specs or jax.tree.map(lambda _: VMEM, out_shape),
         scratch_shapes=list(scratch),
-        compiler_params=pltpu.CompilerParams(vmem_limit_bytes=24 * 2**20),
+        compiler_params=pltpu.CompilerParams(vmem_limit_bytes=grant * 2**20),
         cost_estimate=pl.CostEstimate(flops=flops, bytes_accessed=moved, transcendentals=0),
     )(*args)
 
@@ -105,12 +106,10 @@
 
 
 def local_kernel(
-    sizes, vmix, curve, sea_mix, sky, warmth, brine, wet,
-    rows_of_mix, source_rows, own, *others
+    sizes, last_place, place, vmix, curve, sea_mix, sky, warmth, brine, wet,
+    rows_of_mix, source_rows, own, weights, source_weights, sea_weights, sea_first, middle, warm_out, brine_out, sea_ends,
+    spread, sea_spread,
 ):
-    kept, found, (spread, sea_spread, done) = others[:8], others[8:16], others[16:]
-    weights, source_weights, sea_weights, sea_first, middle, warm_out, brine_out, sea_ends = found
-    moves = copies(list(zip(found, kept)), done)
     levels, rows, steps, sea_levels, sea_rows, stride, sea_stride = sizes
     width = sky.shape[1]
     depth = up_to(levels + 2 * steps, 16)
@@ -154,8 +153,6 @@
     sea = jnp.concatenate([sea, jnp.zeros((sea_stride - sea_levels, 2 * width), f32)], 0)
     sea_weights[...] = three_terms(sea, sea_stride)
     sea_first[...] = jnp.broadcast_to(sea[:, 0:1], sea_first.shape)
-    for move in moves[:4]:
-        move.start()
     sums = [jnp.zeros((rows, width), f32) for _ in range(steps - 1)]
     for l in range(levels):
         x = sky[l * rows : (l + 1) * rows, :]
@@ -164,26 +161,36 @@
     for s in range(steps - 1):
         own[s * rows : (s + 1) * rows, :] = sums[s]
 
-    inner = rows - 2 * HALO
+    before = jnp.where(place[0] > 0, 1.0, 0.0)
+    behind = jnp.where(place[0] < last_place, 1.0, 0.0)
 
     @pl.loop(0, levels // 8)
     def _(c):
         x = [sky[pl.ds(c * 8 * rows + r, 8, stride=rows), :] for r in range(rows)]
-        for _ in range(steps):
-            x = stencil(x)
-        for r in range(inner):
+        none = jnp.zeros_like(x[0])
+        beyond = 0
+        for n in range(steps):
+            if beyond < steps - 1 - n:
+                x = [x[0]] + stencil([none] + x + [none]) + [x[-1]]
+                beyond += 1
+            else:
+                x = stencil(x)
+                beyond -= 1
+            for i in range(beyond):
+                x[i] = x[i] * before
+                x[-1 - i] = x[-1 - i] * behind
+        for r in range(rows):
             spread[pl.ds(pl.multiple_of(r * depth + c * 8, 8), 8), :] = x[r]
 
     if depth > levels:
-        for r in range(inner):
+        for r in range(rows):
             spread[r * depth + levels : (r + 1) * depth, :] = jnp.zeros((depth - levels, width), f32)
     w = weights[:, : 3 * depth]
-    for r in range(0, inner, 2):
+    for r in range(0, rows, 2):
         x = jnp.concatenate([spread[(r + i) * depth : (r + i + 1) * depth, :] for i in range(2)], 1)
         y = product(w, x)
         for i in range(2):
             middle[(r + i) * levels : (r + i + 1) * levels, :] = y[:levels, i * width : (i + 1) * width]
-    moves[4].start()
 
     m = wet[...].astype(f32)
     mark = [m[r : r + 1] for r in range(sea_rows)]
@@ -216,10 +223,6 @@
             if r in (0, sea_rows - 1):
                 at = (2 * f + (r > 0)) * sea_stride
                 sea_ends[at : at + sea_levels, :] = old
-    for move in moves[5:]:
-        move.start()
-    for move in moves:
-        move.wait()
 
 
 def cross(x):
@@ -235,7 +238,7 @@
 
 def flux_kernel(
     sizes, sky, forcing, surface, rate, rows_of_mix, source_rows, own, owners, locals_, below, above,
-    sent, kept, fluxes, halo, done
+    sent, fluxes, halo
 ):
     levels, rows, steps, sea_levels, sea_rows, stride, sea_stride = sizes
     width = sky.shape[1]
@@ -271,8 +274,6 @@
         reach = rows + 2 * HALO
         fluxes[pl.ds(s, reach, stride=2 * steps), :] = force[s]
         fluxes[pl.ds(steps + s, reach, stride=2 * steps), :] = flux[s]
-    move = pltpu.make_async_copy(fluxes, kept, done)
-    move.start()
     total = flux[0][:rows]
     for s in range(1, steps):
         total = total + flux[s][:rows]
@@ -287,32 +288,18 @@
     for t in range(sent.shape[0] // per):
         sent[t * per : t * per + rows, :] = mean
         sent[t * per + rows : (t + 1) * per, :] = table
-    move.wait()
 
 
 def rest_kernel(
-    sizes, sky, fluxes_in, weights_in, source_weights_in, sea_weights_in, middle_in, warm_in, salt_in, sea_ends_in,
-    wet, below, above, out, brine_out, warm_out,
-    ends, fluxes, weights, source_weights, sea_weights, middle, salt, sea_ends, spread, sources, result, done
+    sizes, fluxes, weights, source_weights, sea_weights, middle, warm, salt, sea_ends, wet, below, above,
+    out, brine_out, warm_out, salt_held, spread, sources, result, done
 ):
     levels, rows, steps, sea_levels, sea_rows, stride, sea_stride = sizes
-    width = sky.shape[2]
+    width = above.shape[1]
     depth = up_to(levels + 2 * steps, 16)
-    moves = copies(
-        [
-            (fluxes_in, fluxes), (sky.at[:, 0:8, :], ends.at[0]), (sky.at[:, rows - 8 : rows, :], ends.at[1]),
-            (sea_weights_in, sea_weights), (sea_ends_in, sea_ends), (salt_in, salt), (warm_in, warm_out),
-            (weights_in, weights), (source_weights_in, source_weights), (middle_in, middle),
-        ],
-        done,
-    )
-    count = len(moves)
-    for move in moves:
-        move.start()
     flag = levels + steps + 2
     inside_above, inside_below = above[flag : flag + 1, :], below[flag : flag + 1, :]
 
-    moves[0].wait()
     reach = rows + 2 * HALO
     x = [fluxes[(r % reach) * 2 * steps : (r % reach + 1) * 2 * steps, :] for r in range(1 - steps, rows + steps - 1)]
     field = lax.broadcasted_iota(jnp.int32, (2 * steps, width), 0) % steps
@@ -325,8 +312,8 @@
     for r in range(rows):
         sources[r * 16 : (r + 1) * 16, :] = jnp.concatenate([x[r], jnp.zeros((16 - 2 * steps, width), f32)], 0)
 
-    for move in moves[3:7]:
-        move.wait()
+    warm_out[...] = warm[...]
+    salt_held[...] = salt[...]
     m = wet[...].astype(f32)
     base = HALO * stride
     w = sea_weights[:, : 3 * sea_stride]
@@ -341,36 +328,25 @@
             step = ocean_diffusion * (mark * step)
             x.append(jnp.concatenate([step, jnp.zeros((sea_stride - sea_levels, width), f32)], 0))
         y = product(w, jnp.concatenate(x, 1))
-        for f, to in enumerate((warm_out, salt)):
+        for f, to in enumerate((warm_out, salt_held)):
             rows_at = pl.ds(r, sea_levels, stride=sea_rows)
             to[rows_at, :] = to[rows_at, :] + mark * y[:sea_levels, f * width : (f + 1) * width]
-    leave = [pltpu.make_async_copy(salt, brine_out, done.at[count])]
+    leave = [pltpu.make_async_copy(salt_held, brine_out, done.at[0])]
     leave[0].start()
-
-    moves[1].wait()
-    moves[2].wait()
-    first, final = (ends.at[i].reshape(levels * 8, width) for i in range(2))
 
     @pl.loop(0, levels // 8)
     def _(c):
-        def own(ref, r):
-            return ref[pl.ds(c * 64 + r, 8, stride=8), :]
-
         def other(ref, j):
             return ref[pl.ds(pl.multiple_of(j * stride + c * 8, 8), 8), :]
 
-        top = [other(above, j) for j in range(HALO)] + [own(first, r) for r in range(2 * HALO)]
-        low = [own(final, r) for r in range(2 * HALO)] + [other(below, j) for j in range(HALO)]
+        top, low = ([other(ref, j) for j in range(HALO)] for ref in (above, below))
+        none = jnp.zeros_like(top[0])
         for n in range(steps):
-            top, low = stencil(top), stencil(low)
-            for i in range(steps - 1 - n):
-                top[i] = top[i] * inside_above
-                low[-1 - i] = low[-1 - i] * inside_below
+            top = stencil(top + [none]) + [top[-1]]
+            low = [low[0]] + stencil([none] + low)
         for i, value in enumerate(top + low):
             spread[pl.ds(pl.multiple_of(i * depth + c * 8, 8), 8), :] = value
 
-    for move in moves[7:]:
-        move.wait()
     w = weights[:, : 3 * depth]
     v = source_weights[:, :48]
     for g in range(rows // 8):
@@ -379,11 +355,6 @@
             x = [sources[(r + q) * 16 : (r + q + 1) * 16, :] for q in range(2)]
             if HALO <= r < rows - HALO:
                 y = product(v, jnp.concatenate(x, 1))
-                for q in range(2):
-                    at = (r + q - HALO) * levels
-                    to[pl.ds((r + q) % 8, levels, stride=8), :] = (
-                        middle[at : at + levels, :] + y[:levels, q * width : (q + 1) * width]
-                    )
             else:
                 i = r if r < HALO else r - rows + 2 * HALO
                 x = [
@@ -393,9 +364,11 @@
                     for q in range(2)
                 ]
                 y = product(w, jnp.concatenate(x, 1))
-                for q in range(2):
-                    to[pl.ds((r + q) % 8, levels, stride=8), :] = y[:levels, q * width : (q + 1) * width]
-        leave.append(pltpu.make_async_copy(result.at[g], out.at[:, g], done.at[count + 1 + g]))
+            for q in range(2):
+                to[pl.ds((r + q) % 8, levels, stride=8), :] = (
+                    middle[(r + q) * levels : (r + q + 1) * levels, :] + y[:levels, q * width : (q + 1) * width]
+                )
+        leave.append(pltpu.make_async_copy(result.at[g], out.at[:, g], done.at[1 + g]))
         leave[-1].start()
     for move in leave:
         move.wait()
@@ -452,7 +425,7 @@
     length = HALO * stride + 2 * sea_stride + 8
     up, down = call(
         functools.partial(pack_kernel, sizes), [flat(length)] * 2,
-        sky, forcing, surface, rate, warmth2, brine2, wet, moved=4 << 20, in_specs=[HBM] * 7,
+        sky, forcing, surface, rate, warmth2, brine2, wet, moved=4 << 20, in_specs=[HBM] * 7, grant=FULL,
         scratch=[
             space(2, levels, 8, width), space(steps, rows, width), space(2, sea_levels * sea_rows, width),
             space(2, rows, width), pltpu.VMEM(wet.shape, wet.dtype), pltpu.SemaphoreType.DMA((8,)),
@@ -463,34 +436,29 @@
     below = lax.ppermute(up, ("tile", "comp"), [(i + 1, i) for i in range(count - 1)])
 
     depth = up_to(levels + 2 * steps, 16)
-    inner = rows - 2 * HALO
     mix_rows = up_to(levels, 16)
     sea_flat = flat(sea_levels * sea_rows)
-    kept = [
-        jax.ShapeDtypeStruct((mix_rows, 2 * width), bf16), flat(mix_rows, bf16),
-        jax.ShapeDtypeStruct((sea_stride, 2 * width), bf16), flat(sea_stride), flat(inner * levels),
-        sea_flat, sea_flat, flat(4 * sea_stride),
-    ]
-    found = [pltpu.VMEM(k.shape, k.dtype) for k in kept]
+    at = lax.axis_index(("tile", "comp")).astype(jnp.int32)[None]
     (rows_of_mix, source_rows, own, weights, source_weights, sea_weights, sea_first, middle, warm, salt, sea_ends) = call(
-        functools.partial(local_kernel, sizes),
-        [flat((steps - 1) * levels), flat(8), flat((steps - 1) * rows)] + kept,
-        vmix, curve[None], sea_mix, sky2, warmth2, brine2, wet,
-        out_specs=[VMEM] * 3 + [HBM] * 8,
-        scratch=found + [
-            space(inner * depth, width), space(2, sea_rows * sea_stride, width), pltpu.SemaphoreType.DMA((8,)),
+        functools.partial(local_kernel, sizes, count - 1),
+        [
+            flat((steps - 1) * levels), flat(8), flat((steps - 1) * rows),
+            jax.ShapeDtypeStruct((mix_rows, 2 * width), bf16), flat(mix_rows, bf16),
+            jax.ShapeDtypeStruct((sea_stride, 2 * width), bf16), flat(sea_stride), flat(rows * levels),
+            sea_flat, sea_flat, flat(4 * sea_stride),
         ],
+        at, vmix, curve[None], sea_mix, sky2, warmth2, brine2, wet,
+        in_specs=[pl.BlockSpec(memory_space=pltpu.SMEM)] + [VMEM] * 7,
+        scratch=[space(rows * depth, width), space(2, sea_rows * sea_stride, width)],
         flops=4 << 30, moved=8 << 20,
     )
 
     per = rows + 2 * topk
     tiles = lax.axis_size("tile")
-    reach = 2 * steps * (rows + 2 * HALO)
     sent, fluxes = call(
-        functools.partial(flux_kernel, sizes), [flat(tiles * per), flat(reach)],
+        functools.partial(flux_kernel, sizes), [flat(tiles * per), flat(2 * steps * (rows + 2 * HALO))],
         sky[-1], forcing2, surface, rate, rows_of_mix, source_rows, own, owners.T, locals_.T, below, above,
-        scratch=[space(reach, width), space(2 * HALO * stride, width), pltpu.SemaphoreType.DMA],
-        out_specs=[VMEM, HBM], moved=2 << 20,
+        scratch=[space(2 * HALO * stride, width)], moved=2 << 20,
     )
     got = lax.all_to_all(sent.reshape(tiles, per, width), "tile", split_axis=0, concat_axis=0, tiled=True)
     got = got.reshape(-1, width)
@@ -498,12 +466,11 @@
     sky_out, salt, warm = call(
         functools.partial(rest_kernel, sizes),
         [jax.ShapeDtypeStruct((levels, rows // 8, 8, width), f32), sea_flat, sea_flat],
-        sky, fluxes, weights, source_weights, sea_weights, middle, warm, salt, sea_ends, wet, below, above,
-        in_specs=[HBM] * 9 + [VMEM] * 3, out_specs=[HBM, HBM, VMEM],
+        fluxes, weights, source_weights, sea_weights, middle, warm, salt, sea_ends, wet, below, above,
+        out_specs=[HBM, HBM, VMEM],
         scratch=[
-            space(2, levels, 8, width), space(reach, width), found[0], found[1], found[2], found[4], found[6], found[7],
-            space(2 * HALO * depth, width), space(rows * 16, width), space(rows // 8, levels, 8, width),
-            pltpu.SemaphoreType.DMA((11 + rows // 8,)),
+            space(sea_levels * sea_rows, width), space(2 * HALO * depth, width), space(rows * 16, width),
+            space(rows // 8, levels, 8, width), pltpu.SemaphoreType.DMA((1 + rows // 8,)),
         ],
         flops=2 << 30, moved=8 << 20,
     )

time: 44 us -> 33.3 us (0.76)
  the two profiles are of different devices: /device:TPU:1 before, /device:TPU:0 now
where the time goes in v6:
time: 33.3 us; the launch traced here: 32.9 us
  Pallas kernels  14.4 us (43%)
  starting transfers between devices  11.6 us (35%)
  local copies, waits for them, and re-layouts  3.38 us (10%)
  waiting for transfers between devices  2.64 us (8%)
  between operations  0.89 us (3%)
    pallas_call x5, Pallas kernels, call(): pl.pallas_call(kernel, out_shape=out_shape, in_specs=in_specs or [VMEM] *...  14.4 us
    all_to_all x1, starting transfers between devices, body(): lax.all_to_all(sent.reshape(tiles, per, width), 'tile', split_axis=0, con...  7.26 us
    unnamed x34, local copies, waits for them, and re-layouts  3.38 us
    ppermute x1, starting transfers between devices, body(): lax.ppermute(down, ('tile', 'comp'), [(i, i + 1) for i in range(count - 1)])  3.04 us
    all_to_all x1, waiting for transfers between devices, body(): lax.all_to_all(sent.reshape(tiles, per, width), 'tile', split_axis=0, con...  2.64 us
    ppermute x1, starting transfers between devices, body(): lax.ppermute(up, ('tile', 'comp'), [(i + 1, i) for i in range(count - 1)])  1.29 us
  transfers between devices with their start and end apart: 3, of which 1 were waited for; matrix products, arithmetic and copies ran while one was open for 0% of the time, Pallas kernels for 30%

profile of v6, /device:TPU:0, one launch (start us, length us, event | category | flops | bytes accessed | tf_op | source)
XLA Modules:
  0.0 32.9 jit_solution(16577388552839083944)
XLA Ops:
  0.6 0.0 copy-start.7
  0.6 0.0 copy-start
  0.7 0.0 copy-start.2
  0.7 0.0 copy-start.1
  0.7 0.0 copy-start.11
  0.7 0.0 copy-start.10
  0.7 0.0 copy-start.12
  0.7 2.5 %shard_map.149 = (f32[456,128]{1,0:T(8,128)}, f32[456,128]{1,0:T(8,128)}) custom-call(f32[72,32,128]{2,1,0:T(8,128)} %sky.1, f32[4,32,128]{2,1,0:T(8,128)} %forcing.1, f32[32,128]{1,0:T(8,128)} %surface.3, f32[32,128]{1,0:T(8,128)} %rate.3, f32[992,128]{1,0:T(8,128)} %bitcast.19, f32[992,128]{1,0:T(8,128)} %bitcast.21, s32[16,128]{1,0:T(8,128)} %wet.7), custom_call_target="tpu_custom_call" | custom-call | bytes 4194304 | tf_op jit(solution)/shard_map/pallas_call | solution.py:25
  3.2 1.3 %collective-permute-start = (f32[456,128]{1,0:T(8,128)}, f32[456,128]{1,0:T(8,128)S(1)}, u32[]{:S(2)}, u32[]{:S(2)}) collective-permute-start(f32[456,128]{1,0:T(8,128)} %get-tuple-element.24), channel_id=1, source_target_pairs={{1,0},{2,1},{3,2},{4,3},{5,4},{6,5},{7,6},{8,7},{9,8},{10,9},{11,1... | collective-permute-start | bytes 700424 | tf_op jit(solution)/shard_map/ppermute | solution.py:436
  4.5 3.0 %collective-permute-start.1 = (f32[456,128]{1,0:T(8,128)}, f32[456,128]{1,0:T(8,128)S(1)}, u32[]{:S(2)}, u32[]{:S(2)}) collective-permute-start(f32[456,128]{1,0:T(8,128)} %get-tuple-element.25), channel_id=1, source_target_pairs={{0,1},{1,2},{2,3},{3,4},{4,5},{5,6},{6,7},{7,8},{8,9},{9,10},{10,1... | collective-permute-start | bytes 700424 | tf_op jit(solution)/shard_map/ppermute | solution.py:435
  7.5 0.0 copy-done.7
  7.5 0.0 copy-done
  7.6 0.0 copy-done.2
  7.6 0.0 copy-done.1
  7.6 0.0 copy-done.11
  7.6 0.0 copy-start.3
  7.6 0.0 copy-start.5
  7.6 0.0 copy-start.6
  7.6 0.0 copy-start.8
  7.7 0.0 copy-start.9
  7.7 6.1 %shard_map.148 = (f32[216,128]{1,0:T(8,128)S(1)}, f32[8,128]{1,0:T(8,128)S(1)}, f32[96,128]{1,0:T(8,128)S(1)}, bf16[80,256]{1,0:T(8,128)(2,1)S(1)}, bf16[80,128]...) custom-call(s32[1]{0:T(128)} %bitcast.2.place, ...), custom_call_target="tpu_custom_call" | custom-call | flops 4294967296 | bytes 8388608 | tf_op jit(solution)/shard_map/pallas_call | solution.py:25
  13.8 0.0 copy-start.13
  13.8 1.0 %copy-done.13 = f32[2304,128]{1,0:T(8,128)} copy-done((f32[2304,128]{1,0:T(8,128)}, f32[2304,128]{1,0:T(8,128)S(1)}, u32[]{:S(2)}) %copy-start.13) | copy-done | bytes 1179672
  14.8 0.0 collective-permute-done.below
  14.8 0.0 collective-permute-done.1.above
  14.9 1.1 %shard_map.150 = (f32[320,128]{1,0:T(8,128)}, f32[320,128]{1,0:T(8,128)S(1)}) custom-call(f32[32,128]{1,0:T(8,128)S(1)} %slice_bitcast_fusion.sky, f32[128,128]{1,0:T(8,128)S(1)} %bitcast.23, f32[32,128]{1,0:T(8,128)S(1)} %copy-done.5, f32[32,128]{1,0:T(8,128)S(1)} %copy-done.6, f32[216,128]{1,0:T(8,128)S(1)} %get-tuple-element.21.rows_of_mix, ...), custom_call_target="tpu_custom_call" | custom-call | bytes 2097152 | tf_op jit(solution)/shard_map/pallas_call | solution.py:25
  16.0 7.3 %all-to-all-start = ((f32[8,40,128]{2,1,0:T(8,128)}), f32[8,40,128]{2,1,0:T(8,128)S(1)}, u32[]{:S(2)}, u32[]{:S(2)}) async-start(f32[8,40,128]{2,1,0:T(8,128)} %bitcast.10), calls=%async_computation | async-start | bytes 327680 | tf_op jit(solution)/shard_map/all_to_all | solution.py:463
  23.3 1.3 %copy-done.14 = f32[2304,128]{1,0:T(8,128)S(1)} copy-done((f32[2304,128]{1,0:T(8,128)S(1)}, f32[2304,128]{1,0:T(8,128)}, u32[]{:S(2)}) %copy-start.14) | copy-done | bytes 1179672
  24.5 1.0 %copy-done.16 = f32[992,128]{1,0:T(8,128)S(1)} copy-done((f32[992,128]{1,0:T(8,128)S(1)}, f32[992,128]{1,0:T(8,128)}, u32[]{:S(2)}) %copy-start.16) | copy-done | bytes 507928
  25.6 3.6 %shard_map.151 = (f32[72,4,8,128]{3,2,1,0:T(8,128)}, f32[992,128]{1,0:T(8,128)}, f32[992,128]{1,0:T(8,128)S(1)}) custom-call(f32[320,128]{1,0:T(8,128)S(1)} %get-tuple-element.26.fluxes, bf16[80,256]{1,0:T(8,128)(2,1)S(1)} %get-tuple-element.27.weights, bf16[80,128]{1,0:T(8,128)(2,1)S(1)} %get-tuple-element.28.source_weights, ...), custom_call_target="tpu_custom_call" | custom-call | flops 2147483648 | bytes 8388608 | tf_op jit(solution)/shard_map/pallas_call | solution.py:25
  29.2 2.6 %all-to-all-done = f32[8,40,128]{2,1,0:T(8,128)S(1)} async-done(((f32[8,40,128]{2,1,0:T(8,128)}), f32[8,40,128]{2,1,0:T(8,128)S(1)}, u32[]{:S(2)}, u32[]{:S(2)}) %all-to-all-start) | async-done | bytes 163872 | tf_op jit(solution)/shard_map/all_to_all | solution.py:463
  31.8 1.1 %shard_map.152 = f32[992,128]{1,0:T(8,128)} custom-call(f32[320,128]{1,0:T(8,128)S(1)} %bitcast.18, s32[1]{0:T(128)} %bitcast.12.mine, bf16[512,128]{1,0:T(8,128)(2,1)S(1)} %bitcast.24, s32[16,128]{1,0:T(8,128)S(1)} %copy-done.7, f32[64,128]{1,0:T(8,128)S(1)} %get-tuple-element.36.sea_first, f32[992,128]{1,0:T(8,128)S(1)} %get-tuple-element.37.before), custom_call_target="tpu_custom_call" | custom-call | bytes 2097152 | tf_op jit(solution)/shard_map/pallas_call | solution.py:25
  (14 shorter events, 0.0 us)
Async XLA Ops:
  0.6 6.9 %copy-start.7 = (s32[16,128]{1,0:T(8,128)S(1)}, s32[16,128]{1,0:T(8,128)}, u32[]{:S(2)}) copy-start(s32[16,128]{1,0:T(8,128)} %wet.7) | copy-start | bytes 24580
  0.6 6.9 %copy-start = (f32[72,32,128]{2,1,0:T(8,128)S(1)}, f32[72,32,128]{2,1,0:T(8,128)}, u32[]{:S(2)}) copy-start(f32[72,32,128]{2,1,0:T(8,128)} %sky.1) | copy-start | bytes 3538948
  0.7 6.9 %copy-start.2 = (f32[62,16,128]{2,1,0:T(8,128)S(1)}, f32[62,16,128]{2,1,0:T(8,128)}, u32[]{:S(2)}) copy-start(f32[62,16,128]{2,1,0:T(8,128)} %param.23) | copy-start | bytes 1523716
  0.7 6.9 %copy-start.1 = (f32[62,16,128]{2,1,0:T(8,128)S(1)}, f32[62,16,128]{2,1,0:T(8,128)}, u32[]{:S(2)}) copy-start(f32[62,16,128]{2,1,0:T(8,128)} %param.22) | copy-start | bytes 1523716
  0.7 6.9 %copy-start.11 = (f32[62,62]{1,0:T(8,128)S(1)}, f32[62,62]{1,0:T(8,128)}, u32[]{:S(2)}) copy-start(f32[62,62]{1,0:T(8,128)} %sea_mix.1) | copy-start | bytes 46132
  0.7 6.9 %copy-start.10 = (f32[72,72]{1,0:T(8,128)S(1)}, f32[72,72]{1,0:T(8,128)}, u32[]{:S(2)}) copy-start(f32[72,72]{1,0:T(8,128)} %vmix.1) | copy-start | bytes 62212
  0.7 6.9 %copy-start.12 = (f32[72]{0:T(128)S(1)}, f32[72]{0:T(128)}, u32[]{:S(2)}) copy-start(f32[72]{0:T(128)} %param.15) | copy-start | bytes 868
  3.2 11.7 %collective-permute-start = (f32[456,128]{1,0:T(8,128)}, f32[456,128]{1,0:T(8,128)S(1)}, u32[]{:S(2)}, u32[]{:S(2)}) collective-permute-start(f32[456,128]{1,0:T(8,128)} %get-tuple-element.24), channel_id=1, source_target_pairs={{1,0},{2,1},{3,2},{4,3},{5,4},{6,5},{7,6},{8,7},{9,8},{10,9},{11,1... | collective-permute-start | bytes 700424 | tf_op jit(solution)/shard_map/ppermute | solution.py:436
  4.5 10.4 %collective-permute-start.1 = (f32[456,128]{1,0:T(8,128)}, f32[456,128]{1,0:T(8,128)S(1)}, u32[]{:S(2)}, u32[]{:S(2)}) collective-permute-start(f32[456,128]{1,0:T(8,128)} %get-tuple-element.25), channel_id=1, source_target_pairs={{0,1},{1,2},{2,3},{3,4},{4,5},{5,6},{6,7},{7,8},{8,9},{9,10},{10,1... | collective-permute-start | bytes 700424 | tf_op jit(solution)/shard_map/ppermute | solution.py:435
  7.6 7.2 %copy-start.3 = (f32[4,32,128]{2,1,0:T(8,128)S(1)}, f32[4,32,128]{2,1,0:T(8,128)}, u32[]{:S(2)}) copy-start(f32[4,32,128]{2,1,0:T(8,128)} %forcing.1) | copy-start | bytes 196612
  7.6 7.2 %copy-start.5 = (f32[32,128]{1,0:T(8,128)S(1)}, f32[32,128]{1,0:T(8,128)}, u32[]{:S(2)}) copy-start(f32[32,128]{1,0:T(8,128)} %surface.3) | copy-start | bytes 49156
  7.6 7.2 %copy-start.6 = (f32[32,128]{1,0:T(8,128)S(1)}, f32[32,128]{1,0:T(8,128)}, u32[]{:S(2)}) copy-start(f32[32,128]{1,0:T(8,128)} %rate.3) | copy-start | bytes 49156
  7.6 7.2 %copy-start.8 = (s32[32,4]{0,1:T(4,128)S(1)}, s32[32,4]{0,1:T(4,128)}, u32[]{:S(2)}) copy-start(s32[32,4]{0,1:T(4,128)} %param.20) | copy-start | bytes 1540
  7.7 7.2 %copy-start.9 = (s32[32,4]{0,1:T(4,128)S(1)}, s32[32,4]{0,1:T(4,128)}, u32[]{:S(2)}) copy-start(s32[32,4]{0,1:T(4,128)} %param.21) | copy-start | bytes 1540
  13.8 1.0 %copy-start.13 = (f32[2304,128]{1,0:T(8,128)}, f32[2304,128]{1,0:T(8,128)S(1)}, u32[]{:S(2)}) copy-start(f32[2304,128]{1,0:T(8,128)S(1)} %get-tuple-element.30.middle) | copy-start | bytes 3538948
  14.8 1.1 %copy-start.15 = (f32[992,128]{1,0:T(8,128)}, f32[992,128]{1,0:T(8,128)S(1)}, u32[]{:S(2)}) copy-start(f32[992,128]{1,0:T(8,128)S(1)} %get-tuple-element.32.salt) | copy-start | bytes 1523716
  16.0 15.8 %all-to-all-start = ((f32[8,40,128]{2,1,0:T(8,128)}), f32[8,40,128]{2,1,0:T(8,128)S(1)}, u32[]{:S(2)}, u32[]{:S(2)}) async-start(f32[8,40,128]{2,1,0:T(8,128)} %bitcast.10), calls=%async_computation | async-start | bytes 327680 | tf_op jit(solution)/shard_map/all_to_all | solution.py:463
  23.2 1.3 %copy-start.14 = (f32[2304,128]{1,0:T(8,128)S(1)}, f32[2304,128]{1,0:T(8,128)}, u32[]{:S(2)}) copy-start(f32[2304,128]{1,0:T(8,128)} %copy-done.13) | copy-start | bytes 3538948
  24.5 1.0 %copy-start.16 = (f32[992,128]{1,0:T(8,128)S(1)}, f32[992,128]{1,0:T(8,128)}, u32[]{:S(2)}) copy-start(f32[992,128]{1,0:T(8,128)} %copy-done.15) | copy-start | bytes 1523716
  25.6 6.3 %copy-start.4 = (bf16[4,128,128]{2,1,0:T(8,128)(2,1)S(1)}, bf16[4,128,128]{2,1,0:T(8,128)(2,1)}, u32[]{:S(2)}) copy-start(bf16[4,128,128]{2,1,0:T(8,128)(2,1)} %param.19) | copy-start | bytes 393220

commit v7 on v6

--- a/solution.py
+++ b/solution.py
@@ -11,6 +11,7 @@
 ocean_diffusion = 0.2
 HALO = 4
 FULL = 60
+ROOM = 20
 EXACT = lax.Precision.HIGHEST
 VMEM = pl.BlockSpec(memory_space=pltpu.VMEM)
 HBM = pl.BlockSpec(memory_space=pltpu.HBM)
@@ -107,8 +108,8 @@
 
 def local_kernel(
     sizes, last_place, place, vmix, curve, sea_mix, sky, warmth, brine, wet,
-    rows_of_mix, source_rows, own, weights, source_weights, sea_weights, sea_first, middle, warm_out, brine_out, sea_ends,
-    spread, sea_spread,
+    rows_of_mix, source_rows, own, weights, source_weights, sea_weights, sea_first, sea_ends, store,
+    middle, warm_out, brine_out, spread, sea_spread, done,
 ):
     levels, rows, steps, sea_levels, sea_rows, stride, sea_stride = sizes
     width = sky.shape[1]
@@ -161,37 +162,6 @@
     for s in range(steps - 1):
         own[s * rows : (s + 1) * rows, :] = sums[s]
 
-    before = jnp.where(place[0] > 0, 1.0, 0.0)
-    behind = jnp.where(place[0] < last_place, 1.0, 0.0)
-
-    @pl.loop(0, levels // 8)
-    def _(c):
-        x = [sky[pl.ds(c * 8 * rows + r, 8, stride=rows), :] for r in range(rows)]
-        none = jnp.zeros_like(x[0])
-        beyond = 0
-        for n in range(steps):
-            if beyond < steps - 1 - n:
-                x = [x[0]] + stencil([none] + x + [none]) + [x[-1]]
-                beyond += 1
-            else:
-                x = stencil(x)
-                beyond -= 1
-            for i in range(beyond):
-                x[i] = x[i] * before
-                x[-1 - i] = x[-1 - i] * behind
-        for r in range(rows):
-            spread[pl.ds(pl.multiple_of(r * depth + c * 8, 8), 8), :] = x[r]
-
-    if depth > levels:
-        for r in range(rows):
-            spread[r * depth + levels : (r + 1) * depth, :] = jnp.zeros((depth - levels, width), f32)
-    w = weights[:, : 3 * depth]
-    for r in range(0, rows, 2):
-        x = jnp.concatenate([spread[(r + i) * depth : (r + i + 1) * depth, :] for i in range(2)], 1)
-        y = product(w, x)
-        for i in range(2):
-            middle[(r + i) * levels : (r + i + 1) * levels, :] = y[:levels, i * width : (i + 1) * width]
-
     m = wet[...].astype(f32)
     mark = [m[r : r + 1] for r in range(sea_rows)]
     edge = jnp.zeros((1, width), f32)
@@ -223,6 +193,49 @@
             if r in (0, sea_rows - 1):
                 at = (2 * f + (r > 0)) * sea_stride
                 sea_ends[at : at + sea_levels, :] = old
+    area = sea_levels * sea_rows
+    leave = []
+    for f, out in enumerate((warm_out, brine_out)):
+        part = store.at[pl.ds(rows * levels + f * area, area)]
+        leave.append(pltpu.make_async_copy(out, part, done.at[rows // 8 + f]))
+        leave[-1].start()
+
+    before = jnp.where(place[0] > 0, 1.0, 0.0)
+    behind = jnp.where(place[0] < last_place, 1.0, 0.0)
+
+    @pl.loop(0, levels // 8)
+    def _(c):
+        x = [sky[pl.ds(c * 8 * rows + r, 8, stride=rows), :] for r in range(rows)]
+        none = jnp.zeros_like(x[0])
+        beyond = 0
+        for n in range(steps):
+            if beyond < steps - 1 - n:
+                x = [x[0]] + stencil([none] + x + [none]) + [x[-1]]
+                beyond += 1
+            else:
+                x = stencil(x)
+                beyond -= 1
+            for i in range(beyond):
+                x[i] = x[i] * before
+                x[-1 - i] = x[-1 - i] * behind
+        for r in range(rows):
+            spread[pl.ds(pl.multiple_of(r * depth + c * 8, 8), 8), :] = x[r]
+
+    if depth > levels:
+        for r in range(rows):
+            spread[r * depth + levels : (r + 1) * depth, :] = jnp.zeros((depth - levels, width), f32)
+    w = weights[:, : 3 * depth]
+    for r in range(0, rows, 2):
+        x = jnp.concatenate([spread[(r + i) * depth : (r + i + 1) * depth, :] for i in range(2)], 1)
+        y = product(w, x)
+        for i in range(2):
+            middle[(r + i) * levels : (r + i + 1) * levels, :] = y[:levels, i * width : (i + 1) * width]
+        if (r + 2) % 8 == 0:
+            part = pl.ds((r - 6) * levels, 8 * levels)
+            leave.append(pltpu.make_async_copy(middle.at[part], store.at[part], done.at[r // 8]))
+            leave[-1].start()
+    for move in leave:
+        move.wait()
 
 
 def cross(x):
@@ -237,7 +250,7 @@
 
 
 def flux_kernel(
-    sizes, sky, forcing, surface, rate, rows_of_mix, source_rows, own, owners, locals_, below, above,
+    sizes, sky, forcing, surface, rate, rows_of_mix, source_rows, own, owners, locals_, shares, below, above,
     sent, fluxes, halo
 ):
     levels, rows, steps, sea_levels, sea_rows, stride, sea_stride = sizes
@@ -277,26 +290,40 @@
     total = flux[0][:rows]
     for s in range(1, steps):
         total = total + flux[s][:rows]
-    mean = (total / steps).astype(bf16).astype(f32)
-    times = width // rows
-    owner = owners[...].astype(f32)
-    row = locals_[...].astype(f32)
-    table = jnp.concatenate(
-        [jnp.concatenate([owner] * times, 1), jnp.concatenate([row] * times, 1)], 0
-    )
-    per = mean.shape[0] + table.shape[0]
-    for t in range(sent.shape[0] // per):
-        sent[t * per : t * per + rows, :] = mean
-        sent[t * per + rows : (t + 1) * per, :] = table
+    mean = (total / steps).astype(bf16)
+    topk = owners.shape[0]
+    target = owners[...] * sea_rows + locals_[...]
+    target = jnp.concatenate([target[k : k + 1, :] for k in range(topk)], 1)
+    rowed = jnp.concatenate(
+        [jnp.dot(mean, shares[k * width : (k + 1) * width, :], preferred_element_type=f32) for k in range(topk)], 0
+    )
+    first = rowed.astype(bf16)
+    left = rowed - first.astype(f32)
+    second = left.astype(bf16)
+    third = (left - second.astype(f32)).astype(bf16)
+    hot = lax.broadcasted_iota(jnp.int32, (sent.shape[0], topk * rows), 0) == target
+    hot = jnp.where(hot, 1.0, 0.0).astype(bf16)
+    sent[...] = jnp.dot(
+        jnp.concatenate([hot, hot, hot], 1), jnp.concatenate([first, second, third], 0), preferred_element_type=f32
+    )
 
 
 def rest_kernel(
-    sizes, fluxes, weights, source_weights, sea_weights, middle, warm, salt, sea_ends, wet, below, above,
-    out, brine_out, warm_out, salt_held, spread, sources, result, done
+    sizes, fluxes, weights, source_weights, sea_weights, sea_ends, wet, below, above, store,
+    out, brine_out, warm_out, salt_held, middle, spread, sources, result, done
 ):
     levels, rows, steps, sea_levels, sea_rows, stride, sea_stride = sizes
     width = above.shape[1]
     depth = up_to(levels + 2 * steps, 16)
+    area = sea_levels * sea_rows
+    fetches = [
+        pltpu.make_async_copy(store.at[pl.ds(first, to.shape[0])], to, done.at[i])
+        for i, (first, to) in enumerate(
+            ((rows * levels, warm_out), (rows * levels + area, salt_held), (0, middle))
+        )
+    ]
+    for fetch in fetches:
+        fetch.start()
     flag = levels + steps + 2
     inside_above, inside_below = above[flag : flag + 1, :], below[flag : flag + 1, :]
 
@@ -312,8 +339,21 @@
     for r in range(rows):
         sources[r * 16 : (r + 1) * 16, :] = jnp.concatenate([x[r], jnp.zeros((16 - 2 * steps, width), f32)], 0)
 
-    warm_out[...] = warm[...]
-    salt_held[...] = salt[...]
+    @pl.loop(0, levels // 8)
+    def _(c):
+        def other(ref, j):
+            return ref[pl.ds(pl.multiple_of(j * stride + c * 8, 8), 8), :]
+
+        top, low = ([other(ref, j) for j in range(HALO)] for ref in (above, below))
+        none = jnp.zeros_like(top[0])
+        for n in range(steps):
+            top = stencil(top + [none]) + [top[-1]]
+            low = [low[0]] + stencil([none] + low)
+        for i, value in enumerate(top + low):
+            spread[pl.ds(pl.multiple_of(i * depth + c * 8, 8), 8), :] = value
+
+    for fetch in fetches[:2]:
+        fetch.wait()
     m = wet[...].astype(f32)
     base = HALO * stride
     w = sea_weights[:, : 3 * sea_stride]
@@ -331,22 +371,10 @@
         for f, to in enumerate((warm_out, salt_held)):
             rows_at = pl.ds(r, sea_levels, stride=sea_rows)
             to[rows_at, :] = to[rows_at, :] + mark * y[:sea_levels, f * width : (f + 1) * width]
-    leave = [pltpu.make_async_copy(salt_held, brine_out, done.at[0])]
+    leave = [pltpu.make_async_copy(salt_held, brine_out, done.at[3])]
     leave[0].start()
 
-    @pl.loop(0, levels // 8)
-    def _(c):
-        def other(ref, j):
-            return ref[pl.ds(pl.multiple_of(j * stride + c * 8, 8), 8), :]
-
-        top, low = ([other(ref, j) for j in range(HALO)] for ref in (above, below))
-        none = jnp.zeros_like(top[0])
-        for n in range(steps):
-            top = stencil(top + [none]) + [top[-1]]
-            low = [low[0]] + stencil([none] + low)
-        for i, value in enumerate(top + low):
-            spread[pl.ds(pl.multiple_of(i * depth + c * 8, 8), 8), :] = value
-
+    fetches[2].wait()
     w = weights[:, : 3 * depth]
     v = source_weights[:, :48]
     for g in range(rows // 8):
@@ -368,40 +396,17 @@
                 to[pl.ds((r + q) % 8, levels, stride=8), :] = (
                     middle[(r + q) * levels : (r + q + 1) * levels, :] + y[:levels, q * width : (q + 1) * width]
                 )
-        leave.append(pltpu.make_async_copy(result.at[g], out.at[:, g], done.at[1 + g]))
+        leave.append(pltpu.make_async_copy(result.at[g], out.at[:, g], done.at[4 + g]))
         leave[-1].start()
     for move in leave:
         move.wait()
 
 
-def heat_kernel(sizes, topk, got, mine, shares, wet, sea_first, before, after):
+def heat_kernel(sizes, got, wet, sea_first, before, after):
     levels, rows, steps, sea_levels, sea_rows, stride, sea_stride = sizes
-    width = before.shape[1]
-    per = rows + 2 * topk
-    group = width // rows
-    me = mine[0].astype(f32)
-    part = lax.broadcasted_iota(jnp.int32, (1, width), 1) // rows
-    to = lax.broadcasted_iota(jnp.int32, (sea_rows, width), 0).astype(f32)
-    picked = jnp.zeros((topk * sea_rows, width), f32)
-    for g in range(got.shape[0] // (per * group)):
-        at = [(g * group + i) * per for i in range(group)]
-        mean = jnp.concatenate([got[a : a + rows, :] for a in at], 0).astype(bf16)
-        table = got[at[0] + rows : at[0] + per, :]
-        for i in range(1, group):
-            table = jnp.where(part == i, got[at[i] + rows : at[i] + per, :], table)
-        hot = []
-        for k in range(topk):
-            row = jnp.where(table[k : k + 1] == me, table[topk + k : topk + k + 1], -1.0)
-            hot.append(jnp.where(to == row, 1.0, 0.0))
-        hot = jnp.concatenate(hot, 0).astype(bf16)
-        picked = picked + jnp.dot(hot, mean, preferred_element_type=f32)
-    side = jnp.concatenate([picked[k * sea_rows : (k + 1) * sea_rows] for k in range(topk)], 1)
-    first = side.astype(bf16).astype(f32)
-    second = (side - first).astype(bf16).astype(f32)
-    third = side - first - second
-    parts = jnp.concatenate([first, second, third], 0).astype(bf16)
-    y = jnp.dot(parts, shares[...], preferred_element_type=f32)
-    heat = y[:sea_rows] + y[sea_rows : 2 * sea_rows] + y[2 * sea_rows :]
+    heat = got[:sea_rows, :]
+    for t in range(1, got.shape[0] // sea_rows):
+        heat = heat + got[t * sea_rows : (t + 1) * sea_rows, :]
     heat = wet[...].astype(f32) * heat
     for l in range(sea_levels):
         after[l * sea_rows : (l + 1) * sea_rows, :] = (
@@ -439,47 +444,48 @@
     mix_rows = up_to(levels, 16)
     sea_flat = flat(sea_levels * sea_rows)
     at = lax.axis_index(("tile", "comp")).astype(jnp.int32)[None]
-    (rows_of_mix, source_rows, own, weights, source_weights, sea_weights, sea_first, middle, warm, salt, sea_ends) = call(
+    area = sea_levels * sea_rows
+    large = max(rows * levels + 2 * area, ROOM * 2**20 // (4 * width))
+    (rows_of_mix, source_rows, own, weights, source_weights, sea_weights, sea_first, sea_ends, store) = call(
         functools.partial(local_kernel, sizes, count - 1),
         [
             flat((steps - 1) * levels), flat(8), flat((steps - 1) * rows),
             jax.ShapeDtypeStruct((mix_rows, 2 * width), bf16), flat(mix_rows, bf16),
-            jax.ShapeDtypeStruct((sea_stride, 2 * width), bf16), flat(sea_stride), flat(rows * levels),
-            sea_flat, sea_flat, flat(4 * sea_stride),
+            jax.ShapeDtypeStruct((sea_stride, 2 * width), bf16), flat(sea_stride), flat(4 * sea_stride),
+            flat(large),
         ],
         at, vmix, curve[None], sea_mix, sky2, warmth2, brine2, wet,
-        in_specs=[pl.BlockSpec(memory_space=pltpu.SMEM)] + [VMEM] * 7,
-        scratch=[space(rows * depth, width), space(2, sea_rows * sea_stride, width)],
-        flops=4 << 30, moved=8 << 20,
-    )
-
-    per = rows + 2 * topk
+        in_specs=[pl.BlockSpec(memory_space=pltpu.SMEM)] + [VMEM] * 7, out_specs=[VMEM] * 8 + [HBM],
+        scratch=[
+            space(rows * levels, width), space(area, width), space(area, width),
+            space(rows * depth, width), space(2, sea_rows * sea_stride, width),
+            pltpu.SemaphoreType.DMA((rows // 8 + 2,)),
+        ],
+        flops=4 << 30, moved=8 << 20, grant=48,
+    )
+
     tiles = lax.axis_size("tile")
     sent, fluxes = call(
-        functools.partial(flux_kernel, sizes), [flat(tiles * per), flat(2 * steps * (rows + 2 * HALO))],
-        sky[-1], forcing2, surface, rate, rows_of_mix, source_rows, own, owners.T, locals_.T, below, above,
+        functools.partial(flux_kernel, sizes), [flat(tiles * sea_rows), flat(2 * steps * (rows + 2 * HALO))],
+        sky[-1], forcing2, surface, rate, rows_of_mix, source_rows, own, owners.T, locals_.T,
+        shares.reshape(-1, width), below, above,
         scratch=[space(2 * HALO * stride, width)], moved=2 << 20,
     )
-    got = lax.all_to_all(sent.reshape(tiles, per, width), "tile", split_axis=0, concat_axis=0, tiled=True)
+    got = lax.all_to_all(sent.reshape(tiles, sea_rows, width), "tile", split_axis=0, concat_axis=0, tiled=True)
     got = got.reshape(-1, width)
 
     sky_out, salt, warm = call(
         functools.partial(rest_kernel, sizes),
         [jax.ShapeDtypeStruct((levels, rows // 8, 8, width), f32), sea_flat, sea_flat],
-        fluxes, weights, source_weights, sea_weights, middle, warm, salt, sea_ends, wet, below, above,
-        out_specs=[HBM, HBM, VMEM],
+        fluxes, weights, source_weights, sea_weights, sea_ends, wet, below, above, store,
+        in_specs=[VMEM] * 8 + [HBM], out_specs=[HBM, HBM, VMEM],
         scratch=[
-            space(sea_levels * sea_rows, width), space(2 * HALO * depth, width), space(rows * 16, width),
-            space(rows // 8, levels, 8, width), pltpu.SemaphoreType.DMA((1 + rows // 8,)),
+            space(area, width), space(rows * levels, width), space(2 * HALO * depth, width), space(rows * 16, width),
+            space(rows // 8, levels, 8, width), pltpu.SemaphoreType.DMA((4 + rows // 8,)),
         ],
-        flops=2 << 30, moved=8 << 20,
-    )
-    mine = lax.axis_index("tile").astype(jnp.int32)[None]
-    warm = call(
-        functools.partial(heat_kernel, sizes, topk), flat(sea_levels * sea_rows),
-        got, mine, shares.reshape(-1, width), wet, sea_first, warm,
-        in_specs=[VMEM, pl.BlockSpec(memory_space=pltpu.SMEM)] + [VMEM] * 4, moved=2 << 20,
-    )
+        flops=2 << 30, moved=8 << 20, grant=48,
+    )
+    warm = call(functools.partial(heat_kernel, sizes), sea_flat, got, wet, sea_first, warm, moved=2 << 20)
     return sky_out.reshape(sky.shape), warm.reshape(warmth.shape), salt.reshape(brine.shape)
 
 

time: 33.3 us -> 31.5 us (0.946)
  local copies, waits for them, and re-layouts: 3.38 us -> 0.07 us
  Pallas kernels: 14.4 us -> 15.3 us
  waiting for transfers between devices: 2.64 us -> 3.37 us
    unnamed x34 -> x26, local copies, waits for them, and re-layouts: 3.38 us -> 0.07 us
    pallas_call x5, Pallas kernels: 14.4 us -> 15.3 us  [call(): pl.pallas_call(kernel, out_shape=out_shape, in_specs=in_specs or [VMEM] *...]
    all_to_all x1, waiting for transfers between devices: 2.64 us -> 3.36 us  [body(): lax.all_to_all(sent.reshape(tiles, sea_rows, width), 'tile', split_axis=0...]
  transfers between devices with their start and end apart: 3 -> 3, of which waited for: 1 -> 1; matrix products, arithmetic and copies ran while one was open for 0% -> 0% of each run, Pallas kernels for 30% -> 34%
where the time goes in v7:
time: 31.5 us; the launch traced here: 31.2 us
  Pallas kernels  15.3 us (49%)
  starting transfers between devices  11.6 us (37%)
  waiting for transfers between devices  3.37 us (11%)
  between operations  0.91 us (3%)
    pallas_call x5, Pallas kernels, call(): pl.pallas_call(kernel, out_shape=out_shape, in_specs=in_specs or [VMEM] *...  15.3 us
    all_to_all x1, starting transfers between devices, body(): lax.all_to_all(sent.reshape(tiles, sea_rows, width), 'tile', split_axis=0...  7.25 us
    all_to_all x1, waiting for transfers between devices, body(): lax.all_to_all(sent.reshape(tiles, sea_rows, width), 'tile', split_axis=0...  3.36 us
    ppermute x1, starting transfers between devices, body(): lax.ppermute(down, ('tile', 'comp'), [(i, i + 1) for i in range(count - 1)])  3.04 us
    ppermute x1, starting transfers between devices, body(): lax.ppermute(up, ('tile', 'comp'), [(i + 1, i) for i in range(count - 1)])  1.29 us
  transfers between devices with their start and end apart: 3, of which 1 were waited for; matrix products, arithmetic and copies ran while one was open for 0% of the time, Pallas kernels for 34%

profile of v7, /device:TPU:0, one launch (start us, length us, event | category | flops | bytes accessed | tf_op | source)
XLA Modules:
  0.0 31.2 jit_solution(14506860892050873889)
XLA Ops:
  0.6 0.0 copy-start.5
  0.6 0.0 copy-start
  0.7 0.0 copy-start.2
  0.7 0.0 copy-start.1
  0.7 0.0 copy-start.11
  0.7 0.0 copy-start.10
  0.7 0.0 copy-start.12
  0.7 2.5 %shard_map.149 = (f32[456,128]{1,0:T(8,128)}, f32[456,128]{1,0:T(8,128)}) custom-call(f32[72,32,128]{2,1,0:T(8,128)} %sky.1, f32[4,32,128]{2,1,0:T(8,128)} %forcing.1, f32[32,128]{1,0:T(8,128)} %surface.3, f32[32,128]{1,0:T(8,128)} %rate.3, f32[992,128]{1,0:T(8,128)} %bitcast.17, f32[992,128]{1,0:T(8,128)} %bitcast.19, s32[16,128]{1,0:T(8,128)} %wet.7), custom_call_target="tpu_custom_call" | custom-call | bytes 4194304 | tf_op jit(solution)/shard_map/pallas_call | solution.py:26
  3.2 1.3 %collective-permute-start = (f32[456,128]{1,0:T(8,128)}, f32[456,128]{1,0:T(8,128)S(1)}, u32[]{:S(2)}, u32[]{:S(2)}) collective-permute-start(f32[456,128]{1,0:T(8,128)} %get-tuple-element.22), channel_id=1, source_target_pairs={{1,0},{2,1},{3,2},{4,3},{5,4},{6,5},{7,6},{8,7},{9,8},{10,9},{11,1... | collective-permute-start | bytes 700424 | tf_op jit(solution)/shard_map/ppermute | solution.py:441
  4.5 3.0 %collective-permute-start.1 = (f32[456,128]{1,0:T(8,128)}, f32[456,128]{1,0:T(8,128)S(1)}, u32[]{:S(2)}, u32[]{:S(2)}) collective-permute-start(f32[456,128]{1,0:T(8,128)} %get-tuple-element.23), channel_id=1, source_target_pairs={{0,1},{1,2},{2,3},{3,4},{4,5},{5,6},{6,7},{7,8},{8,9},{9,10},{10,1... | collective-permute-start | bytes 700424 | tf_op jit(solution)/shard_map/ppermute | solution.py:440
  7.5 0.0 copy-done.5
  7.5 0.0 copy-done
  7.6 0.0 copy-done.2
  7.6 0.0 copy-done.1
  7.6 0.0 copy-done.11
  7.6 0.0 copy-done.10
  7.6 0.0 copy-done.12
  7.6 0.0 copy-start.3
  7.6 0.0 copy-start.4
  7.6 0.0 copy-start.6
  7.6 0.0 copy-start.7
  7.7 0.0 copy-start.8
  7.7 0.0 copy-start.9
  7.7 6.9 %shard_map.148 = (f32[216,128]{1,0:T(8,128)S(1)}, f32[8,128]{1,0:T(8,128)S(1)}, f32[96,128]{1,0:T(8,128)S(1)}, bf16[80,256]{1,0:T(8,128)(2,1)S(1)}, bf16[80,128]...) custom-call(s32[1]{0:T(128)} %bitcast.2.place, ...), custom_call_target="tpu_custom_call" | custom-call | flops 4294967296 | bytes 8388608 | tf_op jit(solution)/shard_map/pallas_call | solution.py:26
  14.6 0.0 collective-permute-done.below
  14.6 0.0 collective-permute-done.1.above
  14.6 0.0 copy-done.3
  14.7 1.3 %shard_map.150 = (f32[128,128]{1,0:T(8,128)}, f32[320,128]{1,0:T(8,128)S(1)}) custom-call(f32[32,128]{1,0:T(8,128)S(1)} %slice_bitcast_fusion.sky, f32[128,128]{1,0:T(8,128)S(1)} %bitcast.21, f32[32,128]{1,0:T(8,128)S(1)} %copy-done.6, f32[32,128]{1,0:T(8,128)S(1)} %copy-done.7, f32[216,128]{1,0:T(8,128)S(1)} %get-tuple-element.19.rows_of_mix, ...), custom_call_target="tpu_custom_call" | custom-call | bytes 2097152 | tf_op jit(solution)/shard_map/pallas_call | solution.py:26
  16.0 7.3 %all-to-all-start = ((f32[8,16,128]{2,1,0:T(8,128)}), f32[8,16,128]{2,1,0:T(8,128)S(1)}, u32[]{:S(2)}, u32[]{:S(2)}) async-start(f32[8,16,128]{2,1,0:T(8,128)} %bitcast.11), calls=%async_computation | async-start | bytes 131072 | tf_op jit(solution)/shard_map/all_to_all | solution.py:474
  23.2 3.8 %shard_map.151 = (f32[72,4,8,128]{3,2,1,0:T(8,128)}, f32[992,128]{1,0:T(8,128)}, f32[992,128]{1,0:T(8,128)S(1)}) custom-call(f32[320,128]{1,0:T(8,128)S(1)} %get-tuple-element.24.fluxes, bf16[80,256]{1,0:T(8,128)(2,1)S(1)} %get-tuple-element.25.weights, bf16[80,128]{1,0:T(8,128)(2,1)S(1)} %get-tuple-element.26.source_weights, ...), custom_call_target="tpu_custom_call" | custom-call | flops 2147483648 | bytes 8388608 | tf_op jit(solution)/shard_map/pallas_call | solution.py:26
  27.0 3.4 %all-to-all-done = f32[8,16,128]{2,1,0:T(8,128)S(1)} async-done(((f32[8,16,128]{2,1,0:T(8,128)}), f32[8,16,128]{2,1,0:T(8,128)S(1)}, u32[]{:S(2)}, u32[]{:S(2)}) %all-to-all-start) | async-done | bytes 65568 | tf_op jit(solution)/shard_map/all_to_all | solution.py:474
  30.4 0.8 %shard_map.152 = f32[992,128]{1,0:T(8,128)} custom-call(f32[128,128]{1,0:T(8,128)S(1)} %bitcast.22, s32[16,128]{1,0:T(8,128)S(1)} %copy-done.5, f32[64,128]{1,0:T(8,128)S(1)} %get-tuple-element.32.sea_first, f32[992,128]{1,0:T(8,128)S(1)} %get-tuple-element.33.before), custom_call_target="tpu_custom_call" | custom-call | bytes 2097152 | tf_op jit(solution)/shard_map/pallas_call | solution.py:26
  (6 shorter events, 0.0 us)
Async XLA Ops:
  0.6 6.9 %copy-start.5 = (s32[16,128]{1,0:T(8,128)S(1)}, s32[16,128]{1,0:T(8,128)}, u32[]{:S(2)}) copy-start(s32[16,128]{1,0:T(8,128)} %wet.7) | copy-start | bytes 24580
  0.6 6.9 %copy-start = (f32[72,32,128]{2,1,0:T(8,128)S(1)}, f32[72,32,128]{2,1,0:T(8,128)}, u32[]{:S(2)}) copy-start(f32[72,32,128]{2,1,0:T(8,128)} %sky.1) | copy-start | bytes 3538948
  0.7 6.9 %copy-start.2 = (f32[62,16,128]{2,1,0:T(8,128)S(1)}, f32[62,16,128]{2,1,0:T(8,128)}, u32[]{:S(2)}) copy-start(f32[62,16,128]{2,1,0:T(8,128)} %param.23) | copy-start | bytes 1523716
  0.7 6.9 %copy-start.1 = (f32[62,16,128]{2,1,0:T(8,128)S(1)}, f32[62,16,128]{2,1,0:T(8,128)}, u32[]{:S(2)}) copy-start(f32[62,16,128]{2,1,0:T(8,128)} %param.22) | copy-start | bytes 1523716
  0.7 6.9 %copy-start.11 = (f32[62,62]{1,0:T(8,128)S(1)}, f32[62,62]{1,0:T(8,128)}, u32[]{:S(2)}) copy-start(f32[62,62]{1,0:T(8,128)} %sea_mix.1) | copy-start | bytes 46132
  0.7 6.9 %copy-start.10 = (f32[72,72]{1,0:T(8,128)S(1)}, f32[72,72]{1,0:T(8,128)}, u32[]{:S(2)}) copy-start(f32[72,72]{1,0:T(8,128)} %vmix.1) | copy-start | bytes 62212
  0.7 6.9 %copy-start.12 = (f32[72]{0:T(128)S(1)}, f32[72]{0:T(128)}, u32[]{:S(2)}) copy-start(f32[72]{0:T(128)} %param.15) | copy-start | bytes 868
  3.2 11.4 %collective-permute-start = (f32[456,128]{1,0:T(8,128)}, f32[456,128]{1,0:T(8,128)S(1)}, u32[]{:S(2)}, u32[]{:S(2)}) collective-permute-start(f32[456,128]{1,0:T(8,128)} %get-tuple-element.22), channel_id=1, source_target_pairs={{1,0},{2,1},{3,2},{4,3},{5,4},{6,5},{7,6},{8,7},{9,8},{10,9},{11,1... | collective-permute-start | bytes 700424 | tf_op jit(solution)/shard_map/ppermute | solution.py:441
  4.5 10.1 %collective-permute-start.1 = (f32[456,128]{1,0:T(8,128)}, f32[456,128]{1,0:T(8,128)S(1)}, u32[]{:S(2)}, u32[]{:S(2)}) collective-permute-start(f32[456,128]{1,0:T(8,128)} %get-tuple-element.23), channel_id=1, source_target_pairs={{0,1},{1,2},{2,3},{3,4},{4,5},{5,6},{6,7},{7,8},{8,9},{9,10},{10,1... | collective-permute-start | bytes 700424 | tf_op jit(solution)/shard_map/ppermute | solution.py:440
  7.6 7.0 %copy-start.3 = (f32[4,32,128]{2,1,0:T(8,128)S(1)}, f32[4,32,128]{2,1,0:T(8,128)}, u32[]{:S(2)}) copy-start(f32[4,32,128]{2,1,0:T(8,128)} %forcing.1) | copy-start | bytes 196612
  7.6 7.0 %copy-start.4 = (bf16[4,128,128]{2,1,0:T(8,128)(2,1)S(1)}, bf16[4,128,128]{2,1,0:T(8,128)(2,1)}, u32[]{:S(2)}) copy-start(bf16[4,128,128]{2,1,0:T(8,128)(2,1)} %param.19) | copy-start | bytes 393220
  7.6 7.0 %copy-start.6 = (f32[32,128]{1,0:T(8,128)S(1)}, f32[32,128]{1,0:T(8,128)}, u32[]{:S(2)}) copy-start(f32[32,128]{1,0:T(8,128)} %surface.3) | copy-start | bytes 49156
  7.6 7.0 %copy-start.7 = (f32[32,128]{1,0:T(8,128)S(1)}, f32[32,128]{1,0:T(8,128)}, u32[]{:S(2)}) copy-start(f32[32,128]{1,0:T(8,128)} %rate.3) | copy-start | bytes 49156
  7.7 7.0 %copy-start.8 = (s32[32,4]{0,1:T(4,128)S(1)}, s32[32,4]{0,1:T(4,128)}, u32[]{:S(2)}) copy-start(s32[32,4]{0,1:T(4,128)} %param.20) | copy-start | bytes 1540
  7.7 7.0 %copy-start.9 = (s32[32,4]{0,1:T(4,128)S(1)}, s32[32,4]{0,1:T(4,128)}, u32[]{:S(2)}) copy-start(s32[32,4]{0,1:T(4,128)} %param.21) | copy-start | bytes 1540
  16.0 14.4 %all-to-all-start = ((f32[8,16,128]{2,1,0:T(8,128)}), f32[8,16,128]{2,1,0:T(8,128)S(1)}, u32[]{:S(2)}, u32[]{:S(2)}) async-start(f32[8,16,128]{2,1,0:T(8,128)} %bitcast.11), calls=%async_computation | async-start | bytes 131072 | tf_op jit(solution)/shard_map/all_to_all | solution.py:474

commit v8 on v7

--- a/solution.py
+++ b/solution.py
@@ -11,10 +11,10 @@
 ocean_diffusion = 0.2
 HALO = 4
 FULL = 60
-ROOM = 20
 EXACT = lax.Precision.HIGHEST
 VMEM = pl.BlockSpec(memory_space=pltpu.VMEM)
 HBM = pl.BlockSpec(memory_space=pltpu.HBM)
+SMEM = pl.BlockSpec(memory_space=pltpu.SMEM)
 f32, bf16 = jnp.float32, jnp.bfloat16
 
 
@@ -39,7 +39,7 @@
 
 
 def pack_kernel(
-    sizes, sky, forcing, surface, rate, warmth, brine, wet, up, down,
+    sizes, core, sky, forcing, surface, rate, warmth, brine, wet, inner, outer,
     ends, force, sea, flat, marks, done
 ):
     levels, rows, steps, sea_levels, sea_rows, stride, sea_stride = sizes
@@ -56,19 +56,21 @@
         move.start()
     for move in moves:
         move.wait()
-    m = marks[...].astype(f32)
-    for which, out, first, sea_row in ((0, up, 0, 0), (1, down, rows - HALO, sea_rows - 1)):
-        end = ends.at[which].reshape(levels * 8, width)
+    end = ends.reshape(2 * levels * 8, width)
+    for which, out in enumerate((inner, outer)):
+        last = jnp.where(core[0] == 0, 1 - which, which)
+        sea_row = last * (sea_rows - 1)
         for j in range(HALO):
-            row = first + j
-            out[j * stride : j * stride + levels, :] = end[pl.ds(row - which * low, levels, stride=8), :]
+            row = last * (rows - HALO) + j
+            first = last * (levels * 8 + 8 - HALO) + j
+            out[j * stride : j * stride + levels, :] = end[pl.ds(first, levels, stride=8), :]
             base = j * stride + levels
-            tail = [force[s, row : row + 1, :] for s in range(steps)]
-            tail += [flat[0, row : row + 1, :], flat[1, row : row + 1, :], jnp.ones((1, width), f32)]
+            tail = [force[s, pl.ds(row, 1), :] for s in range(steps)]
+            tail += [flat[0, pl.ds(row, 1), :], flat[1, pl.ds(row, 1), :], jnp.ones((1, width), f32)]
             tail += [jnp.zeros((stride - levels - len(tail), width), f32)]
             out[base : (j + 1) * stride, :] = jnp.concatenate(tail, 0)
         base = HALO * stride
-        edge = m[sea_row : sea_row + 1]
+        edge = marks[pl.ds(sea_row, 1), :].astype(f32)
         for f in range(2):
             out[base : base + sea_levels, :] = sea[f, pl.ds(sea_row, sea_levels, stride=sea_rows), :] * edge
             base += sea_stride
@@ -108,8 +110,8 @@
 
 def local_kernel(
     sizes, last_place, place, vmix, curve, sea_mix, sky, warmth, brine, wet,
-    rows_of_mix, source_rows, own, weights, source_weights, sea_weights, sea_first, sea_ends, store,
-    middle, warm_out, brine_out, spread, sea_spread, done,
+    rows_of_mix, source_rows, own, weights, source_weights, sea_weights, sea_first, sea_ends,
+    middle, warm_out, brine_out, spread, sea_spread,
 ):
     levels, rows, steps, sea_levels, sea_rows, stride, sea_stride = sizes
     width = sky.shape[1]
@@ -193,12 +195,6 @@
             if r in (0, sea_rows - 1):
                 at = (2 * f + (r > 0)) * sea_stride
                 sea_ends[at : at + sea_levels, :] = old
-    area = sea_levels * sea_rows
-    leave = []
-    for f, out in enumerate((warm_out, brine_out)):
-        part = store.at[pl.ds(rows * levels + f * area, area)]
-        leave.append(pltpu.make_async_copy(out, part, done.at[rows // 8 + f]))
-        leave[-1].start()
 
     before = jnp.where(place[0] > 0, 1.0, 0.0)
     behind = jnp.where(place[0] < last_place, 1.0, 0.0)
@@ -230,12 +226,6 @@
         y = product(w, x)
         for i in range(2):
             middle[(r + i) * levels : (r + i + 1) * levels, :] = y[:levels, i * width : (i + 1) * width]
-        if (r + 2) % 8 == 0:
-            part = pl.ds((r - 6) * levels, 8 * levels)
-            leave.append(pltpu.make_async_copy(middle.at[part], store.at[part], done.at[r // 8]))
-            leave[-1].start()
-    for move in leave:
-        move.wait()
 
 
 def cross(x):
@@ -250,11 +240,14 @@
 
 
 def flux_kernel(
-    sizes, sky, forcing, surface, rate, rows_of_mix, source_rows, own, owners, locals_, shares, below, above,
-    sent, fluxes, halo
+    sizes, core, tile, sky, forcing, surface, rate, rows_of_mix, source_rows, own, owners, locals_, shares, inner, outer,
+    keep, send, fluxes, above, below, halo
 ):
     levels, rows, steps, sea_levels, sea_rows, stride, sea_stride = sizes
     width = sky.shape[1]
+    one, two = inner[...], outer[...]
+    above[...] = jnp.where(core[0] == 0, two, one)
+    below[...] = jnp.where(core[0] == 0, one, two)
     halo[: HALO * stride, :] = below[: HALO * stride, :]
     halo[HALO * stride :, :] = above[: HALO * stride, :]
 
@@ -292,7 +285,7 @@
         total = total + flux[s][:rows]
     mean = (total / steps).astype(bf16)
     topk = owners.shape[0]
-    target = owners[...] * sea_rows + locals_[...]
+    target = (owners[...] ^ tile[0]) * sea_rows + locals_[...]
     target = jnp.concatenate([target[k : k + 1, :] for k in range(topk)], 1)
     rowed = jnp.concatenate(
         [jnp.dot(mean, shares[k * width : (k + 1) * width, :], preferred_element_type=f32) for k in range(topk)], 0
@@ -301,29 +294,23 @@
     left = rowed - first.astype(f32)
     second = left.astype(bf16)
     third = (left - second.astype(f32)).astype(bf16)
-    hot = lax.broadcasted_iota(jnp.int32, (sent.shape[0], topk * rows), 0) == target
+    half = keep.shape[0]
+    hot = lax.broadcasted_iota(jnp.int32, (2 * half, topk * rows), 0) == target
     hot = jnp.where(hot, 1.0, 0.0).astype(bf16)
-    sent[...] = jnp.dot(
+    sums = jnp.dot(
         jnp.concatenate([hot, hot, hot], 1), jnp.concatenate([first, second, third], 0), preferred_element_type=f32
     )
+    keep[...] = sums[:half]
+    send[...] = sums[half:]
 
 
 def rest_kernel(
-    sizes, fluxes, weights, source_weights, sea_weights, sea_ends, wet, below, above, store,
-    out, brine_out, warm_out, salt_held, middle, spread, sources, result, done
+    sizes, fluxes, weights, source_weights, sea_weights, sea_ends, wet, below, above, middle, warm, salt,
+    out, brine_out, warm_out, salt_held, spread, sources, result, done
 ):
     levels, rows, steps, sea_levels, sea_rows, stride, sea_stride = sizes
     width = above.shape[1]
     depth = up_to(levels + 2 * steps, 16)
-    area = sea_levels * sea_rows
-    fetches = [
-        pltpu.make_async_copy(store.at[pl.ds(first, to.shape[0])], to, done.at[i])
-        for i, (first, to) in enumerate(
-            ((rows * levels, warm_out), (rows * levels + area, salt_held), (0, middle))
-        )
-    ]
-    for fetch in fetches:
-        fetch.start()
     flag = levels + steps + 2
     inside_above, inside_below = above[flag : flag + 1, :], below[flag : flag + 1, :]
 
@@ -352,8 +339,8 @@
         for i, value in enumerate(top + low):
             spread[pl.ds(pl.multiple_of(i * depth + c * 8, 8), 8), :] = value
 
-    for fetch in fetches[:2]:
-        fetch.wait()
+    warm_out[...] = warm[...]
+    salt_held[...] = salt[...]
     m = wet[...].astype(f32)
     base = HALO * stride
     w = sea_weights[:, : 3 * sea_stride]
@@ -371,10 +358,9 @@
         for f, to in enumerate((warm_out, salt_held)):
             rows_at = pl.ds(r, sea_levels, stride=sea_rows)
             to[rows_at, :] = to[rows_at, :] + mark * y[:sea_levels, f * width : (f + 1) * width]
-    leave = [pltpu.make_async_copy(salt_held, brine_out, done.at[3])]
+    leave = [pltpu.make_async_copy(salt_held, brine_out, done.at[0])]
     leave[0].start()
 
-    fetches[2].wait()
     w = weights[:, : 3 * depth]
     v = source_weights[:, :48]
     for g in range(rows // 8):
@@ -396,17 +382,15 @@
                 to[pl.ds((r + q) % 8, levels, stride=8), :] = (
                     middle[(r + q) * levels : (r + q + 1) * levels, :] + y[:levels, q * width : (q + 1) * width]
                 )
-        leave.append(pltpu.make_async_copy(result.at[g], out.at[:, g], done.at[4 + g]))
+        leave.append(pltpu.make_async_copy(result.at[g], out.at[:, g], done.at[1 + g]))
         leave[-1].start()
     for move in leave:
         move.wait()
 
 
-def heat_kernel(sizes, got, wet, sea_first, before, after):
+def heat_kernel(sizes, kept, got, wet, sea_first, before, after):
     levels, rows, steps, sea_levels, sea_rows, stride, sea_stride = sizes
-    heat = got[:sea_rows, :]
-    for t in range(1, got.shape[0] // sea_rows):
-        heat = heat + got[t * sea_rows : (t + 1) * sea_rows, :]
+    heat = kept[...] + got[...]
     heat = wet[...].astype(f32) * heat
     for l in range(sea_levels):
         after[l * sea_rows : (l + 1) * sea_rows, :] = (
@@ -427,65 +411,73 @@
     flat = lambda n, kind=f32: jax.ShapeDtypeStruct((n, width), kind)
 
     space = lambda *shape: pltpu.VMEM(shape, f32)
+    space = lambda *shape: pltpu.VMEM(shape, f32)
     length = HALO * stride + 2 * sea_stride + 8
-    up, down = call(
+    ring = ("tile", "comp")
+    tiles, count = lax.axis_size("tile"), lax.axis_size(ring)
+    at = lax.axis_index(ring).astype(jnp.int32)[None]
+    core = lax.axis_index("comp").astype(jnp.int32)[None]
+    tile = lax.axis_index("tile").astype(jnp.int32)[None]
+    inner, outer = call(
         functools.partial(pack_kernel, sizes), [flat(length)] * 2,
-        sky, forcing, surface, rate, warmth2, brine2, wet, moved=4 << 20, in_specs=[HBM] * 7, grant=FULL,
+        core, sky, forcing, surface, rate, warmth2, brine2, wet, moved=4 << 20, in_specs=[SMEM] + [HBM] * 7,
         scratch=[
             space(2, levels, 8, width), space(steps, rows, width), space(2, sea_levels * sea_rows, width),
             space(2, rows, width), pltpu.VMEM(wet.shape, wet.dtype), pltpu.SemaphoreType.DMA((8,)),
         ],
-    )
-    count = lax.axis_size(("tile", "comp"))
-    above = lax.ppermute(down, ("tile", "comp"), [(i, i + 1) for i in range(count - 1)])
-    below = lax.ppermute(up, ("tile", "comp"), [(i + 1, i) for i in range(count - 1)])
+        grant=FULL,
+    )
+    swap = lambda first: [(i + a, i + 1 - a) for i in range(first, count - 1, 2) for a in range(2)]
+    inner = lax.ppermute(inner, ring, swap(0))
+    outer = lax.ppermute(outer, ring, swap(1))
 
     depth = up_to(levels + 2 * steps, 16)
     mix_rows = up_to(levels, 16)
-    sea_flat = flat(sea_levels * sea_rows)
-    at = lax.axis_index(("tile", "comp")).astype(jnp.int32)[None]
     area = sea_levels * sea_rows
-    large = max(rows * levels + 2 * area, ROOM * 2**20 // (4 * width))
-    (rows_of_mix, source_rows, own, weights, source_weights, sea_weights, sea_first, sea_ends, store) = call(
+    (
+        rows_of_mix, source_rows, own, weights, source_weights, sea_weights, sea_first, sea_ends, middle, warm, salt
+    ) = call(
         functools.partial(local_kernel, sizes, count - 1),
         [
             flat((steps - 1) * levels), flat(8), flat((steps - 1) * rows),
             jax.ShapeDtypeStruct((mix_rows, 2 * width), bf16), flat(mix_rows, bf16),
             jax.ShapeDtypeStruct((sea_stride, 2 * width), bf16), flat(sea_stride), flat(4 * sea_stride),
-            flat(large),
+            flat(rows * levels), flat(area), flat(area),
         ],
-        at, vmix, curve[None], sea_mix, sky2, warmth2, brine2, wet,
-        in_specs=[pl.BlockSpec(memory_space=pltpu.SMEM)] + [VMEM] * 7, out_specs=[VMEM] * 8 + [HBM],
-        scratch=[
-            space(rows * levels, width), space(area, width), space(area, width),
-            space(rows * depth, width), space(2, sea_rows * sea_stride, width),
-            pltpu.SemaphoreType.DMA((rows // 8 + 2,)),
-        ],
-        flops=4 << 30, moved=8 << 20, grant=48,
-    )
-
-    tiles = lax.axis_size("tile")
-    sent, fluxes = call(
-        functools.partial(flux_kernel, sizes), [flat(tiles * sea_rows), flat(2 * steps * (rows + 2 * HALO))],
-        sky[-1], forcing2, surface, rate, rows_of_mix, source_rows, own, owners.T, locals_.T,
-        shares.reshape(-1, width), below, above,
-        scratch=[space(2 * HALO * stride, width)], moved=2 << 20,
-    )
-    got = lax.all_to_all(sent.reshape(tiles, sea_rows, width), "tile", split_axis=0, concat_axis=0, tiled=True)
-    got = got.reshape(-1, width)
+        at, vmix, curve[None], sea_mix, sky2, warmth2, brine2, wet, in_specs=[SMEM] + [VMEM] * 7,
+        scratch=[space(rows * depth, width), space(2, sea_rows * sea_stride, width)],
+        flops=4 << 30, moved=8 << 20,
+    )
+
+    half = tiles // 2 * sea_rows
+    keep, send, fluxes, above, below = call(
+        functools.partial(flux_kernel, sizes),
+        [flat(half), flat(half), flat(2 * steps * (rows + 2 * HALO)), flat(length), flat(length)],
+        core, tile, sky[-1], forcing2, surface, rate, rows_of_mix, source_rows, own, owners.T, locals_.T,
+        shares.reshape(-1, width), inner, outer,
+        in_specs=[SMEM] * 2 + [VMEM] * 12, scratch=[space(2 * HALO * stride, width)], moved=2 << 20,
+    )
+    bit = tiles // 2
+    while True:
+        got = lax.ppermute(send, "tile", [(i, i ^ bit) for i in range(tiles)])
+        if bit == 1:
+            break
+        bit //= 2
+        both = keep + got
+        keep, send = both[: bit * sea_rows], both[bit * sea_rows :]
 
     sky_out, salt, warm = call(
         functools.partial(rest_kernel, sizes),
-        [jax.ShapeDtypeStruct((levels, rows // 8, 8, width), f32), sea_flat, sea_flat],
-        fluxes, weights, source_weights, sea_weights, sea_ends, wet, below, above, store,
-        in_specs=[VMEM] * 8 + [HBM], out_specs=[HBM, HBM, VMEM],
+        [jax.ShapeDtypeStruct((levels, rows // 8, 8, width), f32), flat(area), flat(area)],
+        fluxes, weights, source_weights, sea_weights, sea_ends, wet, below, above, middle, warm, salt,
+        out_specs=[HBM, HBM, VMEM],
         scratch=[
-            space(area, width), space(rows * levels, width), space(2 * HALO * depth, width), space(rows * 16, width),
-            space(rows // 8, levels, 8, width), pltpu.SemaphoreType.DMA((4 + rows // 8,)),
+            space(area, width), space(2 * HALO * depth, width), space(rows * 16, width),
+            space(rows // 8, levels, 8, width), pltpu.SemaphoreType.DMA((1 + rows // 8,)),
         ],
-        flops=2 << 30, moved=8 << 20, grant=48,
-    )
-    warm = call(functools.partial(heat_kernel, sizes), sea_flat, got, wet, sea_first, warm, moved=2 << 20)
+        flops=2 << 30, moved=8 << 20,
+    )
+    warm = call(functools.partial(heat_kernel, sizes), flat(area), keep, got, wet, sea_first, warm, moved=2 << 20)
     return sky_out.reshape(sky.shape), warm.reshape(warmth.shape), salt.reshape(brine.shape)
 
 

time: 31.5 us -> 30.6 us (0.971)
  Pallas kernels: 15.3 us -> 13.7 us
  starting transfers between devices: 11.6 us -> 12.1 us
    ppermute x2 -> x5, starting transfers between devices: 4.34 us -> 12.1 us  [the longest x3 10.9 us: body(): got = lax.ppermute(send, 'tile', [(i, i ^ bit) for i in range(tiles)])]
    all_to_all x1 -> x0, starting transfers between devices: 7.25 us -> none  [body(): lax.all_to_all(sent.reshape(tiles, sea_rows, width), 'tile', split_axis=0...]
    ppermute x2 -> x5, waiting for transfers between devices: 0.01 us -> 3.66 us  [the longest x3 3.65 us: body(): got = lax.ppermute(send, 'tile', [(i, i ^ bit) for i in range(tiles)])]
    all_to_all x1 -> x0, waiting for transfers between devices: 3.36 us -> none  [body(): lax.all_to_all(sent.reshape(tiles, sea_rows, width), 'tile', split_axis=0...]
    pallas_call x5, Pallas kernels: 15.3 us -> 13.7 us  [call(): pl.pallas_call(kernel, out_shape=out_shape, in_specs=in_specs or [VMEM] *...]
  transfers between devices with their start and end apart: 3 -> 5, of which waited for: 1 -> 2; matrix products, arithmetic and copies ran while one was open for 0% -> 0% of each run, Pallas kernels for 34% -> 32%
where the time goes in v8:
time: 30.6 us; the launch traced here: 30.5 us
  Pallas kernels  13.7 us (45%)
  starting transfers between devices  12.1 us (40%)
  waiting for transfers between devices  3.66 us (12%)
  between operations  0.92 us (3%)
    pallas_call x5, Pallas kernels, call(): pl.pallas_call(kernel, out_shape=out_shape, in_specs=in_specs or [VMEM] *...  13.7 us
    ppermute x3, starting transfers between devices, body(): got = lax.ppermute(send, 'tile', [(i, i ^ bit) for i in range(tiles)])  10.9 us
    ppermute x3, waiting for transfers between devices, body(): got = lax.ppermute(send, 'tile', [(i, i ^ bit) for i in range(tiles)])  3.65 us
    ppermute x1, starting transfers between devices, body(): outer = lax.ppermute(outer, ring, swap(1))  0.66 us
  transfers between devices with their start and end apart: 5, of which 2 were waited for; matrix products, arithmetic and copies ran while one was open for 0% of the time, Pallas kernels for 32%

profile of v8, /device:TPU:0, one launch (start us, length us, event | category | flops | bytes accessed | tf_op | source)
XLA Modules:
  0.0 30.5 jit_solution(1859070247382237282)
XLA Ops:
  0.6 0.0 copy-start.1
  0.6 0.0 copy-start.2
  0.7 0.0 copy-start
  0.7 0.0 copy-start.7
  0.7 0.0 copy-start.12
  0.7 0.0 copy-start.10
  0.7 0.0 copy-start.11
  0.7 2.5 %shard_map.149 = (f32[456,128]{1,0:T(8,128)}, f32[456,128]{1,0:T(8,128)}) custom-call(s32[1]{0:T(128)} %bitcast.core, f32[72,32,128]{2,1,0:T(8,128)} %sky.1, f32[4,32,128]{2,1,0:T(8,128)} %forcing.1, f32[32,128]{1,0:T(8,128)} %surface.3, f32[32,128]{1,0:T(8,128)} %rate.3, f32[992,128]{1,0:T(8,128)} %bitcast.17, f32[992,128]{1,0:T(8,128)} %bitcast.19, ...), custom_call_target="tpu_custom_call" | custom-call | bytes 4194304 | tf_op jit(solution)/shard_map/pallas_call | solution.py:26
  3.2 0.5 %collective-permute-start = (f32[456,128]{1,0:T(8,128)}, f32[456,128]{1,0:T(8,128)S(1)}, u32[]{:S(2)}, u32[]{:S(2)}) collective-permute-start(f32[456,128]{1,0:T(8,128)} %get-tuple-element.27), channel_id=1, source_target_pairs={{0,1},{1,0},{2,3},{3,2},{4,5},{5,4},{6,7},{7,6},{8,9},{9,8},{10,11... | collective-permute-start | bytes 700424 | tf_op jit(solution)/shard_map/ppermute | solution.py:431
  3.7 0.7 %collective-permute-start.1 = (f32[456,128]{1,0:T(8,128)}, f32[456,128]{1,0:T(8,128)S(1)}, u32[]{:S(2)}, u32[]{:S(2)}) collective-permute-start(f32[456,128]{1,0:T(8,128)} %get-tuple-element.28), channel_id=1, source_target_pairs={{1,2},{2,1},{3,4},{4,3},{5,6},{6,5},{7,8},{8,7},{9,10},{10,9},{11,... | collective-permute-start | bytes 700424 | tf_op jit(solution)/shard_map/ppermute | solution.py:432
  4.4 0.0 copy-done.1
  4.4 0.0 copy-done.2
  4.4 0.0 copy-done
  4.5 0.0 copy-done.7
  4.5 0.0 copy-start.3
  4.5 0.0 copy-start.4
  4.5 0.0 copy-start.5
  4.5 0.0 copy-start.6
  4.5 0.0 copy-start.8
  4.6 0.0 copy-start.9
  4.6 6.0 %shard_map.148 = (f32[216,128]{1,0:T(8,128)S(1)}, f32[8,128]{1,0:T(8,128)S(1)}, f32[96,128]{1,0:T(8,128)S(1)}, bf16[80,256]{1,0:T(8,128)(2,1)S(1)}, bf16[80,128]...) custom-call(s32[1]{0:T(128)} %bitcast.4.place, ...), custom_call_target="tpu_custom_call" | custom-call | flops 4294967296 | bytes 8388608 | tf_op jit(solution)/shard_map/pallas_call | solution.py:26
  10.6 0.0 collective-permute-done.inner
  10.6 0.0 collective-permute-done.1.outer
  10.6 0.7 %shard_map.150 = (f32[64,128]{1,0:T(8,128)S(1)}, f32[64,128]{1,0:T(8,128)S(1)}, f32[320,128]{1,0:T(8,128)S(1)}, f32[456,128]{1,0:T(8,128)S(1)}, f32[456,128]{1,0:T(8,128)S(1)}) custom-call(s32[1]{0:T(128)} %bitcast.core, s32[1]{0:T(128)} %bitcast.1.tile, f32[32,128]{1,0:T(8,128)S(1)} %slice_bitcast_fusion.sky, f32[128,128]{1,0:T(8,128)S(1)} %bitcast.21, ...), custom_call_target="tpu_custom_call" | custom-call | bytes 2097152 | tf_op jit(solution)/shard_map/pallas_call | solution.py:26
  11.3 6.4 %collective-permute-start.2 = (f32[64,128]{1,0:T(8,128)S(1)}, f32[64,128]{1,0:T(8,128)S(1)}, u32[]{:S(2)}, u32[]{:S(2)}) collective-permute-start(f32[64,128]{1,0:T(8,128)S(1)} %get-tuple-element.41), channel_id=1, source_target_pairs={{0,8},{2,10},{4,12},{6,14},{8,0},{10,2},{12,4},{14,6},{1,9},{3,11}... | collective-permute-start | bytes 98312 | tf_op jit(solution)/shard_map/ppermute | solution.py:462
  17.7 1.9 %collective-permute-done.2 = f32[64,128]{1,0:T(8,128)S(1)} collective-permute-done((f32[64,128]{1,0:T(8,128)S(1)}, f32[64,128]{1,0:T(8,128)S(1)}, u32[]{:S(2)}, u32[]{:S(2)}) %collective-permute-start.2) | collective-permute-done | bytes 32800 | tf_op jit(solution)/shard_map/ppermute | solution.py:462
  19.7 2.2 %collective-permute-start.3 = (f32[32,128]{1,0:T(8,128)S(1)}, f32[32,128]{1,0:T(8,128)S(1)}, u32[]{:S(2)}, u32[]{:S(2)}) collective-permute-start(f32[32,128]{1,0:T(8,128)S(1)} %slice.21), channel_id=1, source_target_pairs={{0,4},{2,6},{4,0},{6,2},{8,12},{10,14},{12,8},{14,10},{1,5},{3,7},... | collective-permute-start | bytes 49160 | tf_op jit(solution)/shard_map/ppermute | solution.py:462
  21.9 1.7 %collective-permute-done.3 = f32[32,128]{1,0:T(8,128)S(1)} collective-permute-done((f32[32,128]{1,0:T(8,128)S(1)}, f32[32,128]{1,0:T(8,128)S(1)}, u32[]{:S(2)}, u32[]{:S(2)}) %collective-permute-start.3) | collective-permute-done | bytes 16416 | tf_op jit(solution)/shard_map/ppermute | solution.py:462
  23.6 2.3 %collective-permute-start.4 = (f32[16,128]{1,0:T(8,128)S(1)}, f32[16,128]{1,0:T(8,128)S(1)}, u32[]{:S(2)}, u32[]{:S(2)}) collective-permute-start(f32[16,128]{1,0:T(8,128)S(1)} %get-tuple-element.45), channel_id=1, source_target_pairs={{0,2},{2,0},{4,6},{6,4},{8,10},{10,8},{12,14},{14,12},{1,3},{3,1},... | collective-permute-start | bytes 24584 | tf_op jit(solution)/shard_map/ppermute | solution.py:462
  25.9 3.7 %shard_map.151 = (f32[72,4,8,128]{3,2,1,0:T(8,128)}, f32[992,128]{1,0:T(8,128)}, f32[992,128]{1,0:T(8,128)S(1)}) custom-call(f32[320,128]{1,0:T(8,128)S(1)} %get-tuple-element.29.fluxes, bf16[80,256]{1,0:T(8,128)(2,1)S(1)} %get-tuple-element.30.weights, bf16[80,128]{1,0:T(8,128)(2,1)S(1)} %get-tuple-element.31.source_weights, ...), custom_call_target="tpu_custom_call" | custom-call | flops 2147483648 | bytes 8388608 | tf_op jit(solution)/shard_map/pallas_call | solution.py:26
  29.6 0.0 collective-permute-done.4.got
  29.6 0.8 %shard_map.152 = f32[992,128]{1,0:T(8,128)} custom-call(f32[16,128]{1,0:T(8,128)S(1)} %get-tuple-element.46.kept, f32[16,128]{1,0:T(8,128)S(1)} %collective-permute-done.4.got, s32[16,128]{1,0:T(8,128)S(1)} %copy-done.7, f32[64,128]{1,0:T(8,128)S(1)} %get-tuple-element.42.sea_first, f32[992,128]{1,0:T(8,128)S(1)} %get-tuple-element.43.before), custom_call_target="tpu_custom_call" | custom-call | bytes 2097152 | tf_op jit(solution)/shard_map/pallas_call | solution.py:26
  (14 shorter events, 0.0 us)
Async XLA Ops:
  0.6 3.8 %copy-start.1 = (f32[62,16,128]{2,1,0:T(8,128)S(1)}, f32[62,16,128]{2,1,0:T(8,128)}, u32[]{:S(2)}) copy-start(f32[62,16,128]{2,1,0:T(8,128)} %param.22) | copy-start | bytes 1523716
  0.6 3.8 %copy-start.2 = (f32[62,16,128]{2,1,0:T(8,128)S(1)}, f32[62,16,128]{2,1,0:T(8,128)}, u32[]{:S(2)}) copy-start(f32[62,16,128]{2,1,0:T(8,128)} %param.23) | copy-start | bytes 1523716
  0.7 3.8 %copy-start = (f32[72,32,128]{2,1,0:T(8,128)S(1)}, f32[72,32,128]{2,1,0:T(8,128)}, u32[]{:S(2)}) copy-start(f32[72,32,128]{2,1,0:T(8,128)} %sky.1) | copy-start | bytes 3538948
  0.7 3.8 %copy-start.7 = (s32[16,128]{1,0:T(8,128)S(1)}, s32[16,128]{1,0:T(8,128)}, u32[]{:S(2)}) copy-start(s32[16,128]{1,0:T(8,128)} %wet.7) | copy-start | bytes 24580
  0.7 3.8 %copy-start.12 = (f32[72]{0:T(128)S(1)}, f32[72]{0:T(128)}, u32[]{:S(2)}) copy-start(f32[72]{0:T(128)} %param.15) | copy-start | bytes 868
  0.7 3.8 %copy-start.10 = (f32[72,72]{1,0:T(8,128)S(1)}, f32[72,72]{1,0:T(8,128)}, u32[]{:S(2)}) copy-start(f32[72,72]{1,0:T(8,128)} %vmix.1) | copy-start | bytes 62212
  0.7 3.8 %copy-start.11 = (f32[62,62]{1,0:T(8,128)S(1)}, f32[62,62]{1,0:T(8,128)}, u32[]{:S(2)}) copy-start(f32[62,62]{1,0:T(8,128)} %sea_mix.1) | copy-start | bytes 46132
  3.2 7.3 %collective-permute-start = (f32[456,128]{1,0:T(8,128)}, f32[456,128]{1,0:T(8,128)S(1)}, u32[]{:S(2)}, u32[]{:S(2)}) collective-permute-start(f32[456,128]{1,0:T(8,128)} %get-tuple-element.27), channel_id=1, source_target_pairs={{0,1},{1,0},{2,3},{3,2},{4,5},{5,4},{6,7},{7,6},{8,9},{9,8},{10,11... | collective-permute-start | bytes 700424 | tf_op jit(solution)/shard_map/ppermute | solution.py:431
  3.7 6.8 %collective-permute-start.1 = (f32[456,128]{1,0:T(8,128)}, f32[456,128]{1,0:T(8,128)S(1)}, u32[]{:S(2)}, u32[]{:S(2)}) collective-permute-start(f32[456,128]{1,0:T(8,128)} %get-tuple-element.28), channel_id=1, source_target_pairs={{1,2},{2,1},{3,4},{4,3},{5,6},{6,5},{7,8},{8,7},{9,10},{10,9},{11,... | collective-permute-start | bytes 700424 | tf_op jit(solution)/shard_map/ppermute | solution.py:432
  4.5 6.1 %copy-start.3 = (f32[4,32,128]{2,1,0:T(8,128)S(1)}, f32[4,32,128]{2,1,0:T(8,128)}, u32[]{:S(2)}) copy-start(f32[4,32,128]{2,1,0:T(8,128)} %forcing.1) | copy-start | bytes 196612
  4.5 6.1 %copy-start.4 = (bf16[4,128,128]{2,1,0:T(8,128)(2,1)S(1)}, bf16[4,128,128]{2,1,0:T(8,128)(2,1)}, u32[]{:S(2)}) copy-start(bf16[4,128,128]{2,1,0:T(8,128)(2,1)} %param.19) | copy-start | bytes 393220
  4.5 6.1 %copy-start.5 = (f32[32,128]{1,0:T(8,128)S(1)}, f32[32,128]{1,0:T(8,128)}, u32[]{:S(2)}) copy-start(f32[32,128]{1,0:T(8,128)} %surface.3) | copy-start | bytes 49156
  4.5 6.1 %copy-start.6 = (f32[32,128]{1,0:T(8,128)S(1)}, f32[32,128]{1,0:T(8,128)}, u32[]{:S(2)}) copy-start(f32[32,128]{1,0:T(8,128)} %rate.3) | copy-start | bytes 49156
  4.5 6.1 %copy-start.8 = (s32[32,4]{0,1:T(4,128)S(1)}, s32[32,4]{0,1:T(4,128)}, u32[]{:S(2)}) copy-start(s32[32,4]{0,1:T(4,128)} %param.20) | copy-start | bytes 1540
  4.6 6.1 %copy-start.9 = (s32[32,4]{0,1:T(4,128)S(1)}, s32[32,4]{0,1:T(4,128)}, u32[]{:S(2)}) copy-start(s32[32,4]{0,1:T(4,128)} %param.21) | copy-start | bytes 1540
  11.3 8.3 %collective-permute-start.2 = (f32[64,128]{1,0:T(8,128)S(1)}, f32[64,128]{1,0:T(8,128)S(1)}, u32[]{:S(2)}, u32[]{:S(2)}) collective-permute-start(f32[64,128]{1,0:T(8,128)S(1)} %get-tuple-element.41), channel_id=1, source_target_pairs={{0,8},{2,10},{4,12},{6,14},{8,0},{10,2},{12,4},{14,6},{1,9},{3,11}... | collective-permute-start | bytes 98312 | tf_op jit(solution)/shard_map/ppermute | solution.py:462
  19.7 4.0 %collective-permute-start.3 = (f32[32,128]{1,0:T(8,128)S(1)}, f32[32,128]{1,0:T(8,128)S(1)}, u32[]{:S(2)}, u32[]{:S(2)}) collective-permute-start(f32[32,128]{1,0:T(8,128)S(1)} %slice.21), channel_id=1, source_target_pairs={{0,4},{2,6},{4,0},{6,2},{8,12},{10,14},{12,8},{14,10},{1,5},{3,7},... | collective-permute-start | bytes 49160 | tf_op jit(solution)/shard_map/ppermute | solution.py:462
  23.6 6.0 %collective-permute-start.4 = (f32[16,128]{1,0:T(8,128)S(1)}, f32[16,128]{1,0:T(8,128)S(1)}, u32[]{:S(2)}, u32[]{:S(2)}) collective-permute-start(f32[16,128]{1,0:T(8,128)S(1)} %get-tuple-element.45), channel_id=1, source_target_pairs={{0,2},{2,0},{4,6},{6,4},{8,10},{10,8},{12,14},{14,12},{1,3},{3,1},... | collective-permute-start | bytes 24584 | tf_op jit(solution)/shard_map/ppermute | solution.py:462

commit v9 on v8

v9 whole, which is shorter than its diff:
```python
import functools

import jax
import jax.numpy as jnp
from jax import lax
from jax.experimental import pallas as pl
from jax.experimental.pallas import tpu as pltpu
from jax.sharding import PartitionSpec as P

atm_diffusion = 0.2
ocean_diffusion = 0.2
HALO = 4
FULL = 60
FIELDS = 16
EXACT = lax.Precision.HIGHEST
VMEM = pl.BlockSpec(memory_space=pltpu.VMEM)
HBM = pl.BlockSpec(memory_space=pltpu.HBM)
SMEM = pl.BlockSpec(memory_space=pltpu.SMEM)
ANY = pl.BlockSpec(memory_space=pl.ANY)
f32, bf16 = jnp.float32, jnp.bfloat16


def up_to(n, m):
    return -(-n // m) * m


def call(kernel, out_shape, *args, scratch=(), in_specs=None, out_specs=None, flops=0, moved=0, grant=24):
    return pl.pallas_call(
        kernel,
        out_shape=out_shape,
        in_specs=in_specs or [VMEM] * len(args),
        out_specs=out_specs or jax.tree.map(lambda _: VMEM, out_shape),
        scratch_shapes=list(scratch),
        compiler_params=pltpu.CompilerParams(vmem_limit_bytes=grant * 2**20),
        cost_estimate=pl.CostEstimate(flops=flops, bytes_accessed=moved, transcendentals=0),
    )(*args)


def copies(pairs, done):
    return [pltpu.make_async_copy(src, dst, done.at[i]) for i, (src, dst) in enumerate(pairs)]


def side_of(core, which):
    return jnp.where(core[0] == 0, 1 - which, which)


def first_kernel(sizes, core, vmix_in, sky_in, forcing, surface, rate, inner, outer, rows_of_mix, own,
                 vmix, sky, force, flat, done):
    levels, rows, steps, sea_levels, sea_rows, stride, sea_stride = sizes
    width = sky.shape[1]
    moves = copies(
        [(vmix_in, vmix), (sky_in, sky), (forcing, force), (surface, flat.at[0]), (rate, flat.at[1])], done
    )
    for move in moves:
        move.start()
    moves[0].wait()
    last = (lax.broadcasted_iota(jnp.int32, (levels, width), 0) == levels - 1).astype(f32)
    for s in range(steps - 1):
        last = lax.dot_general(
            vmix[...], last, (((0,), (0,)), ((), ())), precision=EXACT, preferred_element_type=f32
        )
        rows_of_mix[s * levels : (s + 1) * levels, :] = last
    for move in moves[1:]:
        move.wait()
    own[:rows, :] = sky[(levels - 1) * rows :, :]
    sums = [jnp.zeros((rows, width), f32) for _ in range(steps - 1)]
    for l in range(levels):
        x = sky[l * rows : (l + 1) * rows, :]
        for s in range(steps - 1):
            sums[s] = sums[s] + rows_of_mix[s * levels + l : s * levels + l + 1, :] * x
    for s in range(steps - 1):
        own[(s + 1) * rows : (s + 2) * rows, :] = sums[s]
    for which, out in enumerate((inner, outer)):
        at = side_of(core, which) * (rows - HALO)
        for j in range(HALO):
            lines = [own[pl.ds(s * rows + at + j, 1), :] for s in range(steps)]
            lines += [force[s, pl.ds(at + j, 1), :] for s in range(steps)]
            lines += [flat[i, pl.ds(at + j, 1), :] for i in range(2)] + [jnp.ones((1, width), f32)]
            lines += [jnp.zeros((FIELDS - len(lines), width), f32)]
            out[j * FIELDS : (j + 1) * FIELDS, :] = jnp.concatenate(lines, 0)


def pack_kernel(sizes, core, sky, warmth, brine, wet, after, inner, outer):
    levels, rows, steps, sea_levels, sea_rows, stride, sea_stride = sizes
    width = sky.shape[1]
    for which, out in enumerate((inner, outer)):
        last = side_of(core, which)
        sea_row = last * (sea_rows - 1)
        for j in range(HALO):
            out[j * stride : j * stride + levels, :] = sky[pl.ds(last * (rows - HALO) + j, levels, stride=rows), :]
        base = HALO * stride
        edge = wet[pl.ds(sea_row, 1), :].astype(f32)
        for field in (warmth, brine):
            out[base : base + sea_levels, :] = field[pl.ds(sea_row, sea_levels, stride=sea_rows), :] * edge
            base += sea_stride
        out[base : base + 8, :] = jnp.concatenate([edge, jnp.zeros((7, width), f32)], 0)


def split(x):
    high = x.astype(bf16)
    return high, (x - high.astype(f32)).astype(bf16)


def three_terms(w, depth):
    high = w.astype(bf16).astype(f32)
    low = w - high
    return (high + pltpu.roll(high, depth, 1) + pltpu.roll(low, 2 * depth, 1)).astype(bf16)


def row_of(ref, first, count, step, size):
    x = ref[pl.ds(first, count, stride=step), :]
    if count < size:
        x = jnp.concatenate([x, jnp.zeros((size - count, x.shape[1]), f32)], 0)
    return x


def beside(x):
    return pltpu.roll(x, 1, 1) + pltpu.roll(x, x.shape[1] - 1, 1)


def stencil(x):
    return [x[i - 1] + x[i] + x[i + 1] + beside(x[i]) for i in range(1, len(x) - 1)]


def product(weights, x):
    high, low = split(x)
    return jnp.dot(weights, jnp.concatenate([high, low, high], 0), preferred_element_type=f32)


def local_kernel(
    sizes, vmix, curve, sea_mix, warmth, brine, wet,
    weights, sea_weights, sea_first, sea_ends, warm_out, brine_out, sea_spread,
):
    levels, rows, steps, sea_levels, sea_rows, stride, sea_stride = sizes
    width = warmth.shape[1]
    depth = up_to(levels + 2 * steps, 16)
    v = vmix[...]
    dot = functools.partial(jnp.dot, precision=EXACT, preferred_element_type=f32)
    powers = [v]
    for _ in range(steps - 1):
        powers.append(dot(v, powers[-1]))
    by_curve = jnp.broadcast_to(curve[...], (width, levels))
    of_curve = [
        lax.dot_general(p, by_curve, (((1,), (1,)), ((), ())), precision=EXACT, preferred_element_type=f32)
        for p in powers
    ]
    of_last = [jnp.broadcast_to(p[:, levels - 1 : levels], (levels, width)) for p in powers]
    lane = lax.broadcasted_iota(jnp.int32, (levels, width), 1)
    wide = jnp.concatenate(
        [powers[-1] * atm_diffusion**steps, jnp.zeros((levels, width - levels), f32)], 1
    )
    for j in range(steps):
        factor = atm_diffusion ** (steps - 1 - j)
        for at, value in ((j, of_curve[steps - 1 - j] * factor), (steps + j, of_last[steps - 1 - j] * -factor)):
            wide = jnp.where(lane == levels + at, value, wide)
    more = jnp.zeros((weights.shape[0] - levels, width), f32)
    wide = jnp.concatenate([wide, more], 0)
    wide = jnp.concatenate([wide, jnp.zeros_like(wide)], 1)
    weights[...] = three_terms(wide, depth)
    sea = sea_mix[...]
    sea = jnp.concatenate([sea, jnp.zeros((sea_levels, 2 * width - sea_levels), f32)], 1)
    sea = jnp.concatenate([sea, jnp.zeros((sea_stride - sea_levels, 2 * width), f32)], 0)
    sea_weights[...] = three_terms(sea, sea_stride)
    sea_first[...] = jnp.broadcast_to(sea[:, 0:1], sea_first.shape)
    m = wet[...].astype(f32)
    mark = [m[r : r + 1] for r in range(sea_rows)]
    edge = jnp.zeros((1, width), f32)

    def near(x):
        x = [jnp.zeros_like(x[0])] + x + [jnp.zeros_like(x[0])]
        return [x[i - 1] + x[i + 1] + beside(x[i]) for i in range(1, len(x) - 1)]

    around = (
        jnp.concatenate([edge, m[:-1]], 0) + jnp.concatenate([m[1:], edge], 0) + beside(m)
    ) * ocean_diffusion
    share = [around[r : r + 1] for r in range(sea_rows)]
    for f, field in enumerate((warmth, brine)):
        for c in range(sea_stride // 8):
            count = min(8, sea_levels - c * 8)
            x = [row_of(field, c * 8 * sea_rows + r, count, sea_rows, 8) for r in range(sea_rows)]
            y = near([mark[r] * x[r] for r in range(sea_rows)])
            for r in range(sea_rows):
                at = r * sea_stride + c * 8
                sea_spread[f, at : at + 8, :] = x[r] + mark[r] * (ocean_diffusion * y[r] - x[r] * share[r])
    w = sea_weights[:, : 3 * sea_stride]
    for r in range(sea_rows):
        x = jnp.concatenate([sea_spread[f, r * sea_stride : (r + 1) * sea_stride, :] for f in range(2)], 1)
        y = product(w, x)
        for f, (field, out) in enumerate(((warmth, warm_out), (brine, brine_out))):
            old = field[pl.ds(r, sea_levels, stride=sea_rows), :]
            new = y[:sea_levels, f * width : (f + 1) * width]
            out[pl.ds(r, sea_levels, stride=sea_rows), :] = mark[r] * new + (1.0 - mark[r]) * old
            if r in (0, sea_rows - 1):
                at = (2 * f + (r > 0)) * sea_stride
                sea_ends[at : at + sea_levels, :] = old


def inside_of(place, last_place):
    return jnp.where(place[0] > 0, 1.0, 0.0), jnp.where(place[0] < last_place, 1.0, 0.0)


def own_kernel(sizes, last_place, place, sky, after, spread):
    levels, rows, steps, sea_levels, sea_rows, stride, sea_stride = sizes
    before, behind = inside_of(place, last_place)


    @pl.loop(0, levels // 8)
    def _(c):
        x = [sky[pl.ds(c * 8 * rows + r, 8, stride=rows), :] for r in range(rows)]
        none = jnp.zeros_like(x[0])
        beyond = 0
        for n in range(steps):
            if beyond < steps - 1 - n:
                x = [x[0]] + stencil([none] + x + [none]) + [x[-1]]
                beyond += 1
            else:
                x = stencil(x)
                beyond -= 1
            for i in range(beyond):
                x[i] = x[i] * before
                x[-1 - i] = x[-1 - i] * behind
        for r in range(rows):
            spread[pl.ds(pl.multiple_of(r * levels + c * 8, 8), 8), :] = x[r]


def cross(x):
    n, w = x.shape
    return (
        x + pltpu.roll(x, 1, 0) + pltpu.roll(x, n - 1, 0) + pltpu.roll(x, 1, 1) + pltpu.roll(x, w - 1, 1)
    )


def masked(x, rows, inside):
    return jnp.concatenate([x[:rows], x[rows:] * inside], 0)


def flux_kernel(
    sizes, core, tile, own, forcing, surface, rate, rows_of_mix, curve, owners, locals_, shares, inner, outer, after,
    keep, send, fluxes, halo
):
    levels, rows, steps, sea_levels, sea_rows, stride, sea_stride = sizes
    width = own.shape[1]
    one, two = inner[...], outer[...]
    halo[: HALO * FIELDS, :] = jnp.where(core[0] == 0, one, two)
    halo[HALO * FIELDS :, :] = jnp.where(core[0] == 0, two, one)

    def edge(l):
        return halo[pl.ds(l, 2 * HALO, stride=FIELDS), :]

    inside = edge(2 * steps + 2)
    by_curve = jnp.broadcast_to(curve[...], (8, levels))
    of_curve = [
        jnp.dot(by_curve, rows_of_mix[s * levels : (s + 1) * levels, :], precision=EXACT, preferred_element_type=f32)[:1]
        for s in range(steps - 1)
    ]
    of_last = [rows_of_mix[(s + 1) * levels - 1 : (s + 1) * levels, :] for s in range(steps - 1)]
    tops = [jnp.concatenate([own[s * rows : (s + 1) * rows, :], edge(s)], 0) for s in range(steps)]
    surf = jnp.concatenate([surface[...], edge(2 * steps)], 0)
    coef = jnp.concatenate([rate[...], edge(2 * steps + 1)], 0)
    force = [
        jnp.concatenate([forcing[s * rows : (s + 1) * rows, :], edge(steps + s)], 0) for s in range(steps)
    ]

    flux = []
    for s in range(steps):
        state = tops[s]
        for i in range(s):
            m = s - 1 - i
            state = masked(cross(state) * atm_diffusion, rows, inside)
            state = state + of_curve[m] * force[i] - of_last[m] * flux[i]
        flux.append(coef * (state - surf))
        reach = rows + 2 * HALO
        fluxes[pl.ds(s, reach, stride=2 * steps), :] = force[s]
        fluxes[pl.ds(steps + s, reach, stride=2 * steps), :] = flux[s]
    total = flux[0][:rows]
    for s in range(1, steps):
        total = total + flux[s][:rows]
    mean = (total / steps).astype(bf16)
    topk = owners.shape[0]
    target = (owners[...] ^ tile[0]) * sea_rows + locals_[...]
    target = jnp.concatenate([target[k : k + 1, :] for k in range(topk)], 1)
    rowed = jnp.concatenate(
        [jnp.dot(mean, shares[k * width : (k + 1) * width, :], preferred_element_type=f32) for k in range(topk)], 0
    )
    first = rowed.astype(bf16)
    left = rowed - first.astype(f32)
    second = left.astype(bf16)
    third = (left - second.astype(f32)).astype(bf16)
    half = keep.shape[0]
    hot = lax.broadcasted_iota(jnp.int32, (2 * half, topk * rows), 0) == target
    hot = jnp.where(hot, 1.0, 0.0).astype(bf16)
    sums = jnp.dot(
        jnp.concatenate([hot, hot, hot], 1), jnp.concatenate([first, second, third], 0), preferred_element_type=f32
    )
    keep[...] = sums[:half]
    send[...] = sums[half:]


def edge_kernel(
    sizes, last_place, core, place, fluxes, own, sea_weights, sea_ends, wet, warm, salt, inner, outer, after,
    spread, warm_out, brine_out, above, below, salt_held, done
):
    levels, rows, steps, sea_levels, sea_rows, stride, sea_stride = sizes
    width = own.shape[1]
    depth = up_to(levels + 2 * steps, 16)
    one, two = inner[...], outer[...]
    above[...] = jnp.where(core[0] == 0, two, one)
    below[...] = jnp.where(core[0] == 0, one, two)
    inside_above, inside_below = inside_of(place, last_place)

    reach = rows + 2 * HALO
    x = [fluxes[(r % reach) * 2 * steps : (r % reach + 1) * 2 * steps, :] for r in range(1 - steps, rows + steps - 1)]
    field = lax.broadcasted_iota(jnp.int32, (2 * steps, width), 0) % steps
    for n in range(1, steps):
        y = stencil(x)
        x = [jnp.where(field < steps - n, y[i], x[i + 1]) for i in range(len(y))]
        for i in range(steps - 1 - n):
            x[i] = x[i] * inside_above
            x[-1 - i] = x[-1 - i] * inside_below
    for r in range(rows):
        spread[r * depth + levels : (r + 1) * depth, :] = x[r]
        if HALO <= r < rows - HALO:
            spread[r * depth : r * depth + levels, :] = own[r * levels : (r + 1) * levels, :]

    warm_out[...] = warm[...]
    salt_held[...] = salt[...]
    m = wet[...].astype(f32)
    base = HALO * stride
    w = sea_weights[:, : 3 * sea_stride]
    for e, (r, other) in enumerate(((0, above), (sea_rows - 1, below))):
        mark = m[r : r + 1]
        far = other[base + 2 * sea_stride : base + 2 * sea_stride + 1, :]
        x = []
        for f in range(2):
            at = base + f * sea_stride
            mine = (2 * f + e) * sea_stride
            step = other[at : at + sea_levels, :] - sea_ends[mine : mine + sea_levels, :] * far
            step = ocean_diffusion * (mark * step)
            x.append(jnp.concatenate([step, jnp.zeros((sea_stride - sea_levels, width), f32)], 0))
        y = product(w, jnp.concatenate(x, 1))
        for f, to in enumerate((warm_out, salt_held)):
            rows_at = pl.ds(r, sea_levels, stride=sea_rows)
            to[rows_at, :] = to[rows_at, :] + mark * y[:sea_levels, f * width : (f + 1) * width]
    leave = [pltpu.make_async_copy(salt_held, brine_out, done.at[0])]
    leave[0].start()

    @pl.loop(0, levels // 8)
    def _(c):
        def other(ref, j):
            return ref[pl.ds(pl.multiple_of(j * stride + c * 8, 8), 8), :]

        top, low = ([other(ref, j) for j in range(HALO)] for ref in (above, below))
        none = jnp.zeros_like(top[0])
        for n in range(steps):
            top = stencil(top + [none]) + [top[-1]]
            low = [low[0]] + stencil([none] + low)
        for i, value in enumerate(top + low):
            r = i if i < HALO else rows - 2 * HALO + i
            value = value + own[pl.ds(pl.multiple_of(r * levels + c * 8, 8), 8), :]
            spread[pl.ds(pl.multiple_of(r * depth + c * 8, 8), 8), :] = value

    for move in leave:
        move.wait()


def mix_kernel(sizes, spread, weights, after, out, result, done):
    levels, rows, steps, sea_levels, sea_rows, stride, sea_stride = sizes
    width = spread.shape[1]
    depth = up_to(levels + 2 * steps, 16)
    w = weights[:, : 3 * depth]
    leave = []
    for g in range(rows // 8):
        to = result.at[g].reshape(levels * 8, width)
        for r in range(g * 8, g * 8 + 8, 2):
            y = product(
                w, jnp.concatenate([spread[(r + q) * depth : (r + q + 1) * depth, :] for q in range(2)], 1)
            )
            for q in range(2):
                to[pl.ds((r + q) % 8, levels, stride=8), :] = y[:levels, q * width : (q + 1) * width]
        leave.append(pltpu.make_async_copy(result.at[g], out.at[:, g], done.at[g]))
        leave[-1].start()
    for move in leave:
        move.wait()


def add_kernel(keep, got, after, kept, send):
    n = kept.shape[0]
    kept[...] = keep[:n] + got[:n]
    send[...] = keep[n:] + got[n:]


def heat_kernel(sizes, kept, got, wet, sea_first, before, after):
    levels, rows, steps, sea_levels, sea_rows, stride, sea_stride = sizes
    heat = kept[...] + got[...]
    heat = wet[...].astype(f32) * heat
    for l in range(sea_levels):
        after[l * sea_rows : (l + 1) * sea_rows, :] = (
            before[l * sea_rows : (l + 1) * sea_rows, :] + sea_first[l : l + 1, :] * heat
        )


def body(sky, forcing, curve, surface, rate, vmix, shares, owners, locals_, warmth, brine, wet, sea_mix):
    levels, rows, width = sky.shape
    steps = forcing.shape[0]
    sea_levels, sea_rows, _ = warmth.shape
    topk = owners.shape[1]
    stride = up_to(levels, 8)
    sea_stride = up_to(sea_levels, 16)
    sizes = (levels, rows, steps, sea_levels, sea_rows, stride, sea_stride)
    sky2, forcing2 = sky.reshape(-1, width), forcing.reshape(-1, width)
    warmth2, brine2 = warmth.reshape(-1, width), brine.reshape(-1, width)
    flat = lambda n, kind=f32: jax.ShapeDtypeStruct((n, width), kind)

    space = lambda *shape: pltpu.VMEM(shape, f32)
    space = lambda *shape: pltpu.VMEM(shape, f32)
    length = HALO * stride + 2 * sea_stride + 8
    ring = ("tile", "comp")
    tiles, count = lax.axis_size("tile"), lax.axis_size(ring)
    at = lax.axis_index(ring).astype(jnp.int32)[None]
    core = lax.axis_index("comp").astype(jnp.int32)[None]
    tile = lax.axis_index("tile").astype(jnp.int32)[None]
    area = sea_levels * sea_rows
    swap = lambda first: [(i + a, i + 1 - a) for i in range(first, count - 1, 2) for a in range(2)]
    inner, outer, rows_of_mix, own = call(
        functools.partial(first_kernel, sizes),
        [flat(HALO * FIELDS)] * 2 + [flat((steps - 1) * levels), flat(steps * rows)],
        core, vmix, sky2, forcing, surface, rate, moved=4 << 20, in_specs=[SMEM] + [HBM] * 5,
        scratch=[
            space(levels, levels), space(levels * rows, width), space(steps, rows, width), space(2, rows, width),
            pltpu.SemaphoreType.DMA((5,)),
        ],
        grant=FULL,
    )
    inner = lax.ppermute(inner, ring, swap(0))
    outer = lax.ppermute(outer, ring, swap(1))
    far_inner, far_outer = call(
        functools.partial(pack_kernel, sizes), [flat(length)] * 2,
        core, sky2, warmth2, brine2, wet, own, moved=4 << 20, in_specs=[SMEM] + [VMEM] * 4 + [ANY],
    )
    far_inner = lax.ppermute(far_inner, ring, swap(0))
    far_outer = lax.ppermute(far_outer, ring, swap(1))

    depth = up_to(levels + 2 * steps, 16)
    weights, sea_weights, sea_first, sea_ends, warm, salt = call(
        functools.partial(local_kernel, sizes),
        [
            jax.ShapeDtypeStruct((up_to(levels, 16), 2 * width), bf16),
            jax.ShapeDtypeStruct((sea_stride, 2 * width), bf16), flat(sea_stride), flat(4 * sea_stride),
            flat(area), flat(area),
        ],
        vmix, curve[None], sea_mix, warmth2, brine2, wet,
        scratch=[space(2, sea_rows * sea_stride, width)],
        flops=2 << 30, moved=4 << 20,
    )

    half = tiles // 2 * sea_rows
    keep, send, fluxes = call(
        functools.partial(flux_kernel, sizes), [flat(half), flat(half), flat(2 * steps * (rows + 2 * HALO))],
        core, tile, own, forcing2, surface, rate, rows_of_mix, curve[None], owners.T, locals_.T,
        shares.reshape(-1, width), inner, outer, weights,
        in_specs=[SMEM] * 2 + [VMEM] * 11 + [ANY], scratch=[space(2 * HALO * FIELDS, width)], moved=2 << 20,
    )
    def own_part(after):
        return call(
            functools.partial(own_kernel, sizes, count - 1), flat(rows * levels), at, sky2, after,
            in_specs=[SMEM, VMEM, ANY], flops=1 << 28, moved=2 << 20,
        )

    def edge_part(spread, after):
        return call(
            functools.partial(edge_kernel, sizes, count - 1), [flat(rows * depth), flat(area), flat(area)],
            core, at, fluxes, spread, sea_weights, sea_ends, wet, warm, salt, far_inner, far_outer, after,
            in_specs=[SMEM] * 2 + [VMEM] * 9 + [ANY], out_specs=[VMEM, VMEM, HBM],
            scratch=[space(length, width), space(length, width), space(area, width), pltpu.SemaphoreType.DMA((1,))],
            flops=1 << 28, moved=4 << 20,
        )

    bit, spread = tiles // 2, None
    while True:
        got = lax.ppermute(send, "tile", [(i, i ^ bit) for i in range(tiles)])
        if bit == 4:
            spread = own_part(keep)
        if bit <= 2 and spread is None:
            spread = own_part(keep)
        if bit == 2 or (bit == 1 and tiles == 2):
            spread, warm, salt = edge_part(spread, keep)
        if bit == 1:
            break
        keep, send = call(
            add_kernel, [flat(bit // 2 * sea_rows)] * 2, keep, got, keep if spread is None else spread,
            in_specs=[VMEM, VMEM, ANY],
        )
        bit //= 2
    sky_out = call(
        functools.partial(mix_kernel, sizes), jax.ShapeDtypeStruct((levels, rows // 8, 8, width), f32),
        spread, weights, keep, in_specs=[VMEM, VMEM, ANY], out_specs=HBM,
        scratch=[space(rows // 8, levels, 8, width), pltpu.SemaphoreType.DMA((rows // 8,))],
        flops=2 << 30, moved=4 << 20,
    )
    warm = call(functools.partial(heat_kernel, sizes), flat(area), keep, got, wet, sea_first, warm, moved=2 << 20)
    return sky_out.reshape(sky.shape), warm.reshape(warmth.shape), salt.reshape(brine.shape)


def solution(mesh):
    both = P(None, ("member", "tile", "comp"), None)
    one = P(("tile", "comp"), None)
    return jax.shard_map(
        body,
        mesh=mesh,
        in_specs=(
            both, both, P(), P(("member", "tile", "comp"), None), one, P(), P(), one, one, both, both, one, P(),
        ),
        out_specs=(both, both, both),
        check_vma=False,
    )
```

time: 30.6 us -> 33.5 us (1.095)
  local copies, waits for them, and re-layouts: 0.08 us -> 2.98 us
  waiting for transfers between devices: 3.66 us -> 1.39 us
  starting transfers between devices: 12.1 us -> 13.2 us
  Pallas kernels: 13.7 us -> 14.6 us
    ppermute x0 -> x2, starting transfers between devices: none -> 4.53 us  [the longest x1 3.87 us: body(): far_inner = lax.ppermute(far_inner, ring, swap(0))]
    ppermute x3, starting transfers between devices: 10.9 us -> 7.53 us  [body(): got = lax.ppermute(send, 'tile', [(i, i ^ bit) for i in range(tiles)])]
    unnamed x26 -> x36, local copies, waits for them, and re-layouts: 0.07 us -> 2.98 us
    ppermute x3, waiting for transfers between devices: 3.65 us -> 1.38 us  [body(): got = lax.ppermute(send, 'tile', [(i, i ^ bit) for i in range(tiles)])]
    pallas_call x5 -> x10, Pallas kernels: 13.7 us -> 14.6 us  [call(): pl.pallas_call(kernel, out_shape=out_shape, in_specs=in_specs or [VMEM] *...]
  transfers between devices with their start and end apart: 5 -> 7, of which waited for: 2 -> 1; matrix products, arithmetic and copies ran while one was open for 0% -> 0% of each run, Pallas kernels for 32% -> 34%
where the time goes in v9:
time: 33.5 us; the launch traced here: 33.2 us
  Pallas kernels  14.6 us (44%)
  starting transfers between devices  13.2 us (39%)
  local copies, waits for them, and re-layouts  2.98 us (9%)
  waiting for transfers between devices  1.39 us (4%)
  between operations  0.98 us (3%)
    pallas_call x10, Pallas kernels, call(): pl.pallas_call(kernel, out_shape=out_shape, in_specs=in_specs or [VMEM] *...  14.6 us
    ppermute x3, starting transfers between devices, body(): got = lax.ppermute(send, 'tile', [(i, i ^ bit) for i in range(tiles)])  7.53 us
    ppermute x1, starting transfers between devices, body(): far_inner = lax.ppermute(far_inner, ring, swap(0))  3.87 us
    unnamed x36, local copies, waits for them, and re-layouts  2.98 us
    ppermute x3, waiting for transfers between devices, body(): got = lax.ppermute(send, 'tile', [(i, i ^ bit) for i in range(tiles)])  1.38 us
  transfers between devices with their start and end apart: 7, of which 1 were waited for; matrix products, arithmetic and copies ran while one was open for 0% of the time, Pallas kernels for 34%

profile of v9, /device:TPU:0, one launch (start us, length us, event | category | flops | bytes accessed | tf_op | source)
XLA Modules:
  0.0 33.2 jit_solution(620439849947612752)
XLA Ops:
  0.7 2.5 %shard_map.148 = (f32[64,128]{1,0:T(8,128)}, f32[64,128]{1,0:T(8,128)}, f32[216,128]{1,0:T(8,128)}, f32[128,128]{1,0:T(8,128)}) custom-call(s32[1]{0:T(128)} %bitcast.core, f32[72,72]{1,0:T(8,128)} %vmix.1, f32[2304,128]{1,0:T(8,128)} %bitcast.14, f32[4,32,128]{2,1,0:T(8,128)} %forcing.1, f32[32,128]{1,0:T(8,128)} %surface.3, f32[32,128]{1,0:T(8,128)} %rate.3), custom_call_target="tpu_custom_call" | custom-call | bytes 4194304 | tf_op jit(solution)/shard_map/pallas_call | solution.py:28
  3.2 0.0 copy-start.16
  3.2 0.5 %collective-permute-start = (f32[64,128]{1,0:T(8,128)}, f32[64,128]{1,0:T(8,128)S(1)}, u32[]{:S(2)}, u32[]{:S(2)}) collective-permute-start(f32[64,128]{1,0:T(8,128)} %get-tuple-element.27), channel_id=1, source_target_pairs={{0,1},{1,0},{2,3},{3,2},{4,5},{5,4},{6,7},{7,6},{8,9},{9,8},{10,11... | collective-permute-start | bytes 98312 | tf_op jit(solution)/shard_map/ppermute | solution.py:434
  3.7 0.7 %collective-permute-start.1 = (f32[64,128]{1,0:T(8,128)}, f32[64,128]{1,0:T(8,128)S(1)}, u32[]{:S(2)}, u32[]{:S(2)}) collective-permute-start(f32[64,128]{1,0:T(8,128)} %get-tuple-element.28), channel_id=1, source_target_pairs={{1,2},{2,1},{3,4},{4,3},{5,6},{6,5},{7,8},{8,7},{9,10},{10,9},{11,... | collective-permute-start | bytes 98312 | tf_op jit(solution)/shard_map/ppermute | solution.py:435
  4.4 0.0 copy-start.1
  4.4 1.0 %copy-done.1 = f32[62,16,128]{2,1,0:T(8,128)S(1)} copy-done((f32[62,16,128]{2,1,0:T(8,128)S(1)}, f32[62,16,128]{2,1,0:T(8,128)}, u32[]{:S(2)}) %copy-start.1) | copy-done | bytes 507928
  5.4 1.0 %copy-done.3 = f32[62,16,128]{2,1,0:T(8,128)S(1)} copy-done((f32[62,16,128]{2,1,0:T(8,128)S(1)}, f32[62,16,128]{2,1,0:T(8,128)}, u32[]{:S(2)}) %copy-start.3) | copy-done | bytes 507928
  6.5 0.8 %copy-done.6 = f32[128,128]{1,0:T(8,128)S(1)} copy-done((f32[128,128]{1,0:T(8,128)S(1)}, f32[128,128]{1,0:T(8,128)}, u32[]{:S(2)}) %copy-start.6) | copy-done | bytes 65560
  7.3 1.0 %shard_map.152 = (f32[424,128]{1,0:T(8,128)}, f32[424,128]{1,0:T(8,128)}) custom-call(s32[1]{0:T(128)} %bitcast.core, f32[2304,128]{1,0:T(8,128)S(1)} %bitcast.15, f32[992,128]{1,0:T(8,128)S(1)} %bitcast.17, f32[992,128]{1,0:T(8,128)S(1)} %bitcast.19, s32[16,128]{1,0:T(8,128)S(1)} %copy-done.10, f32[128,128]{1,0:T(8,128)S(1)} %copy-done.6), custom_call_target="tpu_custom_call" | custom-call | bytes 4194304 | tf_op jit(solution)/shard_map/pallas_call | solution.py:28
  8.3 3.9 %collective-permute-start.2 = (f32[424,128]{1,0:T(8,128)}, f32[424,128]{1,0:T(8,128)S(1)}, u32[]{:S(2)}, u32[]{:S(2)}) collective-permute-start(f32[424,128]{1,0:T(8,128)} %get-tuple-element.36), channel_id=1, source_target_pairs={{0,1},{1,0},{2,3},{3,2},{4,5},{5,4},{6,7},{7,6},{8,9},{9,8},{10,11... | collective-permute-start | bytes 651272 | tf_op jit(solution)/shard_map/ppermute | solution.py:440
  12.2 0.7 %collective-permute-start.3 = (f32[424,128]{1,0:T(8,128)}, f32[424,128]{1,0:T(8,128)S(1)}, u32[]{:S(2)}, u32[]{:S(2)}) collective-permute-start(f32[424,128]{1,0:T(8,128)} %get-tuple-element.37), channel_id=1, source_target_pairs={{1,2},{2,1},{3,4},{4,3},{5,6},{6,5},{7,8},{8,7},{9,10},{10,9},{11,... | collective-permute-start | bytes 651272 | tf_op jit(solution)/shard_map/ppermute | solution.py:441
  12.9 0.0 copy-start.5
  12.9 0.0 copy-start.8
  12.9 0.0 copy-start.9
  12.9 0.0 copy-start.11
  13.0 0.0 copy-start.12
  13.0 0.0 copy-start.14
  13.0 0.0 copy-start.15
  13.0 2.0 %shard_map.149 = (bf16[80,256]{1,0:T(8,128)(2,1)S(1)}, bf16[64,256]{1,0:T(8,128)(2,1)S(1)}, f32[64,128]{1,0:T(8,128)S(1)}, f32[256,128]{1,0:T(8,128)S(1)}, f32[9...) custom-call(f32[72,72]{1,0:T(8,128)S(1)} %copy-done.13, f32[1,72]{1,0:T(1,128)S(1)} %bitcast.25, f32[62,62]{1,0:T(8,128)S(1)} %copy-done.17, ...), custom_call_target="tpu_custom_call" | custom-call | flops 2147483648 | bytes 4194304 | tf_op jit(solution)/shard_map/pallas_call | solution.py:28
  15.0 0.0 collective-permute-done.inner
  15.1 1.4 %shard_map.150 = (f32[64,128]{1,0:T(8,128)S(1)}, f32[64,128]{1,0:T(8,128)}, f32[320,128]{1,0:T(8,128)S(1)}) custom-call(s32[1]{0:T(128)} %bitcast.core, s32[1]{0:T(128)} %bitcast.2.tile, f32[128,128]{1,0:T(8,128)S(1)} %copy-done.7, f32[128,128]{1,0:T(8,128)S(1)} %bitcast.21, f32[32,128]{1,0:T(8,128)S(1)} %copy-done.11, f32[32,128]{1,0:T(8,128)S(1)} %copy-done.12, ...), custom_call_target="tpu_custom_call" | custom-call | bytes 2097152 | tf_op jit(solution)/shard_map/pallas_call | solution.py:28
  16.4 4.9 %collective-permute-start.4 = (f32[64,128]{1,0:T(8,128)}, f32[64,128]{1,0:T(8,128)S(1)}, u32[]{:S(2)}, u32[]{:S(2)}) collective-permute-start(f32[64,128]{1,0:T(8,128)} %get-tuple-element.38), channel_id=1, source_target_pairs={{0,8},{2,10},{4,12},{6,14},{8,0},{10,2},{12,4},{14,6},{1,9},{3,11}... | collective-permute-start | bytes 98312 | tf_op jit(solution)/shard_map/ppermute | solution.py:480
  21.3 3.2 %shard_map.151.after.own = f32[2304,128]{1,0:T(8,128)S(1)} custom-call(s32[1]{0:T(128)} %bitcast.1.place, f32[2304,128]{1,0:T(8,128)S(1)} %bitcast.16, f32[64,128]{1,0:T(8,128)S(1)} %get-tuple-element.31.after.keep), custom_call_target="tpu_custom_call" | custom-call | flops 268435456 | bytes 2097152 | tf_op jit(solution)/shard_map/pallas_call | solution.py:28
  24.5 1.6 %collective-permute-start.5 = (f32[32,128]{1,0:T(8,128)S(1)}, f32[32,128]{1,0:T(8,128)S(1)}, u32[]{:S(2)}, u32[]{:S(2)}) collective-permute-start(f32[32,128]{1,0:T(8,128)S(1)} %get-tuple-element.41), channel_id=1, source_target_pairs={{0,4},{2,6},{4,0},{6,2},{8,12},{10,14},{12,8},{14,10},{1,5},{3,7},... | collective-permute-start | bytes 49160 | tf_op jit(solution)/shard_map/ppermute | solution.py:480
  26.2 0.0 collective-permute-done.2.inner
  26.2 0.0 collective-permute-done.3.outer
  26.2 2.5 %shard_map.154 = (f32[2560,128]{1,0:T(8,128)S(1)}, f32[992,128]{1,0:T(8,128)S(1)}, f32[992,128]{1,0:T(8,128)}) custom-call(s32[1]{0:T(128)} %bitcast.core, s32[1]{0:T(128)} %bitcast.1.place, f32[320,128]{1,0:T(8,128)S(1)} %get-tuple-element.30.fluxes, f32[2304,128]{1,0:T(8,128)S(1)} %shard_map.151.after.own, ...), custom_call_target="tpu_custom_call" | custom-call | flops 268435456 | bytes 4194304 | tf_op jit(solution)/shard_map/pallas_call | solution.py:28
  28.6 0.0 collective-permute-done.5.got
  28.7 1.0 %collective-permute-start.6 = (f32[16,128]{1,0:T(8,128)S(1)}, f32[16,128]{1,0:T(8,128)S(1)}, u32[]{:S(2)}, u32[]{:S(2)}) collective-permute-start(f32[16,128]{1,0:T(8,128)S(1)} %get-tuple-element.43), channel_id=1, source_target_pairs={{0,2},{2,0},{4,6},{6,4},{8,10},{10,8},{12,14},{14,12},{1,3},{3,1},... | collective-permute-start | bytes 24584 | tf_op jit(solution)/shard_map/ppermute | solution.py:480
  29.7 1.3 %shard_map.156 = f32[72,4,8,128]{3,2,1,0:T(8,128)} custom-call(f32[2560,128]{1,0:T(8,128)S(1)} %get-tuple-element.40.after.spread, bf16[80,256]{1,0:T(8,128)(2,1)S(1)} %get-tuple-element.29.after.weights, f32[16,128]{1,0:T(8,128)S(1)} %get-tuple-element.42.after.kept), custom_call_target="tpu_custom_call" | custom-call | flops 2147483648 | bytes 4194304 | tf_op jit(solution)/shard_map/pallas_call | solution.py:28
  31.0 1.4 %collective-permute-done.6.got = f32[16,128]{1,0:T(8,128)S(1)} collective-permute-done((f32[16,128]{1,0:T(8,128)S(1)}, f32[16,128]{1,0:T(8,128)S(1)}, u32[]{:S(2)}, u32[]{:S(2)}) %collective-permute-start.6) | collective-permute-done | bytes 8224 | tf_op jit(solution)/shard_map/ppermute | solution.py:480
  32.4 0.8 %shard_map.157 = f32[992,128]{1,0:T(8,128)} custom-call(f32[16,128]{1,0:T(8,128)S(1)} %get-tuple-element.42.after.kept, f32[16,128]{1,0:T(8,128)S(1)} %collective-permute-done.6.got, s32[16,128]{1,0:T(8,128)S(1)} %copy-done.10, f32[64,128]{1,0:T(8,128)S(1)} %get-tuple-element.44.sea_first, f32[992,128]{1,0:T(8,128)S(1)} %get-tuple-element.45.before), custom_call_target="tpu_custom_call" | custom-call | bytes 2097152 | tf_op jit(solution)/shard_map/pallas_call | solution.py:28
  (28 shorter events, 0.1 us)
Async XLA Ops:
  0.6 3.7 %copy-start = (f32[72,32,128]{2,1,0:T(8,128)S(1)}, f32[72,32,128]{2,1,0:T(8,128)}, u32[]{:S(2)}) copy-start(f32[72,32,128]{2,1,0:T(8,128)} %param.13) | copy-start | bytes 3538948
  0.6 3.7 %copy-start.10 = (s32[16,128]{1,0:T(8,128)S(1)}, s32[16,128]{1,0:T(8,128)}, u32[]{:S(2)}) copy-start(s32[16,128]{1,0:T(8,128)} %wet.7) | copy-start | bytes 24580
  0.7 12.2 %copy-start.13 = (f32[72,72]{1,0:T(8,128)S(1)}, f32[72,72]{1,0:T(8,128)}, u32[]{:S(2)}) copy-start(f32[72,72]{1,0:T(8,128)} %vmix.1) | copy-start | bytes 62212
  0.7 12.2 %copy-start.17 = (f32[62,62]{1,0:T(8,128)S(1)}, f32[62,62]{1,0:T(8,128)}, u32[]{:S(2)}) copy-start(f32[62,62]{1,0:T(8,128)} %sea_mix.1) | copy-start | bytes 46132
  3.2 9.7 %copy-start.16 = (f32[72]{0:T(128)S(1)}, f32[72]{0:T(128)}, u32[]{:S(2)}) copy-start(f32[72]{0:T(128)} %param.15) | copy-start | bytes 868
  3.2 11.8 %collective-permute-start = (f32[64,128]{1,0:T(8,128)}, f32[64,128]{1,0:T(8,128)S(1)}, u32[]{:S(2)}, u32[]{:S(2)}) collective-permute-start(f32[64,128]{1,0:T(8,128)} %get-tuple-element.27), channel_id=1, source_target_pairs={{0,1},{1,0},{2,3},{3,2},{4,5},{5,4},{6,7},{7,6},{8,9},{9,8},{10,11... | collective-permute-start | bytes 98312 | tf_op jit(solution)/shard_map/ppermute | solution.py:434
  3.7 11.3 %collective-permute-start.1 = (f32[64,128]{1,0:T(8,128)}, f32[64,128]{1,0:T(8,128)S(1)}, u32[]{:S(2)}, u32[]{:S(2)}) collective-permute-start(f32[64,128]{1,0:T(8,128)} %get-tuple-element.28), channel_id=1, source_target_pairs={{1,2},{2,1},{3,4},{4,3},{5,6},{6,5},{7,8},{8,7},{9,10},{10,9},{11,... | collective-permute-start | bytes 98312 | tf_op jit(solution)/shard_map/ppermute | solution.py:435
  4.4 1.0 %copy-start.1 = (f32[62,16,128]{2,1,0:T(8,128)S(1)}, f32[62,16,128]{2,1,0:T(8,128)}, u32[]{:S(2)}) copy-start(f32[62,16,128]{2,1,0:T(8,128)} %param.22) | copy-start | bytes 1523716
  5.4 1.0 %copy-start.3 = (f32[62,16,128]{2,1,0:T(8,128)S(1)}, f32[62,16,128]{2,1,0:T(8,128)}, u32[]{:S(2)}) copy-start(f32[62,16,128]{2,1,0:T(8,128)} %param.23) | copy-start | bytes 1523716
  6.5 0.8 %copy-start.6 = (f32[128,128]{1,0:T(8,128)S(1)}, f32[128,128]{1,0:T(8,128)}, u32[]{:S(2)}) copy-start(f32[128,128]{1,0:T(8,128)} %get-tuple-element.25.own.after) | copy-start | bytes 196612
  7.3 5.6 %copy-start.2 = (f32[62,16,128]{2,1,0:T(8,128)S(1)}, f32[62,16,128]{2,1,0:T(8,128)}, u32[]{:S(2)}) copy-start(f32[62,16,128]{2,1,0:T(8,128)} %param.22) | copy-start | bytes 1523716
  7.3 5.6 %copy-start.4 = (f32[62,16,128]{2,1,0:T(8,128)S(1)}, f32[62,16,128]{2,1,0:T(8,128)}, u32[]{:S(2)}) copy-start(f32[62,16,128]{2,1,0:T(8,128)} %param.23) | copy-start | bytes 1523716
  8.3 17.9 %collective-permute-start.2 = (f32[424,128]{1,0:T(8,128)}, f32[424,128]{1,0:T(8,128)S(1)}, u32[]{:S(2)}, u32[]{:S(2)}) collective-permute-start(f32[424,128]{1,0:T(8,128)} %get-tuple-element.36), channel_id=1, source_target_pairs={{0,1},{1,0},{2,3},{3,2},{4,5},{5,4},{6,7},{7,6},{8,9},{9,8},{10,11... | collective-permute-start | bytes 651272 | tf_op jit(solution)/shard_map/ppermute | solution.py:440
  12.2 14.0 %collective-permute-start.3 = (f32[424,128]{1,0:T(8,128)}, f32[424,128]{1,0:T(8,128)S(1)}, u32[]{:S(2)}, u32[]{:S(2)}) collective-permute-start(f32[424,128]{1,0:T(8,128)} %get-tuple-element.37), channel_id=1, source_target_pairs={{1,2},{2,1},{3,4},{4,3},{5,6},{6,5},{7,8},{8,7},{9,10},{10,9},{11,... | collective-permute-start | bytes 651272 | tf_op jit(solution)/shard_map/ppermute | solution.py:441
  12.9 2.1 %copy-start.5 = (f32[4,32,128]{2,1,0:T(8,128)S(1)}, f32[4,32,128]{2,1,0:T(8,128)}, u32[]{:S(2)}) copy-start(f32[4,32,128]{2,1,0:T(8,128)} %forcing.1) | copy-start | bytes 196612
  12.9 2.1 %copy-start.7 = (f32[128,128]{1,0:T(8,128)S(1)}, f32[128,128]{1,0:T(8,128)}, u32[]{:S(2)}) copy-start(f32[128,128]{1,0:T(8,128)} %get-tuple-element.25.own.after) | copy-start | bytes 196612
  12.9 2.1 %copy-start.8 = (bf16[4,128,128]{2,1,0:T(8,128)(2,1)S(1)}, bf16[4,128,128]{2,1,0:T(8,128)(2,1)}, u32[]{:S(2)}) copy-start(bf16[4,128,128]{2,1,0:T(8,128)(2,1)} %param.19) | copy-start | bytes 393220
  12.9 2.1 %copy-start.9 = (f32[216,128]{1,0:T(8,128)S(1)}, f32[216,128]{1,0:T(8,128)}, u32[]{:S(2)}) copy-start(f32[216,128]{1,0:T(8,128)} %get-tuple-element.26.rows_of_mix) | copy-start | bytes 331780
  12.9 2.1 %copy-start.11 = (f32[32,128]{1,0:T(8,128)S(1)}, f32[32,128]{1,0:T(8,128)}, u32[]{:S(2)}) copy-start(f32[32,128]{1,0:T(8,128)} %surface.3) | copy-start | bytes 49156
  13.0 2.1 %copy-start.12 = (f32[32,128]{1,0:T(8,128)S(1)}, f32[32,128]{1,0:T(8,128)}, u32[]{:S(2)}) copy-start(f32[32,128]{1,0:T(8,128)} %rate.3) | copy-start | bytes 49156
  13.0 2.1 %copy-start.14 = (s32[32,4]{0,1:T(4,128)S(1)}, s32[32,4]{0,1:T(4,128)}, u32[]{:S(2)}) copy-start(s32[32,4]{0,1:T(4,128)} %param.20) | copy-start | bytes 1540
  13.0 2.1 %copy-start.15 = (s32[32,4]{0,1:T(4,128)S(1)}, s32[32,4]{0,1:T(4,128)}, u32[]{:S(2)}) copy-start(s32[32,4]{0,1:T(4,128)} %param.21) | copy-start | bytes 1540
  16.4 8.1 %collective-permute-start.4 = (f32[64,128]{1,0:T(8,128)}, f32[64,128]{1,0:T(8,128)S(1)}, u32[]{:S(2)}, u32[]{:S(2)}) collective-permute-start(f32[64,128]{1,0:T(8,128)} %get-tuple-element.38), channel_id=1, source_target_pairs={{0,8},{2,10},{4,12},{6,14},{8,0},{10,2},{12,4},{14,6},{1,9},{3,11}... | collective-permute-start | bytes 98312 | tf_op jit(solution)/shard_map/ppermute | solution.py:480
  24.5 4.1 %collective-permute-start.5 = (f32[32,128]{1,0:T(8,128)S(1)}, f32[32,128]{1,0:T(8,128)S(1)}, u32[]{:S(2)}, u32[]{:S(2)}) collective-permute-start(f32[32,128]{1,0:T(8,128)S(1)} %get-tuple-element.41), channel_id=1, source_target_pairs={{0,4},{2,6},{4,0},{6,2},{8,12},{10,14},{12,8},{14,10},{1,5},{3,7},... | collective-permute-start | bytes 49160 | tf_op jit(solution)/shard_map/ppermute | solution.py:480
  28.7 3.7 %collective-permute-start.6 = (f32[16,128]{1,0:T(8,128)S(1)}, f32[16,128]{1,0:T(8,128)S(1)}, u32[]{:S(2)}, u32[]{:S(2)}) collective-permute-start(f32[16,128]{1,0:T(8,128)S(1)} %get-tuple-element.43), channel_id=1, source_target_pairs={{0,2},{2,0},{4,6},{6,4},{8,10},{10,8},{12,14},{14,12},{1,3},{3,1},... | collective-permute-start | bytes 24584 | tf_op jit(solution)/shard_map/ppermute | solution.py:480

commit v10 on v8

--- a/solution.py
+++ b/solution.py
@@ -15,6 +15,7 @@
 VMEM = pl.BlockSpec(memory_space=pltpu.VMEM)
 HBM = pl.BlockSpec(memory_space=pltpu.HBM)
 SMEM = pl.BlockSpec(memory_space=pltpu.SMEM)
+ANY = pl.BlockSpec(memory_space=pl.ANY)
 f32, bf16 = jnp.float32, jnp.bfloat16
 
 
@@ -110,8 +111,7 @@
 
 def local_kernel(
     sizes, last_place, place, vmix, curve, sea_mix, sky, warmth, brine, wet,
-    rows_of_mix, source_rows, own, weights, source_weights, sea_weights, sea_first, sea_ends,
-    middle, warm_out, brine_out, spread, sea_spread,
+    rows_of_mix, source_rows, own, weights, sea_weights, sea_first, sea_ends, spread, warm_out, brine_out, sea_spread,
 ):
     levels, rows, steps, sea_levels, sea_rows, stride, sea_stride = sizes
     width = sky.shape[1]
@@ -140,17 +140,14 @@
     wide = jnp.concatenate(
         [powers[-1] * atm_diffusion**steps, jnp.zeros((levels, width - levels), f32)], 1
     )
-    sources = jnp.zeros((levels, width), f32)
     for j in range(steps):
         factor = atm_diffusion ** (steps - 1 - j)
         for at, value in ((j, of_curve[steps - 1 - j] * factor), (steps + j, of_last[steps - 1 - j] * -factor)):
             wide = jnp.where(lane == levels + at, value, wide)
-            sources = jnp.where(lane == at, value, sources)
     more = jnp.zeros((weights.shape[0] - levels, width), f32)
     wide = jnp.concatenate([wide, more], 0)
     wide = jnp.concatenate([wide, jnp.zeros_like(wide)], 1)
     weights[...] = three_terms(wide, depth)
-    source_weights[...] = three_terms(jnp.concatenate([sources, more], 0), 16)
     sea = sea_mix[...]
     sea = jnp.concatenate([sea, jnp.zeros((sea_levels, 2 * width - sea_levels), f32)], 1)
     sea = jnp.concatenate([sea, jnp.zeros((sea_stride - sea_levels, 2 * width), f32)], 0)
@@ -215,17 +212,7 @@
                 x[i] = x[i] * before
                 x[-1 - i] = x[-1 - i] * behind
         for r in range(rows):
-            spread[pl.ds(pl.multiple_of(r * depth + c * 8, 8), 8), :] = x[r]
-
-    if depth > levels:
-        for r in range(rows):
-            spread[r * depth + levels : (r + 1) * depth, :] = jnp.zeros((depth - levels, width), f32)
-    w = weights[:, : 3 * depth]
-    for r in range(0, rows, 2):
-        x = jnp.concatenate([spread[(r + i) * depth : (r + i + 1) * depth, :] for i in range(2)], 1)
-        y = product(w, x)
-        for i in range(2):
-            middle[(r + i) * levels : (r + i + 1) * levels, :] = y[:levels, i * width : (i + 1) * width]
+            spread[pl.ds(pl.multiple_of(r * levels + c * 8, 8), 8), :] = x[r]
 
 
 def cross(x):
@@ -304,12 +291,12 @@
     send[...] = sums[half:]
 
 
-def rest_kernel(
-    sizes, fluxes, weights, source_weights, sea_weights, sea_ends, wet, below, above, middle, warm, salt,
-    out, brine_out, warm_out, salt_held, spread, sources, result, done
+def edge_kernel(
+    sizes, fluxes, own, sea_weights, sea_ends, wet, warm, salt, above, below, after,
+    spread, warm_out, brine_out, salt_held, done
 ):
     levels, rows, steps, sea_levels, sea_rows, stride, sea_stride = sizes
-    width = above.shape[1]
+    width = own.shape[1]
     depth = up_to(levels + 2 * steps, 16)
     flag = levels + steps + 2
     inside_above, inside_below = above[flag : flag + 1, :], below[flag : flag + 1, :]
@@ -324,20 +311,9 @@
             x[i] = x[i] * inside_above
             x[-1 - i] = x[-1 - i] * inside_below
     for r in range(rows):
-        sources[r * 16 : (r + 1) * 16, :] = jnp.concatenate([x[r], jnp.zeros((16 - 2 * steps, width), f32)], 0)
-
-    @pl.loop(0, levels // 8)
-    def _(c):
-        def other(ref, j):
-            return ref[pl.ds(pl.multiple_of(j * stride + c * 8, 8), 8), :]
-
-        top, low = ([other(ref, j) for j in range(HALO)] for ref in (above, below))
-        none = jnp.zeros_like(top[0])
-        for n in range(steps):
-            top = stencil(top + [none]) + [top[-1]]
-            low = [low[0]] + stencil([none] + low)
-        for i, value in enumerate(top + low):
-            spread[pl.ds(pl.multiple_of(i * depth + c * 8, 8), 8), :] = value
+        spread[r * depth + levels : (r + 1) * depth, :] = x[r]
+        if HALO <= r < rows - HALO:
+            spread[r * depth : r * depth + levels, :] = own[r * levels : (r + 1) * levels, :]
 
     warm_out[...] = warm[...]
     salt_held[...] = salt[...]
@@ -361,31 +337,49 @@
     leave = [pltpu.make_async_copy(salt_held, brine_out, done.at[0])]
     leave[0].start()
 
+    @pl.loop(0, levels // 8)
+    def _(c):
+        def other(ref, j):
+            return ref[pl.ds(pl.multiple_of(j * stride + c * 8, 8), 8), :]
+
+        top, low = ([other(ref, j) for j in range(HALO)] for ref in (above, below))
+        none = jnp.zeros_like(top[0])
+        for n in range(steps):
+            top = stencil(top + [none]) + [top[-1]]
+            low = [low[0]] + stencil([none] + low)
+        for i, value in enumerate(top + low):
+            r = i if i < HALO else rows - 2 * HALO + i
+            value = value + own[pl.ds(pl.multiple_of(r * levels + c * 8, 8), 8), :]
+            spread[pl.ds(pl.multiple_of(r * depth + c * 8, 8), 8), :] = value
+
+    for move in leave:
+        move.wait()
+
+
+def mix_kernel(sizes, spread, weights, after, out, result, done):
+    levels, rows, steps, sea_levels, sea_rows, stride, sea_stride = sizes
+    width = spread.shape[1]
+    depth = up_to(levels + 2 * steps, 16)
     w = weights[:, : 3 * depth]
-    v = source_weights[:, :48]
+    leave = []
     for g in range(rows // 8):
         to = result.at[g].reshape(levels * 8, width)
         for r in range(g * 8, g * 8 + 8, 2):
-            x = [sources[(r + q) * 16 : (r + q + 1) * 16, :] for q in range(2)]
-            if HALO <= r < rows - HALO:
-                y = product(v, jnp.concatenate(x, 1))
-            else:
-                i = r if r < HALO else r - rows + 2 * HALO
-                x = [
-                    jnp.concatenate(
-                        [spread[(i + q) * depth : (i + q) * depth + levels, :], x[q][: depth - levels]], 0
-                    )
-                    for q in range(2)
-                ]
-                y = product(w, jnp.concatenate(x, 1))
+            y = product(
+                w, jnp.concatenate([spread[(r + q) * depth : (r + q + 1) * depth, :] for q in range(2)], 1)
+            )
             for q in range(2):
-                to[pl.ds((r + q) % 8, levels, stride=8), :] = (
-                    middle[(r + q) * levels : (r + q + 1) * levels, :] + y[:levels, q * width : (q + 1) * width]
-                )
-        leave.append(pltpu.make_async_copy(result.at[g], out.at[:, g], done.at[1 + g]))
+                to[pl.ds((r + q) % 8, levels, stride=8), :] = y[:levels, q * width : (q + 1) * width]
+        leave.append(pltpu.make_async_copy(result.at[g], out.at[:, g], done.at[g]))
         leave[-1].start()
     for move in leave:
         move.wait()
+
+
+def add_kernel(keep, got, after, kept, send):
+    n = kept.shape[0]
+    kept[...] = keep[:n] + got[:n]
+    send[...] = keep[n:] + got[n:]
 
 
 def heat_kernel(sizes, kept, got, wet, sea_first, before, after):
@@ -434,18 +428,16 @@
     depth = up_to(levels + 2 * steps, 16)
     mix_rows = up_to(levels, 16)
     area = sea_levels * sea_rows
-    (
-        rows_of_mix, source_rows, own, weights, source_weights, sea_weights, sea_first, sea_ends, middle, warm, salt
-    ) = call(
+    rows_of_mix, source_rows, own, weights, sea_weights, sea_first, sea_ends, spread, warm, salt = call(
         functools.partial(local_kernel, sizes, count - 1),
         [
             flat((steps - 1) * levels), flat(8), flat((steps - 1) * rows),
-            jax.ShapeDtypeStruct((mix_rows, 2 * width), bf16), flat(mix_rows, bf16),
+            jax.ShapeDtypeStruct((mix_rows, 2 * width), bf16),
             jax.ShapeDtypeStruct((sea_stride, 2 * width), bf16), flat(sea_stride), flat(4 * sea_stride),
             flat(rows * levels), flat(area), flat(area),
         ],
         at, vmix, curve[None], sea_mix, sky2, warmth2, brine2, wet, in_specs=[SMEM] + [VMEM] * 7,
-        scratch=[space(rows * depth, width), space(2, sea_rows * sea_stride, width)],
+        scratch=[space(2, sea_rows * sea_stride, width)],
         flops=4 << 30, moved=8 << 20,
     )
 
@@ -457,25 +449,29 @@
         shares.reshape(-1, width), inner, outer,
         in_specs=[SMEM] * 2 + [VMEM] * 12, scratch=[space(2 * HALO * stride, width)], moved=2 << 20,
     )
-    bit = tiles // 2
+    bit, ready = tiles // 2, None
     while True:
         got = lax.ppermute(send, "tile", [(i, i ^ bit) for i in range(tiles)])
+        if bit <= 4 and ready is None:
+            ready, warm, salt = call(
+                functools.partial(edge_kernel, sizes), [flat(rows * depth), flat(area), flat(area)],
+                fluxes, spread, sea_weights, sea_ends, wet, warm, salt, above, below, keep,
+                in_specs=[VMEM] * 9 + [ANY], out_specs=[VMEM, VMEM, HBM],
+                scratch=[space(area, width), pltpu.SemaphoreType.DMA((1,))],
+                flops=1 << 28, moved=4 << 20,
+            )
         if bit == 1:
             break
+        keep, send = call(
+            add_kernel, [flat(bit // 2 * sea_rows)] * 2, keep, got, keep if ready is None else ready,
+            in_specs=[VMEM, VMEM, ANY],
+        )
         bit //= 2
-        both = keep + got
-        keep, send = both[: bit * sea_rows], both[bit * sea_rows :]
-
-    sky_out, salt, warm = call(
-        functools.partial(rest_kernel, sizes),
-        [jax.ShapeDtypeStruct((levels, rows // 8, 8, width), f32), flat(area), flat(area)],
-        fluxes, weights, source_weights, sea_weights, sea_ends, wet, below, above, middle, warm, salt,
-        out_specs=[HBM, HBM, VMEM],
-        scratch=[
-            space(area, width), space(2 * HALO * depth, width), space(rows * 16, width),
-            space(rows // 8, levels, 8, width), pltpu.SemaphoreType.DMA((1 + rows // 8,)),
-        ],
-        flops=2 << 30, moved=8 << 20,
+    sky_out = call(
+        functools.partial(mix_kernel, sizes), jax.ShapeDtypeStruct((levels, rows // 8, 8, width), f32),
+        ready, weights, keep, in_specs=[VMEM, VMEM, ANY], out_specs=HBM,
+        scratch=[space(rows // 8, levels, 8, width), pltpu.SemaphoreType.DMA((rows // 8,))],
+        flops=2 << 30, moved=4 << 20,
     )
     warm = call(functools.partial(heat_kernel, sizes), flat(area), keep, got, wet, sea_first, warm, moved=2 << 20)
     return sky_out.reshape(sky.shape), warm.reshape(warmth.shape), salt.reshape(brine.shape)

time: 30.6 us -> 28.7 us (0.938)
  waiting for transfers between devices: 3.66 us -> 2.49 us
  starting transfers between devices: 12.1 us -> 11.7 us
  Pallas kernels: 13.7 us -> 13.3 us
    ppermute x3, waiting for transfers between devices: 3.65 us -> 2.49 us  [body(): got = lax.ppermute(send, 'tile', [(i, i ^ bit) for i in range(tiles)])]
    pallas_call x5 -> x8, Pallas kernels: 13.7 us -> 13.3 us  [call(): pl.pallas_call(kernel, out_shape=out_shape, in_specs=in_specs or [VMEM] *...]
    ppermute x3, starting transfers between devices: 10.9 us -> 10.6 us  [body(): got = lax.ppermute(send, 'tile', [(i, i ^ bit) for i in range(tiles)])]
where the time goes in v10:
time: 28.7 us; the launch traced here: 28.5 us
  Pallas kernels  13.3 us (46%)
  starting transfers between devices  11.7 us (41%)
  waiting for transfers between devices  2.49 us (9%)
  between operations  0.94 us (3%)
    pallas_call x8, Pallas kernels, call(): pl.pallas_call(kernel, out_shape=out_shape, in_specs=in_specs or [VMEM] *...  13.3 us
    ppermute x3, starting transfers between devices, body(): got = lax.ppermute(send, 'tile', [(i, i ^ bit) for i in range(tiles)])  10.6 us
    ppermute x3, waiting for transfers between devices, body(): got = lax.ppermute(send, 'tile', [(i, i ^ bit) for i in range(tiles)])  2.49 us
    ppermute x1, starting transfers between devices, body(): outer = lax.ppermute(outer, ring, swap(1))  0.66 us
  transfers between devices with their start and end apart: 5, of which 2 were waited for; matrix products, arithmetic and copies ran while one was open for 0% of the time, Pallas kernels for 32%

profile of v10, /device:TPU:0, one launch (start us, length us, event | category | flops | bytes accessed | tf_op | source)
XLA Modules:
  0.0 28.5 jit_solution(6917317350716420513)
XLA Ops:
  0.6 0.0 copy-start.5
  0.6 0.0 copy-start
  0.7 0.0 copy-start.2
  0.7 0.0 copy-start.1
  0.7 0.0 copy-start.11
  0.7 0.0 copy-start.10
  0.7 0.0 copy-start.12
  0.7 2.5 %shard_map.149 = (f32[456,128]{1,0:T(8,128)}, f32[456,128]{1,0:T(8,128)}) custom-call(s32[1]{0:T(128)} %bitcast.core, f32[72,32,128]{2,1,0:T(8,128)} %sky.1, f32[4,32,128]{2,1,0:T(8,128)} %forcing.1, f32[32,128]{1,0:T(8,128)} %surface.3, f32[32,128]{1,0:T(8,128)} %rate.3, f32[992,128]{1,0:T(8,128)} %bitcast.17, f32[992,128]{1,0:T(8,128)} %bitcast.19, ...), custom_call_target="tpu_custom_call" | custom-call | bytes 4194304 | tf_op jit(solution)/shard_map/pallas_call | solution.py:27
  3.2 0.5 %collective-permute-start = (f32[456,128]{1,0:T(8,128)}, f32[456,128]{1,0:T(8,128)S(1)}, u32[]{:S(2)}, u32[]{:S(2)}) collective-permute-start(f32[456,128]{1,0:T(8,128)} %get-tuple-element.30), channel_id=1, source_target_pairs={{0,1},{1,0},{2,3},{3,2},{4,5},{5,4},{6,7},{7,6},{8,9},{9,8},{10,11... | collective-permute-start | bytes 700424 | tf_op jit(solution)/shard_map/ppermute | solution.py:425
  3.7 0.7 %collective-permute-start.1 = (f32[456,128]{1,0:T(8,128)}, f32[456,128]{1,0:T(8,128)S(1)}, u32[]{:S(2)}, u32[]{:S(2)}) collective-permute-start(f32[456,128]{1,0:T(8,128)} %get-tuple-element.31), channel_id=1, source_target_pairs={{1,2},{2,1},{3,4},{4,3},{5,6},{6,5},{7,8},{8,7},{9,10},{10,9},{11,... | collective-permute-start | bytes 700424 | tf_op jit(solution)/shard_map/ppermute | solution.py:426
  4.4 0.0 copy-done.5
  4.4 0.0 copy-done
  4.4 0.0 copy-done.2
  4.5 0.0 copy-start.3
  4.5 0.0 copy-start.4
  4.5 0.0 copy-start.6
  4.5 0.0 copy-start.7
  4.5 0.0 copy-start.8
  4.6 0.0 copy-start.9
  4.6 5.5 %shard_map.148 = (f32[216,128]{1,0:T(8,128)S(1)}, f32[8,128]{1,0:T(8,128)S(1)}, f32[96,128]{1,0:T(8,128)S(1)}, bf16[80,256]{1,0:T(8,128)(2,1)S(1)}, bf16[64,256]...) custom-call(s32[1]{0:T(128)} %bitcast.4.place, ...), custom_call_target="tpu_custom_call" | custom-call | flops 4294967296 | bytes 8388608 | tf_op jit(solution)/shard_map/pallas_call | solution.py:27
  10.0 0.0 collective-permute-done.inner
  10.1 0.0 collective-permute-done.1.outer
  10.1 0.7 %shard_map.150 = (f32[64,128]{1,0:T(8,128)S(1)}, f32[64,128]{1,0:T(8,128)S(1)}, f32[320,128]{1,0:T(8,128)S(1)}, f32[456,128]{1,0:T(8,128)S(1)}, f32[456,128]{1,0:T(8,128)S(1)}) custom-call(s32[1]{0:T(128)} %bitcast.core, s32[1]{0:T(128)} %bitcast.1.tile, f32[32,128]{1,0:T(8,128)S(1)} %slice_bitcast_fusion.sky, f32[128,128]{1,0:T(8,128)S(1)} %bitcast.21, ...), custom_call_target="tpu_custom_call" | custom-call | bytes 2097152 | tf_op jit(solution)/shard_map/pallas_call | solution.py:27
  10.8 6.4 %collective-permute-start.2 = (f32[64,128]{1,0:T(8,128)S(1)}, f32[64,128]{1,0:T(8,128)S(1)}, u32[]{:S(2)}, u32[]{:S(2)}) collective-permute-start(f32[64,128]{1,0:T(8,128)S(1)} %get-tuple-element.43), channel_id=1, source_target_pairs={{0,8},{2,10},{4,12},{6,14},{8,0},{10,2},{12,4},{14,6},{1,9},{3,11}... | collective-permute-start | bytes 98312 | tf_op jit(solution)/shard_map/ppermute | solution.py:454
  17.2 2.5 %shard_map.151 = (f32[2560,128]{1,0:T(8,128)S(1)}, f32[992,128]{1,0:T(8,128)S(1)}, f32[992,128]{1,0:T(8,128)}) custom-call(f32[320,128]{1,0:T(8,128)S(1)} %get-tuple-element.32.fluxes, f32[2304,128]{1,0:T(8,128)S(1)} %get-tuple-element.33.own, bf16[64,256]{1,0:T(8,128)(2,1)S(1)} %get-tuple-element.34.sea_weights, f32[256,128]{1,0:T(8,128)S(1)} %get-tuple-element.35.sea_ends, ...), custom_call_target="tpu_custom_call" | custom-call | flops 268435456 | bytes 4194304 | tf_op jit(solution)/shard_map/pallas_call | solution.py:27
  19.7 0.0 collective-permute-done.2.got
  19.7 1.6 %collective-permute-start.3 = (f32[32,128]{1,0:T(8,128)S(1)}, f32[32,128]{1,0:T(8,128)S(1)}, u32[]{:S(2)}, u32[]{:S(2)}) collective-permute-start(f32[32,128]{1,0:T(8,128)S(1)} %get-tuple-element.45), channel_id=1, source_target_pairs={{0,4},{2,6},{4,0},{6,2},{8,12},{10,14},{12,8},{14,10},{1,5},{3,7},... | collective-permute-start | bytes 49160 | tf_op jit(solution)/shard_map/ppermute | solution.py:454
  21.3 2.2 %collective-permute-done.3.got = f32[32,128]{1,0:T(8,128)S(1)} collective-permute-done((f32[32,128]{1,0:T(8,128)S(1)}, f32[32,128]{1,0:T(8,128)S(1)}, u32[]{:S(2)}, u32[]{:S(2)}) %collective-permute-start.3) | collective-permute-done | bytes 16416 | tf_op jit(solution)/shard_map/ppermute | solution.py:454
  23.5 2.5 %collective-permute-start.4 = (f32[16,128]{1,0:T(8,128)S(1)}, f32[16,128]{1,0:T(8,128)S(1)}, u32[]{:S(2)}, u32[]{:S(2)}) collective-permute-start(f32[16,128]{1,0:T(8,128)S(1)} %get-tuple-element.47), channel_id=1, source_target_pairs={{0,2},{2,0},{4,6},{6,4},{8,10},{10,8},{12,14},{14,12},{1,3},{3,1},... | collective-permute-start | bytes 24584 | tf_op jit(solution)/shard_map/ppermute | solution.py:454
  26.0 1.3 %shard_map.154 = f32[72,4,8,128]{3,2,1,0:T(8,128)} custom-call(f32[2560,128]{1,0:T(8,128)S(1)} %get-tuple-element.41.after.spread, bf16[80,256]{1,0:T(8,128)(2,1)S(1)} %get-tuple-element.42.weights, f32[16,128]{1,0:T(8,128)S(1)} %get-tuple-element.46.after.kept), custom_call_target="tpu_custom_call" | custom-call | flops 2147483648 | bytes 4194304 | tf_op jit(solution)/shard_map/pallas_call | solution.py:27
  27.3 0.3 %collective-permute-done.4.got = f32[16,128]{1,0:T(8,128)S(1)} collective-permute-done((f32[16,128]{1,0:T(8,128)S(1)}, f32[16,128]{1,0:T(8,128)S(1)}, u32[]{:S(2)}, u32[]{:S(2)}) %collective-permute-start.4) | collective-permute-done | bytes 8224 | tf_op jit(solution)/shard_map/ppermute | solution.py:454
  27.7 0.8 %shard_map.155 = f32[992,128]{1,0:T(8,128)} custom-call(f32[16,128]{1,0:T(8,128)S(1)} %get-tuple-element.46.after.kept, f32[16,128]{1,0:T(8,128)S(1)} %collective-permute-done.4.got, s32[16,128]{1,0:T(8,128)S(1)} %copy-done.5, f32[64,128]{1,0:T(8,128)S(1)} %get-tuple-element.48.sea_first, f32[992,128]{1,0:T(8,128)S(1)} %get-tuple-element.49.before), custom_call_target="tpu_custom_call" | custom-call | bytes 2097152 | tf_op jit(solution)/shard_map/pallas_call | solution.py:27
  (13 shorter events, 0.0 us)
Async XLA Ops:
  0.6 3.8 %copy-start.5 = (s32[16,128]{1,0:T(8,128)S(1)}, s32[16,128]{1,0:T(8,128)}, u32[]{:S(2)}) copy-start(s32[16,128]{1,0:T(8,128)} %wet.7) | copy-start | bytes 24580
  0.6 3.8 %copy-start = (f32[72,32,128]{2,1,0:T(8,128)S(1)}, f32[72,32,128]{2,1,0:T(8,128)}, u32[]{:S(2)}) copy-start(f32[72,32,128]{2,1,0:T(8,128)} %sky.1) | copy-start | bytes 3538948
  0.7 3.8 %copy-start.2 = (f32[62,16,128]{2,1,0:T(8,128)S(1)}, f32[62,16,128]{2,1,0:T(8,128)}, u32[]{:S(2)}) copy-start(f32[62,16,128]{2,1,0:T(8,128)} %param.23) | copy-start | bytes 1523716
  0.7 3.8 %copy-start.1 = (f32[62,16,128]{2,1,0:T(8,128)S(1)}, f32[62,16,128]{2,1,0:T(8,128)}, u32[]{:S(2)}) copy-start(f32[62,16,128]{2,1,0:T(8,128)} %param.22) | copy-start | bytes 1523716
  0.7 3.8 %copy-start.11 = (f32[62,62]{1,0:T(8,128)S(1)}, f32[62,62]{1,0:T(8,128)}, u32[]{:S(2)}) copy-start(f32[62,62]{1,0:T(8,128)} %sea_mix.1) | copy-start | bytes 46132
  0.7 3.8 %copy-start.10 = (f32[72,72]{1,0:T(8,128)S(1)}, f32[72,72]{1,0:T(8,128)}, u32[]{:S(2)}) copy-start(f32[72,72]{1,0:T(8,128)} %vmix.1) | copy-start | bytes 62212
  0.7 3.8 %copy-start.12 = (f32[72]{0:T(128)S(1)}, f32[72]{0:T(128)}, u32[]{:S(2)}) copy-start(f32[72]{0:T(128)} %param.15) | copy-start | bytes 868
  3.2 6.8 %collective-permute-start = (f32[456,128]{1,0:T(8,128)}, f32[456,128]{1,0:T(8,128)S(1)}, u32[]{:S(2)}, u32[]{:S(2)}) collective-permute-start(f32[456,128]{1,0:T(8,128)} %get-tuple-element.30), channel_id=1, source_target_pairs={{0,1},{1,0},{2,3},{3,2},{4,5},{5,4},{6,7},{7,6},{8,9},{9,8},{10,11... | collective-permute-start | bytes 700424 | tf_op jit(solution)/shard_map/ppermute | solution.py:425
  3.7 6.3 %collective-permute-start.1 = (f32[456,128]{1,0:T(8,128)}, f32[456,128]{1,0:T(8,128)S(1)}, u32[]{:S(2)}, u32[]{:S(2)}) collective-permute-start(f32[456,128]{1,0:T(8,128)} %get-tuple-element.31), channel_id=1, source_target_pairs={{1,2},{2,1},{3,4},{4,3},{5,6},{6,5},{7,8},{8,7},{9,10},{10,9},{11,... | collective-permute-start | bytes 700424 | tf_op jit(solution)/shard_map/ppermute | solution.py:426
  4.5 5.6 %copy-start.3 = (f32[4,32,128]{2,1,0:T(8,128)S(1)}, f32[4,32,128]{2,1,0:T(8,128)}, u32[]{:S(2)}) copy-start(f32[4,32,128]{2,1,0:T(8,128)} %forcing.1) | copy-start | bytes 196612
  4.5 5.6 %copy-start.4 = (bf16[4,128,128]{2,1,0:T(8,128)(2,1)S(1)}, bf16[4,128,128]{2,1,0:T(8,128)(2,1)}, u32[]{:S(2)}) copy-start(bf16[4,128,128]{2,1,0:T(8,128)(2,1)} %param.19) | copy-start | bytes 393220
  4.5 5.6 %copy-start.6 = (f32[32,128]{1,0:T(8,128)S(1)}, f32[32,128]{1,0:T(8,128)}, u32[]{:S(2)}) copy-start(f32[32,128]{1,0:T(8,128)} %surface.3) | copy-start | bytes 49156
  4.5 5.6 %copy-start.7 = (f32[32,128]{1,0:T(8,128)S(1)}, f32[32,128]{1,0:T(8,128)}, u32[]{:S(2)}) copy-start(f32[32,128]{1,0:T(8,128)} %rate.3) | copy-start | bytes 49156
  4.5 5.6 %copy-start.8 = (s32[32,4]{0,1:T(4,128)S(1)}, s32[32,4]{0,1:T(4,128)}, u32[]{:S(2)}) copy-start(s32[32,4]{0,1:T(4,128)} %param.20) | copy-start | bytes 1540
  4.6 5.6 %copy-start.9 = (s32[32,4]{0,1:T(4,128)S(1)}, s32[32,4]{0,1:T(4,128)}, u32[]{:S(2)}) copy-start(s32[32,4]{0,1:T(4,128)} %param.21) | copy-start | bytes 1540
  10.8 8.8 %collective-permute-start.2 = (f32[64,128]{1,0:T(8,128)S(1)}, f32[64,128]{1,0:T(8,128)S(1)}, u32[]{:S(2)}, u32[]{:S(2)}) collective-permute-start(f32[64,128]{1,0:T(8,128)S(1)} %get-tuple-element.43), channel_id=1, source_target_pairs={{0,8},{2,10},{4,12},{6,14},{8,0},{10,2},{12,4},{14,6},{1,9},{3,11}... | collective-permute-start | bytes 98312 | tf_op jit(solution)/shard_map/ppermute | solution.py:454
  19.7 3.8 %collective-permute-start.3 = (f32[32,128]{1,0:T(8,128)S(1)}, f32[32,128]{1,0:T(8,128)S(1)}, u32[]{:S(2)}, u32[]{:S(2)}) collective-permute-start(f32[32,128]{1,0:T(8,128)S(1)} %get-tuple-element.45), channel_id=1, source_target_pairs={{0,4},{2,6},{4,0},{6,2},{8,12},{10,14},{12,8},{14,10},{1,5},{3,7},... | collective-permute-start | bytes 49160 | tf_op jit(solution)/shard_map/ppermute | solution.py:454
  23.5 4.2 %collective-permute-start.4 = (f32[16,128]{1,0:T(8,128)S(1)}, f32[16,128]{1,0:T(8,128)S(1)}, u32[]{:S(2)}, u32[]{:S(2)}) collective-permute-start(f32[16,128]{1,0:T(8,128)S(1)} %get-tuple-element.47), channel_id=1, source_target_pairs={{0,2},{2,0},{4,6},{6,4},{8,10},{10,8},{12,14},{14,12},{1,3},{3,1},... | collective-permute-start | bytes 24584 | tf_op jit(solution)/shard_map/ppermute | solution.py:454

commit v11 on v10

--- a/solution.py
+++ b/solution.py
@@ -227,7 +227,7 @@
 
 
 def flux_kernel(
-    sizes, core, tile, sky, forcing, surface, rate, rows_of_mix, source_rows, own, owners, locals_, shares, inner, outer,
+    sizes, core, tile, sky, forcing, surface, rate, rows_of_mix, source_rows, own, owners, locals_, shares, outer, inner,
     keep, send, fluxes, above, below, halo
 ):
     levels, rows, steps, sea_levels, sea_rows, stride, sea_stride = sizes
@@ -292,8 +292,7 @@
 
 
 def edge_kernel(
-    sizes, fluxes, own, sea_weights, sea_ends, wet, warm, salt, above, below, after,
-    spread, warm_out, brine_out, salt_held, done
+    sizes, fluxes, own, above, below, after, spread
 ):
     levels, rows, steps, sea_levels, sea_rows, stride, sea_stride = sizes
     width = own.shape[1]
@@ -315,6 +314,27 @@
         if HALO <= r < rows - HALO:
             spread[r * depth : r * depth + levels, :] = own[r * levels : (r + 1) * levels, :]
 
+    @pl.loop(0, levels // 8)
+    def _(c):
+        def other(ref, j):
+            return ref[pl.ds(pl.multiple_of(j * stride + c * 8, 8), 8), :]
+
+        top, low = ([other(ref, j) for j in range(HALO)] for ref in (above, below))
+        none = jnp.zeros_like(top[0])
+        for n in range(steps):
+            top = stencil(top + [none]) + [top[-1]]
+            low = [low[0]] + stencil([none] + low)
+        for i, value in enumerate(top + low):
+            r = i if i < HALO else rows - 2 * HALO + i
+            value = value + own[pl.ds(pl.multiple_of(r * levels + c * 8, 8), 8), :]
+            spread[pl.ds(pl.multiple_of(r * depth + c * 8, 8), 8), :] = value
+
+
+def shore_kernel(
+    sizes, sea_weights, sea_ends, wet, warm, salt, above, below, after, warm_out, brine_out, salt_held, done
+):
+    levels, rows, steps, sea_levels, sea_rows, stride, sea_stride = sizes
+    width = warm.shape[1]
     warm_out[...] = warm[...]
     salt_held[...] = salt[...]
     m = wet[...].astype(f32)
@@ -336,22 +356,6 @@
             to[rows_at, :] = to[rows_at, :] + mark * y[:sea_levels, f * width : (f + 1) * width]
     leave = [pltpu.make_async_copy(salt_held, brine_out, done.at[0])]
     leave[0].start()
-
-    @pl.loop(0, levels // 8)
-    def _(c):
-        def other(ref, j):
-            return ref[pl.ds(pl.multiple_of(j * stride + c * 8, 8), 8), :]
-
-        top, low = ([other(ref, j) for j in range(HALO)] for ref in (above, below))
-        none = jnp.zeros_like(top[0])
-        for n in range(steps):
-            top = stencil(top + [none]) + [top[-1]]
-            low = [low[0]] + stencil([none] + low)
-        for i, value in enumerate(top + low):
-            r = i if i < HALO else rows - 2 * HALO + i
-            value = value + own[pl.ds(pl.multiple_of(r * levels + c * 8, 8), 8), :]
-            spread[pl.ds(pl.multiple_of(r * depth + c * 8, 8), 8), :] = value
-
     for move in leave:
         move.wait()
 
@@ -422,8 +426,8 @@
         grant=FULL,
     )
     swap = lambda first: [(i + a, i + 1 - a) for i in range(first, count - 1, 2) for a in range(2)]
+    outer = lax.ppermute(outer, ring, swap(1))
     inner = lax.ppermute(inner, ring, swap(0))
-    outer = lax.ppermute(outer, ring, swap(1))
 
     depth = up_to(levels + 2 * steps, 16)
     mix_rows = up_to(levels, 16)
@@ -446,27 +450,41 @@
         functools.partial(flux_kernel, sizes),
         [flat(half), flat(half), flat(2 * steps * (rows + 2 * HALO)), flat(length), flat(length)],
         core, tile, sky[-1], forcing2, surface, rate, rows_of_mix, source_rows, own, owners.T, locals_.T,
-        shares.reshape(-1, width), inner, outer,
+        shares.reshape(-1, width), outer, inner,
         in_specs=[SMEM] * 2 + [VMEM] * 12, scratch=[space(2 * HALO * stride, width)], moved=2 << 20,
     )
-    bit, ready = tiles // 2, None
+    def edge_part(after):
+        return call(
+            functools.partial(edge_kernel, sizes), flat(rows * depth), fluxes, spread, above, below, after,
+            in_specs=[VMEM] * 4 + [ANY], flops=1 << 28, moved=4 << 20,
+        )
+
+    def shore_part(after):
+        return call(
+            functools.partial(shore_kernel, sizes), [flat(area), flat(area)],
+            sea_weights, sea_ends, wet, warm, salt, above, below, after,
+            in_specs=[VMEM] * 7 + [ANY], out_specs=[VMEM, HBM],
+            scratch=[space(area, width), pltpu.SemaphoreType.DMA((1,))], flops=1 << 28, moved=4 << 20,
+        )
+
+    bit, ready, shore = tiles // 2, None, None
     while True:
         got = lax.ppermute(send, "tile", [(i, i ^ bit) for i in range(tiles)])
         if bit <= 4 and ready is None:
-            ready, warm, salt = call(
-                functools.partial(edge_kernel, sizes), [flat(rows * depth), flat(area), flat(area)],
-                fluxes, spread, sea_weights, sea_ends, wet, warm, salt, above, below, keep,
-                in_specs=[VMEM] * 9 + [ANY], out_specs=[VMEM, VMEM, HBM],
-                scratch=[space(area, width), pltpu.SemaphoreType.DMA((1,))],
-                flops=1 << 28, moved=4 << 20,
-            )
+            ready = edge_part(keep)
+            done = ready
+        elif ready is not None and shore is None:
+            shore = shore_part(keep)
+            done = shore[0]
+        else:
+            done = keep
         if bit == 1:
             break
         keep, send = call(
-            add_kernel, [flat(bit // 2 * sea_rows)] * 2, keep, got, keep if ready is None else ready,
-            in_specs=[VMEM, VMEM, ANY],
+            add_kernel, [flat(bit // 2 * sea_rows)] * 2, keep, got, done, in_specs=[VMEM, VMEM, ANY],
         )
         bit //= 2
+    warm, salt = shore_part(keep) if shore is None else shore
     sky_out = call(
         functools.partial(mix_kernel, sizes), jax.ShapeDtypeStruct((levels, rows // 8, 8, width), f32),
         ready, weights, keep, in_specs=[VMEM, VMEM, ANY], out_specs=HBM,

time: 28.7 us -> 28.4 us (0.990)
  waiting for transfers between devices: 2.49 us -> 1.51 us
  Pallas kernels: 13.3 us -> 14.1 us
    ppermute x3, starting transfers between devices: 10.6 us -> 6.66 us  [body(): got = lax.ppermute(send, 'tile', [(i, i ^ bit) for i in range(tiles)])]
    ppermute x1, starting transfers between devices: 0.52 us -> 4.35 us  [body(): inner = lax.ppermute(inner, ring, swap(0))]
    ppermute x3, waiting for transfers between devices: 2.49 us -> 1.51 us  [body(): got = lax.ppermute(send, 'tile', [(i, i ^ bit) for i in range(tiles)])]
    pallas_call x8 -> x9, Pallas kernels: 13.3 us -> 14.1 us  [call(): pl.pallas_call(kernel, out_shape=out_shape, in_specs=in_specs or [VMEM] *...]
  transfers between devices with their start and end apart: 5 -> 5, of which waited for: 2 -> 3; matrix products, arithmetic and copies ran while one was open for 0% -> 0% of each run, Pallas kernels for 32% -> 36%
where the time goes in v11:
time: 28.4 us; the launch traced here: 28.2 us
  Pallas kernels  14.1 us (50%)
  starting transfers between devices  11.7 us (41%)
  waiting for transfers between devices  1.51 us (5%)
  between operations  0.89 us (3%)
    pallas_call x9, Pallas kernels, call(): pl.pallas_call(kernel, out_shape=out_shape, in_specs=in_specs or [VMEM] *...  14.1 us
    ppermute x3, starting transfers between devices, body(): got = lax.ppermute(send, 'tile', [(i, i ^ bit) for i in range(tiles)])  6.66 us
    ppermute x1, starting transfers between devices, body(): inner = lax.ppermute(inner, ring, swap(0))  4.35 us
    ppermute x3, waiting for transfers between devices, body(): got = lax.ppermute(send, 'tile', [(i, i ^ bit) for i in range(tiles)])  1.51 us
    ppermute x1, starting transfers between devices, body(): outer = lax.ppermute(outer, ring, swap(1))  0.68 us
  transfers between devices with their start and end apart: 5, of which 3 were waited for; matrix products, arithmetic and copies ran while one was open for 0% of the time, Pallas kernels for 36%

profile of v11, /device:TPU:0, one launch (start us, length us, event | category | flops | bytes accessed | tf_op | source)
XLA Modules:
  0.0 28.2 jit_solution(17757605193807759265)
XLA Ops:
  0.7 2.5 %shard_map.149 = (f32[456,128]{1,0:T(8,128)}, f32[456,128]{1,0:T(8,128)}) custom-call(s32[1]{0:T(128)} %bitcast.core, f32[72,32,128]{2,1,0:T(8,128)} %sky.1, f32[4,32,128]{2,1,0:T(8,128)} %forcing.1, f32[32,128]{1,0:T(8,128)} %surface.3, f32[32,128]{1,0:T(8,128)} %rate.3, f32[992,128]{1,0:T(8,128)} %bitcast.17, f32[992,128]{1,0:T(8,128)} %bitcast.19, ...), custom_call_target="tpu_custom_call" | custom-call | bytes 4194304 | tf_op jit(solution)/shard_map/pallas_call | solution.py:27
  3.2 0.7 %collective-permute-start = (f32[456,128]{1,0:T(8,128)}, f32[456,128]{1,0:T(8,128)S(1)}, u32[]{:S(2)}, u32[]{:S(2)}) collective-permute-start(f32[456,128]{1,0:T(8,128)} %get-tuple-element.29), channel_id=1, source_target_pairs={{1,2},{2,1},{3,4},{4,3},{5,6},{6,5},{7,8},{8,7},{9,10},{10,9},{11,... | collective-permute-start | bytes 700424 | tf_op jit(solution)/shard_map/ppermute | solution.py:429
  3.9 4.4 %collective-permute-start.1 = (f32[456,128]{1,0:T(8,128)}, f32[456,128]{1,0:T(8,128)S(1)}, u32[]{:S(2)}, u32[]{:S(2)}) collective-permute-start(f32[456,128]{1,0:T(8,128)} %get-tuple-element.30), channel_id=1, source_target_pairs={{0,1},{1,0},{2,3},{3,2},{4,5},{5,4},{6,7},{7,6},{8,9},{9,8},{10,11... | collective-permute-start | bytes 700424 | tf_op jit(solution)/shard_map/ppermute | solution.py:430
  8.3 0.0 copy-done.5
  8.3 0.0 copy-done.11
  8.3 0.0 copy-done.10
  8.3 0.0 copy-done.12
  8.3 0.0 copy-start.3
  8.3 0.0 copy-start.4
  8.3 0.0 copy-start.6
  8.3 0.0 copy-start.7
  8.4 0.0 copy-start.8
  8.4 0.0 copy-start.9
  8.4 5.5 %shard_map.148 = (f32[216,128]{1,0:T(8,128)S(1)}, f32[8,128]{1,0:T(8,128)S(1)}, f32[96,128]{1,0:T(8,128)S(1)}, bf16[80,256]{1,0:T(8,128)(2,1)S(1)}, bf16[64,256]...) custom-call(s32[1]{0:T(128)} %bitcast.4.place, ...), custom_call_target="tpu_custom_call" | custom-call | flops 4294967296 | bytes 8388608 | tf_op jit(solution)/shard_map/pallas_call | solution.py:27
  13.9 0.0 collective-permute-done.outer
  13.9 0.0 collective-permute-done.1.inner
  13.9 0.0 copy-done.3
  13.9 0.0 copy-done.4
  13.9 0.0 copy-done.6
  13.9 0.0 copy-done.7
  13.9 0.0 copy-done.8
  13.9 0.7 %shard_map.150 = (f32[64,128]{1,0:T(8,128)S(1)}, f32[64,128]{1,0:T(8,128)S(1)}, f32[320,128]{1,0:T(8,128)S(1)}, f32[456,128]{1,0:T(8,128)S(1)}, f32[456,128]{1,0:T(8,128)S(1)}) custom-call(s32[1]{0:T(128)} %bitcast.core, s32[1]{0:T(128)} %bitcast.1.tile, f32[32,128]{1,0:T(8,128)S(1)} %slice_bitcast_fusion.sky, f32[128,128]{1,0:T(8,128)S(1)} %bitcast.21, ...), custom_call_target="tpu_custom_call" | custom-call | bytes 2097152 | tf_op jit(solution)/shard_map/pallas_call | solution.py:27
  14.6 2.7 %collective-permute-start.2 = (f32[64,128]{1,0:T(8,128)S(1)}, f32[64,128]{1,0:T(8,128)S(1)}, u32[]{:S(2)}, u32[]{:S(2)}) collective-permute-start(f32[64,128]{1,0:T(8,128)S(1)} %get-tuple-element.37), channel_id=1, source_target_pairs={{0,8},{2,10},{4,12},{6,14},{8,0},{10,2},{12,4},{14,6},{1,9},{3,11}... | collective-permute-start | bytes 98312 | tf_op jit(solution)/shard_map/ppermute | solution.py:472
  17.3 2.3 %shard_map.151.after.spread = f32[2560,128]{1,0:T(8,128)S(1)} custom-call(f32[320,128]{1,0:T(8,128)S(1)} %get-tuple-element.31.fluxes, f32[2304,128]{1,0:T(8,128)S(1)} %get-tuple-element.32.own, f32[456,128]{1,0:T(8,128)S(1)} %get-tuple-element.33.above, f32[456,128]{1,0:T(8,128)S(1)} %get-tuple-element.34.below, f32[64,128]{1,0:T(8,128)S(1)} %get-tuple-element.35.after.keep), custom_call_target="tpu_custom_call" | custom-call | flops 268435456 | bytes 4194304 | tf_op jit(solution)/shard_map/pallas_call | solution.py:27
  19.5 0.1 collective-permute-done.2.got
  19.6 1.6 %collective-permute-start.3 = (f32[32,128]{1,0:T(8,128)S(1)}, f32[32,128]{1,0:T(8,128)S(1)}, u32[]{:S(2)}, u32[]{:S(2)}) collective-permute-start(f32[32,128]{1,0:T(8,128)S(1)} %get-tuple-element.39), channel_id=1, source_target_pairs={{0,4},{2,6},{4,0},{6,2},{8,12},{10,14},{12,8},{14,10},{1,5},{3,7},... | collective-permute-start | bytes 49160 | tf_op jit(solution)/shard_map/ppermute | solution.py:472
  21.2 1.0 %shard_map.153 = (f32[992,128]{1,0:T(8,128)S(1)}, f32[992,128]{1,0:T(8,128)}) custom-call(bf16[64,256]{1,0:T(8,128)(2,1)S(1)} %get-tuple-element.40.sea_weights, f32[256,128]{1,0:T(8,128)S(1)} %get-tuple-element.41.sea_ends, s32[16,128]{1,0:T(8,128)S(1)} %copy-done.5, f32[992,128]{1,0:T(8,128)S(1)} %get-tuple-element.42.warm, ...), custom_call_target="tpu_custom_call" | custom-call | flops 268435456 | bytes 4194304 | tf_op jit(solution)/shard_map/pallas_call | solution.py:27
  22.3 1.1 %collective-permute-done.3.got = f32[32,128]{1,0:T(8,128)S(1)} collective-permute-done((f32[32,128]{1,0:T(8,128)S(1)}, f32[32,128]{1,0:T(8,128)S(1)}, u32[]{:S(2)}, u32[]{:S(2)}) %collective-permute-start.3) | collective-permute-done | bytes 16416 | tf_op jit(solution)/shard_map/ppermute | solution.py:472
  23.4 2.4 %collective-permute-start.4 = (f32[16,128]{1,0:T(8,128)S(1)}, f32[16,128]{1,0:T(8,128)S(1)}, u32[]{:S(2)}, u32[]{:S(2)}) collective-permute-start(f32[16,128]{1,0:T(8,128)S(1)} %get-tuple-element.46), channel_id=1, source_target_pairs={{0,2},{2,0},{4,6},{6,4},{8,10},{10,8},{12,14},{14,12},{1,3},{3,1},... | collective-permute-start | bytes 24584 | tf_op jit(solution)/shard_map/ppermute | solution.py:472
  25.8 1.3 %shard_map.155 = f32[72,4,8,128]{3,2,1,0:T(8,128)} custom-call(f32[2560,128]{1,0:T(8,128)S(1)} %shard_map.151.after.spread, bf16[80,256]{1,0:T(8,128)(2,1)S(1)} %get-tuple-element.36.weights, f32[16,128]{1,0:T(8,128)S(1)} %get-tuple-element.45.after.kept), custom_call_target="tpu_custom_call" | custom-call | flops 2147483648 | bytes 4194304 | tf_op jit(solution)/shard_map/pallas_call | solution.py:27
  27.1 0.3 %collective-permute-done.4.got = f32[16,128]{1,0:T(8,128)S(1)} collective-permute-done((f32[16,128]{1,0:T(8,128)S(1)}, f32[16,128]{1,0:T(8,128)S(1)}, u32[]{:S(2)}, u32[]{:S(2)}) %collective-permute-start.4) | collective-permute-done | bytes 8224 | tf_op jit(solution)/shard_map/ppermute | solution.py:472
  27.4 0.8 %shard_map.156 = f32[992,128]{1,0:T(8,128)} custom-call(f32[16,128]{1,0:T(8,128)S(1)} %get-tuple-element.45.after.kept, f32[16,128]{1,0:T(8,128)S(1)} %collective-permute-done.4.got, s32[16,128]{1,0:T(8,128)S(1)} %copy-done.5, f32[64,128]{1,0:T(8,128)S(1)} %get-tuple-element.47.sea_first, f32[992,128]{1,0:T(8,128)S(1)} %get-tuple-element.44.after.before), custom_call_target="tpu_custom_call" | custom-call | bytes 2097152 | tf_op jit(solution)/shard_map/pallas_call | solution.py:27
  (14 shorter events, 0.0 us)
Async XLA Ops:
  0.6 7.6 %copy-start.5 = (s32[16,128]{1,0:T(8,128)S(1)}, s32[16,128]{1,0:T(8,128)}, u32[]{:S(2)}) copy-start(s32[16,128]{1,0:T(8,128)} %wet.7) | copy-start | bytes 24580
  0.6 7.6 %copy-start = (f32[72,32,128]{2,1,0:T(8,128)S(1)}, f32[72,32,128]{2,1,0:T(8,128)}, u32[]{:S(2)}) copy-start(f32[72,32,128]{2,1,0:T(8,128)} %sky.1) | copy-start | bytes 3538948
  0.7 7.6 %copy-start.2 = (f32[62,16,128]{2,1,0:T(8,128)S(1)}, f32[62,16,128]{2,1,0:T(8,128)}, u32[]{:S(2)}) copy-start(f32[62,16,128]{2,1,0:T(8,128)} %param.23) | copy-start | bytes 1523716
  0.7 7.6 %copy-start.1 = (f32[62,16,128]{2,1,0:T(8,128)S(1)}, f32[62,16,128]{2,1,0:T(8,128)}, u32[]{:S(2)}) copy-start(f32[62,16,128]{2,1,0:T(8,128)} %param.22) | copy-start | bytes 1523716
  0.7 7.6 %copy-start.11 = (f32[62,62]{1,0:T(8,128)S(1)}, f32[62,62]{1,0:T(8,128)}, u32[]{:S(2)}) copy-start(f32[62,62]{1,0:T(8,128)} %sea_mix.1) | copy-start | bytes 46132
  0.7 7.6 %copy-start.10 = (f32[72,72]{1,0:T(8,128)S(1)}, f32[72,72]{1,0:T(8,128)}, u32[]{:S(2)}) copy-start(f32[72,72]{1,0:T(8,128)} %vmix.1) | copy-start | bytes 62212
  0.7 7.6 %copy-start.12 = (f32[72]{0:T(128)S(1)}, f32[72]{0:T(128)}, u32[]{:S(2)}) copy-start(f32[72]{0:T(128)} %param.15) | copy-start | bytes 868
  3.2 10.6 %collective-permute-start = (f32[456,128]{1,0:T(8,128)}, f32[456,128]{1,0:T(8,128)S(1)}, u32[]{:S(2)}, u32[]{:S(2)}) collective-permute-start(f32[456,128]{1,0:T(8,128)} %get-tuple-element.29), channel_id=1, source_target_pairs={{1,2},{2,1},{3,4},{4,3},{5,6},{6,5},{7,8},{8,7},{9,10},{10,9},{11,... | collective-permute-start | bytes 700424 | tf_op jit(solution)/shard_map/ppermute | solution.py:429
  3.9 10.0 %collective-permute-start.1 = (f32[456,128]{1,0:T(8,128)}, f32[456,128]{1,0:T(8,128)S(1)}, u32[]{:S(2)}, u32[]{:S(2)}) collective-permute-start(f32[456,128]{1,0:T(8,128)} %get-tuple-element.30), channel_id=1, source_target_pairs={{0,1},{1,0},{2,3},{3,2},{4,5},{5,4},{6,7},{7,6},{8,9},{9,8},{10,11... | collective-permute-start | bytes 700424 | tf_op jit(solution)/shard_map/ppermute | solution.py:430
  8.3 5.6 %copy-start.3 = (f32[4,32,128]{2,1,0:T(8,128)S(1)}, f32[4,32,128]{2,1,0:T(8,128)}, u32[]{:S(2)}) copy-start(f32[4,32,128]{2,1,0:T(8,128)} %forcing.1) | copy-start | bytes 196612
  8.3 5.6 %copy-start.4 = (bf16[4,128,128]{2,1,0:T(8,128)(2,1)S(1)}, bf16[4,128,128]{2,1,0:T(8,128)(2,1)}, u32[]{:S(2)}) copy-start(bf16[4,128,128]{2,1,0:T(8,128)(2,1)} %param.19) | copy-start | bytes 393220
  8.3 5.6 %copy-start.6 = (f32[32,128]{1,0:T(8,128)S(1)}, f32[32,128]{1,0:T(8,128)}, u32[]{:S(2)}) copy-start(f32[32,128]{1,0:T(8,128)} %surface.3) | copy-start | bytes 49156
  8.3 5.6 %copy-start.7 = (f32[32,128]{1,0:T(8,128)S(1)}, f32[32,128]{1,0:T(8,128)}, u32[]{:S(2)}) copy-start(f32[32,128]{1,0:T(8,128)} %rate.3) | copy-start | bytes 49156
  8.4 5.6 %copy-start.8 = (s32[32,4]{0,1:T(4,128)S(1)}, s32[32,4]{0,1:T(4,128)}, u32[]{:S(2)}) copy-start(s32[32,4]{0,1:T(4,128)} %param.20) | copy-start | bytes 1540
  8.4 5.6 %copy-start.9 = (s32[32,4]{0,1:T(4,128)S(1)}, s32[32,4]{0,1:T(4,128)}, u32[]{:S(2)}) copy-start(s32[32,4]{0,1:T(4,128)} %param.21) | copy-start | bytes 1540
  14.6 5.0 %collective-permute-start.2 = (f32[64,128]{1,0:T(8,128)S(1)}, f32[64,128]{1,0:T(8,128)S(1)}, u32[]{:S(2)}, u32[]{:S(2)}) collective-permute-start(f32[64,128]{1,0:T(8,128)S(1)} %get-tuple-element.37), channel_id=1, source_target_pairs={{0,8},{2,10},{4,12},{6,14},{8,0},{10,2},{12,4},{14,6},{1,9},{3,11}... | collective-permute-start | bytes 98312 | tf_op jit(solution)/shard_map/ppermute | solution.py:472
  19.6 3.8 %collective-permute-start.3 = (f32[32,128]{1,0:T(8,128)S(1)}, f32[32,128]{1,0:T(8,128)S(1)}, u32[]{:S(2)}, u32[]{:S(2)}) collective-permute-start(f32[32,128]{1,0:T(8,128)S(1)} %get-tuple-element.39), channel_id=1, source_target_pairs={{0,4},{2,6},{4,0},{6,2},{8,12},{10,14},{12,8},{14,10},{1,5},{3,7},... | collective-permute-start | bytes 49160 | tf_op jit(solution)/shard_map/ppermute | solution.py:472
  23.4 4.0 %collective-permute-start.4 = (f32[16,128]{1,0:T(8,128)S(1)}, f32[16,128]{1,0:T(8,128)S(1)}, u32[]{:S(2)}, u32[]{:S(2)}) collective-permute-start(f32[16,128]{1,0:T(8,128)S(1)} %get-tuple-element.46), channel_id=1, source_target_pairs={{0,2},{2,0},{4,6},{6,4},{8,10},{10,8},{12,14},{14,12},{1,3},{3,1},... | collective-permute-start | bytes 24584 | tf_op jit(solution)/shard_map/ppermute | solution.py:472

commit v12 on v11

--- a/solution.py
+++ b/solution.py
@@ -228,7 +228,7 @@
 
 def flux_kernel(
     sizes, core, tile, sky, forcing, surface, rate, rows_of_mix, source_rows, own, owners, locals_, shares, outer, inner,
-    keep, send, fluxes, above, below, halo
+    keep, send_1, send_2, send_3, fluxes, above, below, halo
 ):
     levels, rows, steps, sea_levels, sea_rows, stride, sea_stride = sizes
     width = sky.shape[1]
@@ -281,14 +281,14 @@
     left = rowed - first.astype(f32)
     second = left.astype(bf16)
     third = (left - second.astype(f32)).astype(bf16)
-    half = keep.shape[0]
-    hot = lax.broadcasted_iota(jnp.int32, (2 * half, topk * rows), 0) == target
+    part = keep.shape[0]
+    hot = lax.broadcasted_iota(jnp.int32, (4 * part, topk * rows), 0) == target
     hot = jnp.where(hot, 1.0, 0.0).astype(bf16)
     sums = jnp.dot(
         jnp.concatenate([hot, hot, hot], 1), jnp.concatenate([first, second, third], 0), preferred_element_type=f32
     )
-    keep[...] = sums[:half]
-    send[...] = sums[half:]
+    for q, to in enumerate((keep, send_1, send_2, send_3)):
+        to[...] = sums[q * part : (q + 1) * part]
 
 
 def edge_kernel(
@@ -380,10 +380,14 @@
         move.wait()
 
 
-def add_kernel(keep, got, after, kept, send):
+def add_kernel(keep, *others):
+    gots, (after, kept, send) = others[:-3], others[-3:]
+    total = keep[...]
+    for got in gots:
+        total = total + got[...]
     n = kept.shape[0]
-    kept[...] = keep[:n] + got[:n]
-    send[...] = keep[n:] + got[n:]
+    kept[...] = total[:n]
+    send[...] = total[n:]
 
 
 def heat_kernel(sizes, kept, got, wet, sea_first, before, after):
@@ -445,10 +449,10 @@
         flops=4 << 30, moved=8 << 20,
     )
 
-    half = tiles // 2 * sea_rows
-    keep, send, fluxes, above, below = call(
+    part = tiles // 4 * sea_rows
+    keep, send_1, send_2, send_3, fluxes, above, below = call(
         functools.partial(flux_kernel, sizes),
-        [flat(half), flat(half), flat(2 * steps * (rows + 2 * HALO)), flat(length), flat(length)],
+        [flat(part)] * 4 + [flat(2 * steps * (rows + 2 * HALO)), flat(length), flat(length)],
         core, tile, sky[-1], forcing2, surface, rate, rows_of_mix, source_rows, own, owners.T, locals_.T,
         shares.reshape(-1, width), outer, inner,
         in_specs=[SMEM] * 2 + [VMEM] * 12, scratch=[space(2 * HALO * stride, width)], moved=2 << 20,
@@ -467,24 +471,20 @@
             scratch=[space(area, width), pltpu.SemaphoreType.DMA((1,))], flops=1 << 28, moved=4 << 20,
         )
 
-    bit, ready, shore = tiles // 2, None, None
-    while True:
-        got = lax.ppermute(send, "tile", [(i, i ^ bit) for i in range(tiles)])
-        if bit <= 4 and ready is None:
-            ready = edge_part(keep)
-            done = ready
-        elif ready is not None and shore is None:
-            shore = shore_part(keep)
-            done = shore[0]
-        else:
-            done = keep
-        if bit == 1:
-            break
+    bit = tiles // 4
+    gots = [
+        lax.ppermute(x, "tile", [(i, i ^ (q * bit)) for i in range(tiles)])
+        for q, x in ((1, send_1), (2, send_2), (3, send_3))
+    ]
+    ready = edge_part(keep)
+    while bit > 1:
+        bit //= 2
         keep, send = call(
-            add_kernel, [flat(bit // 2 * sea_rows)] * 2, keep, got, done, in_specs=[VMEM, VMEM, ANY],
+            add_kernel, [flat(bit * sea_rows)] * 2, keep, *gots, ready, in_specs=[VMEM] * (1 + len(gots)) + [ANY],
         )
-        bit //= 2
-    warm, salt = shore_part(keep) if shore is None else shore
+        gots = [lax.ppermute(send, "tile", [(i, i ^ bit) for i in range(tiles)])]
+    got = gots[0]
+    warm, salt = shore_part(keep)
     sky_out = call(
         functools.partial(mix_kernel, sizes), jax.ShapeDtypeStruct((levels, rows // 8, 8, width), f32),
         ready, weights, keep, in_specs=[VMEM, VMEM, ANY], out_specs=HBM,

time: 28.4 us -> 29.1 us (1.025)
  waiting for transfers between devices: 1.51 us -> 3.55 us
  starting transfers between devices: 11.7 us -> 10.3 us
    ppermute x3 -> x4, waiting for transfers between devices: 1.51 us -> 3.54 us  [the longest x3 3.04 us: body(): lax.ppermute(x, 'tile', [(i, i ^ q * bit) for i in range(tiles)])]
    ppermute x3 -> x4, starting transfers between devices: 6.66 us -> 5.26 us  [the longest x3 4.45 us: body(): lax.ppermute(x, 'tile', [(i, i ^ q * bit) for i in range(tiles)])]
    pallas_call x9 -> x8, Pallas kernels: 14.1 us -> 14.2 us  [call(): pl.pallas_call(kernel, out_shape=out_shape, in_specs=in_specs or [VMEM] *...]
  transfers between devices with their start and end apart: 5 -> 6, of which waited for: 3 -> 2; matrix products, arithmetic and copies ran while one was open for 0% -> 0% of each run, Pallas kernels for 36% -> 35%
where the time goes in v12:
time: 29.1 us; the launch traced here: 29 us
  Pallas kernels  14.2 us (49%)
  starting transfers between devices  10.3 us (35%)
  waiting for transfers between devices  3.55 us (12%)
  between operations  0.91 us (3%)
    pallas_call x8, Pallas kernels, call(): pl.pallas_call(kernel, out_shape=out_shape, in_specs=in_specs or [VMEM] *...  14.2 us
    ppermute x3, starting transfers between devices, body(): lax.ppermute(x, 'tile', [(i, i ^ q * bit) for i in range(tiles)])  4.45 us
    ppermute x1, starting transfers between devices, body(): inner = lax.ppermute(inner, ring, swap(0))  4.35 us
    ppermute x3, waiting for transfers between devices, body(): lax.ppermute(x, 'tile', [(i, i ^ q * bit) for i in range(tiles)])  3.04 us
    ppermute x1, starting transfers between devices, body(): gots = [lax.ppermute(send, 'tile', [(i, i ^ bit) for i in range(tiles)])]  0.8 us
    ppermute x1, starting transfers between devices, body(): outer = lax.ppermute(outer, ring, swap(1))  0.68 us
  transfers between devices with their start and end apart: 6, of which 2 were waited for; matrix products, arithmetic and copies ran while one was open for 0% of the time, Pallas kernels for 35%

profile of v12, /device:TPU:0, one launch (start us, length us, event | category | flops | bytes accessed | tf_op | source)
XLA Modules:
  0.0 29.0 jit_solution(4003925663019211049)
XLA Ops:
  0.6 0.0 copy-start.5
  0.6 0.0 copy-start
  0.7 0.0 copy-start.2
  0.7 0.0 copy-start.1
  0.7 0.0 copy-start.11
  0.7 0.0 copy-start.10
  0.7 2.5 %shard_map.149 = (f32[456,128]{1,0:T(8,128)}, f32[456,128]{1,0:T(8,128)}) custom-call(s32[1]{0:T(128)} %bitcast.core, f32[72,32,128]{2,1,0:T(8,128)} %sky.1, f32[4,32,128]{2,1,0:T(8,128)} %forcing.1, f32[32,128]{1,0:T(8,128)} %surface.3, f32[32,128]{1,0:T(8,128)} %rate.3, f32[992,128]{1,0:T(8,128)} %bitcast.17, f32[992,128]{1,0:T(8,128)} %bitcast.19, ...), custom_call_target="tpu_custom_call" | custom-call | bytes 4194304 | tf_op jit(solution)/shard_map/pallas_call | solution.py:27
  3.2 0.7 %collective-permute-start = (f32[456,128]{1,0:T(8,128)}, f32[456,128]{1,0:T(8,128)S(1)}, u32[]{:S(2)}, u32[]{:S(2)}) collective-permute-start(f32[456,128]{1,0:T(8,128)} %get-tuple-element.29), channel_id=1, source_target_pairs={{1,2},{2,1},{3,4},{4,3},{5,6},{6,5},{7,8},{8,7},{9,10},{10,9},{11,... | collective-permute-start | bytes 700424 | tf_op jit(solution)/shard_map/ppermute | solution.py:433
  3.9 4.4 %collective-permute-start.1 = (f32[456,128]{1,0:T(8,128)}, f32[456,128]{1,0:T(8,128)S(1)}, u32[]{:S(2)}, u32[]{:S(2)}) collective-permute-start(f32[456,128]{1,0:T(8,128)} %get-tuple-element.30), channel_id=1, source_target_pairs={{0,1},{1,0},{2,3},{3,2},{4,5},{5,4},{6,7},{7,6},{8,9},{9,8},{10,11... | collective-permute-start | bytes 700424 | tf_op jit(solution)/shard_map/ppermute | solution.py:434
  8.3 0.0 copy-done.2
  8.3 0.0 copy-start.3
  8.3 0.0 copy-start.4
  8.3 0.0 copy-start.6
  8.3 0.0 copy-start.7
  8.4 0.0 copy-start.8
  8.4 0.0 copy-start.9
  8.4 5.5 %shard_map.148 = (f32[216,128]{1,0:T(8,128)S(1)}, f32[8,128]{1,0:T(8,128)S(1)}, f32[96,128]{1,0:T(8,128)S(1)}, bf16[80,256]{1,0:T(8,128)(2,1)S(1)}, bf16[64,256]...) custom-call(s32[1]{0:T(128)} %bitcast.4.place, ...), custom_call_target="tpu_custom_call" | custom-call | flops 4294967296 | bytes 8388608 | tf_op jit(solution)/shard_map/pallas_call | solution.py:27
  13.9 0.0 collective-permute-done.outer
  13.9 0.0 collective-permute-done.1.inner
  14.0 0.7 %shard_map.150 = (f32[32,128]{1,0:T(8,128)S(1)}, f32[32,128]{1,0:T(8,128)S(1)}, f32[32,128]{1,0:T(8,128)S(1)}, f32[32,128]{1,0:T(8,128)S(1)}, f32[320,128]{1,0:T...) custom-call(s32[1]{0:T(128)} %bitcast.core, s32[1]{0:T(128)} %bitcast.1.tile, ...), custom_call_target="tpu_custom_call" | custom-call | bytes 2097152 | tf_op jit(solution)/shard_map/pallas_call | solution.py:27
  14.7 1.6 %collective-permute-start.2 = (f32[32,128]{1,0:T(8,128)S(1)}, f32[32,128]{1,0:T(8,128)S(1)}, u32[]{:S(2)}, u32[]{:S(2)}) collective-permute-start(f32[32,128]{1,0:T(8,128)S(1)} %get-tuple-element.37), channel_id=1, source_target_pairs={{0,4},{2,6},{4,0},{6,2},{8,12},{10,14},{12,8},{14,10},{1,5},{3,7},... | collective-permute-start | bytes 49160 | tf_op jit(solution)/shard_map/ppermute | solution.py:476
  16.4 2.6 %collective-permute-start.3 = (f32[32,128]{1,0:T(8,128)S(1)}, f32[32,128]{1,0:T(8,128)S(1)}, u32[]{:S(2)}, u32[]{:S(2)}) collective-permute-start(f32[32,128]{1,0:T(8,128)S(1)} %get-tuple-element.38), channel_id=1, source_target_pairs={{0,8},{2,10},{4,12},{6,14},{8,0},{10,2},{12,4},{14,6},{1,9},{3,11}... | collective-permute-start | bytes 49160 | tf_op jit(solution)/shard_map/ppermute | solution.py:476
  18.9 0.2 collective-permute-start.4
  19.2 2.3 %shard_map.151.others_3_.spread = f32[2560,128]{1,0:T(8,128)S(1)} custom-call(f32[320,128]{1,0:T(8,128)S(1)} %get-tuple-element.31.fluxes, f32[2304,128]{1,0:T(8,128)S(1)} %get-tuple-element.32.own, f32[456,128]{1,0:T(8,128)S(1)} %get-tuple-element.33.above, f32[456,128]{1,0:T(8,128)S(1)} %get-tuple-element.34.below, f32[32,128]{1,0:T(8,128)S(1)} %get-tuple-element.35.after.keep), custom_call_target="tpu_custom_call" | custom-call | flops 268435456 | bytes 4194304 | tf_op jit(solution)/shard_map/pallas_call | solution.py:27
  21.4 0.0 collective-permute-done.2.others_0_
  21.4 0.0 collective-permute-done.3.others_1_
  21.5 3.0 %collective-permute-done.4.others_2_ = f32[32,128]{1,0:T(8,128)S(1)} collective-permute-done((f32[32,128]{1,0:T(8,128)S(1)}, f32[32,128]{1,0:T(8,128)S(1)}, u32[]{:S(2)}, u32[]{:S(2)}) %collective-permute-start.4) | collective-permute-done | bytes 16416 | tf_op jit(solution)/shard_map/ppermute | solution.py:476
  24.5 0.8 %collective-permute-start.5 = (f32[16,128]{1,0:T(8,128)S(1)}, f32[16,128]{1,0:T(8,128)S(1)}, u32[]{:S(2)}, u32[]{:S(2)}) collective-permute-start(f32[16,128]{1,0:T(8,128)S(1)} %get-tuple-element.41), channel_id=1, source_target_pairs={{0,2},{2,0},{4,6},{6,4},{8,10},{10,8},{12,14},{14,12},{1,3},{3,1},... | collective-permute-start | bytes 24584 | tf_op jit(solution)/shard_map/ppermute | solution.py:485
  25.3 1.3 %shard_map.153 = f32[72,4,8,128]{3,2,1,0:T(8,128)} custom-call(f32[2560,128]{1,0:T(8,128)S(1)} %shard_map.151.others_3_.spread, bf16[80,256]{1,0:T(8,128)(2,1)S(1)} %get-tuple-element.36.weights, f32[16,128]{1,0:T(8,128)S(1)} %get-tuple-element.40.after.kept), custom_call_target="tpu_custom_call" | custom-call | flops 2147483648 | bytes 4194304 | tf_op jit(solution)/shard_map/pallas_call | solution.py:27
  26.6 1.0 %shard_map.154 = (f32[992,128]{1,0:T(8,128)S(1)}, f32[992,128]{1,0:T(8,128)}) custom-call(bf16[64,256]{1,0:T(8,128)(2,1)S(1)} %get-tuple-element.43.sea_weights, f32[256,128]{1,0:T(8,128)S(1)} %get-tuple-element.44.sea_ends, s32[16,128]{1,0:T(8,128)S(1)} %copy-done.5, f32[992,128]{1,0:T(8,128)S(1)} %get-tuple-element.45.warm, ...), custom_call_target="tpu_custom_call" | custom-call | flops 268435456 | bytes 4194304 | tf_op jit(solution)/shard_map/pallas_call | solution.py:27
  27.6 0.5 %collective-permute-done.5.got = f32[16,128]{1,0:T(8,128)S(1)} collective-permute-done((f32[16,128]{1,0:T(8,128)S(1)}, f32[16,128]{1,0:T(8,128)S(1)}, u32[]{:S(2)}, u32[]{:S(2)}) %collective-permute-start.5) | collective-permute-done | bytes 8224 | tf_op jit(solution)/shard_map/ppermute | solution.py:485
  28.1 0.8 %shard_map.155 = f32[992,128]{1,0:T(8,128)} custom-call(f32[16,128]{1,0:T(8,128)S(1)} %get-tuple-element.40.after.kept, f32[16,128]{1,0:T(8,128)S(1)} %collective-permute-done.5.got, s32[16,128]{1,0:T(8,128)S(1)} %copy-done.5, f32[64,128]{1,0:T(8,128)S(1)} %get-tuple-element.42.sea_first, f32[992,128]{1,0:T(8,128)S(1)} %get-tuple-element.47.before), custom_call_target="tpu_custom_call" | custom-call | bytes 2097152 | tf_op jit(solution)/shard_map/pallas_call | solution.py:27
  (15 shorter events, 0.0 us)
Async XLA Ops:
  0.6 7.6 %copy-start.5 = (s32[16,128]{1,0:T(8,128)S(1)}, s32[16,128]{1,0:T(8,128)}, u32[]{:S(2)}) copy-start(s32[16,128]{1,0:T(8,128)} %wet.7) | copy-start | bytes 24580
  0.6 7.6 %copy-start = (f32[72,32,128]{2,1,0:T(8,128)S(1)}, f32[72,32,128]{2,1,0:T(8,128)}, u32[]{:S(2)}) copy-start(f32[72,32,128]{2,1,0:T(8,128)} %sky.1) | copy-start | bytes 3538948
  0.7 7.6 %copy-start.2 = (f32[62,16,128]{2,1,0:T(8,128)S(1)}, f32[62,16,128]{2,1,0:T(8,128)}, u32[]{:S(2)}) copy-start(f32[62,16,128]{2,1,0:T(8,128)} %param.23) | copy-start | bytes 1523716
  0.7 7.6 %copy-start.1 = (f32[62,16,128]{2,1,0:T(8,128)S(1)}, f32[62,16,128]{2,1,0:T(8,128)}, u32[]{:S(2)}) copy-start(f32[62,16,128]{2,1,0:T(8,128)} %param.22) | copy-start | bytes 1523716
  0.7 7.6 %copy-start.11 = (f32[62,62]{1,0:T(8,128)S(1)}, f32[62,62]{1,0:T(8,128)}, u32[]{:S(2)}) copy-start(f32[62,62]{1,0:T(8,128)} %sea_mix.1) | copy-start | bytes 46132
  0.7 7.6 %copy-start.10 = (f32[72,72]{1,0:T(8,128)S(1)}, f32[72,72]{1,0:T(8,128)}, u32[]{:S(2)}) copy-start(f32[72,72]{1,0:T(8,128)} %vmix.1) | copy-start | bytes 62212
  0.7 7.6 %copy-start.12 = (f32[72]{0:T(128)S(1)}, f32[72]{0:T(128)}, u32[]{:S(2)}) copy-start(f32[72]{0:T(128)} %param.15) | copy-start | bytes 868
  3.2 10.7 %collective-permute-start = (f32[456,128]{1,0:T(8,128)}, f32[456,128]{1,0:T(8,128)S(1)}, u32[]{:S(2)}, u32[]{:S(2)}) collective-permute-start(f32[456,128]{1,0:T(8,128)} %get-tuple-element.29), channel_id=1, source_target_pairs={{1,2},{2,1},{3,4},{4,3},{5,6},{6,5},{7,8},{8,7},{9,10},{10,9},{11,... | collective-permute-start | bytes 700424 | tf_op jit(solution)/shard_map/ppermute | solution.py:433
  3.9 10.0 %collective-permute-start.1 = (f32[456,128]{1,0:T(8,128)}, f32[456,128]{1,0:T(8,128)S(1)}, u32[]{:S(2)}, u32[]{:S(2)}) collective-permute-start(f32[456,128]{1,0:T(8,128)} %get-tuple-element.30), channel_id=1, source_target_pairs={{0,1},{1,0},{2,3},{3,2},{4,5},{5,4},{6,7},{7,6},{8,9},{9,8},{10,11... | collective-permute-start | bytes 700424 | tf_op jit(solution)/shard_map/ppermute | solution.py:434
  8.3 5.6 %copy-start.3 = (f32[4,32,128]{2,1,0:T(8,128)S(1)}, f32[4,32,128]{2,1,0:T(8,128)}, u32[]{:S(2)}) copy-start(f32[4,32,128]{2,1,0:T(8,128)} %forcing.1) | copy-start | bytes 196612
  8.3 5.6 %copy-start.4 = (bf16[4,128,128]{2,1,0:T(8,128)(2,1)S(1)}, bf16[4,128,128]{2,1,0:T(8,128)(2,1)}, u32[]{:S(2)}) copy-start(bf16[4,128,128]{2,1,0:T(8,128)(2,1)} %param.19) | copy-start | bytes 393220
  8.3 5.6 %copy-start.6 = (f32[32,128]{1,0:T(8,128)S(1)}, f32[32,128]{1,0:T(8,128)}, u32[]{:S(2)}) copy-start(f32[32,128]{1,0:T(8,128)} %surface.3) | copy-start | bytes 49156
  8.3 5.6 %copy-start.7 = (f32[32,128]{1,0:T(8,128)S(1)}, f32[32,128]{1,0:T(8,128)}, u32[]{:S(2)}) copy-start(f32[32,128]{1,0:T(8,128)} %rate.3) | copy-start | bytes 49156
  8.4 5.6 %copy-start.8 = (s32[32,4]{0,1:T(4,128)S(1)}, s32[32,4]{0,1:T(4,128)}, u32[]{:S(2)}) copy-start(s32[32,4]{0,1:T(4,128)} %param.20) | copy-start | bytes 1540
  8.4 5.6 %copy-start.9 = (s32[32,4]{0,1:T(4,128)S(1)}, s32[32,4]{0,1:T(4,128)}, u32[]{:S(2)}) copy-start(s32[32,4]{0,1:T(4,128)} %param.21) | copy-start | bytes 1540
  14.7 6.7 %collective-permute-start.2 = (f32[32,128]{1,0:T(8,128)S(1)}, f32[32,128]{1,0:T(8,128)S(1)}, u32[]{:S(2)}, u32[]{:S(2)}) collective-permute-start(f32[32,128]{1,0:T(8,128)S(1)} %get-tuple-element.37), channel_id=1, source_target_pairs={{0,4},{2,6},{4,0},{6,2},{8,12},{10,14},{12,8},{14,10},{1,5},{3,7},... | collective-permute-start | bytes 49160 | tf_op jit(solution)/shard_map/ppermute | solution.py:476
  16.4 5.1 %collective-permute-start.3 = (f32[32,128]{1,0:T(8,128)S(1)}, f32[32,128]{1,0:T(8,128)S(1)}, u32[]{:S(2)}, u32[]{:S(2)}) collective-permute-start(f32[32,128]{1,0:T(8,128)S(1)} %get-tuple-element.38), channel_id=1, source_target_pairs={{0,8},{2,10},{4,12},{6,14},{8,0},{10,2},{12,4},{14,6},{1,9},{3,11}... | collective-permute-start | bytes 49160 | tf_op jit(solution)/shard_map/ppermute | solution.py:476
  18.9 5.5 %collective-permute-start.4 = (f32[32,128]{1,0:T(8,128)S(1)}, f32[32,128]{1,0:T(8,128)S(1)}, u32[]{:S(2)}, u32[]{:S(2)}) collective-permute-start(f32[32,128]{1,0:T(8,128)S(1)} %get-tuple-element.39), channel_id=1, source_target_pairs={{0,12},{2,14},{4,8},{6,10},{8,4},{10,6},{12,0},{14,2},{1,13},{3,15... | collective-permute-start | bytes 49160 | tf_op jit(solution)/shard_map/ppermute | solution.py:476
  24.5 3.7 %collective-permute-start.5 = (f32[16,128]{1,0:T(8,128)S(1)}, f32[16,128]{1,0:T(8,128)S(1)}, u32[]{:S(2)}, u32[]{:S(2)}) collective-permute-start(f32[16,128]{1,0:T(8,128)S(1)} %get-tuple-element.41), channel_id=1, source_target_pairs={{0,2},{2,0},{4,6},{6,4},{8,10},{10,8},{12,14},{14,12},{1,3},{3,1},... | collective-permute-start | bytes 24584 | tf_op jit(solution)/shard_map/ppermute | solution.py:485

commit v13 on v12

--- a/solution.py
+++ b/solution.py
@@ -474,7 +474,7 @@
     bit = tiles // 4
     gots = [
         lax.ppermute(x, "tile", [(i, i ^ (q * bit)) for i in range(tiles)])
-        for q, x in ((1, send_1), (2, send_2), (3, send_3))
+        for q, x in ((3, send_3), (2, send_2), (1, send_1))
     ]
     ready = edge_part(keep)
     while bit > 1:

time: 29.1 us -> 27.7 us (0.952)
  waiting for transfers between devices: 3.55 us -> 2.09 us
    ppermute x3, waiting for transfers between devices: 3.04 us -> 1.58 us  [body(): lax.ppermute(x, 'tile', [(i, i ^ q * bit) for i in range(tiles)])]
  transfers between devices with their start and end apart: 6 -> 6, of which waited for: 2 -> 2; matrix products, arithmetic and copies ran while one was open for 0% -> 0% of each run, Pallas kernels for 35% -> 37%
where the time goes in v13:
time: 27.7 us; the launch traced here: 27.6 us
  Pallas kernels  14.2 us (51%)
  starting transfers between devices  10.4 us (38%)
  waiting for transfers between devices  2.09 us (8%)
  between operations  0.9 us (3%)
    pallas_call x8, Pallas kernels, call(): pl.pallas_call(kernel, out_shape=out_shape, in_specs=in_specs or [VMEM] *...  14.2 us
    ppermute x3, starting transfers between devices, body(): lax.ppermute(x, 'tile', [(i, i ^ q * bit) for i in range(tiles)])  4.45 us
    ppermute x1, starting transfers between devices, body(): inner = lax.ppermute(inner, ring, swap(0))  4.35 us
    ppermute x3, waiting for transfers between devices, body(): lax.ppermute(x, 'tile', [(i, i ^ q * bit) for i in range(tiles)])  1.58 us
    ppermute x1, starting transfers between devices, body(): gots = [lax.ppermute(send, 'tile', [(i, i ^ bit) for i in range(tiles)])]  0.87 us
    ppermute x1, starting transfers between devices, body(): outer = lax.ppermute(outer, ring, swap(1))  0.68 us
  transfers between devices with their start and end apart: 6, of which 2 were waited for; matrix products, arithmetic and copies ran while one was open for 0% of the time, Pallas kernels for 37%

profile of v13, /device:TPU:0, one launch (start us, length us, event | category | flops | bytes accessed | tf_op | source)
XLA Modules:
  0.0 27.6 jit_solution(2029057551322127432)
XLA Ops:
  0.6 0.0 copy-start.5
  0.6 0.0 copy-start
  0.7 0.0 copy-start.2
  0.7 0.0 copy-start.1
  0.7 0.0 copy-start.11
  0.7 0.0 copy-start.10
  0.7 2.5 %shard_map.149 = (f32[456,128]{1,0:T(8,128)}, f32[456,128]{1,0:T(8,128)}) custom-call(s32[1]{0:T(128)} %bitcast.core, f32[72,32,128]{2,1,0:T(8,128)} %sky.1, f32[4,32,128]{2,1,0:T(8,128)} %forcing.1, f32[32,128]{1,0:T(8,128)} %surface.3, f32[32,128]{1,0:T(8,128)} %rate.3, f32[992,128]{1,0:T(8,128)} %bitcast.17, f32[992,128]{1,0:T(8,128)} %bitcast.19, ...), custom_call_target="tpu_custom_call" | custom-call | bytes 4194304 | tf_op jit(solution)/shard_map/pallas_call | solution.py:27
  3.2 0.7 %collective-permute-start = (f32[456,128]{1,0:T(8,128)}, f32[456,128]{1,0:T(8,128)S(1)}, u32[]{:S(2)}, u32[]{:S(2)}) collective-permute-start(f32[456,128]{1,0:T(8,128)} %get-tuple-element.29), channel_id=1, source_target_pairs={{1,2},{2,1},{3,4},{4,3},{5,6},{6,5},{7,8},{8,7},{9,10},{10,9},{11,... | collective-permute-start | bytes 700424 | tf_op jit(solution)/shard_map/ppermute | solution.py:433
  3.9 4.4 %collective-permute-start.1 = (f32[456,128]{1,0:T(8,128)}, f32[456,128]{1,0:T(8,128)S(1)}, u32[]{:S(2)}, u32[]{:S(2)}) collective-permute-start(f32[456,128]{1,0:T(8,128)} %get-tuple-element.30), channel_id=1, source_target_pairs={{0,1},{1,0},{2,3},{3,2},{4,5},{5,4},{6,7},{7,6},{8,9},{9,8},{10,11... | collective-permute-start | bytes 700424 | tf_op jit(solution)/shard_map/ppermute | solution.py:434
  8.3 0.0 copy-done.2
  8.3 0.0 copy-start.3
  8.3 0.0 copy-start.4
  8.3 0.0 copy-start.6
  8.3 0.0 copy-start.7
  8.4 0.0 copy-start.8
  8.4 0.0 copy-start.9
  8.4 5.5 %shard_map.148 = (f32[216,128]{1,0:T(8,128)S(1)}, f32[8,128]{1,0:T(8,128)S(1)}, f32[96,128]{1,0:T(8,128)S(1)}, bf16[80,256]{1,0:T(8,128)(2,1)S(1)}, bf16[64,256]...) custom-call(s32[1]{0:T(128)} %bitcast.4.place, ...), custom_call_target="tpu_custom_call" | custom-call | flops 4294967296 | bytes 8388608 | tf_op jit(solution)/shard_map/pallas_call | solution.py:27
  13.9 0.0 collective-permute-done.outer
  13.9 0.0 collective-permute-done.1.inner
  14.0 0.7 %shard_map.150 = (f32[32,128]{1,0:T(8,128)S(1)}, f32[32,128]{1,0:T(8,128)S(1)}, f32[32,128]{1,0:T(8,128)S(1)}, f32[32,128]{1,0:T(8,128)S(1)}, f32[320,128]{1,0:T...) custom-call(s32[1]{0:T(128)} %bitcast.core, s32[1]{0:T(128)} %bitcast.1.tile, ...), custom_call_target="tpu_custom_call" | custom-call | bytes 2097152 | tf_op jit(solution)/shard_map/pallas_call | solution.py:27
  14.7 3.7 %collective-permute-start.2 = (f32[32,128]{1,0:T(8,128)S(1)}, f32[32,128]{1,0:T(8,128)S(1)}, u32[]{:S(2)}, u32[]{:S(2)}) collective-permute-start(f32[32,128]{1,0:T(8,128)S(1)} %get-tuple-element.37), channel_id=1, source_target_pairs={{0,12},{2,14},{4,8},{6,10},{8,4},{10,6},{12,0},{14,2},{1,13},{3,15... | collective-permute-start | bytes 49160 | tf_op jit(solution)/shard_map/ppermute | solution.py:476
  18.4 0.0 collective-permute-start.3
  18.4 0.8 %collective-permute-start.4 = (f32[32,128]{1,0:T(8,128)S(1)}, f32[32,128]{1,0:T(8,128)S(1)}, u32[]{:S(2)}, u32[]{:S(2)}) collective-permute-start(f32[32,128]{1,0:T(8,128)S(1)} %get-tuple-element.39), channel_id=1, source_target_pairs={{0,4},{2,6},{4,0},{6,2},{8,12},{10,14},{12,8},{14,10},{1,5},{3,7},... | collective-permute-start | bytes 49160 | tf_op jit(solution)/shard_map/ppermute | solution.py:476
  19.2 2.3 %shard_map.151.others_3_.spread = f32[2560,128]{1,0:T(8,128)S(1)} custom-call(f32[320,128]{1,0:T(8,128)S(1)} %get-tuple-element.31.fluxes, f32[2304,128]{1,0:T(8,128)S(1)} %get-tuple-element.32.own, f32[456,128]{1,0:T(8,128)S(1)} %get-tuple-element.33.above, f32[456,128]{1,0:T(8,128)S(1)} %get-tuple-element.34.below, f32[32,128]{1,0:T(8,128)S(1)} %get-tuple-element.35.after.keep), custom_call_target="tpu_custom_call" | custom-call | flops 268435456 | bytes 4194304 | tf_op jit(solution)/shard_map/pallas_call | solution.py:27
  21.4 0.0 collective-permute-done.2.others_0_
  21.4 1.6 %collective-permute-done.3.others_1_ = f32[32,128]{1,0:T(8,128)S(1)} collective-permute-done((f32[32,128]{1,0:T(8,128)S(1)}, f32[32,128]{1,0:T(8,128)S(1)}, u32[]{:S(2)}, u32[]{:S(2)}) %collective-permute-start.3) | collective-permute-done | bytes 16416 | tf_op jit(solution)/shard_map/ppermute | solution.py:476
  23.0 0.0 collective-permute-done.4.others_2_
  23.0 0.9 %collective-permute-start.5 = (f32[16,128]{1,0:T(8,128)S(1)}, f32[16,128]{1,0:T(8,128)S(1)}, u32[]{:S(2)}, u32[]{:S(2)}) collective-permute-start(f32[16,128]{1,0:T(8,128)S(1)} %get-tuple-element.41), channel_id=1, source_target_pairs={{0,2},{2,0},{4,6},{6,4},{8,10},{10,8},{12,14},{14,12},{1,3},{3,1},... | collective-permute-start | bytes 24584 | tf_op jit(solution)/shard_map/ppermute | solution.py:485
  23.9 1.3 %shard_map.153 = f32[72,4,8,128]{3,2,1,0:T(8,128)} custom-call(f32[2560,128]{1,0:T(8,128)S(1)} %shard_map.151.others_3_.spread, bf16[80,256]{1,0:T(8,128)(2,1)S(1)} %get-tuple-element.36.weights, f32[16,128]{1,0:T(8,128)S(1)} %get-tuple-element.40.after.kept), custom_call_target="tpu_custom_call" | custom-call | flops 2147483648 | bytes 4194304 | tf_op jit(solution)/shard_map/pallas_call | solution.py:27
  25.2 1.0 %shard_map.154 = (f32[992,128]{1,0:T(8,128)S(1)}, f32[992,128]{1,0:T(8,128)}) custom-call(bf16[64,256]{1,0:T(8,128)(2,1)S(1)} %get-tuple-element.43.sea_weights, f32[256,128]{1,0:T(8,128)S(1)} %get-tuple-element.44.sea_ends, s32[16,128]{1,0:T(8,128)S(1)} %copy-done.5, f32[992,128]{1,0:T(8,128)S(1)} %get-tuple-element.45.warm, ...), custom_call_target="tpu_custom_call" | custom-call | flops 268435456 | bytes 4194304 | tf_op jit(solution)/shard_map/pallas_call | solution.py:27
  26.2 0.5 %collective-permute-done.5.got = f32[16,128]{1,0:T(8,128)S(1)} collective-permute-done((f32[16,128]{1,0:T(8,128)S(1)}, f32[16,128]{1,0:T(8,128)S(1)}, u32[]{:S(2)}, u32[]{:S(2)}) %collective-permute-start.5) | collective-permute-done | bytes 8224 | tf_op jit(solution)/shard_map/ppermute | solution.py:485
  26.7 0.8 %shard_map.155 = f32[992,128]{1,0:T(8,128)} custom-call(f32[16,128]{1,0:T(8,128)S(1)} %get-tuple-element.40.after.kept, f32[16,128]{1,0:T(8,128)S(1)} %collective-permute-done.5.got, s32[16,128]{1,0:T(8,128)S(1)} %copy-done.5, f32[64,128]{1,0:T(8,128)S(1)} %get-tuple-element.42.sea_first, f32[992,128]{1,0:T(8,128)S(1)} %get-tuple-element.47.before), custom_call_target="tpu_custom_call" | custom-call | bytes 2097152 | tf_op jit(solution)/shard_map/pallas_call | solution.py:27
  (15 shorter events, 0.0 us)
Async XLA Ops:
  0.6 7.6 %copy-start.5 = (s32[16,128]{1,0:T(8,128)S(1)}, s32[16,128]{1,0:T(8,128)}, u32[]{:S(2)}) copy-start(s32[16,128]{1,0:T(8,128)} %wet.7) | copy-start | bytes 24580
  0.6 7.6 %copy-start = (f32[72,32,128]{2,1,0:T(8,128)S(1)}, f32[72,32,128]{2,1,0:T(8,128)}, u32[]{:S(2)}) copy-start(f32[72,32,128]{2,1,0:T(8,128)} %sky.1) | copy-start | bytes 3538948
  0.7 7.6 %copy-start.2 = (f32[62,16,128]{2,1,0:T(8,128)S(1)}, f32[62,16,128]{2,1,0:T(8,128)}, u32[]{:S(2)}) copy-start(f32[62,16,128]{2,1,0:T(8,128)} %param.23) | copy-start | bytes 1523716
  0.7 7.6 %copy-start.1 = (f32[62,16,128]{2,1,0:T(8,128)S(1)}, f32[62,16,128]{2,1,0:T(8,128)}, u32[]{:S(2)}) copy-start(f32[62,16,128]{2,1,0:T(8,128)} %param.22) | copy-start | bytes 1523716
  0.7 7.6 %copy-start.11 = (f32[62,62]{1,0:T(8,128)S(1)}, f32[62,62]{1,0:T(8,128)}, u32[]{:S(2)}) copy-start(f32[62,62]{1,0:T(8,128)} %sea_mix.1) | copy-start | bytes 46132
  0.7 7.6 %copy-start.10 = (f32[72,72]{1,0:T(8,128)S(1)}, f32[72,72]{1,0:T(8,128)}, u32[]{:S(2)}) copy-start(f32[72,72]{1,0:T(8,128)} %vmix.1) | copy-start | bytes 62212
  0.7 7.6 %copy-start.12 = (f32[72]{0:T(128)S(1)}, f32[72]{0:T(128)}, u32[]{:S(2)}) copy-start(f32[72]{0:T(128)} %param.15) | copy-start | bytes 868
  3.2 10.7 %collective-permute-start = (f32[456,128]{1,0:T(8,128)}, f32[456,128]{1,0:T(8,128)S(1)}, u32[]{:S(2)}, u32[]{:S(2)}) collective-permute-start(f32[456,128]{1,0:T(8,128)} %get-tuple-element.29), channel_id=1, source_target_pairs={{1,2},{2,1},{3,4},{4,3},{5,6},{6,5},{7,8},{8,7},{9,10},{10,9},{11,... | collective-permute-start | bytes 700424 | tf_op jit(solution)/shard_map/ppermute | solution.py:433
  3.9 10.0 %collective-permute-start.1 = (f32[456,128]{1,0:T(8,128)}, f32[456,128]{1,0:T(8,128)S(1)}, u32[]{:S(2)}, u32[]{:S(2)}) collective-permute-start(f32[456,128]{1,0:T(8,128)} %get-tuple-element.30), channel_id=1, source_target_pairs={{0,1},{1,0},{2,3},{3,2},{4,5},{5,4},{6,7},{7,6},{8,9},{9,8},{10,11... | collective-permute-start | bytes 700424 | tf_op jit(solution)/shard_map/ppermute | solution.py:434
  8.3 5.6 %copy-start.3 = (f32[4,32,128]{2,1,0:T(8,128)S(1)}, f32[4,32,128]{2,1,0:T(8,128)}, u32[]{:S(2)}) copy-start(f32[4,32,128]{2,1,0:T(8,128)} %forcing.1) | copy-start | bytes 196612
  8.3 5.6 %copy-start.4 = (bf16[4,128,128]{2,1,0:T(8,128)(2,1)S(1)}, bf16[4,128,128]{2,1,0:T(8,128)(2,1)}, u32[]{:S(2)}) copy-start(bf16[4,128,128]{2,1,0:T(8,128)(2,1)} %param.19) | copy-start | bytes 393220
  8.3 5.6 %copy-start.6 = (f32[32,128]{1,0:T(8,128)S(1)}, f32[32,128]{1,0:T(8,128)}, u32[]{:S(2)}) copy-start(f32[32,128]{1,0:T(8,128)} %surface.3) | copy-start | bytes 49156
  8.3 5.6 %copy-start.7 = (f32[32,128]{1,0:T(8,128)S(1)}, f32[32,128]{1,0:T(8,128)}, u32[]{:S(2)}) copy-start(f32[32,128]{1,0:T(8,128)} %rate.3) | copy-start | bytes 49156
  8.4 5.6 %copy-start.8 = (s32[32,4]{0,1:T(4,128)S(1)}, s32[32,4]{0,1:T(4,128)}, u32[]{:S(2)}) copy-start(s32[32,4]{0,1:T(4,128)} %param.20) | copy-start | bytes 1540
  8.4 5.6 %copy-start.9 = (s32[32,4]{0,1:T(4,128)S(1)}, s32[32,4]{0,1:T(4,128)}, u32[]{:S(2)}) copy-start(s32[32,4]{0,1:T(4,128)} %param.21) | copy-start | bytes 1540
  14.7 6.7 %collective-permute-start.2 = (f32[32,128]{1,0:T(8,128)S(1)}, f32[32,128]{1,0:T(8,128)S(1)}, u32[]{:S(2)}, u32[]{:S(2)}) collective-permute-start(f32[32,128]{1,0:T(8,128)S(1)} %get-tuple-element.37), channel_id=1, source_target_pairs={{0,12},{2,14},{4,8},{6,10},{8,4},{10,6},{12,0},{14,2},{1,13},{3,15... | collective-permute-start | bytes 49160 | tf_op jit(solution)/shard_map/ppermute | solution.py:476
  18.4 4.6 %collective-permute-start.3 = (f32[32,128]{1,0:T(8,128)S(1)}, f32[32,128]{1,0:T(8,128)S(1)}, u32[]{:S(2)}, u32[]{:S(2)}) collective-permute-start(f32[32,128]{1,0:T(8,128)S(1)} %get-tuple-element.38), channel_id=1, source_target_pairs={{0,8},{2,10},{4,12},{6,14},{8,0},{10,2},{12,4},{14,6},{1,9},{3,11}... | collective-permute-start | bytes 49160 | tf_op jit(solution)/shard_map/ppermute | solution.py:476
  18.4 4.6 %collective-permute-start.4 = (f32[32,128]{1,0:T(8,128)S(1)}, f32[32,128]{1,0:T(8,128)S(1)}, u32[]{:S(2)}, u32[]{:S(2)}) collective-permute-start(f32[32,128]{1,0:T(8,128)S(1)} %get-tuple-element.39), channel_id=1, source_target_pairs={{0,4},{2,6},{4,0},{6,2},{8,12},{10,14},{12,8},{14,10},{1,5},{3,7},... | collective-permute-start | bytes 49160 | tf_op jit(solution)/shard_map/ppermute | solution.py:476
  23.0 3.7 %collective-permute-start.5 = (f32[16,128]{1,0:T(8,128)S(1)}, f32[16,128]{1,0:T(8,128)S(1)}, u32[]{:S(2)}, u32[]{:S(2)}) collective-permute-start(f32[16,128]{1,0:T(8,128)S(1)} %get-tuple-element.41), channel_id=1, source_target_pairs={{0,2},{2,0},{4,6},{6,4},{8,10},{10,8},{12,14},{14,12},{1,3},{3,1},... | collective-permute-start | bytes 24584 | tf_op jit(solution)/shard_map/ppermute | solution.py:485

commit v14 on v13

--- a/solution.py
+++ b/solution.py
@@ -474,7 +474,7 @@
     bit = tiles // 4
     gots = [
         lax.ppermute(x, "tile", [(i, i ^ (q * bit)) for i in range(tiles)])
-        for q, x in ((3, send_3), (2, send_2), (1, send_1))
+        for q, x in ((2, send_2), (3, send_3), (1, send_1))
     ]
     ready = edge_part(keep)
     while bit > 1:

time: 27.7 us -> 28.6 us (1.032)
  starting transfers between devices: 10.4 us -> 11.6 us
  waiting for transfers between devices: 2.09 us -> 1.73 us
    ppermute x1, starting transfers between devices: 0.87 us -> 2.34 us  [body(): gots = [lax.ppermute(send, 'tile', [(i, i ^ bit) for i in range(tiles)])]]
    ppermute x1, waiting for transfers between devices: 0.5 us -> 0.01 us  [body(): gots = [lax.ppermute(send, 'tile', [(i, i ^ bit) for i in range(tiles)])]]
  transfers between devices with their start and end apart: 6 -> 6, of which waited for: 2 -> 1; matrix products, arithmetic and copies ran while one was open for 0% -> 0% of each run, Pallas kernels for 37% -> 36%
where the time goes in v14:
time: 28.6 us; the launch traced here: 28.5 us
  Pallas kernels  14.2 us (50%)
  starting transfers between devices  11.6 us (41%)
  waiting for transfers between devices  1.73 us (6%)
  between operations  0.91 us (3%)
    pallas_call x8, Pallas kernels, call(): pl.pallas_call(kernel, out_shape=out_shape, in_specs=in_specs or [VMEM] *...  14.2 us
    ppermute x1, starting transfers between devices, body(): inner = lax.ppermute(inner, ring, swap(0))  4.35 us
    ppermute x3, starting transfers between devices, body(): lax.ppermute(x, 'tile', [(i, i ^ q * bit) for i in range(tiles)])  4.24 us
    ppermute x1, starting transfers between devices, body(): gots = [lax.ppermute(send, 'tile', [(i, i ^ bit) for i in range(tiles)])]  2.34 us
    ppermute x3, waiting for transfers between devices, body(): lax.ppermute(x, 'tile', [(i, i ^ q * bit) for i in range(tiles)])  1.72 us
    ppermute x1, starting transfers between devices, body(): outer = lax.ppermute(outer, ring, swap(1))  0.68 us
  transfers between devices with their start and end apart: 6, of which 1 were waited for; matrix products, arithmetic and copies ran while one was open for 0% of the time, Pallas kernels for 36%

profile of v14, /device:TPU:0, one launch (start us, length us, event | category | flops | bytes accessed | tf_op | source)
XLA Modules:
  0.0 28.5 jit_solution(9065425949842783726)
XLA Ops:
  0.6 0.0 copy-start.5
  0.6 0.0 copy-start
  0.7 0.0 copy-start.2
  0.7 0.0 copy-start.1
  0.7 0.0 copy-start.11
  0.7 0.0 copy-start.10
  0.7 2.5 %shard_map.149 = (f32[456,128]{1,0:T(8,128)}, f32[456,128]{1,0:T(8,128)}) custom-call(s32[1]{0:T(128)} %bitcast.core, f32[72,32,128]{2,1,0:T(8,128)} %sky.1, f32[4,32,128]{2,1,0:T(8,128)} %forcing.1, f32[32,128]{1,0:T(8,128)} %surface.3, f32[32,128]{1,0:T(8,128)} %rate.3, f32[992,128]{1,0:T(8,128)} %bitcast.17, f32[992,128]{1,0:T(8,128)} %bitcast.19, ...), custom_call_target="tpu_custom_call" | custom-call | bytes 4194304 | tf_op jit(solution)/shard_map/pallas_call | solution.py:27
  3.2 0.7 %collective-permute-start = (f32[456,128]{1,0:T(8,128)}, f32[456,128]{1,0:T(8,128)S(1)}, u32[]{:S(2)}, u32[]{:S(2)}) collective-permute-start(f32[456,128]{1,0:T(8,128)} %get-tuple-element.29), channel_id=1, source_target_pairs={{1,2},{2,1},{3,4},{4,3},{5,6},{6,5},{7,8},{8,7},{9,10},{10,9},{11,... | collective-permute-start | bytes 700424 | tf_op jit(solution)/shard_map/ppermute | solution.py:433
  3.9 4.4 %collective-permute-start.1 = (f32[456,128]{1,0:T(8,128)}, f32[456,128]{1,0:T(8,128)S(1)}, u32[]{:S(2)}, u32[]{:S(2)}) collective-permute-start(f32[456,128]{1,0:T(8,128)} %get-tuple-element.30), channel_id=1, source_target_pairs={{0,1},{1,0},{2,3},{3,2},{4,5},{5,4},{6,7},{7,6},{8,9},{9,8},{10,11... | collective-permute-start | bytes 700424 | tf_op jit(solution)/shard_map/ppermute | solution.py:434
  8.3 0.0 copy-done
  8.3 0.0 copy-start.3
  8.3 0.0 copy-start.4
  8.3 0.0 copy-start.6
  8.3 0.0 copy-start.7
  8.4 0.0 copy-start.8
  8.4 0.0 copy-start.9
  8.4 5.5 %shard_map.148 = (f32[216,128]{1,0:T(8,128)S(1)}, f32[8,128]{1,0:T(8,128)S(1)}, f32[96,128]{1,0:T(8,128)S(1)}, bf16[80,256]{1,0:T(8,128)(2,1)S(1)}, bf16[64,256]...) custom-call(s32[1]{0:T(128)} %bitcast.4.place, ...), custom_call_target="tpu_custom_call" | custom-call | flops 4294967296 | bytes 8388608 | tf_op jit(solution)/shard_map/pallas_call | solution.py:27
  13.9 0.0 collective-permute-done.outer
  13.9 0.0 collective-permute-done.1.inner
  14.0 0.7 %shard_map.150 = (f32[32,128]{1,0:T(8,128)S(1)}, f32[32,128]{1,0:T(8,128)S(1)}, f32[32,128]{1,0:T(8,128)S(1)}, f32[32,128]{1,0:T(8,128)S(1)}, f32[320,128]{1,0:T...) custom-call(s32[1]{0:T(128)} %bitcast.core, s32[1]{0:T(128)} %bitcast.1.tile, ...), custom_call_target="tpu_custom_call" | custom-call | bytes 2097152 | tf_op jit(solution)/shard_map/pallas_call | solution.py:27
  14.7 2.7 %collective-permute-start.2 = (f32[32,128]{1,0:T(8,128)S(1)}, f32[32,128]{1,0:T(8,128)S(1)}, u32[]{:S(2)}, u32[]{:S(2)}) collective-permute-start(f32[32,128]{1,0:T(8,128)S(1)} %get-tuple-element.37), channel_id=1, source_target_pairs={{0,8},{2,10},{4,12},{6,14},{8,0},{10,2},{12,4},{14,6},{1,9},{3,11}... | collective-permute-start | bytes 49160 | tf_op jit(solution)/shard_map/ppermute | solution.py:476
  17.4 1.3 %collective-permute-start.3 = (f32[32,128]{1,0:T(8,128)S(1)}, f32[32,128]{1,0:T(8,128)S(1)}, u32[]{:S(2)}, u32[]{:S(2)}) collective-permute-start(f32[32,128]{1,0:T(8,128)S(1)} %get-tuple-element.38), channel_id=1, source_target_pairs={{0,12},{2,14},{4,8},{6,10},{8,4},{10,6},{12,0},{14,2},{1,13},{3,15... | collective-permute-start | bytes 49160 | tf_op jit(solution)/shard_map/ppermute | solution.py:476
  18.7 0.2 collective-permute-start.4
  18.9 2.3 %shard_map.151.others_3_.spread = f32[2560,128]{1,0:T(8,128)S(1)} custom-call(f32[320,128]{1,0:T(8,128)S(1)} %get-tuple-element.31.fluxes, f32[2304,128]{1,0:T(8,128)S(1)} %get-tuple-element.32.own, f32[456,128]{1,0:T(8,128)S(1)} %get-tuple-element.33.above, f32[456,128]{1,0:T(8,128)S(1)} %get-tuple-element.34.below, f32[32,128]{1,0:T(8,128)S(1)} %get-tuple-element.35.after.keep), custom_call_target="tpu_custom_call" | custom-call | flops 268435456 | bytes 4194304 | tf_op jit(solution)/shard_map/pallas_call | solution.py:27
  21.2 0.0 collective-permute-done.2.others_0_
  21.2 1.7 %collective-permute-done.3.others_1_ = f32[32,128]{1,0:T(8,128)S(1)} collective-permute-done((f32[32,128]{1,0:T(8,128)S(1)}, f32[32,128]{1,0:T(8,128)S(1)}, u32[]{:S(2)}, u32[]{:S(2)}) %collective-permute-start.3) | collective-permute-done | bytes 16416 | tf_op jit(solution)/shard_map/ppermute | solution.py:476
  22.9 0.0 collective-permute-done.4.others_2_
  22.9 2.3 %collective-permute-start.5 = (f32[16,128]{1,0:T(8,128)S(1)}, f32[16,128]{1,0:T(8,128)S(1)}, u32[]{:S(2)}, u32[]{:S(2)}) collective-permute-start(f32[16,128]{1,0:T(8,128)S(1)} %get-tuple-element.41), channel_id=1, source_target_pairs={{0,2},{2,0},{4,6},{6,4},{8,10},{10,8},{12,14},{14,12},{1,3},{3,1},... | collective-permute-start | bytes 24584 | tf_op jit(solution)/shard_map/ppermute | solution.py:485
  25.3 1.3 %shard_map.153 = f32[72,4,8,128]{3,2,1,0:T(8,128)} custom-call(f32[2560,128]{1,0:T(8,128)S(1)} %shard_map.151.others_3_.spread, bf16[80,256]{1,0:T(8,128)(2,1)S(1)} %get-tuple-element.36.weights, f32[16,128]{1,0:T(8,128)S(1)} %get-tuple-element.40.after.kept), custom_call_target="tpu_custom_call" | custom-call | flops 2147483648 | bytes 4194304 | tf_op jit(solution)/shard_map/pallas_call | solution.py:27
  26.6 1.0 %shard_map.154 = (f32[992,128]{1,0:T(8,128)S(1)}, f32[992,128]{1,0:T(8,128)}) custom-call(bf16[64,256]{1,0:T(8,128)(2,1)S(1)} %get-tuple-element.43.sea_weights, f32[256,128]{1,0:T(8,128)S(1)} %get-tuple-element.44.sea_ends, s32[16,128]{1,0:T(8,128)S(1)} %copy-done.5, f32[992,128]{1,0:T(8,128)S(1)} %get-tuple-element.45.warm, ...), custom_call_target="tpu_custom_call" | custom-call | flops 268435456 | bytes 4194304 | tf_op jit(solution)/shard_map/pallas_call | solution.py:27
  27.6 0.0 collective-permute-done.5.got
  27.6 0.8 %shard_map.155 = f32[992,128]{1,0:T(8,128)} custom-call(f32[16,128]{1,0:T(8,128)S(1)} %get-tuple-element.40.after.kept, f32[16,128]{1,0:T(8,128)S(1)} %collective-permute-done.5.got, s32[16,128]{1,0:T(8,128)S(1)} %copy-done.5, f32[64,128]{1,0:T(8,128)S(1)} %get-tuple-element.42.sea_first, f32[992,128]{1,0:T(8,128)S(1)} %get-tuple-element.47.before), custom_call_target="tpu_custom_call" | custom-call | bytes 2097152 | tf_op jit(solution)/shard_map/pallas_call | solution.py:27
  (15 shorter events, 0.0 us)
Async XLA Ops:
  0.6 7.6 %copy-start.5 = (s32[16,128]{1,0:T(8,128)S(1)}, s32[16,128]{1,0:T(8,128)}, u32[]{:S(2)}) copy-start(s32[16,128]{1,0:T(8,128)} %wet.7) | copy-start | bytes 24580
  0.6 7.6 %copy-start = (f32[72,32,128]{2,1,0:T(8,128)S(1)}, f32[72,32,128]{2,1,0:T(8,128)}, u32[]{:S(2)}) copy-start(f32[72,32,128]{2,1,0:T(8,128)} %sky.1) | copy-start | bytes 3538948
  0.7 7.6 %copy-start.2 = (f32[62,16,128]{2,1,0:T(8,128)S(1)}, f32[62,16,128]{2,1,0:T(8,128)}, u32[]{:S(2)}) copy-start(f32[62,16,128]{2,1,0:T(8,128)} %param.23) | copy-start | bytes 1523716
  0.7 7.6 %copy-start.1 = (f32[62,16,128]{2,1,0:T(8,128)S(1)}, f32[62,16,128]{2,1,0:T(8,128)}, u32[]{:S(2)}) copy-start(f32[62,16,128]{2,1,0:T(8,128)} %param.22) | copy-start | bytes 1523716
  0.7 7.6 %copy-start.11 = (f32[62,62]{1,0:T(8,128)S(1)}, f32[62,62]{1,0:T(8,128)}, u32[]{:S(2)}) copy-start(f32[62,62]{1,0:T(8,128)} %sea_mix.1) | copy-start | bytes 46132
  0.7 7.6 %copy-start.10 = (f32[72,72]{1,0:T(8,128)S(1)}, f32[72,72]{1,0:T(8,128)}, u32[]{:S(2)}) copy-start(f32[72,72]{1,0:T(8,128)} %vmix.1) | copy-start | bytes 62212
  0.7 7.6 %copy-start.12 = (f32[72]{0:T(128)S(1)}, f32[72]{0:T(128)}, u32[]{:S(2)}) copy-start(f32[72]{0:T(128)} %param.15) | copy-start | bytes 868
  3.2 10.7 %collective-permute-start = (f32[456,128]{1,0:T(8,128)}, f32[456,128]{1,0:T(8,128)S(1)}, u32[]{:S(2)}, u32[]{:S(2)}) collective-permute-start(f32[456,128]{1,0:T(8,128)} %get-tuple-element.29), channel_id=1, source_target_pairs={{1,2},{2,1},{3,4},{4,3},{5,6},{6,5},{7,8},{8,7},{9,10},{10,9},{11,... | collective-permute-start | bytes 700424 | tf_op jit(solution)/shard_map/ppermute | solution.py:433
  3.9 10.0 %collective-permute-start.1 = (f32[456,128]{1,0:T(8,128)}, f32[456,128]{1,0:T(8,128)S(1)}, u32[]{:S(2)}, u32[]{:S(2)}) collective-permute-start(f32[456,128]{1,0:T(8,128)} %get-tuple-element.30), channel_id=1, source_target_pairs={{0,1},{1,0},{2,3},{3,2},{4,5},{5,4},{6,7},{7,6},{8,9},{9,8},{10,11... | collective-permute-start | bytes 700424 | tf_op jit(solution)/shard_map/ppermute | solution.py:434
  8.3 5.6 %copy-start.3 = (f32[4,32,128]{2,1,0:T(8,128)S(1)}, f32[4,32,128]{2,1,0:T(8,128)}, u32[]{:S(2)}) copy-start(f32[4,32,128]{2,1,0:T(8,128)} %forcing.1) | copy-start | bytes 196612
  8.3 5.6 %copy-start.4 = (bf16[4,128,128]{2,1,0:T(8,128)(2,1)S(1)}, bf16[4,128,128]{2,1,0:T(8,128)(2,1)}, u32[]{:S(2)}) copy-start(bf16[4,128,128]{2,1,0:T(8,128)(2,1)} %param.19) | copy-start | bytes 393220
  8.3 5.6 %copy-start.6 = (f32[32,128]{1,0:T(8,128)S(1)}, f32[32,128]{1,0:T(8,128)}, u32[]{:S(2)}) copy-start(f32[32,128]{1,0:T(8,128)} %surface.3) | copy-start | bytes 49156
  8.3 5.6 %copy-start.7 = (f32[32,128]{1,0:T(8,128)S(1)}, f32[32,128]{1,0:T(8,128)}, u32[]{:S(2)}) copy-start(f32[32,128]{1,0:T(8,128)} %rate.3) | copy-start | bytes 49156
  8.4 5.6 %copy-start.8 = (s32[32,4]{0,1:T(4,128)S(1)}, s32[32,4]{0,1:T(4,128)}, u32[]{:S(2)}) copy-start(s32[32,4]{0,1:T(4,128)} %param.20) | copy-start | bytes 1540
  8.4 5.6 %copy-start.9 = (s32[32,4]{0,1:T(4,128)S(1)}, s32[32,4]{0,1:T(4,128)}, u32[]{:S(2)}) copy-start(s32[32,4]{0,1:T(4,128)} %param.21) | copy-start | bytes 1540
  14.7 6.5 %collective-permute-start.2 = (f32[32,128]{1,0:T(8,128)S(1)}, f32[32,128]{1,0:T(8,128)S(1)}, u32[]{:S(2)}, u32[]{:S(2)}) collective-permute-start(f32[32,128]{1,0:T(8,128)S(1)} %get-tuple-element.37), channel_id=1, source_target_pairs={{0,8},{2,10},{4,12},{6,14},{8,0},{10,2},{12,4},{14,6},{1,9},{3,11}... | collective-permute-start | bytes 49160 | tf_op jit(solution)/shard_map/ppermute | solution.py:476
  17.4 5.6 %collective-permute-start.3 = (f32[32,128]{1,0:T(8,128)S(1)}, f32[32,128]{1,0:T(8,128)S(1)}, u32[]{:S(2)}, u32[]{:S(2)}) collective-permute-start(f32[32,128]{1,0:T(8,128)S(1)} %get-tuple-element.38), channel_id=1, source_target_pairs={{0,12},{2,14},{4,8},{6,10},{8,4},{10,6},{12,0},{14,2},{1,13},{3,15... | collective-permute-start | bytes 49160 | tf_op jit(solution)/shard_map/ppermute | solution.py:476
  18.7 4.2 %collective-permute-start.4 = (f32[32,128]{1,0:T(8,128)S(1)}, f32[32,128]{1,0:T(8,128)S(1)}, u32[]{:S(2)}, u32[]{:S(2)}) collective-permute-start(f32[32,128]{1,0:T(8,128)S(1)} %get-tuple-element.39), channel_id=1, source_target_pairs={{0,4},{2,6},{4,0},{6,2},{8,12},{10,14},{12,8},{14,10},{1,5},{3,7},... | collective-permute-start | bytes 49160 | tf_op jit(solution)/shard_map/ppermute | solution.py:476
  22.9 4.7 %collective-permute-start.5 = (f32[16,128]{1,0:T(8,128)S(1)}, f32[16,128]{1,0:T(8,128)S(1)}, u32[]{:S(2)}, u32[]{:S(2)}) collective-permute-start(f32[16,128]{1,0:T(8,128)S(1)} %get-tuple-element.41), channel_id=1, source_target_pairs={{0,2},{2,0},{4,6},{6,4},{8,10},{10,8},{12,14},{14,12},{1,3},{3,1},... | collective-permute-start | bytes 24584 | tf_op jit(solution)/shard_map/ppermute | solution.py:485

commit v15 on v11

--- a/solution.py
+++ b/solution.py
@@ -272,7 +272,8 @@
         total = total + flux[s][:rows]
     mean = (total / steps).astype(bf16)
     topk = owners.shape[0]
-    target = (owners[...] ^ tile[0]) * sea_rows + locals_[...]
+    other = owners[...] ^ tile[0]
+    target = (other & 1) * keep.shape[0] + (other >> 1) * sea_rows + locals_[...]
     target = jnp.concatenate([target[k : k + 1, :] for k in range(topk)], 1)
     rowed = jnp.concatenate(
         [jnp.dot(mean, shares[k * width : (k + 1) * width, :], preferred_element_type=f32) for k in range(topk)], 0
@@ -380,15 +381,16 @@
         move.wait()
 
 
-def add_kernel(keep, got, after, kept, send):
-    n = kept.shape[0]
-    kept[...] = keep[:n] + got[:n]
-    send[...] = keep[n:] + got[n:]
-
-
-def heat_kernel(sizes, kept, got, wet, sea_first, before, after):
-    levels, rows, steps, sea_levels, sea_rows, stride, sea_stride = sizes
-    heat = kept[...] + got[...]
+def add_kernel(keep, got, after, *parts):
+    total = keep[...] + got[...]
+    n = parts[0].shape[0]
+    for q, part in enumerate(parts):
+        part[...] = total[q * n : (q + 1) * n]
+
+
+def heat_kernel(sizes, kept, got_1, got_2, got_3, wet, sea_first, before, after):
+    levels, rows, steps, sea_levels, sea_rows, stride, sea_stride = sizes
+    heat = kept[...] + got_1[...] + got_2[...] + got_3[...]
     heat = wet[...].astype(f32) * heat
     for l in range(sea_levels):
         after[l * sea_rows : (l + 1) * sea_rows, :] = (
@@ -448,7 +450,7 @@
     half = tiles // 2 * sea_rows
     keep, send, fluxes, above, below = call(
         functools.partial(flux_kernel, sizes),
-        [flat(half), flat(half), flat(2 * steps * (rows + 2 * HALO)), flat(length), flat(length)],
+        [flat(half)] * 2 + [flat(2 * steps * (rows + 2 * HALO)), flat(length), flat(length)],
         core, tile, sky[-1], forcing2, surface, rate, rows_of_mix, source_rows, own, owners.T, locals_.T,
         shares.reshape(-1, width), outer, inner,
         in_specs=[SMEM] * 2 + [VMEM] * 12, scratch=[space(2 * HALO * stride, width)], moved=2 << 20,
@@ -467,31 +469,24 @@
             scratch=[space(area, width), pltpu.SemaphoreType.DMA((1,))], flops=1 << 28, moved=4 << 20,
         )
 
-    bit, ready, shore = tiles // 2, None, None
-    while True:
-        got = lax.ppermute(send, "tile", [(i, i ^ bit) for i in range(tiles)])
-        if bit <= 4 and ready is None:
-            ready = edge_part(keep)
-            done = ready
-        elif ready is not None and shore is None:
-            shore = shore_part(keep)
-            done = shore[0]
-        else:
-            done = keep
-        if bit == 1:
-            break
-        keep, send = call(
-            add_kernel, [flat(bit // 2 * sea_rows)] * 2, keep, got, done, in_specs=[VMEM, VMEM, ANY],
-        )
-        bit //= 2
-    warm, salt = shore_part(keep) if shore is None else shore
+    swapped = lambda x, bits: lax.ppermute(x, "tile", [(i, i ^ bits) for i in range(tiles)])
+    got = swapped(send, 1)
+    ready = edge_part(keep)
+    size = tiles // 2
+    while size > 4:
+        keep, send = call(add_kernel, [flat(size // 2 * sea_rows)] * 2, keep, got, ready, in_specs=[VMEM] * 2 + [ANY])
+        got = swapped(send, size)
+        size //= 2
+    keep, *sends = call(add_kernel, [flat(sea_rows)] * 4, keep, got, ready, in_specs=[VMEM] * 2 + [ANY])
+    gots = [swapped(sends[q - 1], 2 * q) for q in (3, 2, 1)]
+    warm, salt = shore_part(keep)
     sky_out = call(
         functools.partial(mix_kernel, sizes), jax.ShapeDtypeStruct((levels, rows // 8, 8, width), f32),
         ready, weights, keep, in_specs=[VMEM, VMEM, ANY], out_specs=HBM,
         scratch=[space(rows // 8, levels, 8, width), pltpu.SemaphoreType.DMA((rows // 8,))],
         flops=2 << 30, moved=4 << 20,
     )
-    warm = call(functools.partial(heat_kernel, sizes), flat(area), keep, got, wet, sea_first, warm, moved=2 << 20)
+    warm = call(functools.partial(heat_kernel, sizes), flat(area), keep, *gots, wet, sea_first, warm, moved=2 << 20)
     return sky_out.reshape(sky.shape), warm.reshape(warmth.shape), salt.reshape(brine.shape)
 
 

time: 28.4 us -> 27.9 us (0.982)
  waiting for transfers between devices: 1.51 us -> 0.76 us
    ppermute x3 -> x4, waiting for transfers between devices: 1.51 us -> 0.75 us  [body(): lax.ppermute(x, 'tile', [(i, i ^ bits) for i in range(tiles)])]
    ppermute x3 -> x4, starting transfers between devices: 6.66 us -> 6.82 us  [body(): lax.ppermute(x, 'tile', [(i, i ^ bits) for i in range(tiles)])]
    pallas_call x9 -> x8, Pallas kernels: 14.1 us -> 14.2 us  [call(): pl.pallas_call(kernel, out_shape=out_shape, in_specs=in_specs or [VMEM] *...]
  transfers between devices with their start and end apart: 5 -> 6, of which waited for: 3 -> 1; matrix products, arithmetic and copies ran while one was open for 0% -> 0% of each run, Pallas kernels for 36% -> 37%
where the time goes in v15:
time: 27.9 us; the launch traced here: 27.7 us
  Pallas kernels  14.2 us (51%)
  starting transfers between devices  11.8 us (42%)
  between operations  0.91 us (3%)
  waiting for transfers between devices  0.76 us (3%)
    pallas_call x8, Pallas kernels, call(): pl.pallas_call(kernel, out_shape=out_shape, in_specs=in_specs or [VMEM] *...  14.2 us
    ppermute x4, starting transfers between devices, body(): lax.ppermute(x, 'tile', [(i, i ^ bits) for i in range(tiles)])  6.82 us
    ppermute x1, starting transfers between devices, body(): inner = lax.ppermute(inner, ring, swap(0))  4.35 us
    ppermute x4, waiting for transfers between devices, body(): lax.ppermute(x, 'tile', [(i, i ^ bits) for i in range(tiles)])  0.75 us
    ppermute x1, starting transfers between devices, body(): outer = lax.ppermute(outer, ring, swap(1))  0.68 us
  transfers between devices with their start and end apart: 6, of which 1 were waited for; matrix products, arithmetic and copies ran while one was open for 0% of the time, Pallas kernels for 37%

profile of v15, /device:TPU:0, one launch (start us, length us, event | category | flops | bytes accessed | tf_op | source)
XLA Modules:
  0.0 27.7 jit_solution(17307287092328507300)
XLA Ops:
  0.6 0.0 copy-start.5
  0.6 0.0 copy-start
  0.7 0.0 copy-start.2
  0.7 0.0 copy-start.1
  0.7 0.0 copy-start.11
  0.7 0.0 copy-start.10
  0.7 2.5 %shard_map.149 = (f32[456,128]{1,0:T(8,128)}, f32[456,128]{1,0:T(8,128)}) custom-call(s32[1]{0:T(128)} %bitcast.core, f32[72,32,128]{2,1,0:T(8,128)} %sky.1, f32[4,32,128]{2,1,0:T(8,128)} %forcing.1, f32[32,128]{1,0:T(8,128)} %surface.3, f32[32,128]{1,0:T(8,128)} %rate.3, f32[992,128]{1,0:T(8,128)} %bitcast.17, f32[992,128]{1,0:T(8,128)} %bitcast.19, ...), custom_call_target="tpu_custom_call" | custom-call | bytes 4194304 | tf_op jit(solution)/shard_map/pallas_call | solution.py:27
  3.2 0.7 %collective-permute-start = (f32[456,128]{1,0:T(8,128)}, f32[456,128]{1,0:T(8,128)S(1)}, u32[]{:S(2)}, u32[]{:S(2)}) collective-permute-start(f32[456,128]{1,0:T(8,128)} %get-tuple-element.29), channel_id=1, source_target_pairs={{1,2},{2,1},{3,4},{4,3},{5,6},{6,5},{7,8},{8,7},{9,10},{10,9},{11,... | collective-permute-start | bytes 700424 | tf_op jit(solution)/shard_map/ppermute | solution.py:431
  3.9 4.4 %collective-permute-start.1 = (f32[456,128]{1,0:T(8,128)}, f32[456,128]{1,0:T(8,128)S(1)}, u32[]{:S(2)}, u32[]{:S(2)}) collective-permute-start(f32[456,128]{1,0:T(8,128)} %get-tuple-element.30), channel_id=1, source_target_pairs={{0,1},{1,0},{2,3},{3,2},{4,5},{5,4},{6,7},{7,6},{8,9},{9,8},{10,11... | collective-permute-start | bytes 700424 | tf_op jit(solution)/shard_map/ppermute | solution.py:432
  8.3 0.0 copy-done.2
  8.3 0.0 copy-start.3
  8.3 0.0 copy-start.4
  8.3 0.0 copy-start.6
  8.3 0.0 copy-start.7
  8.4 0.0 copy-start.8
  8.4 0.0 copy-start.9
  8.4 5.5 %shard_map.148 = (f32[216,128]{1,0:T(8,128)S(1)}, f32[8,128]{1,0:T(8,128)S(1)}, f32[96,128]{1,0:T(8,128)S(1)}, bf16[80,256]{1,0:T(8,128)(2,1)S(1)}, bf16[64,256]...) custom-call(s32[1]{0:T(128)} %bitcast.4.place, ...), custom_call_target="tpu_custom_call" | custom-call | flops 4294967296 | bytes 8388608 | tf_op jit(solution)/shard_map/pallas_call | solution.py:27
  13.9 0.0 collective-permute-done.outer
  13.9 0.0 collective-permute-done.1.inner
  14.0 0.7 %shard_map.150 = (f32[64,128]{1,0:T(8,128)S(1)}, f32[64,128]{1,0:T(8,128)S(1)}, f32[320,128]{1,0:T(8,128)S(1)}, f32[456,128]{1,0:T(8,128)S(1)}, f32[456,128]{1,0:T(8,128)S(1)}) custom-call(s32[1]{0:T(128)} %bitcast.core, s32[1]{0:T(128)} %bitcast.1.tile, f32[32,128]{1,0:T(8,128)S(1)} %slice_bitcast_fusion.sky, f32[128,128]{1,0:T(8,128)S(1)} %bitcast.21, ...), custom_call_target="tpu_custom_call" | custom-call | bytes 2097152 | tf_op jit(solution)/shard_map/pallas_call | solution.py:27
  14.7 2.4 %collective-permute-start.2 = (f32[64,128]{1,0:T(8,128)S(1)}, f32[64,128]{1,0:T(8,128)S(1)}, u32[]{:S(2)}, u32[]{:S(2)}) collective-permute-start(f32[64,128]{1,0:T(8,128)S(1)} %get-tuple-element.37), channel_id=1, source_target_pairs={{0,2},{2,0},{4,6},{6,4},{8,10},{10,8},{12,14},{14,12},{1,3},{3,1},... | collective-permute-start | bytes 98312 | tf_op jit(solution)/shard_map/ppermute | solution.py:472
  17.1 2.3 %shard_map.151.after.spread = f32[2560,128]{1,0:T(8,128)S(1)} custom-call(f32[320,128]{1,0:T(8,128)S(1)} %get-tuple-element.31.fluxes, f32[2304,128]{1,0:T(8,128)S(1)} %get-tuple-element.32.own, f32[456,128]{1,0:T(8,128)S(1)} %get-tuple-element.33.above, f32[456,128]{1,0:T(8,128)S(1)} %get-tuple-element.34.below, f32[64,128]{1,0:T(8,128)S(1)} %get-tuple-element.35.after.keep), custom_call_target="tpu_custom_call" | custom-call | flops 268435456 | bytes 4194304 | tf_op jit(solution)/shard_map/pallas_call | solution.py:27
  19.3 0.0 collective-permute-done.2.got
  19.4 3.0 %collective-permute-start.3 = (f32[16,128]{1,0:T(8,128)S(1)}, f32[16,128]{1,0:T(8,128)S(1)}, u32[]{:S(2)}, u32[]{:S(2)}) collective-permute-start(f32[16,128]{1,0:T(8,128)S(1)} %get-tuple-element.39), channel_id=1, source_target_pairs={{0,12},{2,14},{4,8},{6,10},{8,4},{10,6},{12,0},{14,2},{1,13},{3,15... | collective-permute-start | bytes 24584 | tf_op jit(solution)/shard_map/ppermute | solution.py:472
  22.4 0.1 collective-permute-start.4
  22.5 1.3 %collective-permute-start.5 = (f32[16,128]{1,0:T(8,128)S(1)}, f32[16,128]{1,0:T(8,128)S(1)}, u32[]{:S(2)}, u32[]{:S(2)}) collective-permute-start(f32[16,128]{1,0:T(8,128)S(1)} %get-tuple-element.41), channel_id=1, source_target_pairs={{0,4},{2,6},{4,0},{6,2},{8,12},{10,14},{12,8},{14,10},{1,5},{3,7},... | collective-permute-start | bytes 24584 | tf_op jit(solution)/shard_map/ppermute | solution.py:472
  23.8 1.3 %shard_map.153 = f32[72,4,8,128]{3,2,1,0:T(8,128)} custom-call(f32[2560,128]{1,0:T(8,128)S(1)} %shard_map.151.after.spread, bf16[80,256]{1,0:T(8,128)(2,1)S(1)} %get-tuple-element.36.weights, f32[16,128]{1,0:T(8,128)S(1)} %get-tuple-element.38.after.kept), custom_call_target="tpu_custom_call" | custom-call | flops 2147483648 | bytes 4194304 | tf_op jit(solution)/shard_map/pallas_call | solution.py:27
  25.1 1.0 %shard_map.154 = (f32[992,128]{1,0:T(8,128)S(1)}, f32[992,128]{1,0:T(8,128)}) custom-call(bf16[64,256]{1,0:T(8,128)(2,1)S(1)} %get-tuple-element.43.sea_weights, f32[256,128]{1,0:T(8,128)S(1)} %get-tuple-element.44.sea_ends, s32[16,128]{1,0:T(8,128)S(1)} %copy-done.5, f32[992,128]{1,0:T(8,128)S(1)} %get-tuple-element.45.warm, ...), custom_call_target="tpu_custom_call" | custom-call | flops 268435456 | bytes 4194304 | tf_op jit(solution)/shard_map/pallas_call | solution.py:27
  26.2 0.0 collective-permute-done.3.got_1
  26.2 0.7 %collective-permute-done.4.got_2 = f32[16,128]{1,0:T(8,128)S(1)} collective-permute-done((f32[16,128]{1,0:T(8,128)S(1)}, f32[16,128]{1,0:T(8,128)S(1)}, u32[]{:S(2)}, u32[]{:S(2)}) %collective-permute-start.4) | collective-permute-done | bytes 8224 | tf_op jit(solution)/shard_map/ppermute | solution.py:472
  26.9 0.0 collective-permute-done.5.got_3
  26.9 0.8 %shard_map.155 = f32[992,128]{1,0:T(8,128)} custom-call(f32[16,128]{1,0:T(8,128)S(1)} %get-tuple-element.38.after.kept, f32[16,128]{1,0:T(8,128)S(1)} %collective-permute-done.3.got_1, f32[16,128]{1,0:T(8,128)S(1)} %collective-permute-done.4.got_2, f32[16,128]{1,0:T(8,128)S(1)} %collective-permute-done.5.got_3, s32[16,128]{1,0:T(8,128)S(1)} %copy-done.5, ...), custom_call_target="tpu_custom_call" | custom-call | bytes 2097152 | tf_op jit(solution)/shard_map/pallas_call | solution.py:27
  (15 shorter events, 0.0 us)
Async XLA Ops:
  0.6 7.6 %copy-start.5 = (s32[16,128]{1,0:T(8,128)S(1)}, s32[16,128]{1,0:T(8,128)}, u32[]{:S(2)}) copy-start(s32[16,128]{1,0:T(8,128)} %wet.7) | copy-start | bytes 24580
  0.6 7.6 %copy-start = (f32[72,32,128]{2,1,0:T(8,128)S(1)}, f32[72,32,128]{2,1,0:T(8,128)}, u32[]{:S(2)}) copy-start(f32[72,32,128]{2,1,0:T(8,128)} %sky.1) | copy-start | bytes 3538948
  0.7 7.6 %copy-start.2 = (f32[62,16,128]{2,1,0:T(8,128)S(1)}, f32[62,16,128]{2,1,0:T(8,128)}, u32[]{:S(2)}) copy-start(f32[62,16,128]{2,1,0:T(8,128)} %param.23) | copy-start | bytes 1523716
  0.7 7.6 %copy-start.1 = (f32[62,16,128]{2,1,0:T(8,128)S(1)}, f32[62,16,128]{2,1,0:T(8,128)}, u32[]{:S(2)}) copy-start(f32[62,16,128]{2,1,0:T(8,128)} %param.22) | copy-start | bytes 1523716
  0.7 7.6 %copy-start.11 = (f32[62,62]{1,0:T(8,128)S(1)}, f32[62,62]{1,0:T(8,128)}, u32[]{:S(2)}) copy-start(f32[62,62]{1,0:T(8,128)} %sea_mix.1) | copy-start | bytes 46132
  0.7 7.6 %copy-start.10 = (f32[72,72]{1,0:T(8,128)S(1)}, f32[72,72]{1,0:T(8,128)}, u32[]{:S(2)}) copy-start(f32[72,72]{1,0:T(8,128)} %vmix.1) | copy-start | bytes 62212
  0.7 7.6 %copy-start.12 = (f32[72]{0:T(128)S(1)}, f32[72]{0:T(128)}, u32[]{:S(2)}) copy-start(f32[72]{0:T(128)} %param.15) | copy-start | bytes 868
  3.2 10.7 %collective-permute-start = (f32[456,128]{1,0:T(8,128)}, f32[456,128]{1,0:T(8,128)S(1)}, u32[]{:S(2)}, u32[]{:S(2)}) collective-permute-start(f32[456,128]{1,0:T(8,128)} %get-tuple-element.29), channel_id=1, source_target_pairs={{1,2},{2,1},{3,4},{4,3},{5,6},{6,5},{7,8},{8,7},{9,10},{10,9},{11,... | collective-permute-start | bytes 700424 | tf_op jit(solution)/shard_map/ppermute | solution.py:431
  3.9 10.0 %collective-permute-start.1 = (f32[456,128]{1,0:T(8,128)}, f32[456,128]{1,0:T(8,128)S(1)}, u32[]{:S(2)}, u32[]{:S(2)}) collective-permute-start(f32[456,128]{1,0:T(8,128)} %get-tuple-element.30), channel_id=1, source_target_pairs={{0,1},{1,0},{2,3},{3,2},{4,5},{5,4},{6,7},{7,6},{8,9},{9,8},{10,11... | collective-permute-start | bytes 700424 | tf_op jit(solution)/shard_map/ppermute | solution.py:432
  8.3 5.6 %copy-start.3 = (f32[4,32,128]{2,1,0:T(8,128)S(1)}, f32[4,32,128]{2,1,0:T(8,128)}, u32[]{:S(2)}) copy-start(f32[4,32,128]{2,1,0:T(8,128)} %forcing.1) | copy-start | bytes 196612
  8.3 5.6 %copy-start.4 = (bf16[4,128,128]{2,1,0:T(8,128)(2,1)S(1)}, bf16[4,128,128]{2,1,0:T(8,128)(2,1)}, u32[]{:S(2)}) copy-start(bf16[4,128,128]{2,1,0:T(8,128)(2,1)} %param.19) | copy-start | bytes 393220
  8.3 5.6 %copy-start.6 = (f32[32,128]{1,0:T(8,128)S(1)}, f32[32,128]{1,0:T(8,128)}, u32[]{:S(2)}) copy-start(f32[32,128]{1,0:T(8,128)} %surface.3) | copy-start | bytes 49156
  8.3 5.6 %copy-start.7 = (f32[32,128]{1,0:T(8,128)S(1)}, f32[32,128]{1,0:T(8,128)}, u32[]{:S(2)}) copy-start(f32[32,128]{1,0:T(8,128)} %rate.3) | copy-start | bytes 49156
  8.4 5.6 %copy-start.8 = (s32[32,4]{0,1:T(4,128)S(1)}, s32[32,4]{0,1:T(4,128)}, u32[]{:S(2)}) copy-start(s32[32,4]{0,1:T(4,128)} %param.20) | copy-start | bytes 1540
  8.4 5.6 %copy-start.9 = (s32[32,4]{0,1:T(4,128)S(1)}, s32[32,4]{0,1:T(4,128)}, u32[]{:S(2)}) copy-start(s32[32,4]{0,1:T(4,128)} %param.21) | copy-start | bytes 1540
  14.7 4.6 %collective-permute-start.2 = (f32[64,128]{1,0:T(8,128)S(1)}, f32[64,128]{1,0:T(8,128)S(1)}, u32[]{:S(2)}, u32[]{:S(2)}) collective-permute-start(f32[64,128]{1,0:T(8,128)S(1)} %get-tuple-element.37), channel_id=1, source_target_pairs={{0,2},{2,0},{4,6},{6,4},{8,10},{10,8},{12,14},{14,12},{1,3},{3,1},... | collective-permute-start | bytes 98312 | tf_op jit(solution)/shard_map/ppermute | solution.py:472
  19.4 6.8 %collective-permute-start.3 = (f32[16,128]{1,0:T(8,128)S(1)}, f32[16,128]{1,0:T(8,128)S(1)}, u32[]{:S(2)}, u32[]{:S(2)}) collective-permute-start(f32[16,128]{1,0:T(8,128)S(1)} %get-tuple-element.39), channel_id=1, source_target_pairs={{0,12},{2,14},{4,8},{6,10},{8,4},{10,6},{12,0},{14,2},{1,13},{3,15... | collective-permute-start | bytes 24584 | tf_op jit(solution)/shard_map/ppermute | solution.py:472
  22.4 4.5 %collective-permute-start.4 = (f32[16,128]{1,0:T(8,128)S(1)}, f32[16,128]{1,0:T(8,128)S(1)}, u32[]{:S(2)}, u32[]{:S(2)}) collective-permute-start(f32[16,128]{1,0:T(8,128)S(1)} %get-tuple-element.40), channel_id=1, source_target_pairs={{0,8},{2,10},{4,12},{6,14},{8,0},{10,2},{12,4},{14,6},{1,9},{3,11}... | collective-permute-start | bytes 24584 | tf_op jit(solution)/shard_map/ppermute | solution.py:472
  22.5 4.4 %collective-permute-start.5 = (f32[16,128]{1,0:T(8,128)S(1)}, f32[16,128]{1,0:T(8,128)S(1)}, u32[]{:S(2)}, u32[]{:S(2)}) collective-permute-start(f32[16,128]{1,0:T(8,128)S(1)} %get-tuple-element.41), channel_id=1, source_target_pairs={{0,4},{2,6},{4,0},{6,2},{8,12},{10,14},{12,8},{14,10},{1,5},{3,7},... | collective-permute-start | bytes 24584 | tf_op jit(solution)/shard_map/ppermute | solution.py:472

commit v16 on v13

--- a/solution.py
+++ b/solution.py
@@ -477,6 +477,7 @@
         for q, x in ((3, send_3), (2, send_2), (1, send_1))
     ]
     ready = edge_part(keep)
+    warm, salt = shore_part(keep)
     while bit > 1:
         bit //= 2
         keep, send = call(
@@ -484,7 +485,6 @@
         )
         gots = [lax.ppermute(send, "tile", [(i, i ^ bit) for i in range(tiles)])]
     got = gots[0]
-    warm, salt = shore_part(keep)
     sky_out = call(
         functools.partial(mix_kernel, sizes), jax.ShapeDtypeStruct((levels, rows // 8, 8, width), f32),
         ready, weights, keep, in_specs=[VMEM, VMEM, ANY], out_specs=HBM,

time: 27.7 us -> 27.7 us (level)
  waiting for transfers between devices: 2.09 us -> 1.05 us
  starting transfers between devices: 10.4 us -> 11.4 us
    ppermute x1, starting transfers between devices: 0.87 us -> 1.92 us  [body(): gots = [lax.ppermute(send, 'tile', [(i, i ^ bit) for i in range(tiles)])]]
    ppermute x3, waiting for transfers between devices: 1.58 us -> 0.56 us  [body(): lax.ppermute(x, 'tile', [(i, i ^ q * bit) for i in range(tiles)])]
  transfers between devices with their start and end apart: 6 -> 6, of which waited for: 2 -> 2; matrix products, arithmetic and copies ran while one was open for 0% -> 0% of each run, Pallas kernels for 37% -> 36%
where the time goes in v16:
time: 27.7 us; the launch traced here: 27.5 us
  Pallas kernels  14.1 us (51%)
  starting transfers between devices  11.4 us (41%)
  waiting for transfers between devices  1.05 us (4%)
  between operations  0.9 us (3%)
    pallas_call x8, Pallas kernels, call(): pl.pallas_call(kernel, out_shape=out_shape, in_specs=in_specs or [VMEM] *...  14.1 us
    ppermute x3, starting transfers between devices, body(): lax.ppermute(x, 'tile', [(i, i ^ q * bit) for i in range(tiles)])  4.45 us
    ppermute x1, starting transfers between devices, body(): inner = lax.ppermute(inner, ring, swap(0))  4.35 us
    ppermute x1, starting transfers between devices, body(): gots = [lax.ppermute(send, 'tile', [(i, i ^ bit) for i in range(tiles)])]  1.92 us
    ppermute x1, starting transfers between devices, body(): outer = lax.ppermute(outer, ring, swap(1))  0.68 us
    ppermute x3, waiting for transfers between devices, body(): lax.ppermute(x, 'tile', [(i, i ^ q * bit) for i in range(tiles)])  0.56 us
  transfers between devices with their start and end apart: 6, of which 2 were waited for; matrix products, arithmetic and copies ran while one was open for 0% of the time, Pallas kernels for 36%

profile of v16, /device:TPU:0, one launch (start us, length us, event | category | flops | bytes accessed | tf_op | source)
XLA Modules:
  0.0 27.5 jit_solution(4442981139799996830)
XLA Ops:
  0.7 2.5 %shard_map.149 = (f32[456,128]{1,0:T(8,128)}, f32[456,128]{1,0:T(8,128)}) custom-call(s32[1]{0:T(128)} %bitcast.core, f32[72,32,128]{2,1,0:T(8,128)} %sky.1, f32[4,32,128]{2,1,0:T(8,128)} %forcing.1, f32[32,128]{1,0:T(8,128)} %surface.3, f32[32,128]{1,0:T(8,128)} %rate.3, f32[992,128]{1,0:T(8,128)} %bitcast.17, f32[992,128]{1,0:T(8,128)} %bitcast.19, ...), custom_call_target="tpu_custom_call" | custom-call | bytes 4194304 | tf_op jit(solution)/shard_map/pallas_call | solution.py:27
  3.2 0.7 %collective-permute-start = (f32[456,128]{1,0:T(8,128)}, f32[456,128]{1,0:T(8,128)S(1)}, u32[]{:S(2)}, u32[]{:S(2)}) collective-permute-start(f32[456,128]{1,0:T(8,128)} %get-tuple-element.29), channel_id=1, source_target_pairs={{1,2},{2,1},{3,4},{4,3},{5,6},{6,5},{7,8},{8,7},{9,10},{10,9},{11,... | collective-permute-start | bytes 700424 | tf_op jit(solution)/shard_map/ppermute | solution.py:433
  3.9 4.4 %collective-permute-start.1 = (f32[456,128]{1,0:T(8,128)}, f32[456,128]{1,0:T(8,128)S(1)}, u32[]{:S(2)}, u32[]{:S(2)}) collective-permute-start(f32[456,128]{1,0:T(8,128)} %get-tuple-element.30), channel_id=1, source_target_pairs={{0,1},{1,0},{2,3},{3,2},{4,5},{5,4},{6,7},{7,6},{8,9},{9,8},{10,11... | collective-permute-start | bytes 700424 | tf_op jit(solution)/shard_map/ppermute | solution.py:434
  8.3 0.0 copy-done.5
  8.3 0.0 copy-done.11
  8.3 0.0 copy-done.10
  8.3 0.0 copy-done.12
  8.3 0.0 copy-start.3
  8.3 0.0 copy-start.4
  8.3 0.0 copy-start.6
  8.3 0.0 copy-start.7
  8.4 0.0 copy-start.8
  8.4 0.0 copy-start.9
  8.4 5.5 %shard_map.148 = (f32[216,128]{1,0:T(8,128)S(1)}, f32[8,128]{1,0:T(8,128)S(1)}, f32[96,128]{1,0:T(8,128)S(1)}, bf16[80,256]{1,0:T(8,128)(2,1)S(1)}, bf16[64,256]...) custom-call(s32[1]{0:T(128)} %bitcast.4.place, ...), custom_call_target="tpu_custom_call" | custom-call | flops 4294967296 | bytes 8388608 | tf_op jit(solution)/shard_map/pallas_call | solution.py:27
  13.9 0.0 collective-permute-done.outer
  13.9 0.0 collective-permute-done.1.inner
  13.9 0.0 copy-done.3
  13.9 0.0 copy-done.4
  13.9 0.0 copy-done.6
  13.9 0.7 %shard_map.150 = (f32[32,128]{1,0:T(8,128)S(1)}, f32[32,128]{1,0:T(8,128)S(1)}, f32[32,128]{1,0:T(8,128)S(1)}, f32[32,128]{1,0:T(8,128)S(1)}, f32[320,128]{1,0:T...) custom-call(s32[1]{0:T(128)} %bitcast.core, s32[1]{0:T(128)} %bitcast.1.tile, ...), custom_call_target="tpu_custom_call" | custom-call | bytes 2097152 | tf_op jit(solution)/shard_map/pallas_call | solution.py:27
  14.6 3.7 %collective-permute-start.2 = (f32[32,128]{1,0:T(8,128)S(1)}, f32[32,128]{1,0:T(8,128)S(1)}, u32[]{:S(2)}, u32[]{:S(2)}) collective-permute-start(f32[32,128]{1,0:T(8,128)S(1)} %get-tuple-element.37), channel_id=1, source_target_pairs={{0,12},{2,14},{4,8},{6,10},{8,4},{10,6},{12,0},{14,2},{1,13},{3,15... | collective-permute-start | bytes 49160 | tf_op jit(solution)/shard_map/ppermute | solution.py:476
  18.3 0.0 collective-permute-start.3
  18.3 0.8 %collective-permute-start.4 = (f32[32,128]{1,0:T(8,128)S(1)}, f32[32,128]{1,0:T(8,128)S(1)}, u32[]{:S(2)}, u32[]{:S(2)}) collective-permute-start(f32[32,128]{1,0:T(8,128)S(1)} %get-tuple-element.39), channel_id=1, source_target_pairs={{0,4},{2,6},{4,0},{6,2},{8,12},{10,14},{12,8},{14,10},{1,5},{3,7},... | collective-permute-start | bytes 49160 | tf_op jit(solution)/shard_map/ppermute | solution.py:476
  19.1 2.3 %shard_map.151.others_3_.spread = f32[2560,128]{1,0:T(8,128)S(1)} custom-call(f32[320,128]{1,0:T(8,128)S(1)} %get-tuple-element.31.fluxes, f32[2304,128]{1,0:T(8,128)S(1)} %get-tuple-element.32.own, f32[456,128]{1,0:T(8,128)S(1)} %get-tuple-element.33.above, f32[456,128]{1,0:T(8,128)S(1)} %get-tuple-element.34.below, f32[32,128]{1,0:T(8,128)S(1)} %get-tuple-element.35.after.keep), custom_call_target="tpu_custom_call" | custom-call | flops 268435456 | bytes 4194304 | tf_op jit(solution)/shard_map/pallas_call | solution.py:27
  21.3 1.0 %shard_map.154 = (f32[992,128]{1,0:T(8,128)S(1)}, f32[992,128]{1,0:T(8,128)}) custom-call(bf16[64,256]{1,0:T(8,128)(2,1)S(1)} %get-tuple-element.43.sea_weights, f32[256,128]{1,0:T(8,128)S(1)} %get-tuple-element.44.sea_ends, s32[16,128]{1,0:T(8,128)S(1)} %copy-done.5, f32[992,128]{1,0:T(8,128)S(1)} %get-tuple-element.45.warm, ...), custom_call_target="tpu_custom_call" | custom-call | flops 268435456 | bytes 4194304 | tf_op jit(solution)/shard_map/pallas_call | solution.py:27
  22.4 0.0 collective-permute-done.2.others_0_
  22.4 0.6 %collective-permute-done.3.others_1_ = f32[32,128]{1,0:T(8,128)S(1)} collective-permute-done((f32[32,128]{1,0:T(8,128)S(1)}, f32[32,128]{1,0:T(8,128)S(1)}, u32[]{:S(2)}, u32[]{:S(2)}) %collective-permute-start.3) | collective-permute-done | bytes 16416 | tf_op jit(solution)/shard_map/ppermute | solution.py:476
  22.9 0.0 collective-permute-done.4.others_2_
  23.0 1.9 %collective-permute-start.5 = (f32[16,128]{1,0:T(8,128)S(1)}, f32[16,128]{1,0:T(8,128)S(1)}, u32[]{:S(2)}, u32[]{:S(2)}) collective-permute-start(f32[16,128]{1,0:T(8,128)S(1)} %get-tuple-element.41), channel_id=1, source_target_pairs={{0,2},{2,0},{4,6},{6,4},{8,10},{10,8},{12,14},{14,12},{1,3},{3,1},... | collective-permute-start | bytes 24584 | tf_op jit(solution)/shard_map/ppermute | solution.py:486
  24.9 1.3 %shard_map.153 = f32[72,4,8,128]{3,2,1,0:T(8,128)} custom-call(f32[2560,128]{1,0:T(8,128)S(1)} %shard_map.151.others_3_.spread, bf16[80,256]{1,0:T(8,128)(2,1)S(1)} %get-tuple-element.36.weights, f32[16,128]{1,0:T(8,128)S(1)} %get-tuple-element.40.after.kept), custom_call_target="tpu_custom_call" | custom-call | flops 2147483648 | bytes 4194304 | tf_op jit(solution)/shard_map/pallas_call | solution.py:27
  26.2 0.5 %collective-permute-done.5.got = f32[16,128]{1,0:T(8,128)S(1)} collective-permute-done((f32[16,128]{1,0:T(8,128)S(1)}, f32[16,128]{1,0:T(8,128)S(1)}, u32[]{:S(2)}, u32[]{:S(2)}) %collective-permute-start.5) | collective-permute-done | bytes 8224 | tf_op jit(solution)/shard_map/ppermute | solution.py:486
  26.7 0.8 %shard_map.155 = f32[992,128]{1,0:T(8,128)} custom-call(f32[16,128]{1,0:T(8,128)S(1)} %get-tuple-element.40.after.kept, f32[16,128]{1,0:T(8,128)S(1)} %collective-permute-done.5.got, s32[16,128]{1,0:T(8,128)S(1)} %copy-done.5, f32[64,128]{1,0:T(8,128)S(1)} %get-tuple-element.42.sea_first, f32[992,128]{1,0:T(8,128)S(1)} %get-tuple-element.47.before), custom_call_target="tpu_custom_call" | custom-call | bytes 2097152 | tf_op jit(solution)/shard_map/pallas_call | solution.py:27
  (15 shorter events, 0.0 us)
Async XLA Ops:
  0.6 7.6 %copy-start.5 = (s32[16,128]{1,0:T(8,128)S(1)}, s32[16,128]{1,0:T(8,128)}, u32[]{:S(2)}) copy-start(s32[16,128]{1,0:T(8,128)} %wet.7) | copy-start | bytes 24580
  0.6 7.6 %copy-start = (f32[72,32,128]{2,1,0:T(8,128)S(1)}, f32[72,32,128]{2,1,0:T(8,128)}, u32[]{:S(2)}) copy-start(f32[72,32,128]{2,1,0:T(8,128)} %sky.1) | copy-start | bytes 3538948
  0.7 7.6 %copy-start.2 = (f32[62,16,128]{2,1,0:T(8,128)S(1)}, f32[62,16,128]{2,1,0:T(8,128)}, u32[]{:S(2)}) copy-start(f32[62,16,128]{2,1,0:T(8,128)} %param.23) | copy-start | bytes 1523716
  0.7 7.6 %copy-start.1 = (f32[62,16,128]{2,1,0:T(8,128)S(1)}, f32[62,16,128]{2,1,0:T(8,128)}, u32[]{:S(2)}) copy-start(f32[62,16,128]{2,1,0:T(8,128)} %param.22) | copy-start | bytes 1523716
  0.7 7.6 %copy-start.11 = (f32[62,62]{1,0:T(8,128)S(1)}, f32[62,62]{1,0:T(8,128)}, u32[]{:S(2)}) copy-start(f32[62,62]{1,0:T(8,128)} %sea_mix.1) | copy-start | bytes 46132
  0.7 7.6 %copy-start.10 = (f32[72,72]{1,0:T(8,128)S(1)}, f32[72,72]{1,0:T(8,128)}, u32[]{:S(2)}) copy-start(f32[72,72]{1,0:T(8,128)} %vmix.1) | copy-start | bytes 62212
  0.7 7.6 %copy-start.12 = (f32[72]{0:T(128)S(1)}, f32[72]{0:T(128)}, u32[]{:S(2)}) copy-start(f32[72]{0:T(128)} %param.15) | copy-start | bytes 868
  3.2 10.6 %collective-permute-start = (f32[456,128]{1,0:T(8,128)}, f32[456,128]{1,0:T(8,128)S(1)}, u32[]{:S(2)}, u32[]{:S(2)}) collective-permute-start(f32[456,128]{1,0:T(8,128)} %get-tuple-element.29), channel_id=1, source_target_pairs={{1,2},{2,1},{3,4},{4,3},{5,6},{6,5},{7,8},{8,7},{9,10},{10,9},{11,... | collective-permute-start | bytes 700424 | tf_op jit(solution)/shard_map/ppermute | solution.py:433
  3.9 10.0 %collective-permute-start.1 = (f32[456,128]{1,0:T(8,128)}, f32[456,128]{1,0:T(8,128)S(1)}, u32[]{:S(2)}, u32[]{:S(2)}) collective-permute-start(f32[456,128]{1,0:T(8,128)} %get-tuple-element.30), channel_id=1, source_target_pairs={{0,1},{1,0},{2,3},{3,2},{4,5},{5,4},{6,7},{7,6},{8,9},{9,8},{10,11... | collective-permute-start | bytes 700424 | tf_op jit(solution)/shard_map/ppermute | solution.py:434
  8.3 5.6 %copy-start.3 = (f32[4,32,128]{2,1,0:T(8,128)S(1)}, f32[4,32,128]{2,1,0:T(8,128)}, u32[]{:S(2)}) copy-start(f32[4,32,128]{2,1,0:T(8,128)} %forcing.1) | copy-start | bytes 196612
  8.3 5.6 %copy-start.4 = (bf16[4,128,128]{2,1,0:T(8,128)(2,1)S(1)}, bf16[4,128,128]{2,1,0:T(8,128)(2,1)}, u32[]{:S(2)}) copy-start(bf16[4,128,128]{2,1,0:T(8,128)(2,1)} %param.19) | copy-start | bytes 393220
  8.3 5.6 %copy-start.6 = (f32[32,128]{1,0:T(8,128)S(1)}, f32[32,128]{1,0:T(8,128)}, u32[]{:S(2)}) copy-start(f32[32,128]{1,0:T(8,128)} %surface.3) | copy-start | bytes 49156
  8.3 5.6 %copy-start.7 = (f32[32,128]{1,0:T(8,128)S(1)}, f32[32,128]{1,0:T(8,128)}, u32[]{:S(2)}) copy-start(f32[32,128]{1,0:T(8,128)} %rate.3) | copy-start | bytes 49156
  8.4 5.6 %copy-start.8 = (s32[32,4]{0,1:T(4,128)S(1)}, s32[32,4]{0,1:T(4,128)}, u32[]{:S(2)}) copy-start(s32[32,4]{0,1:T(4,128)} %param.20) | copy-start | bytes 1540
  8.4 5.6 %copy-start.9 = (s32[32,4]{0,1:T(4,128)S(1)}, s32[32,4]{0,1:T(4,128)}, u32[]{:S(2)}) copy-start(s32[32,4]{0,1:T(4,128)} %param.21) | copy-start | bytes 1540
  14.6 7.7 %collective-permute-start.2 = (f32[32,128]{1,0:T(8,128)S(1)}, f32[32,128]{1,0:T(8,128)S(1)}, u32[]{:S(2)}, u32[]{:S(2)}) collective-permute-start(f32[32,128]{1,0:T(8,128)S(1)} %get-tuple-element.37), channel_id=1, source_target_pairs={{0,12},{2,14},{4,8},{6,10},{8,4},{10,6},{12,0},{14,2},{1,13},{3,15... | collective-permute-start | bytes 49160 | tf_op jit(solution)/shard_map/ppermute | solution.py:476
  18.3 4.6 %collective-permute-start.3 = (f32[32,128]{1,0:T(8,128)S(1)}, f32[32,128]{1,0:T(8,128)S(1)}, u32[]{:S(2)}, u32[]{:S(2)}) collective-permute-start(f32[32,128]{1,0:T(8,128)S(1)} %get-tuple-element.38), channel_id=1, source_target_pairs={{0,8},{2,10},{4,12},{6,14},{8,0},{10,2},{12,4},{14,6},{1,9},{3,11}... | collective-permute-start | bytes 49160 | tf_op jit(solution)/shard_map/ppermute | solution.py:476
  18.3 4.6 %collective-permute-start.4 = (f32[32,128]{1,0:T(8,128)S(1)}, f32[32,128]{1,0:T(8,128)S(1)}, u32[]{:S(2)}, u32[]{:S(2)}) collective-permute-start(f32[32,128]{1,0:T(8,128)S(1)} %get-tuple-element.39), channel_id=1, source_target_pairs={{0,4},{2,6},{4,0},{6,2},{8,12},{10,14},{12,8},{14,10},{1,5},{3,7},... | collective-permute-start | bytes 49160 | tf_op jit(solution)/shard_map/ppermute | solution.py:476
  23.0 3.7 %collective-permute-start.5 = (f32[16,128]{1,0:T(8,128)S(1)}, f32[16,128]{1,0:T(8,128)S(1)}, u32[]{:S(2)}, u32[]{:S(2)}) collective-permute-start(f32[16,128]{1,0:T(8,128)S(1)} %get-tuple-element.41), channel_id=1, source_target_pairs={{0,2},{2,0},{4,6},{6,4},{8,10},{10,8},{12,14},{14,12},{1,3},{3,1},... | collective-permute-start | bytes 24584 | tf_op jit(solution)/shard_map/ppermute | solution.py:486
